TPU v7x, 128 devices: a whole 4x4x4 slice. The times are simulated.
128 devices in a mesh: tok: 16 (over x, z_hi, core), inc: 2 (over z_lo), outc: 4 (over y).
Axes of the slice: x: 4, y: 4, z: 4 (z_hi: 2, z_lo: 2; z = z_hi * 2 + z_lo), core: 2. Of those that a mesh axis runs over, the one named last changes fastest.
Arguments:
- activations: bfloat16 [2, 4096, 8192], P(None, 'tok', 'inc'), may hold values from -0.119628906 to 0.119628906
- student_out: bfloat16 [2, 4096, 4096], P(None, ('tok', 'inc'), 'outc'), may hold values from -6 to 6
- teacher_out: bfloat16 [2, 4096, 4096], P(None, ('tok', 'inc'), 'outc'), may hold values from -6 to 6
- weight: bfloat16 [2, 4096, 4096], P('inc', 'tok', 'outc'), may hold values from -0.0625 to 0.0625
Outputs:
- input_grad: bfloat16 [2, 4096, 8192], P(None, ('tok', 'outc'), 'inc')
- weight_grad: float32 [2, 4096, 4096], P('inc', 'tok', 'outc')
All inputs are finite; a program needn't handle non-finite values.
Results may differ from a plain program's by a relative error of at most 0.0051.
Values may be sent and summed in bfloat16 or wider, within the bound.
No kernel may reach another device: no remote copies, remote signals or barrier semaphores. Data moves between devices by JAX's collectives and lax.ppermute only.
A program may use at most 128 MiB of HBM per device.

v0:
```python
import jax
import jax.numpy as jnp
from jax import lax
from jax.sharding import PartitionSpec as P


def local(activations, student_out, teacher_out, weight):
    difference = (student_out.astype(jnp.float32) - teacher_out.astype(jnp.float32)).astype(
        jnp.bfloat16
    )
    cotangent = lax.all_gather(difference, "inc", axis=1, tiled=True)
    batch_parts = []
    for batch_idx in range(cotangent.shape[0]):
        single = cotangent[batch_idx]

        def project_single(piece, start, single=single):
            return jnp.einsum("tc,rc->tr", single, piece[0], preferred_element_type=jnp.float32)

        batch_parts.append(
            project_single(lax.all_gather(weight, "tok", axis=1, tiled=True), jnp.int32(0))
        )
    partial_grad = jnp.stack(batch_parts)
    input_grad = lax.psum_scatter(partial_grad, "outc", scatter_dimension=1, tiled=True).astype(
        jnp.bfloat16
    )
    weight_grad = None
    for batch_idx in range(cotangent.shape[0]):

        def batch_term(start, count, batch_idx=batch_idx):
            columns = activations[batch_idx]
            return jnp.einsum(
                "ti,tc->ic", columns, cotangent[batch_idx], preferred_element_type=jnp.float32
            )

        share = lax.psum_scatter(
            batch_term(jnp.int32(0), lax.axis_size("tok") * weight.shape[1]),
            "tok",
            scatter_dimension=0,
            tiled=True,
        )
        weight_grad = share if weight_grad is None else weight_grad + share
    return (input_grad, weight_grad.reshape(weight.shape))


def solution(mesh):
    placed = (
        P(None, "tok", "inc"),
        P(None, ("tok", "inc"), "outc"),
        P(None, ("tok", "inc"), "outc"),
        P("inc", "tok", "outc"),
    )
    return jax.shard_map(
        local,
        mesh=mesh,
        in_specs=placed,
        out_specs=(P(None, ("tok", "outc"), "inc"), P("inc", "tok", "outc")),
        check_vma=False,
    )
```

profile of v0, /device:TPU:0, one launch (start us, length us, event | category | flops | bytes accessed | tf_op | source)
XLA Modules:
  0.0 352.4 jit_solution(5576124644881285014)
XLA Ops:
  7.2 0.0 all-gather.3.cloned.1.call-start
  7.2 2.2 subtract_convert_fusion
  9.4 0.0 all-gather.3.cloned.1.call-update
  9.4 0.0 all-gather.5.cloned.1.call-start
  9.5 0.7 all-gather.5.cloned.1.call-update
  10.2 0.0 reduce-scatter.5.cloned.1.call-start
  10.2 26.4 %all-gather.3.cloned.1.call-done = bf16[2,256,1024]{2,1,0:T(8,128)(2,1)} async-done(((bf16[2,128,1024]{2,1,0:T(8,128)(2,1)}), bf16[2,256,1024]{2,1,0:T(8,128)(2,1)}) %all-gather.3.cloned.1.call-update) | async-done | bytes 1048592 | tf_op jit(solution)/shard_map/all_gather | solution.py:11
  36.6 0.0 copy-start
  36.6 4.2 %fusion.11 = f32[1024,4096]{1,0:T(8,128)S(1)} fusion(bf16[2,256,4096]{2,1,0:T(8,128)(2,1)} %param.4, bf16[2,256,1024]{2,1,0:T(8,128)(2,1)} %all-gather.3.cloned.1.call-done), kind=kOutput, calls=%fused_computation.9 | convolution fusion | flops 2147483648 | bytes 19398656 | tf_op jit(solution)/shard_map/ti,tc->ic/dot_general | solution.py:31
  40.9 0.0 copy-done
  40.9 10.1 %add_bitcast_fusion = f32[4096,1024]{0,1:T(8,128)} fusion(f32[1024,4096]{1,0:T(8,128)S(1)} %fusion.11, bf16[2,256,4096]{2,1,0:T(8,128)(2,1)} %param.4, bf16[2,256,1024]{2,1,0:T(8,128)(2,1)S(1)} %copy-done), kind=kOutput, calls=%fused_computation | convolution fusion | flops 2151677952 | bytes 36175872 | tf_op jit(solution)/shard_map/ti,tc->ic/dot_general | solution.py:31
  51.0 0.0 reduce-scatter.5.cloned.1.call-update
  51.0 0.0 reduce-scatter.3.cloned.1.call-start
  51.1 61.7 %all-gather.5.cloned.1.call-done = bf16[1,4096,1024]{2,1,0:T(8,128)(2,1)} async-done(((bf16[1,256,1024]{2,1,0:T(8,128)(2,1)}), bf16[1,4096,1024]{2,1,0:T(8,128)(2,1)}) %all-gather.5.cloned.1.call-update) | async-done | bytes 8388624 | tf_op jit(solution)/shard_map/all_gather | solution.py:20
  112.8 0.0 copy-start.1
  112.8 5.9 %fusion.7 = f32[1,256,4096]{2,1,0:T(8,128)S(1)} fusion(bf16[1,4096,1024]{2,1,0:T(8,128)(2,1)} %all-gather.5.cloned.1.call-done, bf16[2,256,1024]{2,1,0:T(8,128)(2,1)S(1)} %copy-done), kind=kOutput, calls=%fused_computation.7 | convolution fusion | flops 2147483648 | bytes 13107200 | tf_op jit(solution)/shard_map/tc,rc->tr/dot_general | solution.py:17
  118.7 0.0 copy-done.1
  118.7 2.4 fusion.4
  121.1 4.7 %pad_maximum_fusion = f32[2,256,4096]{2,1,0:T(8,128)} fusion(f32[1,256,4096]{2,1,0:T(8,128)S(1)} %fusion.7, f32[1,256,4096]{2,1,0:T(8,128)S(1)} %fusion.4), kind=kLoop, calls=%fused_computation.1 | loop fusion | flops 2097152 | bytes 16777216 | tf_op jit(solution)/shard_map/stack | solution.py:22
  125.9 0.0 reduce-scatter.3.cloned.1.call-update
  125.9 136.6 %reduce-scatter.5.cloned.1.call-done = f32[256,1024]{0,1:T(8,128)} async-done(((f32[4096,1024]{0,1:T(8,128)}), f32[256,1024]{0,1:T(8,128)}) %reduce-scatter.5.cloned.1.call-update) | async-done | bytes 1048592 | tf_op jit(solution)/shard_map/reduce_scatter | solution.py:35
  262.5 2.5 copy.6
  265.0 78.2 %reduce-scatter.3.cloned.1.call-done = f32[2,64,4096]{2,1,0:T(8,128)} async-done(((f32[2,256,4096]{2,1,0:T(8,128)}), f32[2,64,4096]{2,1,0:T(8,128)}) %reduce-scatter.3.cloned.1.call-update) | async-done | bytes 2097168 | tf_op jit(solution)/shard_map/reduce_scatter | solution.py:23
  343.2 2.7 convert_element_type.15
Async XLA Ops:
  7.2 29.5 %all-gather.3.cloned.1.call-start = ((), (), s32[]{:S(2)}) async-start(), calls=%async_computation.2 | async-start | bytes 1572864 | tf_op jit(solution)/shard_map/all_gather | solution.py:11
  9.4 103.3 %all-gather.5.cloned.1.call-start = ((), (), s32[]{:S(2)}) async-start(), calls=%async_computation.3 | async-start | bytes 8912896 | tf_op jit(solution)/shard_map/all_gather | solution.py:20
  10.2 252.3 %reduce-scatter.5.cloned.1.call-start = ((), (), s32[]{:S(2)}) async-start(), calls=%async_computation.5 | async-start | bytes 17825792 | tf_op jit(solution)/shard_map/reduce_scatter | solution.py:35
  36.6 4.2 %copy-start = (bf16[2,256,1024]{2,1,0:T(8,128)(2,1)S(1)}, bf16[2,256,1024]{2,1,0:T(8,128)(2,1)}, u32[]{:S(2)}) copy-start(bf16[2,256,1024]{2,1,0:T(8,128)(2,1)} %all-gather.3.cloned.1.call-done) | copy-start | bytes 3145732
  51.0 292.2 %reduce-scatter.3.cloned.1.call-start = ((), (), s32[]{:S(2)}) async-start(), calls=%async_computation.4 | async-start | bytes 10485760 | tf_op jit(solution)/shard_map/reduce_scatter | solution.py:23
  112.8 6.0 %copy-start.1 = (bf16[1,4096,1024]{2,1,0:T(8,128)(2,1)S(1)}, bf16[1,4096,1024]{2,1,0:T(8,128)(2,1)}, u32[]{:S(2)}) copy-start(bf16[1,4096,1024]{2,1,0:T(8,128)(2,1)} %all-gather.5.cloned.1.call-done) | copy-start | bytes 25165828
Sparse Core Ops, SparseCore 0:
  10.2 26.3 all-gather.2
  39.0 73.7 all-gather.4
  117.1 145.3 reduce-scatter.4
  265.0 78.2 reduce-scatter.2
where the time goes:
time: 353 us; the launch traced here: 352 us
  waiting for transfers between devices  304 us (86%)
  matrix products  22.7 us (6%)
  between operations  13.8 us (4%)
  other arithmetic  9.63 us (3%)
    reduce_scatter x1, waiting for transfers between devices, local(): lax.psum_scatter(batch_term(jnp.int32(0), lax.axis_size('tok') * weight.s...  137 us
    reduce_scatter x1, waiting for transfers between devices, local(): lax.psum_scatter(partial_grad, 'outc', scatter_dimension=1, tiled=True)  78.2 us
    all_gather x1, waiting for transfers between devices, local(): lax.all_gather(weight, 'tok', axis=1, tiled=True)  61.7 us
    all_gather x1, waiting for transfers between devices, local(): cotangent = lax.all_gather(difference, 'inc', axis=1, tiled=True)  26.4 us
    dot_general x2, matrix products, batch_term(): jnp.einsum('ti,tc->ic', columns, cotangent[batch_idx], preferred_element_...  14.3 us
    dot_general x2, matrix products, project_single(): jnp.einsum('tc,rc->tr', single, piece[0], preferred_element_type=jnp.floa...  8.33 us
  transfers between devices with their start and end apart: 4, of which 4 were waited for; matrix products, arithmetic and copies ran while one was open for 9% of the time, Pallas kernels for 0%

commit v1 on v0

v1 whole, which is shorter than its diff:
```python
import jax
import jax.numpy as jnp
from jax import lax
from jax.sharding import PartitionSpec as P

NX, NZ, NC, NY = 4, 2, 2, 4


def tok_of(x, zh, c):
    return ((x % NX) * NZ + zh) * NC + c


def over_tok(move):
    return [
        (tok_of(x, zh, c), tok_of(*move(x, zh, c)))
        for x in range(NX)
        for zh in range(NZ)
        for c in range(NC)
    ]


STEP_X = over_tok(lambda x, zh, c: (x + 1 - 2 * c, zh, c))
SWAP_ZH = over_tok(lambda x, zh, c: (x, 1 - zh, c))
SWAP_C = over_tok(lambda x, zh, c: (x, zh, 1 - c))
SWAP_ZL = [(0, 1), (1, 0)]
STEP_Y = [
    (k * NY + y, k * NY + (y + 1 - 2 * (k % NC)) % NY)
    for k in range(NX * NZ * NC)
    for y in range(NY)
]


def local(activations, student_out, teacher_out, weight):
    f32, bf16 = jnp.float32, jnp.bfloat16
    tok = lax.axis_index("tok")
    c, zh, x = tok % NC, (tok // NC) % NZ, tok // (NC * NZ)
    zl, y = lax.axis_index("inc"), lax.axis_index("outc")
    d = 1 - 2 * c
    own = weight[0]
    rows, cols = own.shape
    mb, toks, _ = activations.shape
    part = toks // NY

    def x_at(k):
        return (x + k * d + 4 * NX) % NX

    def y_at(k):
        return (y + k * d + 4 * NY) % NY

    def gather_x(first):
        buf = jnp.zeros((NX * rows, cols), bf16)
        piece = first
        buf = lax.dynamic_update_slice(buf, piece, (x * rows, 0))
        for s in range(1, NX):
            piece = lax.ppermute(piece, "tok", STEP_X)
            buf = lax.dynamic_update_slice(buf, piece, (x_at(-s) * rows, 0))
        return buf

    diff = (student_out.astype(f32) - teacher_out.astype(f32)).astype(bf16)
    diff_z = lax.ppermute(diff, "inc", SWAP_ZL)
    w_other = lax.ppermute(own, "tok", SWAP_ZH)
    w_o = gather_x(own)

    def act_piece(k, core):
        return lax.dynamic_slice(
            activations, (0, 0, (k * NC + core) * rows), (mb, toks, rows)
        )

    act_send = jnp.stack([act_piece(k, 1 - c) for k in range(NX * NZ)])
    act_got = lax.ppermute(act_send, "tok", SWAP_C)

    mine = jnp.where(
        zl == 0,
        jnp.concatenate([diff, diff_z], axis=1),
        jnp.concatenate([diff_z, diff], axis=1),
    )
    theirs = lax.ppermute(mine, "tok", SWAP_C)
    w_p = gather_x(w_other)

    def dw_part(xt, zt):
        k = xt * NZ + zt
        got = lax.dynamic_index_in_dim(act_got, k, 0, keepdims=False)
        return jnp.einsum(
            "mtr,mtc->rc", act_piece(k, c), mine, preferred_element_type=f32
        ) + jnp.einsum("mtr,mtc->rc", got, theirs, preferred_element_type=f32)

    def dw_ring(zt):
        send = dw_part(x_at(3), zt).astype(bf16)
        for k in (2, 1, 0):
            got = lax.ppermute(send, "tok", STEP_X)
            total = dw_part(x_at(k), zt) + got.astype(f32)
            send = total.astype(bf16)
        return total

    def dx_part(yt, w):
        a = lax.dynamic_slice(mine, (0, yt * part, 0), (mb, part, cols))
        b = lax.dynamic_slice(theirs, (0, yt * part, 0), (mb, part, cols))
        both = jnp.concatenate([a, b]).reshape(2 * mb * part, cols)
        return jnp.einsum("tc,rc->tr", both, w, preferred_element_type=f32)

    def dx_ring(w):
        send = dx_part(y_at(3), w).astype(bf16)
        for k in (2, 1, 0):
            got = lax.ppermute(send, ("tok", "outc"), STEP_Y)
            send = (dx_part(y_at(k), w) + got.astype(f32)).astype(bf16)
        return send

    dw_p = dw_ring(1 - zh)
    dw_cross = lax.ppermute(dw_p.astype(bf16), "tok", SWAP_ZH)
    dw_o = dw_ring(zh)
    weight_grad = dw_o + dw_cross.astype(f32)

    half = mb * part
    dx_o, dx_p = dx_ring(w_o), dx_ring(w_p)
    got_o = lax.ppermute(dx_o[half:], "tok", SWAP_C)
    got_p = lax.ppermute(dx_p[half:], "tok", SWAP_C)
    dx_o, dx_p = dx_o[:half], dx_p[:half]
    pieces = []
    for xt in range(NX):
        at = slice(xt * rows, (xt + 1) * rows)
        for zt in range(NZ):
            here = jnp.where(zh == zt, dx_o[:, at], dx_p[:, at])
            there = jnp.where(zh == zt, got_o[:, at], got_p[:, at])
            pieces += [jnp.where(c == 0, here, there), jnp.where(c == 0, there, here)]
    input_grad = jnp.concatenate(pieces, axis=1).reshape(mb, part, -1)
    return input_grad, weight_grad.reshape(weight.shape)


def solution(mesh):
    placed = (
        P(None, "tok", "inc"),
        P(None, ("tok", "inc"), "outc"),
        P(None, ("tok", "inc"), "outc"),
        P("inc", "tok", "outc"),
    )
    return jax.shard_map(
        local,
        mesh=mesh,
        in_specs=placed,
        out_specs=(P(None, ("tok", "outc"), "inc"), P("inc", "tok", "outc")),
        check_vma=False,
    )
```

time: 353 us -> 130 us (0.37)
  waiting for transfers between devices: 304 us -> 64.8 us
  starting transfers between devices: 0.16 us -> 20 us
  local copies, waits for them, and re-layouts: 2.54 us -> 17.1 us
  between operations: 13.8 us -> 1.15 us
  other arithmetic: 9.63 us -> 2.89 us
    reduce_scatter x2 -> x0, waiting for transfers between devices: 215 us -> none  [the longest x1 137 us: local(): lax.psum_scatter(batch_term(jnp.int32(0), lax.axis_size('tok') * weight.s...]
    all_gather x2 -> x0, waiting for transfers between devices: 88.1 us -> none  [the longest x1 61.7 us: local(): lax.all_gather(weight, 'tok', axis=1, tiled=True)]
    ppermute x0 -> x25, waiting for transfers between devices: none -> 64.8 us  [the longest x6 23 us: gather_x(): piece = lax.ppermute(piece, 'tok', STEP_X)]
    ppermute x0 -> x25, starting transfers between devices: none -> 20 us  [the longest x6 6.92 us: dx_ring(): got = lax.ppermute(send, ('tok', 'outc'), STEP_Y)]
    unnamed x5 -> x13, local copies, waits for them, and re-layouts: 2.54 us -> 12.3 us
    another operation x1 -> x0, other arithmetic: 4.74 us -> none  [local(): partial_grad = jnp.stack(batch_parts)]
    dot_general x4 -> x24, matrix products: 22.7 us -> 22.3 us  [the longest x8 11.4 us: dw_part(): jnp.einsum('mtr,mtc->rc', got, theirs, preferred_element_type=f32)]
  transfers between devices with their start and end apart: 4 -> 25, of which waited for: 4 -> 13; matrix products, arithmetic and copies ran while one was open for 9% -> 31% of each run, Pallas kernels for 0% -> 0%
where the time goes in v1:
time: 130 us; the launch traced here: 128 us
  waiting for transfers between devices  64.8 us (50%)
  matrix products  22.3 us (17%)
  starting transfers between devices  20 us (15%)
  local copies, waits for them, and re-layouts  17.1 us (13%)
  other arithmetic  2.89 us (2%)
    ppermute x6, waiting for transfers between devices, gather_x(): piece = lax.ppermute(piece, 'tok', STEP_X)  23 us
    ppermute x1, waiting for transfers between devices, local(): diff_z = lax.ppermute(diff, 'inc', SWAP_ZL)  12.5 us
    unnamed x13, local copies, waits for them, and re-layouts  12.3 us
    ppermute x1, waiting for transfers between devices, local(): dw_cross = lax.ppermute(dw_p.astype(bf16), 'tok', SWAP_ZH)  11.9 us
    dot_general x8, matrix products, dw_part(): jnp.einsum('mtr,mtc->rc', got, theirs, preferred_element_type=f32)  11.4 us
    ppermute x6, waiting for transfers between devices, dx_ring(): got = lax.ppermute(send, ('tok', 'outc'), STEP_Y)  8.9 us
    ppermute x6, waiting for transfers between devices, dw_ring(): got = lax.ppermute(send, 'tok', STEP_X)  8.48 us
    ppermute x6, starting transfers between devices, dx_ring(): got = lax.ppermute(send, ('tok', 'outc'), STEP_Y)  6.92 us
  transfers between devices with their start and end apart: 25, of which 13 were waited for; matrix products, arithmetic and copies ran while one was open for 31% of the time, Pallas kernels for 0%

profile of v1, /device:TPU:0, one launch (start us, length us, event | category | flops | bytes accessed | tf_op | source)
XLA Modules:
  0.0 128.4 jit_solution(15144660965135941786)
XLA Ops:
  0.6 1.6 %collective-permute-start.2 = (bf16[256,1024]{1,0:T(8,128)(2,1)}, bf16[256,1024]{1,0:T(8,128)(2,1)S(1)}, u32[]{:S(2)}, u32[]{:S(2)}) collective-permute-start(bf16[256,1024]{1,0:T(8,128)(2,1)} %bitcast.175), channel_id=1, source_target_pairs={{0,32},{8,104},{16,48},{24,120},{32,64},{40,8},{48,80},{56,24},{64... | collective-permute-start | bytes 1572872 | tf_op jit(solution)/shard_map/ppermute | solution.py:55
  2.3 3.9 %collective-permute-start.8 = (bf16[256,1024]{1,0:T(8,128)(2,1)}, bf16[256,1024]{1,0:T(8,128)(2,1)}, u32[]{:S(2)}, u32[]{:S(2)}) collective-permute-start(bf16[256,1024]{1,0:T(8,128)(2,1)} %bitcast.176), channel_id=1, source_target_pairs={{0,16},{8,24},{16,0},{24,8},{32,48},{40,56},{48,32},{56,40},{64,80... | collective-permute-start | bytes 1572872 | tf_op jit(solution)/shard_map/ppermute | solution.py:61
  8.6 1.7 %bitcast_dynamic-update-slice_fusion.7 = bf16[8,2,256,256]{3,2,1,0:T(8,128)(2,1)} fusion(bf16[2,256,4096]{2,1,0:T(8,128)(2,1)} %param.4, s32[]{:T(128)S(6)} %select_n.399), kind=kLoop, calls=%fused_computation.74 | loop fusion | bytes 524292
  10.3 1.7 %bitcast_dynamic-update-slice_fusion.6 = bf16[8,2,256,256]{3,2,1,0:T(8,128)(2,1)} fusion(bf16[8,2,256,256]{3,2,1,0:T(8,128)(2,1)} %bitcast_dynamic-update-slice_fusion.7, bf16[2,256,4096]{2,1,0:T(8,128)(2,1)} %param.4, s32[]{:T(128)S(6)} %select_n.400), kind=kLoop, calls=%fused_computation.73 | loop fusion | bytes 524292
  12.0 1.7 %bitcast_dynamic-update-slice_fusion.5 = bf16[8,2,256,256]{3,2,1,0:T(8,128)(2,1)} fusion(bf16[8,2,256,256]{3,2,1,0:T(8,128)(2,1)} %bitcast_dynamic-update-slice_fusion.6, bf16[2,256,4096]{2,1,0:T(8,128)(2,1)} %param.4, s32[]{:T(128)S(6)} %select_n.401), kind=kLoop, calls=%fused_computation.72 | loop fusion | bytes 524292
  13.7 1.7 %bitcast_dynamic-update-slice_fusion.4 = bf16[8,2,256,256]{3,2,1,0:T(8,128)(2,1)} fusion(bf16[8,2,256,256]{3,2,1,0:T(8,128)(2,1)} %bitcast_dynamic-update-slice_fusion.5, bf16[2,256,4096]{2,1,0:T(8,128)(2,1)} %param.4, s32[]{:T(128)S(6)} %select_n.402), kind=kLoop, calls=%fused_computation.71 | loop fusion | bytes 524292
  15.3 1.7 %bitcast_dynamic-update-slice_fusion.3 = bf16[8,2,256,256]{3,2,1,0:T(8,128)(2,1)} fusion(bf16[8,2,256,256]{3,2,1,0:T(8,128)(2,1)} %bitcast_dynamic-update-slice_fusion.4, bf16[2,256,4096]{2,1,0:T(8,128)(2,1)} %param.4, s32[]{:T(128)S(6)} %select_n.403), kind=kLoop, calls=%fused_computation.70 | loop fusion | bytes 524292
  17.0 1.7 %bitcast_dynamic-update-slice_fusion.2 = bf16[8,2,256,256]{3,2,1,0:T(8,128)(2,1)} fusion(bf16[8,2,256,256]{3,2,1,0:T(8,128)(2,1)} %bitcast_dynamic-update-slice_fusion.3, bf16[2,256,4096]{2,1,0:T(8,128)(2,1)} %param.4, s32[]{:T(128)S(6)} %select_n.404), kind=kLoop, calls=%fused_computation.69 | loop fusion | bytes 524292
  18.7 12.5 %collective-permute-done = bf16[2,128,1024]{2,1,0:T(8,128)(2,1)S(1)} collective-permute-done((bf16[2,128,1024]{2,1,0:T(8,128)(2,1)S(1)}, bf16[2,128,1024]{2,1,0:T(8,128)(2,1)S(1)}, u32[]{:S(2)}, u32[]{:S(2)}) %collective-permute-start) | collective-permute-done | bytes 524320 | tf_op jit(solution)/shard_map/ppermute | solution.py:60
  31.8 1.7 %bitcast_dynamic-update-slice_fusion.1 = bf16[8,2,256,256]{3,2,1,0:T(8,128)(2,1)} fusion(bf16[8,2,256,256]{3,2,1,0:T(8,128)(2,1)} %bitcast_dynamic-update-slice_fusion.2, bf16[2,256,4096]{2,1,0:T(8,128)(2,1)} %param.4, s32[]{:T(128)S(6)} %select_n.405), kind=kLoop, calls=%fused_computation.68 | loop fusion | bytes 524292
  33.5 1.7 %bitcast_dynamic-update-slice_fusion = bf16[8,2,256,256]{3,2,1,0:T(8,128)(2,1)} fusion(bf16[8,2,256,256]{3,2,1,0:T(8,128)(2,1)} %bitcast_dynamic-update-slice_fusion.1, bf16[2,256,4096]{2,1,0:T(8,128)(2,1)} %param.4, s32[]{:T(128)S(6)} %select_n.406), kind=kLoop, calls=%fused_computation.67 | loop fusion | bytes 524292 | tf_op jit(solution)/shard_map/stack | solution.py:69
  38.2 8.0 %collective-permute-done.3 = bf16[256,1024]{1,0:T(8,128)(2,1)} collective-permute-done((bf16[256,1024]{1,0:T(8,128)(2,1)S(1)}, bf16[256,1024]{1,0:T(8,128)(2,1)}, u32[]{:S(2)}, u32[]{:S(2)}) %collective-permute-start.3) | collective-permute-done | bytes 524320 | tf_op jit(solution)/shard_map/ppermute | solution.py:55
  46.2 5.5 %collective-permute-done.9 = bf16[256,1024]{1,0:T(8,128)(2,1)S(1)} collective-permute-done((bf16[256,1024]{1,0:T(8,128)(2,1)}, bf16[256,1024]{1,0:T(8,128)(2,1)S(1)}, u32[]{:S(2)}, u32[]{:S(2)}) %collective-permute-start.9) | collective-permute-done | bytes 524320 | tf_op jit(solution)/shard_map/ppermute | solution.py:55
  53.0 4.3 %collective-permute-done.4 = bf16[256,1024]{1,0:T(8,128)(2,1)S(1)} collective-permute-done((bf16[256,1024]{1,0:T(8,128)(2,1)}, bf16[256,1024]{1,0:T(8,128)(2,1)S(1)}, u32[]{:S(2)}, u32[]{:S(2)}) %collective-permute-start.4) | collective-permute-done | bytes 524320 | tf_op jit(solution)/shard_map/ppermute | solution.py:55
  58.1 1.6 %collective-permute-start.5 = (bf16[256,1024]{1,0:T(8,128)(2,1)S(1)}, bf16[256,1024]{1,0:T(8,128)(2,1)S(1)}, u32[]{:S(2)}, u32[]{:S(2)}) collective-permute-start(bf16[256,1024]{1,0:T(8,128)(2,1)S(1)} %convolution_convert_fusion.1), channel_id=1, source_target_pairs={{0,1},{1,2},{2,3},{3,0},{8,11},{9,8},{10,9},{11,10},{16,17},{17,18... | collective-permute-start | bytes 1572872 | tf_op jit(solution)/shard_map/ppermute | solution.py:104
  59.7 3.2 %collective-permute-done.10 = bf16[256,1024]{1,0:T(8,128)(2,1)S(1)} collective-permute-done((bf16[256,1024]{1,0:T(8,128)(2,1)S(1)}, bf16[256,1024]{1,0:T(8,128)(2,1)S(1)}, u32[]{:S(2)}, u32[]{:S(2)}) %collective-permute-start.10) | collective-permute-done | bytes 524320 | tf_op jit(solution)/shard_map/ppermute | solution.py:55
  63.1 1.6 %convolution_bitcast_fusion.8 = f32[256,1024]{1,0:T(8,128)S(1)} fusion(bf16[2,256,1024]{2,1,0:T(8,128)(2,1)S(1)} %collective-permute-done.1, bf16[8,2,256,256]{3,2,1,0:T(8,128)(2,1)} %collective-permute-done.17, s32[]{:T(128)S(6)} %select_n.416), kind=kOutput, calls=%fused_computation.8 | convolution fusion | flops 268435456 | bytes 2359300 | tf_op jit(solution)/shard_map/mtr,mtc->rc/dot_general | solution.py:85
  69.6 1.6 %collective-permute-start.6 = (bf16[256,1024]{1,0:T(8,128)(2,1)S(1)}, bf16[256,1024]{1,0:T(8,128)(2,1)S(1)}, u32[]{:S(2)}, u32[]{:S(2)}) collective-permute-start(bf16[256,1024]{1,0:T(8,128)(2,1)S(1)} %fusion.25), channel_id=1, source_target_pairs={{0,1},{1,2},{2,3},{3,0},{8,11},{9,8},{10,9},{11,10},{16,17},{17,18... | collective-permute-start | bytes 1572872 | tf_op jit(solution)/shard_map/ppermute | solution.py:104
  71.2 2.0 %collective-permute-done.11 = bf16[256,1024]{1,0:T(8,128)(2,1)S(1)} collective-permute-done((bf16[256,1024]{1,0:T(8,128)(2,1)S(1)}, bf16[256,1024]{1,0:T(8,128)(2,1)S(1)}, u32[]{:S(2)}, u32[]{:S(2)}) %collective-permute-start.11) | collective-permute-done | bytes 524320 | tf_op jit(solution)/shard_map/ppermute | solution.py:55
  74.1 1.8 %collective-permute-start.12 = (bf16[256,1024]{1,0:T(8,128)(2,1)S(1)}, bf16[256,1024]{1,0:T(8,128)(2,1)S(1)}, u32[]{:S(2)}, u32[]{:S(2)}) collective-permute-start(bf16[256,1024]{1,0:T(8,128)(2,1)S(1)} %convolution_convert_fusion), channel_id=1, source_target_pairs={{0,1},{1,2},{2,3},{3,0},{8,11},{9,8},{10,9},{11,10},{16,17},{17,18... | collective-permute-start | bytes 1572872 | tf_op jit(solution)/shard_map/ppermute | solution.py:104
  77.3 1.4 %convolution_bitcast_fusion.12 = f32[256,1024]{1,0:T(8,128)S(1)} fusion(bf16[2,256,1024]{2,1,0:T(8,128)(2,1)S(1)} %collective-permute-done.1, bf16[8,2,256,256]{3,2,1,0:T(8,128)(2,1)} %collective-permute-done.17, s32[]{:T(128)S(6)} %select_n.410), kind=kOutput, calls=%fused_computation.12 | convolution fusion | flops 268435456 | bytes 2359300 | tf_op jit(solution)/shard_map/mtr,mtc->rc/dot_general | solution.py:85
  78.7 1.4 %convolution_bitcast_fusion.2 = f32[256,1024]{1,0:T(8,128)S(1)} fusion(bf16[2,256,1024]{2,1,0:T(8,128)(2,1)S(1)} %collective-permute-done.1, bf16[8,2,256,256]{3,2,1,0:T(8,128)(2,1)} %collective-permute-done.17, s32[]{:T(128)S(6)} %select_n.422), kind=kOutput, calls=%fused_computation.2 | convolution fusion | flops 268435456 | bytes 2359300 | tf_op jit(solution)/shard_map/mtr,mtc->rc/dot_general | solution.py:85
  80.1 1.4 %convolution_bitcast_fusion.4 = f32[256,1024]{1,0:T(8,128)S(1)} fusion(bf16[2,256,1024]{2,1,0:T(8,128)(2,1)S(1)} %collective-permute-done.1, bf16[8,2,256,256]{3,2,1,0:T(8,128)(2,1)} %collective-permute-done.17, s32[]{:T(128)S(6)} %select_n.420), kind=kOutput, calls=%fused_computation.4 | convolution fusion | flops 268435456 | bytes 2359300 | tf_op jit(solution)/shard_map/mtr,mtc->rc/dot_general | solution.py:85
  84.9 1.6 %collective-permute-start.19 = (bf16[256,1024]{1,0:T(8,128)(2,1)S(1)}, bf16[256,1024]{1,0:T(8,128)(2,1)S(1)}, u32[]{:S(2)}, u32[]{:S(2)}) collective-permute-start(bf16[256,1024]{1,0:T(8,128)(2,1)S(1)} %fusion.21), channel_id=1, source_target_pairs={{0,32},{8,104},{16,48},{24,120},{32,64},{40,8},{48,80},{56,24},{64... | collective-permute-start | bytes 1572872 | tf_op jit(solution)/shard_map/ppermute | solution.py:90
  90.3 5.0 %collective-permute-done.19 = bf16[256,1024]{1,0:T(8,128)(2,1)S(1)} collective-permute-done((bf16[256,1024]{1,0:T(8,128)(2,1)S(1)}, bf16[256,1024]{1,0:T(8,128)(2,1)S(1)}, u32[]{:S(2)}, u32[]{:S(2)}) %collective-permute-start.19) | collective-permute-done | bytes 524320 | tf_op jit(solution)/shard_map/ppermute | solution.py:90
  96.3 2.1 %collective-permute-done.13 = bf16[256,1024]{1,0:T(8,128)(2,1)S(1)} collective-permute-done((bf16[256,1024]{1,0:T(8,128)(2,1)S(1)}, bf16[256,1024]{1,0:T(8,128)(2,1)S(1)}, u32[]{:S(2)}, u32[]{:S(2)}) %collective-permute-start.13) | collective-permute-done | bytes 524320 | tf_op jit(solution)/shard_map/ppermute | solution.py:104
  99.3 1.7 %collective-permute-done.22 = bf16[256,1024]{1,0:T(8,128)(2,1)S(1)} collective-permute-done((bf16[256,1024]{1,0:T(8,128)(2,1)S(1)}, bf16[256,1024]{1,0:T(8,128)(2,1)S(1)}, u32[]{:S(2)}, u32[]{:S(2)}) %collective-permute-start.22) | collective-permute-done | bytes 524320 | tf_op jit(solution)/shard_map/ppermute | solution.py:90
  101.9 2.1 %collective-permute-done.7 = bf16[256,1024]{1,0:T(8,128)(2,1)S(1)} collective-permute-done((bf16[256,1024]{1,0:T(8,128)(2,1)S(1)}, bf16[256,1024]{1,0:T(8,128)(2,1)S(1)}, u32[]{:S(2)}, u32[]{:S(2)}) %collective-permute-start.7) | collective-permute-done | bytes 524320 | tf_op jit(solution)/shard_map/ppermute | solution.py:104
  104.9 4.7 %collective-permute-done.14 = bf16[256,1024]{1,0:T(8,128)(2,1)S(1)} collective-permute-done((bf16[256,1024]{1,0:T(8,128)(2,1)S(1)}, bf16[256,1024]{1,0:T(8,128)(2,1)S(1)}, u32[]{:S(2)}, u32[]{:S(2)}) %collective-permute-start.14) | collective-permute-done | bytes 524320 | tf_op jit(solution)/shard_map/ppermute | solution.py:104
  110.5 1.7 %collective-permute-done.23 = bf16[256,1024]{1,0:T(8,128)(2,1)S(1)} collective-permute-done((bf16[256,1024]{1,0:T(8,128)(2,1)S(1)}, bf16[256,1024]{1,0:T(8,128)(2,1)S(1)}, u32[]{:S(2)}, u32[]{:S(2)}) %collective-permute-start.23) | collective-permute-done | bytes 524320 | tf_op jit(solution)/shard_map/ppermute | solution.py:90
  114.9 11.9 %collective-permute-done.24 = bf16[256,1024]{1,0:T(8,128)(2,1)S(1)} collective-permute-done((bf16[256,1024]{1,0:T(8,128)(2,1)S(1)}, bf16[256,1024]{1,0:T(8,128)(2,1)S(1)}, u32[]{:S(2)}, u32[]{:S(2)}) %collective-permute-start.24) | collective-permute-done | bytes 524320 | tf_op jit(solution)/shard_map/ppermute | solution.py:109
  126.9 1.5 %fusion.3 = f32[1,256,1024]{2,1,0:T(8,128)} fusion(f32[256,1024]{1,0:T(8,128)S(1)} %convolution_bitcast_fusion.14, bf16[2,256,1024]{2,1,0:T(8,128)(2,1)S(1)} %maximum_select_fusion, bf16[256,1024]{1,0:T(8,128)(2,1)S(1)} %collective-permute-done.24, bf16[256,1024]{1,0:T(8,128)(2,1)S(1)} %collective-permute-done.20, bf16[2,256,4096]{2,1,0:T(8,128)(2,1)S(1)} %copy-done, ...), kind=kOutput, calls=%fused_computation.25 | convolution fusion | flops 269746176 | bytes 4456452 | tf_op jit(solution)/shard_map/mtr,mtc->rc/dot_general | solution.py:83
  (92 shorter events, 29.4 us)
Async XLA Ops:
  0.6 35.0 %collective-permute-start.2 = (bf16[256,1024]{1,0:T(8,128)(2,1)}, bf16[256,1024]{1,0:T(8,128)(2,1)S(1)}, u32[]{:S(2)}, u32[]{:S(2)}) collective-permute-start(bf16[256,1024]{1,0:T(8,128)(2,1)} %bitcast.175), channel_id=1, source_target_pairs={{0,32},{8,104},{16,48},{24,120},{32,64},{40,8},{48,80},{56,24},{64... | collective-permute-start | bytes 1572872 | tf_op jit(solution)/shard_map/ppermute | solution.py:55
  2.3 33.4 %collective-permute-start.8 = (bf16[256,1024]{1,0:T(8,128)(2,1)}, bf16[256,1024]{1,0:T(8,128)(2,1)}, u32[]{:S(2)}, u32[]{:S(2)}) collective-permute-start(bf16[256,1024]{1,0:T(8,128)(2,1)} %bitcast.176), channel_id=1, source_target_pairs={{0,16},{8,24},{16,0},{24,8},{32,48},{40,56},{48,32},{56,40},{64,80... | collective-permute-start | bytes 1572872 | tf_op jit(solution)/shard_map/ppermute | solution.py:61
  7.5 23.7 %collective-permute-start = (bf16[2,128,1024]{2,1,0:T(8,128)(2,1)S(1)}, bf16[2,128,1024]{2,1,0:T(8,128)(2,1)S(1)}, u32[]{:S(2)}, u32[]{:S(2)}) collective-permute-start(bf16[2,128,1024]{2,1,0:T(8,128)(2,1)S(1)} %subtract_convert_fusion), channel_id=1, source_target_pairs={{0,4},{4,0},{1,5},{5,1},{2,6},{6,2},{3,7},{7,3},{8,12},{12,8},{9,1... | collective-permute-start | bytes 1572872 | tf_op jit(solution)/shard_map/ppermute | solution.py:60
  31.7 4.9 %copy-start.1 = (bf16[1,256,1024]{2,1,0:T(8,128)(2,1)S(1)}, bf16[1,256,1024]{2,1,0:T(8,128)(2,1)}, u32[]{:S(2)}) copy-start(bf16[1,256,1024]{2,1,0:T(8,128)(2,1)} %param.7) | copy-start | bytes 1572868
  31.7 21.1 %collective-permute-start.1 = (bf16[2,256,1024]{2,1,0:T(8,128)(2,1)S(1)}, bf16[2,256,1024]{2,1,0:T(8,128)(2,1)S(1)}, u32[]{:S(2)}, u32[]{:S(2)}) collective-permute-start(bf16[2,256,1024]{2,1,0:T(8,128)(2,1)S(1)} %maximum_select_fusion), channel_id=1, source_target_pairs={{0,8},{8,0},{16,24},{24,16},{32,40},{40,32},{48,56},{56,48},{64,72... | collective-permute-start | bytes 3145736 | tf_op jit(solution)/shard_map/ppermute | solution.py:77
  35.2 27.9 %collective-permute-start.17 = (bf16[8,2,256,256]{3,2,1,0:T(8,128)(2,1)}, bf16[8,2,256,256]{3,2,1,0:T(8,128)(2,1)}, u32[]{:S(2)}, u32[]{:S(2)}) collective-permute-start(bf16[8,2,256,256]{3,2,1,0:T(8,128)(2,1)} %bitcast_dynamic-update-slice_fusion), channel_id=1, source_target_pairs={{0,8},{8,0},{16,24},{24,16},{32,40},{40,32},{48,56},{56,48},{64,72... | collective-permute-start | bytes 6291464 | tf_op jit(solution)/shard_map/ppermute | solution.py:70
  35.6 10.5 %collective-permute-start.3 = (bf16[256,1024]{1,0:T(8,128)(2,1)S(1)}, bf16[256,1024]{1,0:T(8,128)(2,1)}, u32[]{:S(2)}, u32[]{:S(2)}) collective-permute-start(bf16[256,1024]{1,0:T(8,128)(2,1)S(1)} %collective-permute-done.2), channel_id=1, source_target_pairs={{0,32},{8,104},{16,48},{24,120},{32,64},{40,8},{48,80},{56,24},{64... | collective-permute-start | bytes 1572872 | tf_op jit(solution)/shard_map/ppermute | solution.py:55
  35.7 16.0 %collective-permute-start.9 = (bf16[256,1024]{1,0:T(8,128)(2,1)}, bf16[256,1024]{1,0:T(8,128)(2,1)S(1)}, u32[]{:S(2)}, u32[]{:S(2)}) collective-permute-start(bf16[256,1024]{1,0:T(8,128)(2,1)} %collective-permute-done.8), channel_id=1, source_target_pairs={{0,32},{8,104},{16,48},{24,120},{32,64},{40,8},{48,80},{56,24},{64... | collective-permute-start | bytes 1572872 | tf_op jit(solution)/shard_map/ppermute | solution.py:55
  46.1 11.1 %collective-permute-start.4 = (bf16[256,1024]{1,0:T(8,128)(2,1)}, bf16[256,1024]{1,0:T(8,128)(2,1)S(1)}, u32[]{:S(2)}, u32[]{:S(2)}) collective-permute-start(bf16[256,1024]{1,0:T(8,128)(2,1)} %collective-permute-done.3), channel_id=1, source_target_pairs={{0,32},{8,104},{16,48},{24,120},{32,64},{40,8},{48,80},{56,24},{64... | collective-permute-start | bytes 1572872 | tf_op jit(solution)/shard_map/ppermute | solution.py:55
  51.7 11.2 %collective-permute-start.10 = (bf16[256,1024]{1,0:T(8,128)(2,1)S(1)}, bf16[256,1024]{1,0:T(8,128)(2,1)S(1)}, u32[]{:S(2)}, u32[]{:S(2)}) collective-permute-start(bf16[256,1024]{1,0:T(8,128)(2,1)S(1)} %collective-permute-done.9), channel_id=1, source_target_pairs={{0,32},{8,104},{16,48},{24,120},{32,64},{40,8},{48,80},{56,24},{64... | collective-permute-start | bytes 1572872 | tf_op jit(solution)/shard_map/ppermute | solution.py:55
  58.1 10.8 %collective-permute-start.5 = (bf16[256,1024]{1,0:T(8,128)(2,1)S(1)}, bf16[256,1024]{1,0:T(8,128)(2,1)S(1)}, u32[]{:S(2)}, u32[]{:S(2)}) collective-permute-start(bf16[256,1024]{1,0:T(8,128)(2,1)S(1)} %convolution_convert_fusion.1), channel_id=1, source_target_pairs={{0,1},{1,2},{2,3},{3,0},{8,11},{9,8},{10,9},{11,10},{16,17},{17,18... | collective-permute-start | bytes 1572872 | tf_op jit(solution)/shard_map/ppermute | solution.py:104
  62.9 10.4 %collective-permute-start.11 = (bf16[256,1024]{1,0:T(8,128)(2,1)S(1)}, bf16[256,1024]{1,0:T(8,128)(2,1)S(1)}, u32[]{:S(2)}, u32[]{:S(2)}) collective-permute-start(bf16[256,1024]{1,0:T(8,128)(2,1)S(1)} %collective-permute-done.10), channel_id=1, source_target_pairs={{0,32},{8,104},{16,48},{24,120},{32,64},{40,8},{48,80},{56,24},{64... | collective-permute-start | bytes 1572872 | tf_op jit(solution)/shard_map/ppermute | solution.py:55
  63.0 2.3 %copy-start = (bf16[2,256,4096]{2,1,0:T(8,128)(2,1)S(1)}, bf16[2,256,4096]{2,1,0:T(8,128)(2,1)}, u32[]{:S(2)}) copy-start(bf16[2,256,4096]{2,1,0:T(8,128)(2,1)} %param.4) | copy-start | bytes 12582916
  65.7 18.6 %collective-permute-start.18 = (bf16[256,1024]{1,0:T(8,128)(2,1)S(1)}, bf16[256,1024]{1,0:T(8,128)(2,1)S(1)}, u32[]{:S(2)}, u32[]{:S(2)}) collective-permute-start(bf16[256,1024]{1,0:T(8,128)(2,1)S(1)} %fusion.20), channel_id=1, source_target_pairs={{0,32},{8,104},{16,48},{24,120},{32,64},{40,8},{48,80},{56,24},{64... | collective-permute-start | bytes 1572872 | tf_op jit(solution)/shard_map/ppermute | solution.py:90
  67.7 18.8 %collective-permute-start.21 = (bf16[256,1024]{1,0:T(8,128)(2,1)S(1)}, bf16[256,1024]{1,0:T(8,128)(2,1)S(1)}, u32[]{:S(2)}, u32[]{:S(2)}) collective-permute-start(bf16[256,1024]{1,0:T(8,128)(2,1)S(1)} %fusion.16), channel_id=1, source_target_pairs={{0,32},{8,104},{16,48},{24,120},{32,64},{40,8},{48,80},{56,24},{64... | collective-permute-start | bytes 1572872 | tf_op jit(solution)/shard_map/ppermute | solution.py:90
  69.6 19.7 %collective-permute-start.6 = (bf16[256,1024]{1,0:T(8,128)(2,1)S(1)}, bf16[256,1024]{1,0:T(8,128)(2,1)S(1)}, u32[]{:S(2)}, u32[]{:S(2)}) collective-permute-start(bf16[256,1024]{1,0:T(8,128)(2,1)S(1)} %fusion.25), channel_id=1, source_target_pairs={{0,1},{1,2},{2,3},{3,0},{8,11},{9,8},{10,9},{11,10},{16,17},{17,18... | collective-permute-start | bytes 1572872 | tf_op jit(solution)/shard_map/ppermute | solution.py:104
  74.1 13.1 %collective-permute-start.12 = (bf16[256,1024]{1,0:T(8,128)(2,1)S(1)}, bf16[256,1024]{1,0:T(8,128)(2,1)S(1)}, u32[]{:S(2)}, u32[]{:S(2)}) collective-permute-start(bf16[256,1024]{1,0:T(8,128)(2,1)S(1)} %convolution_convert_fusion), channel_id=1, source_target_pairs={{0,1},{1,2},{2,3},{3,0},{8,11},{9,8},{10,9},{11,10},{16,17},{17,18... | collective-permute-start | bytes 1572872 | tf_op jit(solution)/shard_map/ppermute | solution.py:104
  84.9 10.5 %collective-permute-start.19 = (bf16[256,1024]{1,0:T(8,128)(2,1)S(1)}, bf16[256,1024]{1,0:T(8,128)(2,1)S(1)}, u32[]{:S(2)}, u32[]{:S(2)}) collective-permute-start(bf16[256,1024]{1,0:T(8,128)(2,1)S(1)} %fusion.21), channel_id=1, source_target_pairs={{0,32},{8,104},{16,48},{24,120},{32,64},{40,8},{48,80},{56,24},{64... | collective-permute-start | bytes 1572872 | tf_op jit(solution)/shard_map/ppermute | solution.py:90
  87.0 13.9 %collective-permute-start.22 = (bf16[256,1024]{1,0:T(8,128)(2,1)S(1)}, bf16[256,1024]{1,0:T(8,128)(2,1)S(1)}, u32[]{:S(2)}, u32[]{:S(2)}) collective-permute-start(bf16[256,1024]{1,0:T(8,128)(2,1)S(1)} %fusion.17), channel_id=1, source_target_pairs={{0,32},{8,104},{16,48},{24,120},{32,64},{40,8},{48,80},{56,24},{64... | collective-permute-start | bytes 1572872 | tf_op jit(solution)/shard_map/ppermute | solution.py:90
  87.9 10.5 %collective-permute-start.13 = (bf16[256,1024]{1,0:T(8,128)(2,1)S(1)}, bf16[256,1024]{1,0:T(8,128)(2,1)S(1)}, u32[]{:S(2)}, u32[]{:S(2)}) collective-permute-start(bf16[256,1024]{1,0:T(8,128)(2,1)S(1)} %fusion.28), channel_id=1, source_target_pairs={{0,1},{1,2},{2,3},{3,0},{8,11},{9,8},{10,9},{11,10},{16,17},{17,18... | collective-permute-start | bytes 1572872 | tf_op jit(solution)/shard_map/ppermute | solution.py:104
  90.0 14.0 %collective-permute-start.7 = (bf16[256,1024]{1,0:T(8,128)(2,1)S(1)}, bf16[256,1024]{1,0:T(8,128)(2,1)S(1)}, u32[]{:S(2)}, u32[]{:S(2)}) collective-permute-start(bf16[256,1024]{1,0:T(8,128)(2,1)S(1)} %fusion.24), channel_id=1, source_target_pairs={{0,1},{1,2},{2,3},{3,0},{8,11},{9,8},{10,9},{11,10},{16,17},{17,18... | collective-permute-start | bytes 1572872 | tf_op jit(solution)/shard_map/ppermute | solution.py:104
  95.8 19.1 %collective-permute-start.20 = (bf16[256,1024]{1,0:T(8,128)(2,1)S(1)}, bf16[256,1024]{1,0:T(8,128)(2,1)S(1)}, u32[]{:S(2)}, u32[]{:S(2)}) collective-permute-start(bf16[256,1024]{1,0:T(8,128)(2,1)S(1)} %fusion.22), channel_id=1, source_target_pairs={{0,32},{8,104},{16,48},{24,120},{32,64},{40,8},{48,80},{56,24},{64... | collective-permute-start | bytes 1572872 | tf_op jit(solution)/shard_map/ppermute | solution.py:90
  99.1 10.5 %collective-permute-start.14 = (bf16[256,1024]{1,0:T(8,128)(2,1)S(1)}, bf16[256,1024]{1,0:T(8,128)(2,1)S(1)}, u32[]{:S(2)}, u32[]{:S(2)}) collective-permute-start(bf16[256,1024]{1,0:T(8,128)(2,1)S(1)} %fusion.27), channel_id=1, source_target_pairs={{0,1},{1,2},{2,3},{3,0},{8,11},{9,8},{10,9},{11,10},{16,17},{17,18... | collective-permute-start | bytes 1572872 | tf_op jit(solution)/shard_map/ppermute | solution.py:104
  101.5 10.7 %collective-permute-start.23 = (bf16[256,1024]{1,0:T(8,128)(2,1)S(1)}, bf16[256,1024]{1,0:T(8,128)(2,1)S(1)}, u32[]{:S(2)}, u32[]{:S(2)}) collective-permute-start(bf16[256,1024]{1,0:T(8,128)(2,1)S(1)} %fusion.18), channel_id=1, source_target_pairs={{0,32},{8,104},{16,48},{24,120},{32,64},{40,8},{48,80},{56,24},{64... | collective-permute-start | bytes 1572872 | tf_op jit(solution)/shard_map/ppermute | solution.py:90
  104.8 9.2 %collective-permute-start.15 = (bf16[128,1024]{1,0:T(8,128)(2,1)S(1)}, bf16[128,1024]{1,0:T(8,128)(2,1)S(1)}, u32[]{:S(2)}, u32[]{:S(2)}) collective-permute-start(bf16[128,1024]{1,0:T(8,128)(2,1)S(1)} %slice.100), channel_id=1, source_target_pairs={{0,8},{8,0},{16,24},{24,16},{32,40},{40,32},{48,56},{56,48},{64,72... | collective-permute-start | bytes 786440 | tf_op jit(solution)/shard_map/ppermute | solution.py:115
  110.4 3.6 %collective-permute-start.16 = (bf16[128,1024]{1,0:T(8,128)(2,1)S(1)}, bf16[128,1024]{1,0:T(8,128)(2,1)S(1)}, u32[]{:S(2)}, u32[]{:S(2)}) collective-permute-start(bf16[128,1024]{1,0:T(8,128)(2,1)S(1)} %slice.102), channel_id=1, source_target_pairs={{0,8},{8,0},{16,24},{24,16},{32,40},{40,32},{48,56},{56,48},{64,72... | collective-permute-start | bytes 786440 | tf_op jit(solution)/shard_map/ppermute | solution.py:116
  112.7 14.2 %collective-permute-start.24 = (bf16[256,1024]{1,0:T(8,128)(2,1)S(1)}, bf16[256,1024]{1,0:T(8,128)(2,1)S(1)}, u32[]{:S(2)}, u32[]{:S(2)}) collective-permute-start(bf16[256,1024]{1,0:T(8,128)(2,1)S(1)} %fusion.19), channel_id=1, source_target_pairs={{0,16},{8,24},{16,0},{24,8},{32,48},{40,56},{48,32},{56,40},{64,80... | collective-permute-start | bytes 1572872 | tf_op jit(solution)/shard_map/ppermute | solution.py:109
  114.9 13.5 %copy-start.2 = (bf16[128,4096]{1,0:T(8,128)(2,1)}, bf16[128,4096]{1,0:T(8,128)(2,1)S(1)}, u32[]{:S(2)}) copy-start(bf16[128,4096]{1,0:T(8,128)(2,1)S(1)} %select_dynamic-update-slice_fusion) | copy-start | bytes 3145732

commit v2 on v0

v2 whole, which is shorter than its diff:
```python
import functools

import jax
import jax.numpy as jnp
from jax import lax
from jax.experimental import pallas as pl
from jax.experimental.pallas import tpu as pltpu
from jax.sharding import Mesh
from jax.sharding import PartitionSpec as P

NX, NZ, NC, NL, NY = 4, 2, 2, 2, 4
F32, BF16 = jnp.float32, jnp.bfloat16


def cost(flops, *arrays):
    moved = sum(a.size * a.dtype.itemsize for a in arrays)
    return pl.CostEstimate(flops=flops, bytes_accessed=moved, transcendentals=0)


def other_columns(act, c):
    mb, toks, width = act.shape
    n = NX * NZ
    rows = width // (n * NC)

    def body(core, a_ref, out_ref):
        out_ref[0] = a_ref[...]

    out = jax.ShapeDtypeStruct((n, mb, toks, rows), act.dtype)
    return pl.pallas_call(
        body,
        out_shape=out,
        grid_spec=pltpu.PrefetchScalarGridSpec(
            num_scalar_prefetch=1,
            grid=(n,),
            in_specs=[
                pl.BlockSpec(
                    (mb, toks, rows), lambda k, core: (0, 0, k * NC + 1 - core[0])
                )
            ],
            out_specs=pl.BlockSpec((1, mb, toks, rows), lambda k, core: (k, 0, 0, 0)),
        ),
        cost_estimate=cost(0, out, out),
        name="other_columns",
    )(c.reshape(1), act)


def dw_body(n, n_add, at, *refs):
    zl = at[0]
    mine, refs = refs[:n], refs[n:]
    theirs, refs = refs[:n], refs[n:]
    diffs, refs = refs[:4], refs[4:]
    adds, outs = refs[:n_add], refs[n_add:]
    mb, part, cols = diffs[0].shape
    for k in range(n):
        total = None
        for j, diff in enumerate(diffs):
            start = pl.multiple_of((zl if j % 2 == 0 else 1 - zl) * part, part)
            if j < 2:
                a = mine[k][:, pl.ds(start, part), :]
            else:
                a = theirs[k][0, :, pl.ds(start, part), :]
            term = lax.dot_general(
                a.reshape(mb * part, a.shape[-1]),
                diff[...].reshape(mb * part, cols),
                (((0,), (0,)), ((), ())),
                preferred_element_type=F32,
            )
            total = term if total is None else total + term
        for add in adds:
            total = total + add[...].astype(F32)
        outs[k][...] = total.astype(outs[k].dtype)


def dw_sums(act, act_got, diffs, chunks, c, zl, adds=(), dtype=BF16):
    mb, toks, width = act.shape
    rows = width // (NX * NZ * NC)
    cols = diffs[0].shape[-1]
    n, steps = len(chunks), 2
    wide = cols // steps
    at = jnp.stack([zl, *(k * NC + c for k in chunks), *chunks])
    out = jax.ShapeDtypeStruct((rows, cols), dtype)

    def column(k):
        return pl.BlockSpec((mb, toks, rows), lambda i, at: (0, 0, at[1 + k]))

    def chunk(k):
        return pl.BlockSpec((1, mb, toks, rows), lambda i, at: (at[1 + n + k], 0, 0, 0))

    diff_spec = pl.BlockSpec((mb, toks // 2, wide), lambda i, at: (0, 0, i))
    flat_spec = pl.BlockSpec((rows, wide), lambda i, at: (0, i))
    return pl.pallas_call(
        functools.partial(dw_body, n, len(adds)),
        out_shape=[out] * n,
        grid_spec=pltpu.PrefetchScalarGridSpec(
            num_scalar_prefetch=1,
            grid=(steps,),
            in_specs=[
                *(column(k) for k in range(n)),
                *(chunk(k) for k in range(n)),
                *([diff_spec] * 4),
                *([flat_spec] * len(adds)),
            ],
            out_specs=[flat_spec] * n,
        ),
        cost_estimate=cost(4 * n * mb * toks * rows * cols, *diffs, *([out] * n)),
        name="dw_sums",
    )(at, *([act] * n), *([act_got] * n), *diffs, *adds)


def dx_body(at, *refs):
    diffs, pieces, out = refs[:4], refs[4:8], refs[8]
    c, zl = at[0], at[1]
    _, part, cols = diffs[0].shape
    rows = pieces[0].shape[0]
    half = part // 2
    for p, piece in enumerate(pieces):
        w = piece[...]
        lanes = pl.ds(pl.multiple_of(at[2 + p] * rows, rows), rows)
        for j, diff in enumerate(diffs):
            got = lax.dot_general(
                diff[0], w, (((1,), (1,)), ((), ())), preferred_element_type=F32
            ).astype(BF16)
            core = c if j < 2 else 1 - c
            first = core * NY + 2 * (zl if j % 2 == 0 else 1 - zl)
            for h in range(2):
                out[first + h, :, lanes] = got[h * half : (h + 1) * half]


def dx_sums(diffs, pieces, where, c, zl):
    mb, part, cols = diffs[0].shape
    rows = pieces[0].shape[0]
    half = part // 2
    out = jax.ShapeDtypeStruct((NC * NY, mb * half, NX * rows), BF16)
    return pl.pallas_call(
        dx_body,
        out_shape=out,
        grid_spec=pltpu.PrefetchScalarGridSpec(
            num_scalar_prefetch=1,
            grid=(mb,),
            in_specs=[
                *([pl.BlockSpec((1, part, cols), lambda m, at: (m, 0, 0))] * 4),
                *([pl.BlockSpec((rows, cols), lambda m, at: (0, 0))] * NX),
            ],
            out_specs=pl.BlockSpec(
                (NC * NY, half, NX * rows), lambda m, at: (0, m, 0)
            ),
        ),
        cost_estimate=cost(8 * mb * part * cols * NX * rows, out, *diffs, *pieces),
        name="dx_sums",
    )(jnp.stack([c, zl, *where]), *diffs, *pieces)


def join_body(at, o_ref, p_ref, out_ref):
    zh = at[0]
    width = o_ref.shape[-1]
    rows = width // NX
    for ref, z in ((o_ref, zh), (p_ref, 1 - zh)):
        for n in range(NC):
            total = ref[n * NY].astype(F32)
            for k in range(1, NY):
                total = total + ref[n * NY + k].astype(F32)
            total = total.astype(BF16)
            for xt in range(NX):
                start = ((xt * NZ + z) * NC + n) * rows
                lanes = pl.ds(pl.multiple_of(start, rows), rows)
                out_ref[0, :, lanes] = total[:, xt * rows : (xt + 1) * rows]


def join(got_o, got_p, zh, mb):
    n, toks, width = got_o.shape
    part = toks // mb
    out = jax.ShapeDtypeStruct((mb, part, NZ * NC * width), BF16)
    spec = pl.BlockSpec((n, part, width), lambda m, at: (0, m, 0))
    return pl.pallas_call(
        join_body,
        out_shape=out,
        grid_spec=pltpu.PrefetchScalarGridSpec(
            num_scalar_prefetch=1,
            grid=(mb,),
            in_specs=[spec, spec],
            out_specs=pl.BlockSpec((1, part, NZ * NC * width), lambda m, at: (m, 0, 0)),
        ),
        cost_estimate=cost(2 * got_o.size, got_o, got_p, out),
        name="join",
    )(zh.reshape(1), got_o, got_p)


def after(value, *others):
    return lax.optimization_barrier((value, *others))[0]


def by_x(k):
    return [(x, (x + k) % NX) for x in range(NX)]


STEP_X = [
    (x * NC + c, (x + 1 - 2 * c) % NX * NC + c) for x in range(NX) for c in range(NC)
]
SWAP = [(0, 1), (1, 0)]


def local(activations, student_out, teacher_out, weight):
    x, zh, c = (lax.axis_index(n) for n in ("x", "zh", "core"))
    zl = lax.axis_index("inc")
    d = 1 - 2 * c
    own = weight[0]
    mb = activations.shape[0]

    def x_at(k):
        return (x + k * d) & (NX - 1)

    def step_x(value):
        return lax.ppermute(value, ("x", "core"), STEP_X)

    def round_x(piece):
        below = lax.ppermute(piece, "x", by_x(1))
        above = lax.ppermute(piece, "x", by_x(-1))
        far = step_x(jnp.where(c == 0, below, above))
        return (piece, below, above, far), tuple((x + k) & 3 for k in (0, -1, 1, 2))

    diff = (student_out.astype(F32) - teacher_out.astype(F32)).astype(BF16)
    diff_z = lax.ppermute(diff, "inc", SWAP)
    w_z = lax.ppermute(own, "zh", SWAP)
    w_o, at_o = round_x(own)
    act_got = lax.ppermute(other_columns(activations, c), "core", SWAP)
    diffs = (
        diff,
        diff_z,
        lax.ppermute(diff, "core", SWAP),
        lax.ppermute(diff_z, "core", SWAP),
    )
    w_p, at_p = round_x(w_z)

    def dw(ks, z, adds=(), dtype=BF16):
        chunks = [x_at(k) * NZ + z for k in ks]
        return dw_sums(activations, act_got, diffs, chunks, c, zl, adds, dtype)

    def swap_zh(value):
        return lax.ppermute(value, "zh", SWAP)

    z = {}
    (part,) = dw((3,), 1 - zh)
    z[3] = swap_zh(part)
    for k, part in zip((2, 1, 0), dw((2, 1, 0), 1 - zh), strict=True):
        z[k] = swap_zh(part)
    (total,) = dw((3,), zh, (z[3],))
    for k in (2, 1, 0):
        got = step_x(total)
        (total,) = dw((k,), zh, (z[k], got), F32 if k == 0 else BF16)

    def over_y(pieces, where):
        partial = dx_sums(diffs, pieces, where, c, zl)
        return lax.all_to_all(partial, ("core", "outc"), 0, 0, tiled=True)

    input_grad = join(over_y(w_o, at_o), over_y(w_p, at_p), zh, mb)
    return input_grad, total.reshape(weight.shape)


def solution(mesh):
    fine = Mesh(
        mesh.devices.reshape(NX, NZ, NC, NL, NY), ("x", "zh", "core", "inc", "outc")
    )
    tok = ("x", "zh", "core")
    placed = (
        P(None, tok, "inc"),
        P(None, (*tok, "inc"), "outc"),
        P(None, (*tok, "inc"), "outc"),
        P("inc", tok, "outc"),
    )
    return jax.shard_map(
        local,
        mesh=fine,
        in_specs=placed,
        out_specs=(P(None, (*tok, "outc"), "inc"), P("inc", tok, "outc")),
        check_vma=False,
    )
```

time: 353 us -> 146 us (0.41)
  waiting for transfers between devices: 304 us -> 47.2 us
  Pallas kernels: 0 us -> 52.8 us
  starting transfers between devices: 0.16 us -> 31.5 us
  matrix products: 22.7 us -> 0 us
  between operations: 13.8 us -> 0.72 us
  local copies, waits for them, and re-layouts: 2.54 us -> 6.44 us
    reduce_scatter x2 -> x0, waiting for transfers between devices: 215 us -> none  [the longest x1 137 us: local(): lax.psum_scatter(batch_term(jnp.int32(0), lax.axis_size('tok') * weight.s...]
    all_gather x2 -> x0, waiting for transfers between devices: 88.1 us -> none  [the longest x1 61.7 us: local(): lax.all_gather(weight, 'tok', axis=1, tiled=True)]
    pallas_call x0 -> x10, Pallas kernels: none -> 52.8 us  [the longest x6 25.4 us: dw_sums(): pl.pallas_call(functools.partial(dw_body, n, len(adds)), out_shape=[out]...]
    ppermute x0 -> x18, waiting for transfers between devices: none -> 47.2 us  [the longest x2 15.3 us: round_x(): below = lax.ppermute(piece, 'x', by_x(1))]
    dot_general x4 -> x0, matrix products: 22.7 us -> none  [the longest x2 14.3 us: batch_term(): jnp.einsum('ti,tc->ic', columns, cotangent[batch_idx], preferred_element_...]
    ppermute x0 -> x18, starting transfers between devices: none -> 22.5 us  [the longest x4 7.32 us: swap_zh(): return lax.ppermute(value, 'zh', SWAP)]
    all_to_all x0 -> x2, starting transfers between devices: none -> 8.99 us  [over_y(): return lax.all_to_all(partial, ('core', 'outc'), 0, 0, tiled=True)]
  transfers between devices with their start and end apart: 4 -> 20, of which waited for: 4 -> 9; matrix products, arithmetic and copies ran while one was open for 9% -> 4% of each run, Pallas kernels for 0% -> 34%
where the time goes in v2:
time: 146 us; the launch traced here: 145 us
  Pallas kernels  52.8 us (36%)
  waiting for transfers between devices  47.2 us (32%)
  starting transfers between devices  31.5 us (22%)
  local copies, waits for them, and re-layouts  6.44 us (4%)
  other arithmetic  6.32 us (4%)
    pallas_call x6, Pallas kernels, dw_sums(): pl.pallas_call(functools.partial(dw_body, n, len(adds)), out_shape=[out]...  25.4 us
    pallas_call x2, Pallas kernels, dx_sums(): pl.pallas_call(dx_body, out_shape=out, grid_spec=pltpu.PrefetchScalarGrid...  18.5 us
    ppermute x2, waiting for transfers between devices, round_x(): below = lax.ppermute(piece, 'x', by_x(1))  15.3 us
    ppermute x5, waiting for transfers between devices, step_x(): return lax.ppermute(value, ('x', 'core'), STEP_X)  13.8 us
    ppermute x4, waiting for transfers between devices, swap_zh(): return lax.ppermute(value, 'zh', SWAP)  9.39 us
    all_to_all x2, starting transfers between devices, over_y(): return lax.all_to_all(partial, ('core', 'outc'), 0, 0, tiled=True)  8.99 us
    ppermute x1, waiting for transfers between devices, local(): diff_z = lax.ppermute(diff, 'inc', SWAP)  8.68 us
    ppermute x4, starting transfers between devices, swap_zh(): return lax.ppermute(value, 'zh', SWAP)  7.32 us
  transfers between devices with their start and end apart: 20, of which 9 were waited for; matrix products, arithmetic and copies ran while one was open for 4% of the time, Pallas kernels for 34%

profile of v2, /device:TPU:0, one launch (start us, length us, event | category | flops | bytes accessed | tf_op | source)
XLA Modules:
  0.0 144.9 jit_solution(9519912250025149701)
XLA Ops:
  0.6 1.4 subtract_convert_fusion.refs_0_.refs_6_.refs_2_
  2.0 2.1 %collective-permute-start = (bf16[2,128,1024]{2,1,0:T(8,128)(2,1)S(1)}, bf16[2,128,1024]{2,1,0:T(8,128)(2,1)S(1)}, u32[]{:S(2)}, u32[]{:S(2)}) collective-permute-start(bf16[2,128,1024]{2,1,0:T(8,128)(2,1)S(1)} %subtract_convert_fusion.refs_0_.refs_6_.refs_2_), channel_id=1, source_target_pairs={{0,4},{4,0},{1,5},{5,1},{2,6},{6,2},{3,7},{7,3},{8,12},{12,8},{9,1... | collective-permute-start | bytes 1572872 | tf_op jit(solution)/shard_map/ppermute | solution.py:222
  4.1 1.5 %collective-permute-start.3 = (bf16[256,1024]{1,0:T(8,128)(2,1)}, bf16[256,1024]{1,0:T(8,128)(2,1)S(1)}, u32[]{:S(2)}, u32[]{:S(2)}) collective-permute-start(bf16[256,1024]{1,0:T(8,128)(2,1)} %bitcast.26), channel_id=1, source_target_pairs={{0,32},{32,64},{64,96},{96,0},{1,33},{33,65},{65,97},{97,1},{2,34}... | collective-permute-start | bytes 1572872 | tf_op jit(solution)/shard_map/ppermute | solution.py:216
  5.6 1.7 %collective-permute-start.4 = (bf16[256,1024]{1,0:T(8,128)(2,1)}, bf16[256,1024]{1,0:T(8,128)(2,1)S(1)}, u32[]{:S(2)}, u32[]{:S(2)}) collective-permute-start(bf16[256,1024]{1,0:T(8,128)(2,1)} %bitcast.27), channel_id=1, source_target_pairs={{0,96},{32,0},{64,32},{96,64},{1,97},{33,1},{65,33},{97,65},{2,98}... | collective-permute-start | bytes 1572872 | tf_op jit(solution)/shard_map/ppermute | solution.py:217
  7.4 8.7 %collective-permute-done.refs_1_.refs_7_.refs_3_ = bf16[2,128,1024]{2,1,0:T(8,128)(2,1)S(1)} collective-permute-done((bf16[2,128,1024]{2,1,0:T(8,128)(2,1)S(1)}, bf16[2,128,1024]{2,1,0:T(8,128)(2,1)S(1)}, u32[]{:S(2)}, u32[]{:S(2)}) %collective-permute-start) | collective-permute-done | bytes 524320 | tf_op jit(solution)/shard_map/ppermute | solution.py:222
  16.0 2.9 %collective-permute-done.3.refs_5_ = bf16[256,1024]{1,0:T(8,128)(2,1)S(1)} collective-permute-done((bf16[256,1024]{1,0:T(8,128)(2,1)}, bf16[256,1024]{1,0:T(8,128)(2,1)S(1)}, u32[]{:S(2)}, u32[]{:S(2)}) %collective-permute-start.3) | collective-permute-done | bytes 524320 | tf_op jit(solution)/shard_map/ppermute | solution.py:216
  19.9 1.5 %collective-permute-start.5 = (bf16[256,1024]{1,0:T(8,128)(2,1)}, bf16[256,1024]{1,0:T(8,128)(2,1)}, u32[]{:S(2)}, u32[]{:S(2)}) collective-permute-start(bf16[256,1024]{1,0:T(8,128)(2,1)} %broadcast_select_fusion.1), channel_id=1, source_target_pairs={{0,32},{8,104},{32,64},{40,8},{64,96},{72,40},{96,0},{104,72},{1,3... | collective-permute-start | bytes 1572872 | tf_op jit(solution)/shard_map/ppermute | solution.py:213
  21.4 5.6 %other_columns.1 = bf16[8,2,256,256]{3,2,1,0:T(8,128)(2,1)} custom-call(s32[1]{0:T(128)} %bitcast.1.core, bf16[2,256,4096]{2,1,0:T(8,128)(2,1)} %refs_0_.11), custom_call_target="tpu_custom_call" | custom-call | bytes 4194304 | tf_op jit(solution)/shard_map/other_columns/pallas_call | solution.py:29
  27.0 3.7 %collective-permute-start.6 = (bf16[256,1024]{1,0:T(8,128)(2,1)}, bf16[256,1024]{1,0:T(8,128)(2,1)}, u32[]{:S(2)}, u32[]{:S(2)}) collective-permute-start(bf16[256,1024]{1,0:T(8,128)(2,1)} %bitcast.28), channel_id=1, source_target_pairs={{0,16},{16,0},{1,17},{17,1},{2,18},{18,2},{3,19},{19,3},{4,20},{20... | collective-permute-start | bytes 1572872 | tf_op jit(solution)/shard_map/ppermute | solution.py:223
  31.4 9.2 %dx_sums.2 = bf16[8,128,1024]{2,1,0:T(8,128)(2,1)} custom-call(s32[6]{0:T(128)} %stack.106.at, bf16[2,128,1024]{2,1,0:T(8,128)(2,1)} %copy-done.1, bf16[2,128,1024]{2,1,0:T(8,128)(2,1)} %copy-done.2, bf16[2,128,1024]{2,1,0:T(8,128)(2,1)} %collective-permute-done.1.refs_2_.refs_8_.refs_4_, ...), custom_call_target="tpu_custom_call" | custom-call | flops 2147483648 | bytes 6291456 | tf_op jit(solution)/shard_map/dx_sums/pallas_call | solution.py:134
  40.6 4.5 %all-to-all-start = ((bf16[8,128,1024]{2,1,0:T(8,128)(2,1)}), bf16[8,128,1024]{2,1,0:T(8,128)(2,1)}, u32[]{:S(2)}, u32[]{:S(2)}) async-start(bf16[8,128,1024]{2,1,0:T(8,128)(2,1)} %dx_sums.2), calls=%async_computation | async-start | bytes 4194304 | tf_op jit(solution)/shard_map/all_to_all | solution.py:253
  46.3 2.0 %collective-permute-start.8 = (bf16[256,1024]{1,0:T(8,128)(2,1)}, bf16[256,1024]{1,0:T(8,128)(2,1)S(1)}, u32[]{:S(2)}, u32[]{:S(2)}) collective-permute-start(bf16[256,1024]{1,0:T(8,128)(2,1)} %collective-permute-done.6.refs_4_), channel_id=1, source_target_pairs={{0,96},{32,0},{64,32},{96,64},{1,97},{33,1},{65,33},{97,65},{2,98}... | collective-permute-start | bytes 1572872 | tf_op jit(solution)/shard_map/ppermute | solution.py:217
  48.4 12.4 %collective-permute-done.7.refs_5_ = bf16[256,1024]{1,0:T(8,128)(2,1)S(1)} collective-permute-done((bf16[256,1024]{1,0:T(8,128)(2,1)}, bf16[256,1024]{1,0:T(8,128)(2,1)S(1)}, u32[]{:S(2)}, u32[]{:S(2)}) %collective-permute-start.7) | collective-permute-done | bytes 524320 | tf_op jit(solution)/shard_map/ppermute | solution.py:216
  61.8 1.4 collective-permute-start.9
  65.1 3.8 %dw_sums.7 = bf16[256,1024]{1,0:T(8,128)(2,1)} custom-call(s32[3]{0:T(128)} %pad_add_fusion.4.at, bf16[2,256,4096]{2,1,0:T(8,128)(2,1)} %refs_0_.11, bf16[8,2,256,256]{3,2,1,0:T(8,128)(2,1)} %copy-done, bf16[2,128,1024]{2,1,0:T(8,128)(2,1)} %copy-done.1, bf16[2,128,1024]{2,1,0:T(8,128)(2,1)} %copy-done.2, ...), custom_call_target="tpu_custom_call" | custom-call | flops 536870912 | bytes 2621440 | tf_op jit(solution)/shard_map/dw_sums/pallas_call | solution.py:91
  68.9 1.4 collective-permute-start.14
  72.5 9.3 %dx_sums.3 = bf16[8,128,1024]{2,1,0:T(8,128)(2,1)} custom-call(s32[6]{0:T(128)} %stack.106.at, bf16[2,128,1024]{2,1,0:T(8,128)(2,1)} %copy-done.1, bf16[2,128,1024]{2,1,0:T(8,128)(2,1)} %copy-done.2, bf16[2,128,1024]{2,1,0:T(8,128)(2,1)} %collective-permute-done.1.refs_2_.refs_8_.refs_4_, ...), custom_call_target="tpu_custom_call" | custom-call | flops 2147483648 | bytes 6291456 | tf_op jit(solution)/shard_map/dx_sums/pallas_call | solution.py:134
  81.7 4.5 %all-to-all-start.1 = ((bf16[8,128,1024]{2,1,0:T(8,128)(2,1)}), bf16[8,128,1024]{2,1,0:T(8,128)(2,1)S(1)}, u32[]{:S(2)}, u32[]{:S(2)}) async-start(bf16[8,128,1024]{2,1,0:T(8,128)(2,1)} %dx_sums.3), calls=%async_computation.1 | async-start | bytes 4194304 | tf_op jit(solution)/shard_map/all_to_all | solution.py:253
  86.3 5.3 %dw_sums.6 = (bf16[256,1024]{1,0:T(8,128)(2,1)}, bf16[256,1024]{1,0:T(8,128)(2,1)}, bf16[256,1024]{1,0:T(8,128)(2,1)}) custom-call(s32[7]{0:T(128)} %stack.116.at, bf16[2,256,4096]{2,1,0:T(8,128)(2,1)} %refs_0_.11, bf16[2,256,4096]{2,1,0:T(8,128)(2,1)} %refs_0_.11, bf16[2,256,4096]{2,1,0:T(8,128)(2,1)} %refs_0_.11, bf16[8,2,256,256]{3,2,1,0:T(8,128)(2,1)} %copy-done, ...), custom_call_target="tpu_custom_call" | custom-call | flops 1610612736 | bytes 3670016 | tf_op jit(solution)/shard_map/dw_sums/pallas_call | solution.py:91
  91.5 2.7 %collective-permute-start.13 = (bf16[256,1024]{1,0:T(8,128)(2,1)}, bf16[256,1024]{1,0:T(8,128)(2,1)S(1)}, u32[]{:S(2)}, u32[]{:S(2)}) collective-permute-start(bf16[256,1024]{1,0:T(8,128)(2,1)} %get-tuple-element.7), channel_id=1, source_target_pairs={{0,16},{16,0},{1,17},{17,1},{2,18},{18,2},{3,19},{19,3},{4,20},{20... | collective-permute-start | bytes 1572872 | tf_op jit(solution)/shard_map/ppermute | solution.py:239
  95.1 4.0 %dw_sums.8 = bf16[256,1024]{1,0:T(8,128)(2,1)} custom-call(s32[3]{0:T(128)} %pad_add_fusion.3.at, bf16[2,256,4096]{2,1,0:T(8,128)(2,1)} %refs_0_.11, bf16[8,2,256,256]{3,2,1,0:T(8,128)(2,1)} %copy-done, bf16[2,128,1024]{2,1,0:T(8,128)(2,1)} %copy-done.1, bf16[2,128,1024]{2,1,0:T(8,128)(2,1)} %copy-done.2, ...), custom_call_target="tpu_custom_call" | custom-call | flops 536870912 | bytes 2621440 | tf_op jit(solution)/shard_map/dw_sums/pallas_call | solution.py:91
  99.7 1.4 collective-permute-start.12
  101.2 6.8 %collective-permute-done.13.refs_6_ = bf16[256,1024]{1,0:T(8,128)(2,1)S(1)} collective-permute-done((bf16[256,1024]{1,0:T(8,128)(2,1)}, bf16[256,1024]{1,0:T(8,128)(2,1)S(1)}, u32[]{:S(2)}, u32[]{:S(2)}) %collective-permute-start.13) | collective-permute-done | bytes 524320 | tf_op jit(solution)/shard_map/ppermute | solution.py:239
  108.0 1.8 %collective-permute-done.15.refs_7_ = bf16[256,1024]{1,0:T(8,128)(2,1)} collective-permute-done((bf16[256,1024]{1,0:T(8,128)(2,1)}, bf16[256,1024]{1,0:T(8,128)(2,1)}, u32[]{:S(2)}, u32[]{:S(2)}) %collective-permute-start.15) | collective-permute-done | bytes 524320 | tf_op jit(solution)/shard_map/ppermute | solution.py:213
  109.8 4.1 %dw_sums.9 = bf16[256,1024]{1,0:T(8,128)(2,1)} custom-call(s32[3]{0:T(128)} %pad_add_fusion.2.at, bf16[2,256,4096]{2,1,0:T(8,128)(2,1)} %refs_0_.11, bf16[8,2,256,256]{3,2,1,0:T(8,128)(2,1)} %copy-done, bf16[2,128,1024]{2,1,0:T(8,128)(2,1)} %copy-done.1, bf16[2,128,1024]{2,1,0:T(8,128)(2,1)} %copy-done.2, ...), custom_call_target="tpu_custom_call" | custom-call | flops 536870912 | bytes 2621440 | tf_op jit(solution)/shard_map/dw_sums/pallas_call | solution.py:91
  114.5 1.7 %collective-permute-start.11 = (bf16[256,1024]{1,0:T(8,128)(2,1)}, bf16[256,1024]{1,0:T(8,128)(2,1)}, u32[]{:S(2)}, u32[]{:S(2)}) collective-permute-start(bf16[256,1024]{1,0:T(8,128)(2,1)} %get-tuple-element.5), channel_id=1, source_target_pairs={{0,16},{16,0},{1,17},{17,1},{2,18},{18,2},{3,19},{19,3},{4,20},{20... | collective-permute-start | bytes 1572872 | tf_op jit(solution)/shard_map/ppermute | solution.py:239
  116.2 2.6 %collective-permute-done.12.refs_6_ = bf16[256,1024]{1,0:T(8,128)(2,1)S(1)} collective-permute-done((bf16[256,1024]{1,0:T(8,128)(2,1)}, bf16[256,1024]{1,0:T(8,128)(2,1)S(1)}, u32[]{:S(2)}, u32[]{:S(2)}) %collective-permute-start.12) | collective-permute-done | bytes 524320 | tf_op jit(solution)/shard_map/ppermute | solution.py:239
  118.8 5.7 %collective-permute-done.16.refs_7_ = bf16[256,1024]{1,0:T(8,128)(2,1)S(1)} collective-permute-done((bf16[256,1024]{1,0:T(8,128)(2,1)}, bf16[256,1024]{1,0:T(8,128)(2,1)S(1)}, u32[]{:S(2)}, u32[]{:S(2)}) %collective-permute-start.16) | collective-permute-done | bytes 524320 | tf_op jit(solution)/shard_map/ppermute | solution.py:213
  125.3 4.1 %dw_sums.10 = bf16[256,1024]{1,0:T(8,128)(2,1)} custom-call(s32[3]{0:T(128)} %pad_add_fusion.1.at, bf16[2,256,4096]{2,1,0:T(8,128)(2,1)} %refs_0_.11, bf16[8,2,256,256]{3,2,1,0:T(8,128)(2,1)} %copy-done, bf16[2,128,1024]{2,1,0:T(8,128)(2,1)} %copy-done.1, bf16[2,128,1024]{2,1,0:T(8,128)(2,1)} %copy-done.2, ...), custom_call_target="tpu_custom_call" | custom-call | flops 536870912 | bytes 2621440 | tf_op jit(solution)/shard_map/dw_sums/pallas_call | solution.py:91
  131.4 3.2 %join.1 = bf16[2,64,4096]{2,1,0:T(8,128)(2,1)} custom-call(s32[1]{0:T(128)} %bitcast.at, bf16[8,128,1024]{2,1,0:T(8,128)(2,1)} %all-to-all-done.o_ref, bf16[8,128,1024]{2,1,0:T(8,128)(2,1)} %copy-done.3), custom_call_target="tpu_custom_call" | custom-call | flops 2097152 | bytes 5242880 | tf_op jit(solution)/shard_map/join/pallas_call | solution.py:174
  134.6 5.4 %collective-permute-done.17.refs_7_ = bf16[256,1024]{1,0:T(8,128)(2,1)S(1)} collective-permute-done((bf16[256,1024]{1,0:T(8,128)(2,1)}, bf16[256,1024]{1,0:T(8,128)(2,1)S(1)}, u32[]{:S(2)}, u32[]{:S(2)}) %collective-permute-start.17) | collective-permute-done | bytes 524320 | tf_op jit(solution)/shard_map/ppermute | solution.py:213
  140.8 4.1 %dw_sums.11 = f32[256,1024]{1,0:T(8,128)} custom-call(s32[3]{0:T(128)} %pad_add_fusion.at, bf16[2,256,4096]{2,1,0:T(8,128)(2,1)} %refs_0_.11, bf16[8,2,256,256]{3,2,1,0:T(8,128)(2,1)} %copy-done, bf16[2,128,1024]{2,1,0:T(8,128)(2,1)} %copy-done.1, bf16[2,128,1024]{2,1,0:T(8,128)(2,1)} %copy-done.2, ...), custom_call_target="tpu_custom_call" | custom-call | flops 536870912 | bytes 3145728 | tf_op jit(solution)/shard_map/dw_sums/pallas_call | solution.py:91
  (54 shorter events, 13.6 us)
Async XLA Ops:
  2.0 25.0 %copy-start.1 = (bf16[2,128,1024]{2,1,0:T(8,128)(2,1)}, bf16[2,128,1024]{2,1,0:T(8,128)(2,1)S(1)}, u32[]{:S(2)}) copy-start(bf16[2,128,1024]{2,1,0:T(8,128)(2,1)S(1)} %subtract_convert_fusion.refs_0_.refs_6_.refs_2_) | copy-start | bytes 1572868
  2.0 14.0 %collective-permute-start = (bf16[2,128,1024]{2,1,0:T(8,128)(2,1)S(1)}, bf16[2,128,1024]{2,1,0:T(8,128)(2,1)S(1)}, u32[]{:S(2)}, u32[]{:S(2)}) collective-permute-start(bf16[2,128,1024]{2,1,0:T(8,128)(2,1)S(1)} %subtract_convert_fusion.refs_0_.refs_6_.refs_2_), channel_id=1, source_target_pairs={{0,4},{4,0},{1,5},{5,1},{2,6},{6,2},{3,7},{7,3},{8,12},{12,8},{9,1... | collective-permute-start | bytes 1572872 | tf_op jit(solution)/shard_map/ppermute | solution.py:222
  4.1 14.8 %collective-permute-start.3 = (bf16[256,1024]{1,0:T(8,128)(2,1)}, bf16[256,1024]{1,0:T(8,128)(2,1)S(1)}, u32[]{:S(2)}, u32[]{:S(2)}) collective-permute-start(bf16[256,1024]{1,0:T(8,128)(2,1)} %bitcast.26), channel_id=1, source_target_pairs={{0,32},{32,64},{64,96},{96,0},{1,33},{33,65},{65,97},{97,1},{2,34}... | collective-permute-start | bytes 1572872 | tf_op jit(solution)/shard_map/ppermute | solution.py:216
  5.6 13.3 %collective-permute-start.4 = (bf16[256,1024]{1,0:T(8,128)(2,1)}, bf16[256,1024]{1,0:T(8,128)(2,1)S(1)}, u32[]{:S(2)}, u32[]{:S(2)}) collective-permute-start(bf16[256,1024]{1,0:T(8,128)(2,1)} %bitcast.27), channel_id=1, source_target_pairs={{0,96},{32,0},{64,32},{96,64},{1,97},{33,1},{65,33},{97,65},{2,98}... | collective-permute-start | bytes 1572872 | tf_op jit(solution)/shard_map/ppermute | solution.py:217
  7.4 24.0 %collective-permute-start.1 = (bf16[2,128,1024]{2,1,0:T(8,128)(2,1)S(1)}, bf16[2,128,1024]{2,1,0:T(8,128)(2,1)}, u32[]{:S(2)}, u32[]{:S(2)}) collective-permute-start(bf16[2,128,1024]{2,1,0:T(8,128)(2,1)S(1)} %subtract_convert_fusion.refs_0_.refs_6_.refs_2_), channel_id=1, source_target_pairs={{0,8},{8,0},{1,9},{9,1},{2,10},{10,2},{3,11},{11,3},{4,12},{12,4},... | collective-permute-start | bytes 1572872 | tf_op jit(solution)/shard_map/ppermute | solution.py:229
  16.0 11.0 %copy-start.2 = (bf16[2,128,1024]{2,1,0:T(8,128)(2,1)}, bf16[2,128,1024]{2,1,0:T(8,128)(2,1)S(1)}, u32[]{:S(2)}) copy-start(bf16[2,128,1024]{2,1,0:T(8,128)(2,1)S(1)} %collective-permute-done.refs_1_.refs_7_.refs_3_) | copy-start | bytes 1572868
  16.0 15.3 %collective-permute-start.2 = (bf16[2,128,1024]{2,1,0:T(8,128)(2,1)S(1)}, bf16[2,128,1024]{2,1,0:T(8,128)(2,1)}, u32[]{:S(2)}, u32[]{:S(2)}) collective-permute-start(bf16[2,128,1024]{2,1,0:T(8,128)(2,1)S(1)} %collective-permute-done.refs_1_.refs_7_.refs_3_), channel_id=1, source_target_pairs={{0,8},{8,0},{1,9},{9,1},{2,10},{10,2},{3,11},{11,3},{4,12},{12,4},... | collective-permute-start | bytes 1572872 | tf_op jit(solution)/shard_map/ppermute | solution.py:230
  18.9 2.4 %copy-start.10 = (bf16[256,1024]{1,0:T(8,128)(2,1)}, bf16[256,1024]{1,0:T(8,128)(2,1)S(1)}, u32[]{:S(2)}) copy-start(bf16[256,1024]{1,0:T(8,128)(2,1)S(1)} %collective-permute-done.3.refs_5_) | copy-start | bytes 1572868
  18.9 2.4 %copy-start.11 = (bf16[256,1024]{1,0:T(8,128)(2,1)}, bf16[256,1024]{1,0:T(8,128)(2,1)S(1)}, u32[]{:S(2)}) copy-start(bf16[256,1024]{1,0:T(8,128)(2,1)S(1)} %collective-permute-done.4.refs_6_) | copy-start | bytes 1572868
  19.9 11.5 %collective-permute-start.5 = (bf16[256,1024]{1,0:T(8,128)(2,1)}, bf16[256,1024]{1,0:T(8,128)(2,1)}, u32[]{:S(2)}, u32[]{:S(2)}) collective-permute-start(bf16[256,1024]{1,0:T(8,128)(2,1)} %broadcast_select_fusion.1), channel_id=1, source_target_pairs={{0,32},{8,104},{32,64},{40,8},{64,96},{72,40},{96,0},{104,72},{1,3... | collective-permute-start | bytes 1572872 | tf_op jit(solution)/shard_map/ppermute | solution.py:213
  27.0 36.8 %collective-permute-start.10 = (bf16[8,2,256,256]{3,2,1,0:T(8,128)(2,1)}, bf16[8,2,256,256]{3,2,1,0:T(8,128)(2,1)S(1)}, u32[]{:S(2)}, u32[]{:S(2)}) collective-permute-start(bf16[8,2,256,256]{3,2,1,0:T(8,128)(2,1)} %other_columns.1), channel_id=1, source_target_pairs={{0,8},{8,0},{1,9},{9,1},{2,10},{10,2},{3,11},{11,3},{4,12},{12,4},... | collective-permute-start | bytes 6291464 | tf_op jit(solution)/shard_map/ppermute | solution.py:225
  27.0 18.1 %collective-permute-start.6 = (bf16[256,1024]{1,0:T(8,128)(2,1)}, bf16[256,1024]{1,0:T(8,128)(2,1)}, u32[]{:S(2)}, u32[]{:S(2)}) collective-permute-start(bf16[256,1024]{1,0:T(8,128)(2,1)} %bitcast.28), channel_id=1, source_target_pairs={{0,16},{16,0},{1,17},{17,1},{2,18},{18,2},{3,19},{19,3},{4,20},{20... | collective-permute-start | bytes 1572872 | tf_op jit(solution)/shard_map/ppermute | solution.py:223
  40.6 41.2 %all-to-all-start = ((bf16[8,128,1024]{2,1,0:T(8,128)(2,1)}), bf16[8,128,1024]{2,1,0:T(8,128)(2,1)}, u32[]{:S(2)}, u32[]{:S(2)}) async-start(bf16[8,128,1024]{2,1,0:T(8,128)(2,1)} %dx_sums.2), calls=%async_computation | async-start | bytes 4194304 | tf_op jit(solution)/shard_map/all_to_all | solution.py:253
  45.1 15.8 %collective-permute-start.7 = (bf16[256,1024]{1,0:T(8,128)(2,1)}, bf16[256,1024]{1,0:T(8,128)(2,1)S(1)}, u32[]{:S(2)}, u32[]{:S(2)}) collective-permute-start(bf16[256,1024]{1,0:T(8,128)(2,1)} %collective-permute-done.6.refs_4_), channel_id=1, source_target_pairs={{0,32},{32,64},{64,96},{96,0},{1,33},{33,65},{65,97},{97,1},{2,34}... | collective-permute-start | bytes 1572872 | tf_op jit(solution)/shard_map/ppermute | solution.py:216
  46.3 14.5 %collective-permute-start.8 = (bf16[256,1024]{1,0:T(8,128)(2,1)}, bf16[256,1024]{1,0:T(8,128)(2,1)S(1)}, u32[]{:S(2)}, u32[]{:S(2)}) collective-permute-start(bf16[256,1024]{1,0:T(8,128)(2,1)} %collective-permute-done.6.refs_4_), channel_id=1, source_target_pairs={{0,96},{32,0},{64,32},{96,64},{1,97},{33,1},{65,33},{97,65},{2,98}... | collective-permute-start | bytes 1572872 | tf_op jit(solution)/shard_map/ppermute | solution.py:217
  60.8 8.1 %copy-start.8 = (bf16[256,1024]{1,0:T(8,128)(2,1)}, bf16[256,1024]{1,0:T(8,128)(2,1)S(1)}, u32[]{:S(2)}) copy-start(bf16[256,1024]{1,0:T(8,128)(2,1)S(1)} %collective-permute-done.7.refs_5_) | copy-start | bytes 1572868
  60.8 2.9 %copy-start.9 = (bf16[256,1024]{1,0:T(8,128)(2,1)}, bf16[256,1024]{1,0:T(8,128)(2,1)S(1)}, u32[]{:S(2)}) copy-start(bf16[256,1024]{1,0:T(8,128)(2,1)S(1)} %collective-permute-done.8.refs_6_) | copy-start | bytes 1572868
  61.8 10.7 %collective-permute-start.9 = (bf16[256,1024]{1,0:T(8,128)(2,1)}, bf16[256,1024]{1,0:T(8,128)(2,1)}, u32[]{:S(2)}, u32[]{:S(2)}) collective-permute-start(bf16[256,1024]{1,0:T(8,128)(2,1)} %broadcast_select_fusion), channel_id=1, source_target_pairs={{0,32},{8,104},{32,64},{40,8},{64,96},{72,40},{96,0},{104,72},{1,3... | collective-permute-start | bytes 1572872 | tf_op jit(solution)/shard_map/ppermute | solution.py:213
  63.8 1.3 copy-start
  68.9 25.3 %collective-permute-start.14 = (bf16[256,1024]{1,0:T(8,128)(2,1)}, bf16[256,1024]{1,0:T(8,128)(2,1)S(1)}, u32[]{:S(2)}, u32[]{:S(2)}) collective-permute-start(bf16[256,1024]{1,0:T(8,128)(2,1)} %dw_sums.7), channel_id=1, source_target_pairs={{0,16},{16,0},{1,17},{17,1},{2,18},{18,2},{3,19},{19,3},{4,20},{20... | collective-permute-start | bytes 1572872 | tf_op jit(solution)/shard_map/ppermute | solution.py:239
  81.7 48.3 %all-to-all-start.1 = ((bf16[8,128,1024]{2,1,0:T(8,128)(2,1)}), bf16[8,128,1024]{2,1,0:T(8,128)(2,1)S(1)}, u32[]{:S(2)}, u32[]{:S(2)}) async-start(bf16[8,128,1024]{2,1,0:T(8,128)(2,1)} %dx_sums.3), calls=%async_computation.1 | async-start | bytes 4194304 | tf_op jit(solution)/shard_map/all_to_all | solution.py:253
  91.5 16.4 %collective-permute-start.13 = (bf16[256,1024]{1,0:T(8,128)(2,1)}, bf16[256,1024]{1,0:T(8,128)(2,1)S(1)}, u32[]{:S(2)}, u32[]{:S(2)}) collective-permute-start(bf16[256,1024]{1,0:T(8,128)(2,1)} %get-tuple-element.7), channel_id=1, source_target_pairs={{0,16},{16,0},{1,17},{17,1},{2,18},{18,2},{3,19},{19,3},{4,20},{20... | collective-permute-start | bytes 1572872 | tf_op jit(solution)/shard_map/ppermute | solution.py:239
  94.3 0.8 copy-start.4
  99.1 10.7 %collective-permute-start.15 = (bf16[256,1024]{1,0:T(8,128)(2,1)}, bf16[256,1024]{1,0:T(8,128)(2,1)}, u32[]{:S(2)}, u32[]{:S(2)}) collective-permute-start(bf16[256,1024]{1,0:T(8,128)(2,1)} %dw_sums.8), channel_id=1, source_target_pairs={{0,32},{8,104},{32,64},{40,8},{64,96},{72,40},{96,0},{104,72},{1,3... | collective-permute-start | bytes 1572872 | tf_op jit(solution)/shard_map/ppermute | solution.py:213
  99.7 19.1 %collective-permute-start.12 = (bf16[256,1024]{1,0:T(8,128)(2,1)}, bf16[256,1024]{1,0:T(8,128)(2,1)S(1)}, u32[]{:S(2)}, u32[]{:S(2)}) collective-permute-start(bf16[256,1024]{1,0:T(8,128)(2,1)} %get-tuple-element.6), channel_id=1, source_target_pairs={{0,16},{16,0},{1,17},{17,1},{2,18},{18,2},{3,19},{19,3},{4,20},{20... | collective-permute-start | bytes 1572872 | tf_op jit(solution)/shard_map/ppermute | solution.py:239
  108.0 1.8 %copy-start.6 = (bf16[256,1024]{1,0:T(8,128)(2,1)}, bf16[256,1024]{1,0:T(8,128)(2,1)S(1)}, u32[]{:S(2)}) copy-start(bf16[256,1024]{1,0:T(8,128)(2,1)S(1)} %collective-permute-done.13.refs_6_) | copy-start | bytes 1572868
  113.9 10.6 %collective-permute-start.16 = (bf16[256,1024]{1,0:T(8,128)(2,1)}, bf16[256,1024]{1,0:T(8,128)(2,1)S(1)}, u32[]{:S(2)}, u32[]{:S(2)}) collective-permute-start(bf16[256,1024]{1,0:T(8,128)(2,1)} %dw_sums.9), channel_id=1, source_target_pairs={{0,32},{8,104},{32,64},{40,8},{64,96},{72,40},{96,0},{104,72},{1,3... | collective-permute-start | bytes 1572872 | tf_op jit(solution)/shard_map/ppermute | solution.py:213
  114.5 20.1 %collective-permute-start.11 = (bf16[256,1024]{1,0:T(8,128)(2,1)}, bf16[256,1024]{1,0:T(8,128)(2,1)}, u32[]{:S(2)}, u32[]{:S(2)}) collective-permute-start(bf16[256,1024]{1,0:T(8,128)(2,1)} %get-tuple-element.5), channel_id=1, source_target_pairs={{0,16},{16,0},{1,17},{17,1},{2,18},{18,2},{3,19},{19,3},{4,20},{20... | collective-permute-start | bytes 1572872 | tf_op jit(solution)/shard_map/ppermute | solution.py:239
  118.8 5.7 %copy-start.5 = (bf16[256,1024]{1,0:T(8,128)(2,1)}, bf16[256,1024]{1,0:T(8,128)(2,1)S(1)}, u32[]{:S(2)}) copy-start(bf16[256,1024]{1,0:T(8,128)(2,1)S(1)} %collective-permute-done.12.refs_6_) | copy-start | bytes 1572868
  129.4 10.6 %collective-permute-start.17 = (bf16[256,1024]{1,0:T(8,128)(2,1)}, bf16[256,1024]{1,0:T(8,128)(2,1)S(1)}, u32[]{:S(2)}, u32[]{:S(2)}) collective-permute-start(bf16[256,1024]{1,0:T(8,128)(2,1)} %dw_sums.10), channel_id=1, source_target_pairs={{0,32},{8,104},{32,64},{40,8},{64,96},{72,40},{96,0},{104,72},{1,3... | collective-permute-start | bytes 1572872 | tf_op jit(solution)/shard_map/ppermute | solution.py:213
  130.0 1.4 copy-start.3
  140.0 0.8 copy-start.12
  (1 other events, 0.8 us)

commit v3 on v0

v3 whole, which is shorter than its diff:
```python
import jax
import jax.numpy as jnp
from jax import lax
from jax.experimental import pallas as pl
from jax.experimental.pallas import tpu as pltpu
from jax.sharding import Mesh
from jax.sharding import PartitionSpec as P

NX, NZ, NC, NL, NY = 4, 2, 2, 2, 4
F32, BF16 = jnp.float32, jnp.bfloat16
PIECES = (0, -1, 1, 2)


def cost(flops, *arrays):
    moved = sum(a.size * a.dtype.itemsize for a in arrays)
    return pl.CostEstimate(flops=flops, bytes_accessed=moved, transcendentals=0)


def split_columns(act, c):
    mb, toks, width = act.shape
    n = NX * NZ
    rows = width // (n * NC)

    def body(core, a_ref, mine_ref, other_ref):
        own = core[0] == 0
        first, second = a_ref[:, :, :rows], a_ref[:, :, rows:]
        mine_ref[0] = jnp.where(own, first, second)
        other_ref[0] = jnp.where(own, second, first)

    out = jax.ShapeDtypeStruct((n, mb, toks, rows), act.dtype)
    spec = pl.BlockSpec((1, mb, toks, rows), lambda k, core: (k, 0, 0, 0))
    return pl.pallas_call(
        body,
        out_shape=(out, out),
        grid_spec=pltpu.PrefetchScalarGridSpec(
            num_scalar_prefetch=1,
            grid=(n,),
            in_specs=[pl.BlockSpec((mb, toks, NC * rows), lambda k, core: (0, 0, k))],
            out_specs=[spec, spec],
        ),
        compiler_params=pltpu.CompilerParams(vmem_limit_bytes=8 << 20),
        cost_estimate=cost(0, act, act),
        name="split_columns",
    )(c.reshape(1), act)


def dx_body(core, mine, theirs, *refs):
    pieces, out, lhs = refs[:NX], refs[NX], refs[NX + 1]
    mb, toks, cols = mine.shape
    part = toks // NY
    rows = pieces[0].shape[0]
    for diff, n in ((mine, core[0]), (theirs, 1 - core[0])):
        for yt in range(NY):
            for m in range(mb):
                lhs[n, yt, m] = diff[m, yt * part : (yt + 1) * part]
    left = lhs[...].reshape(NC * NY * mb * part, cols)
    for p, piece in enumerate(pieces):
        got = lax.dot_general(
            left, piece[...], (((1,), (1,)), ((), ())), preferred_element_type=F32
        )
        got = got.astype(BF16).reshape(NC * NY, mb * part, rows)
        out[:, :, p * rows : (p + 1) * rows] = got


def dx_sums(mine, theirs, pieces, c):
    mb, toks, cols = mine.shape
    rows = pieces[0].shape[0]
    part = toks // NY
    out = jax.ShapeDtypeStruct((NC * NY, mb * part, NX * rows), BF16)
    vmem = pl.BlockSpec(memory_space=pltpu.VMEM)
    return pl.pallas_call(
        dx_body,
        out_shape=out,
        in_specs=[pl.BlockSpec(memory_space=pltpu.SMEM), *([vmem] * (2 + NX))],
        out_specs=vmem,
        scratch_shapes=[pltpu.VMEM((NC, NY, mb, part, cols), BF16)],
        compiler_params=pltpu.CompilerParams(vmem_limit_bytes=20 << 20),
        cost_estimate=cost(4 * out.size * cols, out, mine, theirs, *pieces),
        name="dx_sums",
    )(c.reshape(1), mine, theirs, *pieces)


def join_body(at, o_ref, p_ref, out_ref):
    x, zh = at[0], at[1]
    width = o_ref.shape[-1]
    rows = width // NX
    for ref, z in ((o_ref, zh), (p_ref, 1 - zh)):
        for n in range(NC):
            total = ref[n * NY].astype(F32)
            for k in range(1, NY):
                total = total + ref[n * NY + k].astype(F32)
            total = total.astype(BF16)
            for p, away in enumerate(PIECES):
                start = ((((x + away) & (NX - 1)) * NZ + z) * NC + n) * rows
                lanes = pl.ds(pl.multiple_of(start, rows), rows)
                out_ref[0, :, lanes] = total[:, p * rows : (p + 1) * rows]


def join(got_o, got_p, x, zh, mb):
    n, toks, width = got_o.shape
    part = toks // mb
    out = jax.ShapeDtypeStruct((mb, part, NZ * NC * width), BF16)
    spec = pl.BlockSpec((n, part, width), lambda m, at: (0, m, 0))
    return pl.pallas_call(
        join_body,
        out_shape=out,
        grid_spec=pltpu.PrefetchScalarGridSpec(
            num_scalar_prefetch=1,
            grid=(mb,),
            in_specs=[spec, spec],
            out_specs=pl.BlockSpec((1, part, NZ * NC * width), lambda m, at: (m, 0, 0)),
        ),
        compiler_params=pltpu.CompilerParams(vmem_limit_bytes=16 << 20),
        cost_estimate=cost(2 * got_o.size, got_o, got_p, out),
        name="join",
    )(jnp.stack([x, zh]), got_o, got_p)


def after(value, *others):
    return lax.optimization_barrier((value, *others))[0]


def by_x(k):
    return [(x, (x + k) % NX) for x in range(NX)]


STEP_X, BACK_X = (
    [
        (x * NC + c, (x + way * (1 - 2 * c)) % NX * NC + c)
        for x in range(NX)
        for c in range(NC)
    ]
    for way in (1, -1)
)
SWAP = [(0, 1), (1, 0)]


def local(activations, student_out, teacher_out, weight):
    x, zh, c = (lax.axis_index(n) for n in ("x", "zh", "core"))
    zl = lax.axis_index("inc")
    d = 1 - 2 * c
    own = weight[0]
    mb = activations.shape[0]

    def step_x(value):
        return lax.ppermute(value, ("x", "core"), STEP_X)

    def back_x(value):
        return lax.ppermute(value, ("x", "core"), BACK_X)

    def swap_zh(value):
        return lax.ppermute(value, "zh", SWAP)

    def round_x(piece):
        below = lax.ppermute(piece, "x", by_x(1))
        above = lax.ppermute(piece, "x", by_x(-1))
        return piece, below, above, step_x(jnp.where(c == 0, below, above))

    diff = (student_out.astype(F32) - teacher_out.astype(F32)).astype(BF16)
    diff_z = lax.ppermute(diff, "inc", SWAP)
    w_o = round_x(own)
    w_z = swap_zh(after(own, diff_z))
    act_mine, act_send = split_columns(after(activations, diff), c)
    act_got = lax.ppermute(act_send, "core", SWAP)
    diff_z = after(diff_z, w_o[1], w_o[2])
    mine = jnp.where(
        zl == 0,
        jnp.concatenate([diff, diff_z], axis=1),
        jnp.concatenate([diff_z, diff], axis=1),
    )
    theirs = lax.ppermute(mine, "core", SWAP)

    def dw(k, z, *got):
        at = ((x + k * d) & (NX - 1)) * NZ + z
        total = None
        for act, part in ((act_mine, mine), (act_got, theirs)):
            a = lax.dynamic_index_in_dim(act, at, 0, keepdims=False)
            term = jnp.einsum("mtr,mtc->rc", a, part, preferred_element_type=F32)
            total = term if total is None else total + term
        for g in got:
            total = total + g.astype(F32)
        return total

    p, o = 1 - zh, zh
    send_p, send_o = dw(2, p).astype(BF16), dw(2, o).astype(BF16)
    far_p, far_o = step_x(send_p), step_x(send_o)

    def over_y(partial):
        return lax.all_to_all(partial, ("core", "outc"), 0, 0, tiled=True)

    partial_o = dx_sums(mine, after(theirs, send_p, send_o), w_o, c)
    got_o = over_y(partial_o)
    mine, theirs, act_got, w_z = lax.optimization_barrier(
        (mine, theirs, act_got, w_z, partial_o)
    )[:4]
    w_p = round_x(w_z)
    back_p = back_x(dw(-1, p).astype(BF16))
    fwd_p = step_x(dw(1, p, far_p).astype(BF16))
    back_o = back_x(dw(-1, o).astype(BF16))
    fwd_o = step_x(dw(1, o, far_o).astype(BF16))
    cross = swap_zh(dw(0, p, back_p, fwd_p).astype(BF16))
    weight_grad = dw(0, o, back_o, fwd_o) + cross.astype(F32)

    partial_p = dx_sums(mine, theirs, w_p, c)
    got_p = over_y(after(partial_p, got_o))
    input_grad = join(got_o, got_p, x, zh, mb)
    return input_grad, weight_grad.reshape(weight.shape)


def solution(mesh):
    fine = Mesh(
        mesh.devices.reshape(NX, NZ, NC, NL, NY), ("x", "zh", "core", "inc", "outc")
    )
    tok = ("x", "zh", "core")
    placed = (
        P(None, tok, "inc"),
        P(None, (*tok, "inc"), "outc"),
        P(None, (*tok, "inc"), "outc"),
        P("inc", tok, "outc"),
    )
    return jax.shard_map(
        local,
        mesh=fine,
        in_specs=placed,
        out_specs=(P(None, (*tok, "outc"), "inc"), P("inc", tok, "outc")),
        check_vma=False,
    )
```

time: 353 us -> 136 us (0.39)
  waiting for transfers between devices: 304 us -> 45.8 us
  starting transfers between devices: 0.16 us -> 33.3 us
  Pallas kernels: 0 us -> 14.1 us
  between operations: 13.8 us -> 0.83 us
  matrix products: 22.7 us -> 30.1 us
  other arithmetic: 9.63 us -> 4.14 us
  local copies, waits for them, and re-layouts: 2.54 us -> 6.3 us
    reduce_scatter x2 -> x0, waiting for transfers between devices: 215 us -> none  [the longest x1 137 us: local(): lax.psum_scatter(batch_term(jnp.int32(0), lax.axis_size('tok') * weight.s...]
    all_gather x2 -> x0, waiting for transfers between devices: 88.1 us -> none  [the longest x1 61.7 us: local(): lax.all_gather(weight, 'tok', axis=1, tiled=True)]
    ppermute x0 -> x17, waiting for transfers between devices: none -> 45.8 us  [the longest x6 22.2 us: step_x(): return lax.ppermute(value, ('x', 'core'), STEP_X)]
    ppermute x0 -> x17, starting transfers between devices: none -> 24 us  [the longest x2 6.83 us: swap_zh(): return lax.ppermute(value, 'zh', SWAP)]
    pallas_call x0 -> x4, Pallas kernels: none -> 14.1 us  [the longest x2 6.97 us: dx_sums(): pl.pallas_call(dx_body, out_shape=out, in_specs=[pl.BlockSpec(memory_spac...]
    all_to_all x0 -> x2, starting transfers between devices: none -> 9.28 us  [over_y(): return lax.all_to_all(partial, ('core', 'outc'), 0, 0, tiled=True)]
    dot_general x4 -> x16, matrix products: 22.7 us -> 30.1 us  [dw(): term = jnp.einsum('mtr,mtc->rc', a, part, preferred_element_type=F32)]
    another operation x1, other arithmetic: 4.74 us -> 0.07 us  [join(): jnp.stack([x, zh])]
  transfers between devices with their start and end apart: 4 -> 19, of which waited for: 4 -> 9; matrix products, arithmetic and copies ran while one was open for 9% -> 24% of each run, Pallas kernels for 0% -> 5%
where the time goes in v3:
time: 136 us; the launch traced here: 135 us
  waiting for transfers between devices  45.8 us (34%)
  starting transfers between devices  33.3 us (24%)
  matrix products  30.1 us (22%)
  Pallas kernels  14.1 us (10%)
  local copies, waits for them, and re-layouts  6.3 us (5%)
  other arithmetic  4.14 us (3%)
    dot_general x16, matrix products, dw(): term = jnp.einsum('mtr,mtc->rc', a, part, preferred_element_type=F32)  30.1 us
    ppermute x6, waiting for transfers between devices, step_x(): return lax.ppermute(value, ('x', 'core'), STEP_X)  22.2 us
    ppermute x2, waiting for transfers between devices, round_x(): below = lax.ppermute(piece, 'x', by_x(1))  11.4 us
    ppermute x2, waiting for transfers between devices, swap_zh(): return lax.ppermute(value, 'zh', SWAP)  9.68 us
    all_to_all x2, starting transfers between devices, over_y(): return lax.all_to_all(partial, ('core', 'outc'), 0, 0, tiled=True)  9.28 us
    pallas_call x2, Pallas kernels, dx_sums(): pl.pallas_call(dx_body, out_shape=out, in_specs=[pl.BlockSpec(memory_spac...  6.97 us
    ppermute x2, starting transfers between devices, swap_zh(): return lax.ppermute(value, 'zh', SWAP)  6.83 us
    unnamed x10, local copies, waits for them, and re-layouts  6.3 us
  transfers between devices with their start and end apart: 19, of which 9 were waited for; matrix products, arithmetic and copies ran while one was open for 24% of the time, Pallas kernels for 5%

profile of v3, /device:TPU:0, one launch (start us, length us, event | category | flops | bytes accessed | tf_op | source)
XLA Modules:
  0.0 134.5 jit_solution(17150209905435120149)
XLA Ops:
  0.6 2.2 %subtract_convert_fusion = bf16[2,128,1024]{2,1,0:T(8,128)(2,1)} fusion(bf16[2,128,1024]{2,1,0:T(8,128)(2,1)} %param.6, bf16[2,128,1024]{2,1,0:T(8,128)(2,1)} %param.5), kind=kLoop, calls=%fused_computation.40 | loop fusion | flops 1048576 | bytes 1572864 | tf_op jit(solution)/shard_map/convert_element_type | solution.py:159
  2.8 2.2 %copy-done = bf16[2,256,4096]{2,1,0:T(8,128)(2,1)S(1)} copy-done((bf16[2,256,4096]{2,1,0:T(8,128)(2,1)S(1)}, bf16[2,256,4096]{2,1,0:T(8,128)(2,1)}, u32[]{:S(2)}) %copy-start) | copy-done | bytes 4194328
  5.0 3.3 %split_columns.1 = (bf16[8,2,256,256]{3,2,1,0:T(8,128)(2,1)S(1)}, bf16[8,2,256,256]{3,2,1,0:T(8,128)(2,1)}) custom-call(s32[1]{0:T(128)} %bitcast.2.core, bf16[2,256,4096]{2,1,0:T(8,128)(2,1)S(1)} %copy-done), custom_call_target="tpu_custom_call" | custom-call | bytes 8388608 | tf_op jit(solution)/shard_map/split_columns/pallas_call | solution.py:32
  9.7 1.6 %collective-permute-start.1 = (bf16[256,1024]{1,0:T(8,128)(2,1)}, bf16[256,1024]{1,0:T(8,128)(2,1)S(1)}, u32[]{:S(2)}, u32[]{:S(2)}) collective-permute-start(bf16[256,1024]{1,0:T(8,128)(2,1)} %bitcast.3.refs_0_), channel_id=1, source_target_pairs={{0,32},{32,64},{64,96},{96,0},{1,33},{33,65},{65,97},{97,1},{2,34}... | collective-permute-start | bytes 1572872 | tf_op jit(solution)/shard_map/ppermute | solution.py:155
  11.2 1.7 %collective-permute-start.2 = (bf16[256,1024]{1,0:T(8,128)(2,1)}, bf16[256,1024]{1,0:T(8,128)(2,1)S(1)}, u32[]{:S(2)}, u32[]{:S(2)}) collective-permute-start(bf16[256,1024]{1,0:T(8,128)(2,1)} %bitcast.3.refs_0_), channel_id=1, source_target_pairs={{0,96},{32,0},{64,32},{96,64},{1,97},{33,1},{65,33},{97,65},{2,98}... | collective-permute-start | bytes 1572872 | tf_op jit(solution)/shard_map/ppermute | solution.py:156
  12.9 2.0 %collective-permute-start = (bf16[2,128,1024]{2,1,0:T(8,128)(2,1)}, bf16[2,128,1024]{2,1,0:T(8,128)(2,1)S(1)}, u32[]{:S(2)}, u32[]{:S(2)}) collective-permute-start(bf16[2,128,1024]{2,1,0:T(8,128)(2,1)} %subtract_convert_fusion), channel_id=1, source_target_pairs={{0,4},{4,0},{1,5},{5,1},{2,6},{6,2},{3,7},{7,3},{8,12},{12,8},{9,1... | collective-permute-start | bytes 1572872 | tf_op jit(solution)/shard_map/ppermute | solution.py:160
  14.9 10.5 %collective-permute-done.1.refs_1_ = bf16[256,1024]{1,0:T(8,128)(2,1)S(1)} collective-permute-done((bf16[256,1024]{1,0:T(8,128)(2,1)}, bf16[256,1024]{1,0:T(8,128)(2,1)S(1)}, u32[]{:S(2)}, u32[]{:S(2)}) %collective-permute-start.1) | collective-permute-done | bytes 524320 | tf_op jit(solution)/shard_map/ppermute | solution.py:155
  25.5 1.6 %collective-permute-done = bf16[2,128,1024]{2,1,0:T(8,128)(2,1)S(1)} collective-permute-done((bf16[2,128,1024]{2,1,0:T(8,128)(2,1)}, bf16[2,128,1024]{2,1,0:T(8,128)(2,1)S(1)}, u32[]{:S(2)}, u32[]{:S(2)}) %collective-permute-start) | collective-permute-done | bytes 524320 | tf_op jit(solution)/shard_map/ppermute | solution.py:160
  27.1 1.8 %maximum_select_fusion.mine = bf16[2,256,1024]{2,1,0:T(8,128)(2,1)S(1)} fusion(bf16[2,128,1024]{2,1,0:T(8,128)(2,1)S(1)} %collective-permute-done, bf16[2,128,1024]{2,1,0:T(8,128)(2,1)} %subtract_convert_fusion, pred[]{:T(512)S(6)} %eq.7), kind=kLoop, calls=%fused_computation.39 | loop fusion | flops 4718592 | bytes 2097153 | tf_op jit(solution)/shard_map/jit(_where)/select_n | solution.py:166
  29.4 3.7 %collective-permute-start.6 = (bf16[256,1024]{1,0:T(8,128)(2,1)}, bf16[256,1024]{1,0:T(8,128)(2,1)}, u32[]{:S(2)}, u32[]{:S(2)}) collective-permute-start(bf16[256,1024]{1,0:T(8,128)(2,1)} %bitcast.3.refs_0_), channel_id=1, source_target_pairs={{0,16},{16,0},{1,17},{17,1},{2,18},{18,2},{3,19},{19,3},{4,20},{20... | collective-permute-start | bytes 1572872 | tf_op jit(solution)/shard_map/ppermute | solution.py:152
  36.0 2.2 %fusion.21 = bf16[256,1024]{1,0:T(8,128)(2,1)} fusion(f32[256,1024]{1,0:T(8,128)S(1)} %convolution_bitcast_fusion.13, bf16[2,256,1024]{2,1,0:T(8,128)(2,1)S(1)} %collective-permute-done.3.theirs, bf16[8,2,256,256]{3,2,1,0:T(8,128)(2,1)} %collective-permute-done.4, s32[]{:T(128)S(6)} %select_n.56), kind=kOutput, calls=%fused_computation.37 | convolution fusion | flops 268959744 | bytes 2883588 | tf_op jit(solution)/shard_map/mtr,mtc->rc/dot_general | solution.py:178
  38.2 2.2 %fusion.22 = bf16[256,1024]{1,0:T(8,128)(2,1)} fusion(f32[256,1024]{1,0:T(8,128)S(1)} %convolution_bitcast_fusion.15, bf16[2,256,1024]{2,1,0:T(8,128)(2,1)S(1)} %collective-permute-done.3.theirs, bf16[8,2,256,256]{3,2,1,0:T(8,128)(2,1)} %collective-permute-done.4, s32[]{:T(128)S(6)} %select_n.55), kind=kOutput, calls=%fused_computation.38 | convolution fusion | flops 268959744 | bytes 2883588 | tf_op jit(solution)/shard_map/mtr,mtc->rc/dot_general | solution.py:178
  40.4 3.5 %dx_sums.2 = bf16[8,128,1024]{2,1,0:T(8,128)(2,1)S(1)} custom-call(s32[1]{0:T(128)} %bitcast.2.core, bf16[2,256,1024]{2,1,0:T(8,128)(2,1)S(1)} %maximum_select_fusion.mine, bf16[2,256,1024]{2,1,0:T(8,128)(2,1)S(1)} %collective-permute-done.3.theirs, bf16[256,1024]{1,0:T(8,128)(2,1)} %bitcast.3.refs_0_, bf16[256,1024]{1,0:T(8,128)(2,1)S(1)} %collective-permute-done.1.refs_1_, ...), custom_call_target="tpu_custom_call" | custom-call | flops 4294967296 | bytes 6291456 | tf_op jit(solution)/shard_map/dx_sums/pallas_call | solution.py:71
  45.5 2.0 %collective-permute-start.7 = (bf16[256,1024]{1,0:T(8,128)(2,1)}, bf16[256,1024]{1,0:T(8,128)(2,1)S(1)}, u32[]{:S(2)}, u32[]{:S(2)}) collective-permute-start(bf16[256,1024]{1,0:T(8,128)(2,1)} %collective-permute-done.6.refs_0_), channel_id=1, source_target_pairs={{0,32},{32,64},{64,96},{96,0},{1,33},{33,65},{65,97},{97,1},{2,34}... | collective-permute-start | bytes 1572872 | tf_op jit(solution)/shard_map/ppermute | solution.py:155
  48.7 4.5 %all-to-all-start = ((bf16[8,128,1024]{2,1,0:T(8,128)(2,1)}), bf16[8,128,1024]{2,1,0:T(8,128)(2,1)}, u32[]{:S(2)}, u32[]{:S(2)}) async-start(bf16[8,128,1024]{2,1,0:T(8,128)(2,1)} %copy-done.2), calls=%async_computation | async-start | bytes 4194304 | tf_op jit(solution)/shard_map/all_to_all | solution.py:189
  55.9 2.2 %fusion.20 = bf16[256,1024]{1,0:T(8,128)(2,1)} fusion(f32[256,1024]{1,0:T(8,128)S(1)} %convolution_bitcast_fusion.8, bf16[2,256,1024]{2,1,0:T(8,128)(2,1)S(1)} %maximum_select_fusion.mine, bf16[8,2,256,256]{3,2,1,0:T(8,128)(2,1)} %copy-done.1, s32[]{:T(128)S(6)} %select_n.61), kind=kOutput, calls=%fused_computation.36 | convolution fusion | flops 268959744 | bytes 2883588 | tf_op jit(solution)/shard_map/mtr,mtc->rc/dot_general | solution.py:178
  58.1 2.7 %collective-permute-start.10 = (bf16[256,1024]{1,0:T(8,128)(2,1)}, bf16[256,1024]{1,0:T(8,128)(2,1)}, u32[]{:S(2)}, u32[]{:S(2)}) collective-permute-start(bf16[256,1024]{1,0:T(8,128)(2,1)} %fusion.20), channel_id=1, source_target_pairs={{0,96},{8,40},{32,0},{40,72},{64,32},{72,104},{96,64},{104,8},{1,9... | collective-permute-start | bytes 1572872 | tf_op jit(solution)/shard_map/ppermute | solution.py:149
  64.6 2.2 %fusion.17 = bf16[256,1024]{1,0:T(8,128)(2,1)} fusion(f32[256,1024]{1,0:T(8,128)S(1)} %convolution_bitcast_fusion.2, bf16[2,256,1024]{2,1,0:T(8,128)(2,1)S(1)} %maximum_select_fusion.mine, bf16[8,2,256,256]{3,2,1,0:T(8,128)(2,1)} %copy-done.1, s32[]{:T(128)S(6)} %select_n.64), kind=kOutput, calls=%fused_computation.33 | convolution fusion | flops 268959744 | bytes 2883588 | tf_op jit(solution)/shard_map/mtr,mtc->rc/dot_general | solution.py:178
  66.8 2.7 %collective-permute-start.13 = (bf16[256,1024]{1,0:T(8,128)(2,1)}, bf16[256,1024]{1,0:T(8,128)(2,1)}, u32[]{:S(2)}, u32[]{:S(2)}) collective-permute-start(bf16[256,1024]{1,0:T(8,128)(2,1)} %fusion.17), channel_id=1, source_target_pairs={{0,96},{8,40},{32,0},{40,72},{64,32},{72,104},{96,64},{104,8},{1,9... | collective-permute-start | bytes 1572872 | tf_op jit(solution)/shard_map/ppermute | solution.py:149
  69.5 2.4 %convolution_bitcast_fusion = f32[256,1024]{1,0:T(8,128)} fusion(bf16[2,256,1024]{2,1,0:T(8,128)(2,1)S(1)} %collective-permute-done.3.theirs, bf16[8,2,256,256]{3,2,1,0:T(8,128)(2,1)} %collective-permute-done.4, s32[]{:T(128)S(6)} %select_n.65), kind=kOutput, calls=%fused_computation | convolution fusion | flops 268435456 | bytes 2359300 | tf_op jit(solution)/shard_map/mtr,mtc->rc/dot_general | solution.py:178
  71.9 17.9 %collective-permute-done.9.refs_3_ = bf16[256,1024]{1,0:T(8,128)(2,1)S(1)} collective-permute-done((bf16[256,1024]{1,0:T(8,128)(2,1)S(1)}, bf16[256,1024]{1,0:T(8,128)(2,1)S(1)}, u32[]{:S(2)}, u32[]{:S(2)}) %collective-permute-start.9) | collective-permute-done | bytes 524320 | tf_op jit(solution)/shard_map/ppermute | solution.py:146
  89.8 3.5 %dx_sums.3 = bf16[8,128,1024]{2,1,0:T(8,128)(2,1)S(1)} custom-call(s32[1]{0:T(128)} %bitcast.2.core, bf16[2,256,1024]{2,1,0:T(8,128)(2,1)S(1)} %maximum_select_fusion.mine, bf16[2,256,1024]{2,1,0:T(8,128)(2,1)S(1)} %collective-permute-done.3.theirs, bf16[256,1024]{1,0:T(8,128)(2,1)} %collective-permute-done.6.refs_0_, ...), custom_call_target="tpu_custom_call" | custom-call | flops 4294967296 | bytes 6291456 | tf_op jit(solution)/shard_map/dx_sums/pallas_call | solution.py:71
  94.7 4.8 %all-to-all-start.1 = ((bf16[8,128,1024]{2,1,0:T(8,128)(2,1)}), bf16[8,128,1024]{2,1,0:T(8,128)(2,1)}, u32[]{:S(2)}, u32[]{:S(2)}) async-start(bf16[8,128,1024]{2,1,0:T(8,128)(2,1)} %copy-done.3), calls=%async_computation.1 | async-start | bytes 4194304 | tf_op jit(solution)/shard_map/all_to_all | solution.py:189
  99.5 1.6 %fusion.16 = bf16[256,1024]{1,0:T(8,128)(2,1)S(1)} fusion(f32[256,1024]{1,0:T(8,128)S(1)} %copy-done.4, bf16[2,256,1024]{2,1,0:T(8,128)(2,1)S(1)} %maximum_select_fusion.mine, bf16[256,1024]{1,0:T(8,128)(2,1)} %collective-permute-done.14, bf16[8,2,256,256]{3,2,1,0:T(8,128)(2,1)} %copy-done.1, s32[]{:T(128)S(6)} %select_n.65), kind=kOutput, calls=%fused_computation.32 | convolution fusion | flops 269484032 | bytes 3407876 | tf_op jit(solution)/shard_map/mtr,mtc->rc/dot_general | solution.py:178
  102.6 1.4 %convolution_bitcast_fusion.4 = f32[256,1024]{1,0:T(8,128)S(1)} fusion(bf16[2,256,1024]{2,1,0:T(8,128)(2,1)S(1)} %collective-permute-done.3.theirs, bf16[8,2,256,256]{3,2,1,0:T(8,128)(2,1)} %collective-permute-done.4, s32[]{:T(128)S(6)} %select_n.63), kind=kOutput, calls=%fused_computation.4 | convolution fusion | flops 268435456 | bytes 2359300 | tf_op jit(solution)/shard_map/mtr,mtc->rc/dot_general | solution.py:178
  104.0 2.4 %fusion.19 = bf16[256,1024]{1,0:T(8,128)(2,1)} fusion(f32[256,1024]{1,0:T(8,128)S(1)} %convolution_bitcast_fusion.6, bf16[2,256,1024]{2,1,0:T(8,128)(2,1)S(1)} %maximum_select_fusion.mine, bf16[256,1024]{1,0:T(8,128)(2,1)} %collective-permute-done.11, bf16[8,2,256,256]{3,2,1,0:T(8,128)(2,1)} %copy-done.1, s32[]{:T(128)S(6)} %select_n.62), kind=kOutput, calls=%fused_computation.35 | convolution fusion | flops 269484032 | bytes 3407876 | tf_op jit(solution)/shard_map/mtr,mtc->rc/dot_general | solution.py:178
  107.3 4.3 %collective-permute-done.15 = bf16[256,1024]{1,0:T(8,128)(2,1)S(1)} collective-permute-done((bf16[256,1024]{1,0:T(8,128)(2,1)S(1)}, bf16[256,1024]{1,0:T(8,128)(2,1)S(1)}, u32[]{:S(2)}, u32[]{:S(2)}) %collective-permute-start.15) | collective-permute-done | bytes 524320 | tf_op jit(solution)/shard_map/ppermute | solution.py:146
  111.5 2.4 %fusion.18 = bf16[256,1024]{1,0:T(8,128)(2,1)} fusion(f32[256,1024]{1,0:T(8,128)S(1)} %convolution_bitcast_fusion.4, bf16[2,256,1024]{2,1,0:T(8,128)(2,1)S(1)} %maximum_select_fusion.mine, bf16[256,1024]{1,0:T(8,128)(2,1)S(1)} %collective-permute-done.15, bf16[256,1024]{1,0:T(8,128)(2,1)} %collective-permute-done.13, ...), kind=kOutput, calls=%fused_computation.34 | convolution fusion | flops 270008320 | bytes 3932164 | tf_op jit(solution)/shard_map/mtr,mtc->rc/dot_general | solution.py:178
  114.0 3.1 %collective-permute-start.16 = (bf16[256,1024]{1,0:T(8,128)(2,1)}, bf16[256,1024]{1,0:T(8,128)(2,1)S(1)}, u32[]{:S(2)}, u32[]{:S(2)}) collective-permute-start(bf16[256,1024]{1,0:T(8,128)(2,1)} %fusion.18), channel_id=1, source_target_pairs={{0,16},{16,0},{1,17},{17,1},{2,18},{18,2},{3,19},{19,3},{4,20},{20... | collective-permute-start | bytes 1572872 | tf_op jit(solution)/shard_map/ppermute | solution.py:152
  118.6 9.5 %collective-permute-done.16 = bf16[256,1024]{1,0:T(8,128)(2,1)S(1)} collective-permute-done((bf16[256,1024]{1,0:T(8,128)(2,1)}, bf16[256,1024]{1,0:T(8,128)(2,1)S(1)}, u32[]{:S(2)}, u32[]{:S(2)}) %collective-permute-start.16) | collective-permute-done | bytes 524320 | tf_op jit(solution)/shard_map/ppermute | solution.py:152
  128.1 2.7 %fusion.6 = f32[1,256,1024]{2,1,0:T(8,128)} fusion(f32[256,1024]{1,0:T(8,128)S(1)} %convolution_bitcast_fusion.10, bf16[2,256,1024]{2,1,0:T(8,128)(2,1)S(1)} %maximum_select_fusion.mine, bf16[256,1024]{1,0:T(8,128)(2,1)S(1)} %collective-permute-done.16, bf16[256,1024]{1,0:T(8,128)(2,1)S(1)} %collective-permute-done.12, ...), kind=kOutput, calls=%fused_computation.22 | convolution fusion | flops 270270464 | bytes 4980740 | tf_op jit(solution)/shard_map/mtr,mtc->rc/dot_general | solution.py:178
  130.7 3.8 %join.1 = bf16[2,64,4096]{2,1,0:T(8,128)(2,1)} custom-call(s32[2]{0:T(128)S(1)} %pad_add_fusion.at, bf16[8,128,1024]{2,1,0:T(8,128)(2,1)} %all-to-all-done.o_ref, bf16[8,128,1024]{2,1,0:T(8,128)(2,1)} %all-to-all-done.1.p_ref), custom_call_target="tpu_custom_call" | custom-call | flops 2097152 | bytes 5242880 | tf_op jit(solution)/shard_map/join/pallas_call | solution.py:104
  (41 shorter events, 19.2 us)
Async XLA Ops:
  2.8 2.2 %copy-start = (bf16[2,256,4096]{2,1,0:T(8,128)(2,1)S(1)}, bf16[2,256,4096]{2,1,0:T(8,128)(2,1)}, u32[]{:S(2)}) copy-start(bf16[2,256,4096]{2,1,0:T(8,128)(2,1)} %a_ref) | copy-start | bytes 12582916
  8.3 1.3 copy-start.1
  9.6 26.3 %collective-permute-start.4 = (bf16[8,2,256,256]{3,2,1,0:T(8,128)(2,1)}, bf16[8,2,256,256]{3,2,1,0:T(8,128)(2,1)}, u32[]{:S(2)}, u32[]{:S(2)}) collective-permute-start(bf16[8,2,256,256]{3,2,1,0:T(8,128)(2,1)} %get-tuple-element.16), channel_id=1, source_target_pairs={{0,8},{8,0},{1,9},{9,1},{2,10},{10,2},{3,11},{11,3},{4,12},{12,4},... | collective-permute-start | bytes 6291464 | tf_op jit(solution)/shard_map/ppermute | solution.py:164
  9.7 15.8 %collective-permute-start.1 = (bf16[256,1024]{1,0:T(8,128)(2,1)}, bf16[256,1024]{1,0:T(8,128)(2,1)S(1)}, u32[]{:S(2)}, u32[]{:S(2)}) collective-permute-start(bf16[256,1024]{1,0:T(8,128)(2,1)} %bitcast.3.refs_0_), channel_id=1, source_target_pairs={{0,32},{32,64},{64,96},{96,0},{1,33},{33,65},{65,97},{97,1},{2,34}... | collective-permute-start | bytes 1572872 | tf_op jit(solution)/shard_map/ppermute | solution.py:155
  11.2 14.3 %collective-permute-start.2 = (bf16[256,1024]{1,0:T(8,128)(2,1)}, bf16[256,1024]{1,0:T(8,128)(2,1)S(1)}, u32[]{:S(2)}, u32[]{:S(2)}) collective-permute-start(bf16[256,1024]{1,0:T(8,128)(2,1)} %bitcast.3.refs_0_), channel_id=1, source_target_pairs={{0,96},{32,0},{64,32},{96,64},{1,97},{33,1},{65,33},{97,65},{2,98}... | collective-permute-start | bytes 1572872 | tf_op jit(solution)/shard_map/ppermute | solution.py:156
  12.9 14.2 %collective-permute-start = (bf16[2,128,1024]{2,1,0:T(8,128)(2,1)}, bf16[2,128,1024]{2,1,0:T(8,128)(2,1)S(1)}, u32[]{:S(2)}, u32[]{:S(2)}) collective-permute-start(bf16[2,128,1024]{2,1,0:T(8,128)(2,1)} %subtract_convert_fusion), channel_id=1, source_target_pairs={{0,4},{4,0},{1,5},{5,1},{2,6},{6,2},{3,7},{7,3},{8,12},{12,8},{9,1... | collective-permute-start | bytes 1572872 | tf_op jit(solution)/shard_map/ppermute | solution.py:160
  28.9 7.1 %collective-permute-start.3 = (bf16[2,256,1024]{2,1,0:T(8,128)(2,1)S(1)}, bf16[2,256,1024]{2,1,0:T(8,128)(2,1)S(1)}, u32[]{:S(2)}, u32[]{:S(2)}) collective-permute-start(bf16[2,256,1024]{2,1,0:T(8,128)(2,1)S(1)} %maximum_select_fusion.mine), channel_id=1, source_target_pairs={{0,8},{8,0},{1,9},{9,1},{2,10},{10,2},{3,11},{11,3},{4,12},{12,4},... | collective-permute-start | bytes 3145736 | tf_op jit(solution)/shard_map/ppermute | solution.py:171
  29.1 11.3 %collective-permute-start.5 = (bf16[256,1024]{1,0:T(8,128)(2,1)S(1)}, bf16[256,1024]{1,0:T(8,128)(2,1)S(1)}, u32[]{:S(2)}, u32[]{:S(2)}) collective-permute-start(bf16[256,1024]{1,0:T(8,128)(2,1)S(1)} %broadcast_select_fusion.1), channel_id=1, source_target_pairs={{0,32},{8,104},{32,64},{40,8},{64,96},{72,40},{96,0},{104,72},{1,3... | collective-permute-start | bytes 1572872 | tf_op jit(solution)/shard_map/ppermute | solution.py:146
  29.4 16.1 %collective-permute-start.6 = (bf16[256,1024]{1,0:T(8,128)(2,1)}, bf16[256,1024]{1,0:T(8,128)(2,1)}, u32[]{:S(2)}, u32[]{:S(2)}) collective-permute-start(bf16[256,1024]{1,0:T(8,128)(2,1)} %bitcast.3.refs_0_), channel_id=1, source_target_pairs={{0,16},{16,0},{1,17},{17,1},{2,18},{18,2},{3,19},{19,3},{4,20},{20... | collective-permute-start | bytes 1572872 | tf_op jit(solution)/shard_map/ppermute | solution.py:152
  43.9 1.4 %copy-start.2 = (bf16[8,128,1024]{2,1,0:T(8,128)(2,1)}, bf16[8,128,1024]{2,1,0:T(8,128)(2,1)S(1)}, u32[]{:S(2)}) copy-start(bf16[8,128,1024]{2,1,0:T(8,128)(2,1)S(1)} %dx_sums.2) | copy-start | bytes 6291460
  45.5 16.2 %collective-permute-start.7 = (bf16[256,1024]{1,0:T(8,128)(2,1)}, bf16[256,1024]{1,0:T(8,128)(2,1)S(1)}, u32[]{:S(2)}, u32[]{:S(2)}) collective-permute-start(bf16[256,1024]{1,0:T(8,128)(2,1)} %collective-permute-done.6.refs_0_), channel_id=1, source_target_pairs={{0,32},{32,64},{64,96},{96,0},{1,33},{33,65},{65,97},{97,1},{2,34}... | collective-permute-start | bytes 1572872 | tf_op jit(solution)/shard_map/ppermute | solution.py:155
  47.5 15.1 %collective-permute-start.8 = (bf16[256,1024]{1,0:T(8,128)(2,1)}, bf16[256,1024]{1,0:T(8,128)(2,1)S(1)}, u32[]{:S(2)}, u32[]{:S(2)}) collective-permute-start(bf16[256,1024]{1,0:T(8,128)(2,1)} %collective-permute-done.6.refs_0_), channel_id=1, source_target_pairs={{0,96},{32,0},{64,32},{96,64},{1,97},{33,1},{65,33},{97,65},{2,98}... | collective-permute-start | bytes 1572872 | tf_op jit(solution)/shard_map/ppermute | solution.py:156
  48.7 46.0 %all-to-all-start = ((bf16[8,128,1024]{2,1,0:T(8,128)(2,1)}), bf16[8,128,1024]{2,1,0:T(8,128)(2,1)}, u32[]{:S(2)}, u32[]{:S(2)}) async-start(bf16[8,128,1024]{2,1,0:T(8,128)(2,1)} %copy-done.2), calls=%async_computation | async-start | bytes 4194304 | tf_op jit(solution)/shard_map/all_to_all | solution.py:189
  53.2 50.8 %collective-permute-start.11 = (bf16[256,1024]{1,0:T(8,128)(2,1)}, bf16[256,1024]{1,0:T(8,128)(2,1)}, u32[]{:S(2)}, u32[]{:S(2)}) collective-permute-start(bf16[256,1024]{1,0:T(8,128)(2,1)} %fusion.21), channel_id=1, source_target_pairs={{0,32},{8,104},{32,64},{40,8},{64,96},{72,40},{96,0},{104,72},{1,3... | collective-permute-start | bytes 1572872 | tf_op jit(solution)/shard_map/ppermute | solution.py:146
  54.0 45.5 %collective-permute-start.14 = (bf16[256,1024]{1,0:T(8,128)(2,1)}, bf16[256,1024]{1,0:T(8,128)(2,1)}, u32[]{:S(2)}, u32[]{:S(2)}) collective-permute-start(bf16[256,1024]{1,0:T(8,128)(2,1)} %fusion.22), channel_id=1, source_target_pairs={{0,32},{8,104},{32,64},{40,8},{64,96},{72,40},{96,0},{104,72},{1,3... | collective-permute-start | bytes 1572872 | tf_op jit(solution)/shard_map/ppermute | solution.py:146
  58.1 60.5 %collective-permute-start.10 = (bf16[256,1024]{1,0:T(8,128)(2,1)}, bf16[256,1024]{1,0:T(8,128)(2,1)}, u32[]{:S(2)}, u32[]{:S(2)}) collective-permute-start(bf16[256,1024]{1,0:T(8,128)(2,1)} %fusion.20), channel_id=1, source_target_pairs={{0,96},{8,40},{32,0},{40,72},{64,32},{72,104},{96,64},{104,8},{1,9... | collective-permute-start | bytes 1572872 | tf_op jit(solution)/shard_map/ppermute | solution.py:149
  62.6 27.2 %collective-permute-start.9 = (bf16[256,1024]{1,0:T(8,128)(2,1)S(1)}, bf16[256,1024]{1,0:T(8,128)(2,1)S(1)}, u32[]{:S(2)}, u32[]{:S(2)}) collective-permute-start(bf16[256,1024]{1,0:T(8,128)(2,1)S(1)} %broadcast_select_fusion), channel_id=1, source_target_pairs={{0,32},{8,104},{32,64},{40,8},{64,96},{72,40},{96,0},{104,72},{1,3... | collective-permute-start | bytes 1572872 | tf_op jit(solution)/shard_map/ppermute | solution.py:146
  66.8 40.5 %collective-permute-start.13 = (bf16[256,1024]{1,0:T(8,128)(2,1)}, bf16[256,1024]{1,0:T(8,128)(2,1)}, u32[]{:S(2)}, u32[]{:S(2)}) collective-permute-start(bf16[256,1024]{1,0:T(8,128)(2,1)} %fusion.17), channel_id=1, source_target_pairs={{0,96},{8,40},{32,0},{40,72},{64,32},{72,104},{96,64},{104,8},{1,9... | collective-permute-start | bytes 1572872 | tf_op jit(solution)/shard_map/ppermute | solution.py:149
  93.3 1.4 %copy-start.3 = (bf16[8,128,1024]{2,1,0:T(8,128)(2,1)}, bf16[8,128,1024]{2,1,0:T(8,128)(2,1)S(1)}, u32[]{:S(2)}) copy-start(bf16[8,128,1024]{2,1,0:T(8,128)(2,1)S(1)} %dx_sums.3) | copy-start | bytes 6291460
  94.7 4.8 %copy-start.4 = (f32[256,1024]{1,0:T(8,128)S(1)}, f32[256,1024]{1,0:T(8,128)}, u32[]{:S(2)}) copy-start(f32[256,1024]{1,0:T(8,128)} %convolution_bitcast_fusion) | copy-start | bytes 3145732
  94.7 36.0 %all-to-all-start.1 = ((bf16[8,128,1024]{2,1,0:T(8,128)(2,1)}), bf16[8,128,1024]{2,1,0:T(8,128)(2,1)}, u32[]{:S(2)}, u32[]{:S(2)}) async-start(bf16[8,128,1024]{2,1,0:T(8,128)(2,1)} %copy-done.3), calls=%async_computation.1 | async-start | bytes 4194304 | tf_op jit(solution)/shard_map/all_to_all | solution.py:189
  101.1 10.5 %collective-permute-start.15 = (bf16[256,1024]{1,0:T(8,128)(2,1)S(1)}, bf16[256,1024]{1,0:T(8,128)(2,1)S(1)}, u32[]{:S(2)}, u32[]{:S(2)}) collective-permute-start(bf16[256,1024]{1,0:T(8,128)(2,1)S(1)} %fusion.16), channel_id=1, source_target_pairs={{0,32},{8,104},{32,64},{40,8},{64,96},{72,40},{96,0},{104,72},{1,3... | collective-permute-start | bytes 1572872 | tf_op jit(solution)/shard_map/ppermute | solution.py:146
  106.4 12.2 %collective-permute-start.12 = (bf16[256,1024]{1,0:T(8,128)(2,1)}, bf16[256,1024]{1,0:T(8,128)(2,1)S(1)}, u32[]{:S(2)}, u32[]{:S(2)}) collective-permute-start(bf16[256,1024]{1,0:T(8,128)(2,1)} %fusion.19), channel_id=1, source_target_pairs={{0,32},{8,104},{32,64},{40,8},{64,96},{72,40},{96,0},{104,72},{1,3... | collective-permute-start | bytes 1572872 | tf_op jit(solution)/shard_map/ppermute | solution.py:146
  114.0 14.1 %collective-permute-start.16 = (bf16[256,1024]{1,0:T(8,128)(2,1)}, bf16[256,1024]{1,0:T(8,128)(2,1)S(1)}, u32[]{:S(2)}, u32[]{:S(2)}) collective-permute-start(bf16[256,1024]{1,0:T(8,128)(2,1)} %fusion.18), channel_id=1, source_target_pairs={{0,16},{16,0},{1,17},{17,1},{2,18},{18,2},{3,19},{19,3},{4,20},{20... | collective-permute-start | bytes 1572872 | tf_op jit(solution)/shard_map/ppermute | solution.py:152

commit v4 on v0

v4 whole, which is shorter than its diff:
```python
import jax
import jax.numpy as jnp
from jax import lax
from jax.experimental import pallas as pl
from jax.experimental.pallas import tpu as pltpu
from jax.sharding import Mesh
from jax.sharding import PartitionSpec as P

NX, NZ, NC, NL, NY = 4, 2, 2, 2, 4
F32, BF16 = jnp.float32, jnp.bfloat16
PIECES = (0, -1, 1, 2)


def cost(flops, *arrays):
    moved = sum(a.size * a.dtype.itemsize for a in arrays)
    return pl.CostEstimate(flops=flops, bytes_accessed=moved, transcendentals=0)


def other_columns(act, c):
    mb, toks, width = act.shape
    n = NX * NZ
    rows = width // (n * NC)

    def body(core, a_ref, out_ref):
        pick = core[0] == 0
        out_ref[0] = jnp.where(pick, a_ref[:, :, rows:], a_ref[:, :, :rows])

    out = jax.ShapeDtypeStruct((n, mb, toks, rows), act.dtype)
    return pl.pallas_call(
        body,
        out_shape=out,
        grid_spec=pltpu.PrefetchScalarGridSpec(
            num_scalar_prefetch=1,
            grid=(n,),
            in_specs=[pl.BlockSpec((mb, toks, NC * rows), lambda k, core: (0, 0, k))],
            out_specs=pl.BlockSpec((1, mb, toks, rows), lambda k, core: (k, 0, 0, 0)),
        ),
        compiler_params=pltpu.CompilerParams(vmem_limit_bytes=8 << 20),
        cost_estimate=cost(0, act, out),
        name="other_columns",
    )(c.reshape(1), act)


def four_terms(rows, cols):
    return [jax.ShapeDtypeStruct((rows, cols), t) for t in (BF16, BF16, F32, F32)]


def dw_body(at, act, got, mine, theirs, *outs):
    mb, toks, cols = mine.shape
    rows = got.shape[-1]
    wide = cols // 2
    for k, out in enumerate(outs):
        lanes = pl.ds(pl.multiple_of((at[k] * NC + at[len(outs)]) * rows, rows), rows)
        a = act[:, :, lanes].reshape(mb * toks, rows)
        b = got[at[k]].reshape(mb * toks, rows)
        for j in range(0, cols, wide):
            total = None
            for lhs, diff in ((a, mine), (b, theirs)):
                term = lax.dot_general(
                    lhs,
                    diff[:, :, j : j + wide].reshape(mb * toks, wide),
                    (((0,), (0,)), ((), ())),
                    preferred_element_type=F32,
                )
                total = term if total is None else total + term
            out[:, j : j + wide] = total.astype(out.dtype)


def dw_terms(at, act, got, mine, theirs):
    outs = four_terms(got.shape[-1], mine.shape[-1])
    vmem = pl.BlockSpec(memory_space=pltpu.VMEM)
    return pl.pallas_call(
        dw_body,
        out_shape=outs,
        in_specs=[pl.BlockSpec(memory_space=pltpu.SMEM), *([vmem] * 4)],
        out_specs=[vmem] * 4,
        compiler_params=pltpu.CompilerParams(vmem_limit_bytes=6 << 20),
        cost_estimate=cost(16 * mine.size * got.shape[-1], *outs, mine, theirs, got),
        name="dw_terms",
    )(at, act, got, mine, theirs)


def dx_body(at, mine, theirs, *refs):
    pieces, outs, lhs = refs[:NX], refs[NX : NX + 4], refs[NX + 4]
    mb, toks, cols = mine.shape
    part = toks // NY
    rows = pieces[0].shape[0]
    for k in range(4):
        start = pl.multiple_of(at[k] * part, part)
        for n, diff in enumerate((mine, theirs)):
            for m in range(mb):
                lhs[k, n, m] = diff[m, pl.ds(start, part)]
    each = NC * mb * part
    left = lhs[...].reshape(4 * each, cols)
    for p, piece in enumerate(pieces):
        got = lax.dot_general(
            left, piece[...], (((1,), (1,)), ((), ())), preferred_element_type=F32
        )
        for k, out in enumerate(outs):
            term = got[k * each : (k + 1) * each]
            out[:, p * rows : (p + 1) * rows] = term.astype(out.dtype)


def dx_terms(at, mine, theirs, pieces):
    mb, toks, cols = mine.shape
    part = toks // NY
    outs = four_terms(NC * mb * part, NX * pieces[0].shape[0])
    vmem = pl.BlockSpec(memory_space=pltpu.VMEM)
    return pl.pallas_call(
        dx_body,
        out_shape=outs,
        in_specs=[pl.BlockSpec(memory_space=pltpu.SMEM), *([vmem] * (2 + NX))],
        out_specs=[vmem] * 4,
        scratch_shapes=[pltpu.VMEM((4, NC, mb, part, cols), BF16)],
        compiler_params=pltpu.CompilerParams(vmem_limit_bytes=8 << 20),
        cost_estimate=cost(8 * outs[0].size * cols, *outs, mine, theirs, *pieces),
        name="dx_terms",
    )(at, mine, theirs, *pieces)


def place_body(at, keep_o, got_o, keep_p, got_p, out_ref):
    x, zh, c = at[0], at[1], at[2]
    mb, part, _ = out_ref.shape
    rows = keep_o.shape[-1] // NX
    for ref, z, n in (
        (keep_o, zh, c),
        (got_o, zh, 1 - c),
        (keep_p, 1 - zh, c),
        (got_p, 1 - zh, 1 - c),
    ):
        for p, away in enumerate(PIECES):
            start = ((((x + away) & (NX - 1)) * NZ + z) * NC + n) * rows
            lanes = pl.ds(pl.multiple_of(start, rows), rows)
            for m in range(mb):
                out_ref[m, :, lanes] = ref[
                    m * part : (m + 1) * part, p * rows : (p + 1) * rows
                ]


def place(at, mb, *parts):
    toks, width = parts[0].shape
    out = jax.ShapeDtypeStruct((mb, toks // mb, NZ * NC * width), BF16)
    vmem = pl.BlockSpec(memory_space=pltpu.VMEM)
    return pl.pallas_call(
        place_body,
        out_shape=out,
        in_specs=[pl.BlockSpec(memory_space=pltpu.SMEM), *([vmem] * 4)],
        out_specs=vmem,
        compiler_params=pltpu.CompilerParams(vmem_limit_bytes=8 << 20),
        cost_estimate=cost(0, out, out),
        name="place",
    )(at, *parts)


def after(value, *others):
    return lax.optimization_barrier((value, *others))[0]


def by_x(k):
    return [(x, (x + k) % NX) for x in range(NX)]


def by_core(n, way, core_first):
    def index(k, c):
        return c * n + k % n if core_first else (k % n) * NC + c

    return [
        (index(k, c), index(k + way * (1 - 2 * c), c)) for k in range(n) for c in range(NC)
    ]


SWAP = [(0, 1), (1, 0)]


def local(activations, student_out, teacher_out, weight):
    x, zh, c, y = (lax.axis_index(n) for n in ("x", "zh", "core", "outc"))
    zl = lax.axis_index("inc")
    d = 1 - 2 * c
    own = weight[0]
    mb = activations.shape[0]

    def step_x(value, way=1):
        return lax.ppermute(value, ("x", "core"), by_core(NX, way, False))

    def step_y(value, way=1):
        return lax.ppermute(value, ("core", "outc"), by_core(NY, way, True))

    def swap_zh(value):
        return lax.ppermute(value, "zh", SWAP)

    def swap_core(value):
        return lax.ppermute(value, "core", SWAP)

    def neighbours(piece):
        return lax.ppermute(piece, "x", by_x(1)), lax.ppermute(piece, "x", by_x(-1))

    def pick(below, above):
        return jnp.where(c == 0, below, above)

    ways = (2, -d, d, 0)
    at_y = jnp.stack([(y + k) & (NY - 1) for k in ways])
    at_o = jnp.stack([*(((x + k) & (NX - 1)) * NZ + zh for k in ways), c])
    at_p = jnp.stack([*(((x + k) & (NX - 1)) * NZ + 1 - zh for k in ways), c])

    diff = (student_out.astype(F32) - teacher_out.astype(F32)).astype(BF16)
    diff_z = lax.ppermute(diff, "inc", SWAP)
    near_o = neighbours(own)
    w_z = swap_zh(own)
    act_send = other_columns(after(activations, *near_o), c)
    act_got = swap_core(act_send)
    w_o = (own, *near_o, step_x(pick(*near_o)))
    near_p = neighbours(w_z)
    w_p = (w_z, *near_p, step_x(pick(*near_p)))
    diff_z = after(diff_z, w_z, act_send, w_o[3])
    mine = jnp.where(
        zl == 0,
        jnp.concatenate([diff, diff_z], axis=1),
        jnp.concatenate([diff_z, diff], axis=1),
    )
    theirs = swap_core(mine)

    def add(*terms):
        total = terms[0].astype(F32)
        for t in terms[1:]:
            total = total + t.astype(F32)
        return total

    def ring(step, terms):
        far, back, ahead, here = terms
        far, back = step(far), step(back, -1)
        return add(here, back, step(add(ahead, far).astype(BF16)))

    terms = dx_terms(at_y, mine, theirs, w_o)
    theirs_w = after(theirs, *terms)
    dx_o = ring(step_y, terms).astype(BF16)
    terms_p = dw_terms(at_p, activations, act_got, mine, theirs_w)
    terms_o = dw_terms(at_o, activations, act_got, mine, after(theirs_w, *terms_p))
    cross = swap_zh(ring(step_x, terms_p).astype(BF16))
    weight_grad = ring(step_x, terms_o) + cross.astype(F32)
    dx_p = ring(step_y, dx_terms(at_y, mine, after(theirs, *terms_o), w_p)).astype(BF16)

    half = dx_o.shape[0] // 2
    got_o, got_p = swap_core(dx_o[half:]), swap_core(dx_p[half:])
    input_grad = place(
        jnp.stack([x, zh, c]), mb, dx_o[:half], got_o, dx_p[:half], got_p
    )
    return input_grad, weight_grad.reshape(weight.shape)


def solution(mesh):
    fine = Mesh(
        mesh.devices.reshape(NX, NZ, NC, NL, NY), ("x", "zh", "core", "inc", "outc")
    )
    tok = ("x", "zh", "core")
    placed = (
        P(None, tok, "inc"),
        P(None, (*tok, "inc"), "outc"),
        P(None, (*tok, "inc"), "outc"),
        P("inc", tok, "outc"),
    )
    return jax.shard_map(
        local,
        mesh=fine,
        in_specs=placed,
        out_specs=(P(None, (*tok, "outc"), "inc"), P("inc", tok, "outc")),
        check_vma=False,
    )
```

time: 353 us -> 119 us (0.34)
  waiting for transfers between devices: 304 us -> 45 us
  starting transfers between devices: 0.16 us -> 31.5 us
  matrix products: 22.7 us -> 0 us
  Pallas kernels: 0 us -> 20.5 us
  between operations: 13.8 us -> 0.87 us
  local copies, waits for them, and re-layouts: 2.54 us -> 10.5 us
    reduce_scatter x2 -> x0, waiting for transfers between devices: 215 us -> none  [the longest x1 137 us: local(): lax.psum_scatter(batch_term(jnp.int32(0), lax.axis_size('tok') * weight.s...]
    all_gather x2 -> x0, waiting for transfers between devices: 88.1 us -> none  [the longest x1 61.7 us: local(): lax.all_gather(weight, 'tok', axis=1, tiled=True)]
    ppermute x0 -> x25, waiting for transfers between devices: none -> 45 us  [the longest x8 14.8 us: step_x(): return lax.ppermute(value, ('x', 'core'), by_core(NX, way, False))]
    ppermute x0 -> x25, starting transfers between devices: none -> 31.5 us  [the longest x8 9.81 us: step_x(): return lax.ppermute(value, ('x', 'core'), by_core(NX, way, False))]
    dot_general x4 -> x0, matrix products: 22.7 us -> none  [the longest x2 14.3 us: batch_term(): jnp.einsum('ti,tc->ic', columns, cotangent[batch_idx], preferred_element_...]
    pallas_call x0 -> x6, Pallas kernels: none -> 20.5 us  [the longest x2 8.44 us: dx_terms(): pl.pallas_call(dx_body, out_shape=outs, in_specs=[pl.BlockSpec(memory_spa...]
    unnamed x5 -> x24, local copies, waits for them, and re-layouts: 2.54 us -> 10.3 us
    another operation x1 -> x2, other arithmetic: 4.74 us -> 0.15 us  [the longest x1 0.08 us: local(): jnp.stack([x, zh, c])]
  transfers between devices with their start and end apart: 4 -> 25, of which waited for: 4 -> 11; matrix products, arithmetic and copies ran while one was open for 9% -> 8% of each run, Pallas kernels for 0% -> 17%
where the time goes in v4:
time: 119 us
  waiting for transfers between devices  45 us (38%)
  starting transfers between devices  31.5 us (26%)
  Pallas kernels  20.5 us (17%)
  local copies, waits for them, and re-layouts  10.5 us (9%)
  other arithmetic  10.2 us (9%)
    ppermute x8, waiting for transfers between devices, step_x(): return lax.ppermute(value, ('x', 'core'), by_core(NX, way, False))  14.8 us
    unnamed x24, local copies, waits for them, and re-layouts  10.3 us
    ppermute x8, starting transfers between devices, step_x(): return lax.ppermute(value, ('x', 'core'), by_core(NX, way, False))  9.81 us
    ppermute x6, waiting for transfers between devices, step_y(): return lax.ppermute(value, ('core', 'outc'), by_core(NY, way, True))  9.63 us
    ppermute x6, starting transfers between devices, step_y(): return lax.ppermute(value, ('core', 'outc'), by_core(NY, way, True))  9.4 us
    pallas_call x2, Pallas kernels, dx_terms(): pl.pallas_call(dx_body, out_shape=outs, in_specs=[pl.BlockSpec(memory_spa...  8.44 us
    pallas_call x2, Pallas kernels, dw_terms(): pl.pallas_call(dw_body, out_shape=outs, in_specs=[pl.BlockSpec(memory_spa...  7.2 us
    ppermute x2, waiting for transfers between devices, neighbours(): lax.ppermute(piece, 'x', by_x(1))  6.72 us
  transfers between devices with their start and end apart: 25, of which 11 were waited for; matrix products, arithmetic and copies ran while one was open for 8% of the time, Pallas kernels for 17%

profile of v4, /device:TPU:0, one launch (start us, length us, event | category | flops | bytes accessed | tf_op | source)
XLA Modules:
  0.0 118.6 jit_solution(12114307305419561914)
XLA Ops:
  0.6 2.9 %collective-permute-start.3 = (bf16[256,1024]{1,0:T(8,128)(2,1)}, bf16[256,1024]{1,0:T(8,128)(2,1)S(1)}, u32[]{:S(2)}, u32[]{:S(2)}) collective-permute-start(bf16[256,1024]{1,0:T(8,128)(2,1)} %bitcast.18), channel_id=1, source_target_pairs={{0,96},{32,0},{64,32},{96,64},{1,97},{33,1},{65,33},{97,65},{2,98}... | collective-permute-start | bytes 1572872 | tf_op jit(solution)/shard_map/ppermute | solution.py:195
  3.5 3.9 %collective-permute-start.1 = (bf16[256,1024]{1,0:T(8,128)(2,1)}, bf16[256,1024]{1,0:T(8,128)(2,1)}, u32[]{:S(2)}, u32[]{:S(2)}) collective-permute-start(bf16[256,1024]{1,0:T(8,128)(2,1)} %bitcast.20), channel_id=1, source_target_pairs={{0,16},{16,0},{1,17},{17,1},{2,18},{18,2},{3,19},{19,3},{4,20},{20... | collective-permute-start | bytes 1572872 | tf_op jit(solution)/shard_map/ppermute | solution.py:189
  7.4 2.2 %subtract_convert_fusion = bf16[2,128,1024]{2,1,0:T(8,128)(2,1)} fusion(bf16[2,128,1024]{2,1,0:T(8,128)(2,1)} %param.6, bf16[2,128,1024]{2,1,0:T(8,128)(2,1)} %param.5), kind=kLoop, calls=%fused_computation.9 | loop fusion | flops 1048576 | bytes 1572864 | tf_op jit(solution)/shard_map/convert_element_type | solution.py:205
  10.6 4.4 %collective-permute-done.3.refs_2_ = bf16[256,1024]{1,0:T(8,128)(2,1)S(1)} collective-permute-done((bf16[256,1024]{1,0:T(8,128)(2,1)}, bf16[256,1024]{1,0:T(8,128)(2,1)S(1)}, u32[]{:S(2)}, u32[]{:S(2)}) %collective-permute-start.3) | collective-permute-done | bytes 524320 | tf_op jit(solution)/shard_map/ppermute | solution.py:195
  15.0 3.3 %collective-permute-done.2.refs_1_ = bf16[256,1024]{1,0:T(8,128)(2,1)S(1)} collective-permute-done((bf16[256,1024]{1,0:T(8,128)(2,1)}, bf16[256,1024]{1,0:T(8,128)(2,1)S(1)}, u32[]{:S(2)}, u32[]{:S(2)}) %collective-permute-start.2) | collective-permute-done | bytes 524320 | tf_op jit(solution)/shard_map/ppermute | solution.py:195
  19.3 2.2 %copy-done = bf16[2,256,4096]{2,1,0:T(8,128)(2,1)S(1)} copy-done((bf16[2,256,4096]{2,1,0:T(8,128)(2,1)S(1)}, bf16[2,256,4096]{2,1,0:T(8,128)(2,1)}, u32[]{:S(2)}) %copy-start) | copy-done | bytes 4194328
  21.5 3.2 %other_columns.1 = bf16[8,2,256,256]{3,2,1,0:T(8,128)(2,1)} custom-call(s32[1]{0:T(128)} %bitcast.2.core, bf16[2,256,4096]{2,1,0:T(8,128)(2,1)S(1)} %copy-done), custom_call_target="tpu_custom_call" | custom-call | bytes 6291456 | tf_op jit(solution)/shard_map/other_columns/pallas_call | solution.py:29
  24.7 6.6 %collective-permute-done = bf16[2,128,1024]{2,1,0:T(8,128)(2,1)} collective-permute-done((bf16[2,128,1024]{2,1,0:T(8,128)(2,1)}, bf16[2,128,1024]{2,1,0:T(8,128)(2,1)}, u32[]{:S(2)}, u32[]{:S(2)}) %collective-permute-start) | collective-permute-done | bytes 524320 | tf_op jit(solution)/shard_map/ppermute | solution.py:206
  31.4 2.2 %maximum_select_fusion.mine = bf16[2,256,1024]{2,1,0:T(8,128)(2,1)S(1)} fusion(bf16[2,128,1024]{2,1,0:T(8,128)(2,1)} %collective-permute-done, bf16[2,128,1024]{2,1,0:T(8,128)(2,1)} %subtract_convert_fusion, pred[]{:T(512)S(6)} %eq.7), kind=kLoop, calls=%fused_computation | loop fusion | flops 4718592 | bytes 2097153 | tf_op jit(solution)/shard_map/jit(_where)/select_n | solution.py:215
  33.6 3.0 %collective-permute-start.12 = (bf16[256,1024]{1,0:T(8,128)(2,1)}, bf16[256,1024]{1,0:T(8,128)(2,1)}, u32[]{:S(2)}, u32[]{:S(2)}) collective-permute-start(bf16[256,1024]{1,0:T(8,128)(2,1)} %collective-permute-done.1.refs_0_), channel_id=1, source_target_pairs={{0,96},{32,0},{64,32},{96,64},{1,97},{33,1},{65,33},{97,65},{2,98}... | collective-permute-start | bytes 1572872 | tf_op jit(solution)/shard_map/ppermute | solution.py:195
  39.9 4.3 %dx_terms.2 = (bf16[256,1024]{1,0:T(8,128)(2,1)}, bf16[256,1024]{1,0:T(8,128)(2,1)S(1)}, f32[256,1024]{1,0:T(8,128)S(1)}, f32[256,1024]{1,0:T(8,128)S(1)}) custom-call(s32[4]{0:T(128)S(1)} %pad_add_fusion.1.at, bf16[2,256,1024]{2,1,0:T(8,128)(2,1)S(1)} %maximum_select_fusion.mine, bf16[2,256,1024]{2,1,0:T(8,128)(2,1)} %collective-permute-done.5.theirs, ...), custom_call_target="tpu_custom_call" | custom-call | flops 2147483648 | bytes 7340032 | tf_op jit(solution)/shard_map/dx_terms/pallas_call | solution.py:109
  47.0 1.6 %collective-permute-start.7 = (bf16[256,1024]{1,0:T(8,128)(2,1)}, bf16[256,1024]{1,0:T(8,128)(2,1)}, u32[]{:S(2)}, u32[]{:S(2)}) collective-permute-start(bf16[256,1024]{1,0:T(8,128)(2,1)} %get-tuple-element.28), channel_id=1, source_target_pairs={{0,1},{8,11},{1,2},{9,8},{2,3},{10,9},{3,0},{11,10},{4,5},{12,15},... | collective-permute-start | bytes 1572872 | tf_op jit(solution)/shard_map/ppermute | solution.py:186
  48.7 3.4 %collective-permute-done.11.refs_1_ = bf16[256,1024]{1,0:T(8,128)(2,1)} collective-permute-done((bf16[256,1024]{1,0:T(8,128)(2,1)}, bf16[256,1024]{1,0:T(8,128)(2,1)}, u32[]{:S(2)}, u32[]{:S(2)}) %collective-permute-start.11) | collective-permute-done | bytes 524320 | tf_op jit(solution)/shard_map/ppermute | solution.py:195
  53.3 3.1 %collective-permute-start.6 = (bf16[256,1024]{1,0:T(8,128)(2,1)}, bf16[256,1024]{1,0:T(8,128)(2,1)S(1)}, u32[]{:S(2)}, u32[]{:S(2)}) collective-permute-start(bf16[256,1024]{1,0:T(8,128)(2,1)} %copy-done.11), channel_id=1, source_target_pairs={{0,3},{8,9},{1,0},{9,10},{2,1},{10,11},{3,2},{11,8},{4,7},{12,13},... | collective-permute-start | bytes 1572872 | tf_op jit(solution)/shard_map/ppermute | solution.py:186
  56.4 1.2 %collective-permute-done.7 = bf16[256,1024]{1,0:T(8,128)(2,1)} collective-permute-done((bf16[256,1024]{1,0:T(8,128)(2,1)}, bf16[256,1024]{1,0:T(8,128)(2,1)}, u32[]{:S(2)}, u32[]{:S(2)}) %collective-permute-start.7) | collective-permute-done | bytes 524320 | tf_op jit(solution)/shard_map/ppermute | solution.py:186
  57.7 1.2 %add_convert_fusion.6 = bf16[256,1024]{1,0:T(8,128)(2,1)S(1)} fusion(f32[256,1024]{1,0:T(8,128)S(1)} %copy-done.5, bf16[256,1024]{1,0:T(8,128)(2,1)} %collective-permute-done.7), kind=kLoop, calls=%fused_computation.8 | loop fusion | flops 786432 | bytes 2097152 | tf_op jit(solution)/shard_map/convert_element_type | solution.py:231
  59.8 2.2 %copy-done.1 = bf16[2,256,4096]{2,1,0:T(8,128)(2,1)S(1)} copy-done((bf16[2,256,4096]{2,1,0:T(8,128)(2,1)S(1)}, bf16[2,256,4096]{2,1,0:T(8,128)(2,1)}, u32[]{:S(2)}) %copy-start.1) | copy-done | bytes 4194328
  62.0 3.6 %dw_terms.2 = (bf16[256,1024]{1,0:T(8,128)(2,1)S(1)}, bf16[256,1024]{1,0:T(8,128)(2,1)S(1)}, f32[256,1024]{1,0:T(8,128)S(1)}, f32[256,1024]{1,0:T(8,128)S(1)}) custom-call(s32[5]{0:T(128)S(1)} %stack.77.at, bf16[2,256,4096]{2,1,0:T(8,128)(2,1)S(1)} %copy-done.1, bf16[8,2,256,256]{3,2,1,0:T(8,128)(2,1)S(1)} %collective-permute-done.10.got, ...), custom_call_target="tpu_custom_call" | custom-call | flops 2147483648 | bytes 7340032 | tf_op jit(solution)/shard_map/dw_terms/pallas_call | solution.py:72
  65.7 6.4 %collective-permute-start.21 = (bf16[256,1024]{1,0:T(8,128)(2,1)S(1)}, bf16[256,1024]{1,0:T(8,128)(2,1)S(1)}, u32[]{:S(2)}, u32[]{:S(2)}) collective-permute-start(bf16[256,1024]{1,0:T(8,128)(2,1)S(1)} %get-tuple-element.31), channel_id=1, source_target_pairs={{0,96},{8,40},{32,0},{40,72},{64,32},{72,104},{96,64},{104,8},{1,9... | collective-permute-start | bytes 1572872 | tf_op jit(solution)/shard_map/ppermute | solution.py:183
  72.1 3.6 %dw_terms.3 = (bf16[256,1024]{1,0:T(8,128)(2,1)S(1)}, bf16[256,1024]{1,0:T(8,128)(2,1)S(1)}, f32[256,1024]{1,0:T(8,128)S(1)}, f32[256,1024]{1,0:T(8,128)S(1)}) custom-call(s32[5]{0:T(128)S(1)} %stack.72.at, bf16[2,256,4096]{2,1,0:T(8,128)(2,1)S(1)} %copy-done.1, bf16[8,2,256,256]{3,2,1,0:T(8,128)(2,1)S(1)} %collective-permute-done.10.got, ...), custom_call_target="tpu_custom_call" | custom-call | flops 2147483648 | bytes 7340032 | tf_op jit(solution)/shard_map/dw_terms/pallas_call | solution.py:72
  75.8 4.1 %dx_terms.3 = (bf16[256,1024]{1,0:T(8,128)(2,1)S(1)}, bf16[256,1024]{1,0:T(8,128)(2,1)S(1)}, f32[256,1024]{1,0:T(8,128)S(1)}, f32[256,1024]{1,0:T(8,128)S(1)}) custom-call(s32[4]{0:T(128)S(1)} %pad_add_fusion.1.at, bf16[2,256,1024]{2,1,0:T(8,128)(2,1)S(1)} %maximum_select_fusion.mine, bf16[2,256,1024]{2,1,0:T(8,128)(2,1)} %collective-permute-done.5.theirs, ...), custom_call_target="tpu_custom_call" | custom-call | flops 2147483648 | bytes 7340032 | tf_op jit(solution)/shard_map/dx_terms/pallas_call | solution.py:109
  79.9 3.2 %collective-permute-start.18 = (bf16[256,1024]{1,0:T(8,128)(2,1)S(1)}, bf16[256,1024]{1,0:T(8,128)(2,1)S(1)}, u32[]{:S(2)}, u32[]{:S(2)}) collective-permute-start(bf16[256,1024]{1,0:T(8,128)(2,1)S(1)} %get-tuple-element.36), channel_id=1, source_target_pairs={{0,96},{8,40},{32,0},{40,72},{64,32},{72,104},{96,64},{104,8},{1,9... | collective-permute-start | bytes 1572872 | tf_op jit(solution)/shard_map/ppermute | solution.py:183
  83.1 1.6 %collective-permute-start.15 = (bf16[256,1024]{1,0:T(8,128)(2,1)S(1)}, bf16[256,1024]{1,0:T(8,128)(2,1)S(1)}, u32[]{:S(2)}, u32[]{:S(2)}) collective-permute-start(bf16[256,1024]{1,0:T(8,128)(2,1)S(1)} %get-tuple-element.43), channel_id=1, source_target_pairs={{0,1},{8,11},{1,2},{9,8},{2,3},{10,9},{3,0},{11,10},{4,5},{12,15},... | collective-permute-start | bytes 1572872 | tf_op jit(solution)/shard_map/ppermute | solution.py:186
  85.0 1.7 %collective-permute-start.14 = (bf16[256,1024]{1,0:T(8,128)(2,1)S(1)}, bf16[256,1024]{1,0:T(8,128)(2,1)S(1)}, u32[]{:S(2)}, u32[]{:S(2)}) collective-permute-start(bf16[256,1024]{1,0:T(8,128)(2,1)S(1)} %get-tuple-element.41), channel_id=1, source_target_pairs={{0,3},{8,9},{1,0},{9,10},{2,1},{10,11},{3,2},{11,8},{4,7},{12,13},... | collective-permute-start | bytes 1572872 | tf_op jit(solution)/shard_map/ppermute | solution.py:186
  86.9 8.4 %collective-permute-done.15 = bf16[256,1024]{1,0:T(8,128)(2,1)S(1)} collective-permute-done((bf16[256,1024]{1,0:T(8,128)(2,1)S(1)}, bf16[256,1024]{1,0:T(8,128)(2,1)S(1)}, u32[]{:S(2)}, u32[]{:S(2)}) %collective-permute-start.15) | collective-permute-done | bytes 524320 | tf_op jit(solution)/shard_map/ppermute | solution.py:186
  96.3 9.3 %collective-permute-done.23 = bf16[256,1024]{1,0:T(8,128)(2,1)S(1)} collective-permute-done((bf16[256,1024]{1,0:T(8,128)(2,1)S(1)}, bf16[256,1024]{1,0:T(8,128)(2,1)S(1)}, u32[]{:S(2)}, u32[]{:S(2)}) %collective-permute-start.23) | collective-permute-done | bytes 524320 | tf_op jit(solution)/shard_map/ppermute | solution.py:183
  105.9 1.2 %collective-permute-start.24 = (bf16[256,1024]{1,0:T(8,128)(2,1)S(1)}, bf16[256,1024]{1,0:T(8,128)(2,1)S(1)}, u32[]{:S(2)}, u32[]{:S(2)}) collective-permute-start(bf16[256,1024]{1,0:T(8,128)(2,1)S(1)} %add_convert_fusion), channel_id=1, source_target_pairs={{0,16},{16,0},{1,17},{17,1},{2,18},{18,2},{3,19},{19,3},{4,20},{20... | collective-permute-start | bytes 1572872 | tf_op jit(solution)/shard_map/ppermute | solution.py:189
  107.6 1.4 %collective-permute-done.17.got_p = bf16[128,1024]{1,0:T(8,128)(2,1)S(1)} collective-permute-done((bf16[128,1024]{1,0:T(8,128)(2,1)S(1)}, bf16[128,1024]{1,0:T(8,128)(2,1)S(1)}, u32[]{:S(2)}, u32[]{:S(2)}) %collective-permute-start.17) | collective-permute-done | bytes 262176 | tf_op jit(solution)/shard_map/ppermute | solution.py:192
  109.1 1.7 %place.1 = bf16[2,64,4096]{2,1,0:T(8,128)(2,1)} custom-call(s32[3]{0:T(128)S(1)} %pad_add_fusion.at, bf16[128,1024]{1,0:T(8,128)(2,1)S(1)} %get-tuple-element.47.keep_o, bf16[128,1024]{1,0:T(8,128)(2,1)S(1)} %collective-permute-done.9.got_o, bf16[128,1024]{1,0:T(8,128)(2,1)S(1)} %get-tuple-element.45.keep_p, bf16[128,1024]{1,0:T(8,128)(2,1)S(1)} %collective-permute-done.17.got_p), custom_call_target="tpu_custom_call" | custom-call | bytes 2097152 | tf_op jit(solution)/shard_map/place/pallas_call | solution.py:144
  110.7 5.3 %collective-permute-done.20 = bf16[256,1024]{1,0:T(8,128)(2,1)S(1)} collective-permute-done((bf16[256,1024]{1,0:T(8,128)(2,1)S(1)}, bf16[256,1024]{1,0:T(8,128)(2,1)S(1)}, u32[]{:S(2)}, u32[]{:S(2)}) %collective-permute-start.20) | collective-permute-done | bytes 524320 | tf_op jit(solution)/shard_map/ppermute | solution.py:183
  116.0 1.3 %collective-permute-done.24 = bf16[256,1024]{1,0:T(8,128)(2,1)S(1)} collective-permute-done((bf16[256,1024]{1,0:T(8,128)(2,1)S(1)}, bf16[256,1024]{1,0:T(8,128)(2,1)S(1)}, u32[]{:S(2)}, u32[]{:S(2)}) %collective-permute-start.24) | collective-permute-done | bytes 524320 | tf_op jit(solution)/shard_map/ppermute | solution.py:189
  117.4 1.3 %add_bitcast_fusion = f32[1,256,1024]{2,1,0:T(8,128)} fusion(bf16[256,1024]{1,0:T(8,128)(2,1)S(1)} %collective-permute-done.24, bf16[256,1024]{1,0:T(8,128)(2,1)S(1)} %collective-permute-done.20, f32[256,1024]{1,0:T(8,128)S(1)} %get-tuple-element.38, bf16[256,1024]{1,0:T(8,128)(2,1)S(1)} %collective-permute-done.18), kind=kLoop, calls=%fused_computation.1 | loop fusion | flops 1572864 | bytes 3670016 | tf_op jit(solution)/shard_map/reshape | solution.py:247
  (66 shorter events, 12.7 us)
Async XLA Ops:
  0.6 14.4 %collective-permute-start.3 = (bf16[256,1024]{1,0:T(8,128)(2,1)}, bf16[256,1024]{1,0:T(8,128)(2,1)S(1)}, u32[]{:S(2)}, u32[]{:S(2)}) collective-permute-start(bf16[256,1024]{1,0:T(8,128)(2,1)} %bitcast.18), channel_id=1, source_target_pairs={{0,96},{32,0},{64,32},{96,64},{1,97},{33,1},{65,33},{97,65},{2,98}... | collective-permute-start | bytes 1572872 | tf_op jit(solution)/shard_map/ppermute | solution.py:195
  3.5 14.8 %collective-permute-start.2 = (bf16[256,1024]{1,0:T(8,128)(2,1)}, bf16[256,1024]{1,0:T(8,128)(2,1)S(1)}, u32[]{:S(2)}, u32[]{:S(2)}) collective-permute-start(bf16[256,1024]{1,0:T(8,128)(2,1)} %bitcast.19), channel_id=1, source_target_pairs={{0,32},{32,64},{64,96},{96,0},{1,33},{33,65},{65,97},{97,1},{2,34}... | collective-permute-start | bytes 1572872 | tf_op jit(solution)/shard_map/ppermute | solution.py:195
  3.5 27.8 %collective-permute-start.1 = (bf16[256,1024]{1,0:T(8,128)(2,1)}, bf16[256,1024]{1,0:T(8,128)(2,1)}, u32[]{:S(2)}, u32[]{:S(2)}) collective-permute-start(bf16[256,1024]{1,0:T(8,128)(2,1)} %bitcast.20), channel_id=1, source_target_pairs={{0,16},{16,0},{1,17},{17,1},{2,18},{18,2},{3,19},{19,3},{4,20},{20... | collective-permute-start | bytes 1572872 | tf_op jit(solution)/shard_map/ppermute | solution.py:189
  9.6 21.7 %collective-permute-start = (bf16[2,128,1024]{2,1,0:T(8,128)(2,1)}, bf16[2,128,1024]{2,1,0:T(8,128)(2,1)}, u32[]{:S(2)}, u32[]{:S(2)}) collective-permute-start(bf16[2,128,1024]{2,1,0:T(8,128)(2,1)} %subtract_convert_fusion), channel_id=1, source_target_pairs={{0,4},{4,0},{1,5},{5,1},{2,6},{6,2},{3,7},{7,3},{8,12},{12,8},{9,1... | collective-permute-start | bytes 1572872 | tf_op jit(solution)/shard_map/ppermute | solution.py:206
  15.0 9.7 %copy-start.6 = (bf16[256,1024]{1,0:T(8,128)(2,1)}, bf16[256,1024]{1,0:T(8,128)(2,1)S(1)}, u32[]{:S(2)}) copy-start(bf16[256,1024]{1,0:T(8,128)(2,1)S(1)} %collective-permute-done.3.refs_2_) | copy-start | bytes 1572868
  18.3 6.4 %copy-start.8 = (bf16[256,1024]{1,0:T(8,128)(2,1)}, bf16[256,1024]{1,0:T(8,128)(2,1)S(1)}, u32[]{:S(2)}) copy-start(bf16[256,1024]{1,0:T(8,128)(2,1)S(1)} %collective-permute-done.2.refs_1_) | copy-start | bytes 1572868
  19.3 12.1 %collective-permute-start.4 = (bf16[256,1024]{1,0:T(8,128)(2,1)}, bf16[256,1024]{1,0:T(8,128)(2,1)}, u32[]{:S(2)}, u32[]{:S(2)}) collective-permute-start(bf16[256,1024]{1,0:T(8,128)(2,1)} %broadcast_select_fusion.1), channel_id=1, source_target_pairs={{0,32},{8,104},{32,64},{40,8},{64,96},{72,40},{96,0},{104,72},{1,3... | collective-permute-start | bytes 1572872 | tf_op jit(solution)/shard_map/ppermute | solution.py:183
  19.3 2.2 %copy-start = (bf16[2,256,4096]{2,1,0:T(8,128)(2,1)S(1)}, bf16[2,256,4096]{2,1,0:T(8,128)(2,1)}, u32[]{:S(2)}) copy-start(bf16[2,256,4096]{2,1,0:T(8,128)(2,1)} %act.3) | copy-start | bytes 12582916
  24.7 35.1 %collective-permute-start.10 = (bf16[8,2,256,256]{3,2,1,0:T(8,128)(2,1)}, bf16[8,2,256,256]{3,2,1,0:T(8,128)(2,1)S(1)}, u32[]{:S(2)}, u32[]{:S(2)}) collective-permute-start(bf16[8,2,256,256]{3,2,1,0:T(8,128)(2,1)} %other_columns.1), channel_id=1, source_target_pairs={{0,8},{8,0},{1,9},{9,1},{2,10},{10,2},{3,11},{11,3},{4,12},{12,4},... | collective-permute-start | bytes 6291464 | tf_op jit(solution)/shard_map/ppermute | solution.py:192
  33.5 3.2 %collective-permute-start.5 = (bf16[2,256,1024]{2,1,0:T(8,128)(2,1)S(1)}, bf16[2,256,1024]{2,1,0:T(8,128)(2,1)}, u32[]{:S(2)}, u32[]{:S(2)}) collective-permute-start(bf16[2,256,1024]{2,1,0:T(8,128)(2,1)S(1)} %maximum_select_fusion.mine), channel_id=1, source_target_pairs={{0,8},{8,0},{1,9},{9,1},{2,10},{10,2},{3,11},{11,3},{4,12},{12,4},... | collective-permute-start | bytes 3145736 | tf_op jit(solution)/shard_map/ppermute | solution.py:192
  33.6 15.1 %collective-permute-start.12 = (bf16[256,1024]{1,0:T(8,128)(2,1)}, bf16[256,1024]{1,0:T(8,128)(2,1)}, u32[]{:S(2)}, u32[]{:S(2)}) collective-permute-start(bf16[256,1024]{1,0:T(8,128)(2,1)} %collective-permute-done.1.refs_0_), channel_id=1, source_target_pairs={{0,96},{32,0},{64,32},{96,64},{1,97},{33,1},{65,33},{97,65},{2,98}... | collective-permute-start | bytes 1572872 | tf_op jit(solution)/shard_map/ppermute | solution.py:195
  36.7 15.5 %collective-permute-start.11 = (bf16[256,1024]{1,0:T(8,128)(2,1)}, bf16[256,1024]{1,0:T(8,128)(2,1)}, u32[]{:S(2)}, u32[]{:S(2)}) collective-permute-start(bf16[256,1024]{1,0:T(8,128)(2,1)} %collective-permute-done.1.refs_0_), channel_id=1, source_target_pairs={{0,32},{32,64},{64,96},{96,0},{1,33},{33,65},{65,97},{97,1},{2,34}... | collective-permute-start | bytes 1572872 | tf_op jit(solution)/shard_map/ppermute | solution.py:195
  36.7 1.0 copy-start.7
  47.0 10.7 %collective-permute-start.7 = (bf16[256,1024]{1,0:T(8,128)(2,1)}, bf16[256,1024]{1,0:T(8,128)(2,1)}, u32[]{:S(2)}, u32[]{:S(2)}) collective-permute-start(bf16[256,1024]{1,0:T(8,128)(2,1)} %get-tuple-element.28), channel_id=1, source_target_pairs={{0,1},{8,11},{1,2},{9,8},{2,3},{10,9},{3,0},{11,10},{4,5},{12,15},... | collective-permute-start | bytes 1572872 | tf_op jit(solution)/shard_map/ppermute | solution.py:186
  48.7 9.0 %copy-start.5 = (f32[256,1024]{1,0:T(8,128)S(1)}, f32[256,1024]{1,0:T(8,128)}, u32[]{:S(2)}) copy-start(f32[256,1024]{1,0:T(8,128)} %copy-done.4) | copy-start | bytes 3145732
  53.3 22.4 %collective-permute-start.13 = (bf16[256,1024]{1,0:T(8,128)(2,1)S(1)}, bf16[256,1024]{1,0:T(8,128)(2,1)S(1)}, u32[]{:S(2)}, u32[]{:S(2)}) collective-permute-start(bf16[256,1024]{1,0:T(8,128)(2,1)S(1)} %broadcast_select_fusion), channel_id=1, source_target_pairs={{0,32},{8,104},{32,64},{40,8},{64,96},{72,40},{96,0},{104,72},{1,3... | collective-permute-start | bytes 1572872 | tf_op jit(solution)/shard_map/ppermute | solution.py:183
  53.3 26.6 %collective-permute-start.6 = (bf16[256,1024]{1,0:T(8,128)(2,1)}, bf16[256,1024]{1,0:T(8,128)(2,1)S(1)}, u32[]{:S(2)}, u32[]{:S(2)}) collective-permute-start(bf16[256,1024]{1,0:T(8,128)(2,1)} %copy-done.11), channel_id=1, source_target_pairs={{0,3},{8,9},{1,0},{9,10},{2,1},{10,11},{3,2},{11,8},{4,7},{12,13},... | collective-permute-start | bytes 1572872 | tf_op jit(solution)/shard_map/ppermute | solution.py:186
  58.9 24.3 %collective-permute-start.8 = (bf16[256,1024]{1,0:T(8,128)(2,1)S(1)}, bf16[256,1024]{1,0:T(8,128)(2,1)S(1)}, u32[]{:S(2)}, u32[]{:S(2)}) collective-permute-start(bf16[256,1024]{1,0:T(8,128)(2,1)S(1)} %add_convert_fusion.6), channel_id=1, source_target_pairs={{0,1},{8,11},{1,2},{9,8},{2,3},{10,9},{3,0},{11,10},{4,5},{12,15},... | collective-permute-start | bytes 1572872 | tf_op jit(solution)/shard_map/ppermute | solution.py:186
  59.8 2.2 %copy-start.1 = (bf16[2,256,4096]{2,1,0:T(8,128)(2,1)S(1)}, bf16[2,256,4096]{2,1,0:T(8,128)(2,1)}, u32[]{:S(2)}) copy-start(bf16[2,256,4096]{2,1,0:T(8,128)(2,1)} %act.3) | copy-start | bytes 12582916
  65.6 19.4 %collective-permute-start.22 = (bf16[256,1024]{1,0:T(8,128)(2,1)S(1)}, bf16[256,1024]{1,0:T(8,128)(2,1)S(1)}, u32[]{:S(2)}, u32[]{:S(2)}) collective-permute-start(bf16[256,1024]{1,0:T(8,128)(2,1)S(1)} %get-tuple-element.30), channel_id=1, source_target_pairs={{0,32},{8,104},{32,64},{40,8},{64,96},{72,40},{96,0},{104,72},{1,3... | collective-permute-start | bytes 1572872 | tf_op jit(solution)/shard_map/ppermute | solution.py:183
  65.7 30.5 %collective-permute-start.21 = (bf16[256,1024]{1,0:T(8,128)(2,1)S(1)}, bf16[256,1024]{1,0:T(8,128)(2,1)S(1)}, u32[]{:S(2)}, u32[]{:S(2)}) collective-permute-start(bf16[256,1024]{1,0:T(8,128)(2,1)S(1)} %get-tuple-element.31), channel_id=1, source_target_pairs={{0,96},{8,40},{32,0},{40,72},{64,32},{72,104},{96,64},{104,8},{1,9... | collective-permute-start | bytes 1572872 | tf_op jit(solution)/shard_map/ppermute | solution.py:183
  75.7 9.0 %copy-start.3 = (f32[256,1024]{1,0:T(8,128)S(1)}, f32[256,1024]{1,0:T(8,128)}, u32[]{:S(2)}) copy-start(f32[256,1024]{1,0:T(8,128)} %copy-done.2) | copy-start | bytes 3145732
  75.7 19.8 %collective-permute-start.19 = (bf16[256,1024]{1,0:T(8,128)(2,1)S(1)}, bf16[256,1024]{1,0:T(8,128)(2,1)S(1)}, u32[]{:S(2)}, u32[]{:S(2)}) collective-permute-start(bf16[256,1024]{1,0:T(8,128)(2,1)S(1)} %get-tuple-element.35), channel_id=1, source_target_pairs={{0,32},{8,104},{32,64},{40,8},{64,96},{72,40},{96,0},{104,72},{1,3... | collective-permute-start | bytes 1572872 | tf_op jit(solution)/shard_map/ppermute | solution.py:183
  79.9 30.8 %collective-permute-start.18 = (bf16[256,1024]{1,0:T(8,128)(2,1)S(1)}, bf16[256,1024]{1,0:T(8,128)(2,1)S(1)}, u32[]{:S(2)}, u32[]{:S(2)}) collective-permute-start(bf16[256,1024]{1,0:T(8,128)(2,1)S(1)} %get-tuple-element.36), channel_id=1, source_target_pairs={{0,96},{8,40},{32,0},{40,72},{64,32},{72,104},{96,64},{104,8},{1,9... | collective-permute-start | bytes 1572872 | tf_op jit(solution)/shard_map/ppermute | solution.py:183
  83.1 12.1 %collective-permute-start.15 = (bf16[256,1024]{1,0:T(8,128)(2,1)S(1)}, bf16[256,1024]{1,0:T(8,128)(2,1)S(1)}, u32[]{:S(2)}, u32[]{:S(2)}) collective-permute-start(bf16[256,1024]{1,0:T(8,128)(2,1)S(1)} %get-tuple-element.43), channel_id=1, source_target_pairs={{0,1},{8,11},{1,2},{9,8},{2,3},{10,9},{3,0},{11,10},{4,5},{12,15},... | collective-permute-start | bytes 1572872 | tf_op jit(solution)/shard_map/ppermute | solution.py:186
  85.0 20.9 %collective-permute-start.14 = (bf16[256,1024]{1,0:T(8,128)(2,1)S(1)}, bf16[256,1024]{1,0:T(8,128)(2,1)S(1)}, u32[]{:S(2)}, u32[]{:S(2)}) collective-permute-start(bf16[256,1024]{1,0:T(8,128)(2,1)S(1)} %get-tuple-element.41), channel_id=1, source_target_pairs={{0,3},{8,9},{1,0},{9,10},{2,1},{10,11},{3,2},{11,8},{4,7},{12,13},... | collective-permute-start | bytes 1572872 | tf_op jit(solution)/shard_map/ppermute | solution.py:186
  95.2 10.4 %collective-permute-start.23 = (bf16[256,1024]{1,0:T(8,128)(2,1)S(1)}, bf16[256,1024]{1,0:T(8,128)(2,1)S(1)}, u32[]{:S(2)}, u32[]{:S(2)}) collective-permute-start(bf16[256,1024]{1,0:T(8,128)(2,1)S(1)} %add_convert_fusion.1), channel_id=1, source_target_pairs={{0,32},{8,104},{32,64},{40,8},{64,96},{72,40},{96,0},{104,72},{1,3... | collective-permute-start | bytes 1572872 | tf_op jit(solution)/shard_map/ppermute | solution.py:183
  95.5 11.6 %collective-permute-start.16 = (bf16[256,1024]{1,0:T(8,128)(2,1)S(1)}, bf16[256,1024]{1,0:T(8,128)(2,1)S(1)}, u32[]{:S(2)}, u32[]{:S(2)}) collective-permute-start(bf16[256,1024]{1,0:T(8,128)(2,1)S(1)} %add_convert_fusion.4), channel_id=1, source_target_pairs={{0,1},{8,11},{1,2},{9,8},{2,3},{10,9},{3,0},{11,10},{4,5},{12,15},... | collective-permute-start | bytes 1572872 | tf_op jit(solution)/shard_map/ppermute | solution.py:186
  96.2 11.4 %collective-permute-start.9 = (bf16[128,1024]{1,0:T(8,128)(2,1)S(1)}, bf16[128,1024]{1,0:T(8,128)(2,1)S(1)}, u32[]{:S(2)}, u32[]{:S(2)}) collective-permute-start(bf16[128,1024]{1,0:T(8,128)(2,1)S(1)} %get-tuple-element.46), channel_id=1, source_target_pairs={{0,8},{8,0},{1,9},{9,1},{2,10},{10,2},{3,11},{11,3},{4,12},{12,4},... | collective-permute-start | bytes 786440 | tf_op jit(solution)/shard_map/ppermute | solution.py:192
  105.6 10.4 %collective-permute-start.20 = (bf16[256,1024]{1,0:T(8,128)(2,1)S(1)}, bf16[256,1024]{1,0:T(8,128)(2,1)S(1)}, u32[]{:S(2)}, u32[]{:S(2)}) collective-permute-start(bf16[256,1024]{1,0:T(8,128)(2,1)S(1)} %add_convert_fusion.2), channel_id=1, source_target_pairs={{0,32},{8,104},{32,64},{40,8},{64,96},{72,40},{96,0},{104,72},{1,3... | collective-permute-start | bytes 1572872 | tf_op jit(solution)/shard_map/ppermute | solution.py:183
  105.9 11.4 %collective-permute-start.24 = (bf16[256,1024]{1,0:T(8,128)(2,1)S(1)}, bf16[256,1024]{1,0:T(8,128)(2,1)S(1)}, u32[]{:S(2)}, u32[]{:S(2)}) collective-permute-start(bf16[256,1024]{1,0:T(8,128)(2,1)S(1)} %add_convert_fusion), channel_id=1, source_target_pairs={{0,16},{16,0},{1,17},{17,1},{2,18},{18,2},{3,19},{19,3},{4,20},{20... | collective-permute-start | bytes 1572872 | tf_op jit(solution)/shard_map/ppermute | solution.py:189
  107.4 1.6 %collective-permute-start.17 = (bf16[128,1024]{1,0:T(8,128)(2,1)S(1)}, bf16[128,1024]{1,0:T(8,128)(2,1)S(1)}, u32[]{:S(2)}, u32[]{:S(2)}) collective-permute-start(bf16[128,1024]{1,0:T(8,128)(2,1)S(1)} %get-tuple-element.44), channel_id=1, source_target_pairs={{0,8},{8,0},{1,9},{9,1},{2,10},{10,2},{3,11},{11,3},{4,12},{12,4},... | collective-permute-start | bytes 786440 | tf_op jit(solution)/shard_map/ppermute | solution.py:192
  (5 other events, 4.9 us)

commit v5 on v4

v5 whole, which is shorter than its diff:
```python
import math

import jax
import jax.numpy as jnp
from jax import lax
from jax.experimental import pallas as pl
from jax.experimental.pallas import tpu as pltpu
from jax.sharding import Mesh
from jax.sharding import PartitionSpec as P

NX, NZ, NC, NL, NY = 4, 2, 2, 2, 4
F32, BF16 = jnp.float32, jnp.bfloat16
PIECES = (0, -1, 1, 2)


def cost(flops, *arrays):
    moved = sum(math.prod(a.shape) * jnp.dtype(a.dtype).itemsize for a in arrays)
    return pl.CostEstimate(flops=flops, bytes_accessed=moved, transcendentals=0)


HBM = pl.BlockSpec(memory_space=pltpu.HBM)
SMEM = pl.BlockSpec(memory_space=pltpu.SMEM)


def in_hbm(array):
    return pltpu.with_memory_space_constraint(array, pltpu.HBM)


def start_all(pairs, sems, first=0):
    copies = [
        pltpu.make_async_copy(src, dst, sems.at[first + k])
        for k, (src, dst) in enumerate(pairs)
    ]
    for copy in copies:
        copy.start()
    return copies


def wait_all(copies):
    for copy in copies:
        copy.wait()


def other_columns(act, c):
    mb, toks, width = act.shape
    n = NX * NZ
    rows = width // (n * NC)

    def body(core, act_ref, out_ref, sems):
        pairs = []
        for k in range(n):
            start = pl.multiple_of((k * NC + 1 - core[0]) * rows, rows)
            pairs.append((act_ref.at[:, :, pl.ds(start, rows)], out_ref.at[k]))
        wait_all(start_all(pairs, sems))

    out = pltpu.HBM((n, mb, toks, rows), act.dtype)
    return pl.pallas_call(
        body,
        out_shape=out,
        in_specs=[SMEM, HBM],
        out_specs=HBM,
        scratch_shapes=[pltpu.SemaphoreType.DMA((n,))],
        compiler_params=pltpu.CompilerParams(vmem_limit_bytes=1 << 20),
        cost_estimate=cost(0, out, out),
        name="other_columns",
    )(c.reshape(1), in_hbm(act))


def four_terms(rows, cols):
    return [pltpu.HBM((rows, cols), t) for t in (BF16, BF16, F32, F32)]


def dw_body(at, act, got, *refs):
    diffs, outs = refs[:4], refs[4:8]
    lhs, rhs, narrow, wide, sems = refs[8:]
    mb, part, cols = diffs[0].shape
    rows = got.shape[-1]
    toks = NL * part
    c, zl = at[4], at[5]
    loads = []
    for j, diff in enumerate(diffs):
        start = pl.multiple_of((zl if j % 2 == 0 else 1 - zl) * part, part)
        loads.append((diff, rhs.at[j // 2, :, pl.ds(start, part)]))
    for k in range(4):
        start = pl.multiple_of((at[k] * NC + c) * rows, rows)
        loads.append((act.at[:, :, pl.ds(start, rows)], lhs.at[k, 0]))
        loads.append((got.at[at[k]], lhs.at[k, 1]))
    loads = start_all(loads, sems)
    wait_all(loads[:4])
    stores = []
    step = cols // 2
    for k, out in enumerate(outs):
        wait_all(loads[4 + 2 * k : 6 + 2 * k])
        held = narrow.at[k] if k < 2 else wide.at[k - 2]
        for j in range(0, cols, step):
            total = None
            for n in range(NC):
                term = lax.dot_general(
                    lhs[k, n].reshape(mb * toks, rows),
                    rhs[n, :, :, j : j + step].reshape(mb * toks, step),
                    (((0,), (0,)), ((), ())),
                    preferred_element_type=F32,
                )
                total = term if total is None else total + term
            held[:, j : j + step] = total.astype(held.dtype)
        stores += start_all([(held, out)], sems, len(loads) + k)
    wait_all(stores)


def dw_terms(at, act, got, diffs):
    mb, part, cols = diffs[0].shape
    rows = got.shape[-1]
    toks = NL * part
    outs = four_terms(rows, cols)
    return pl.pallas_call(
        dw_body,
        out_shape=outs,
        in_specs=[SMEM, *([HBM] * 6)],
        out_specs=[HBM] * 4,
        scratch_shapes=[
            pltpu.VMEM((4, NC, mb, toks, rows), BF16),
            pltpu.VMEM((NC, mb, toks, cols), BF16),
            pltpu.VMEM((2, rows, cols), BF16),
            pltpu.VMEM((2, rows, cols), F32),
            pltpu.SemaphoreType.DMA((16,)),
        ],
        compiler_params=pltpu.CompilerParams(vmem_limit_bytes=20 << 20),
        cost_estimate=cost(16 * NC * mb * toks * rows * cols // 2, *outs, *diffs, got),
        name="dw_terms",
    )(at, in_hbm(act), got, *map(in_hbm, diffs))


def dx_body(at, *refs):
    diffs, pieces, outs = refs[:4], refs[4:8], refs[8:12]
    lhs, rhs, narrow, wide, sems = refs[12:]
    mb, toks, cols = diffs[0].shape
    part = toks // 2
    rows = pieces[0].shape[0]
    loads = [(piece, rhs.at[p]) for p, piece in enumerate(pieces)]
    for j, diff in enumerate(diffs):
        for h in range(2):
            k = at[j % 2 * 2 + h]
            for m in range(mb):
                src = diff.at[m, h * part : (h + 1) * part]
                loads.append((src, lhs.at[k, j // 2, m]))
    wait_all(start_all(loads, sems))
    each = NC * mb * part
    stores = []
    for g, held in enumerate((narrow, wide)):
        left = lhs[2 * g : 2 * g + 2].reshape(2 * each, cols)
        for p in range(NX):
            got = lax.dot_general(
                left, rhs[p], (((1,), (1,)), ((), ())), preferred_element_type=F32
            )
            for k in range(2):
                term = got[k * each : (k + 1) * each]
                held[k, :, p * rows : (p + 1) * rows] = term.astype(held.dtype)
        pairs = [(held.at[k], outs[2 * g + k]) for k in range(2)]
        stores += start_all(pairs, sems, len(loads) + 2 * g)
    wait_all(stores)


def dx_terms(at, diffs, pieces):
    mb, toks, cols = diffs[0].shape
    part = toks // 2
    rows = pieces[0].shape[0]
    outs = four_terms(NC * mb * part, NX * rows)
    return pl.pallas_call(
        dx_body,
        out_shape=outs,
        in_specs=[SMEM, *([HBM] * (4 + NX))],
        out_specs=[HBM] * 4,
        scratch_shapes=[
            pltpu.VMEM((4, NC, mb, part, cols), BF16),
            pltpu.VMEM((NX, rows, cols), BF16),
            pltpu.VMEM((2, NC * mb * part, NX * rows), BF16),
            pltpu.VMEM((2, NC * mb * part, NX * rows), F32),
            pltpu.SemaphoreType.DMA((NX + 16 + 4,)),
        ],
        compiler_params=pltpu.CompilerParams(vmem_limit_bytes=20 << 20),
        cost_estimate=cost(8 * math.prod(outs[0].shape) * cols, *outs, *diffs, *pieces),
        name="dx_terms",
    )(at, *map(in_hbm, (*diffs, *pieces)))


def place_body(at, keep_o, got_o, keep_p, got_p, out_ref):
    x, zh, c = at[0], at[1], at[2]
    mb, part, _ = out_ref.shape
    rows = keep_o.shape[-1] // NX
    for ref, z, n in (
        (keep_o, zh, c),
        (got_o, zh, 1 - c),
        (keep_p, 1 - zh, c),
        (got_p, 1 - zh, 1 - c),
    ):
        for p, away in enumerate(PIECES):
            start = ((((x + away) & (NX - 1)) * NZ + z) * NC + n) * rows
            lanes = pl.ds(pl.multiple_of(start, rows), rows)
            for m in range(mb):
                out_ref[m, :, lanes] = ref[
                    m * part : (m + 1) * part, p * rows : (p + 1) * rows
                ]


def place(at, mb, *parts):
    toks, width = parts[0].shape
    out = jax.ShapeDtypeStruct((mb, toks // mb, NZ * NC * width), BF16)
    vmem = pl.BlockSpec(memory_space=pltpu.VMEM)
    return pl.pallas_call(
        place_body,
        out_shape=out,
        in_specs=[pl.BlockSpec(memory_space=pltpu.SMEM), *([vmem] * 4)],
        out_specs=vmem,
        compiler_params=pltpu.CompilerParams(vmem_limit_bytes=8 << 20),
        cost_estimate=cost(0, out, out),
        name="place",
    )(at, *parts)


def after(value, *others):
    return lax.optimization_barrier((value, *others))[0]


def by_x(k):
    return [(x, (x + k) % NX) for x in range(NX)]


def by_core(n, way, core_first):
    def index(k, c):
        return c * n + k % n if core_first else (k % n) * NC + c

    return [
        (index(k, c), index(k + way * (1 - 2 * c), c)) for k in range(n) for c in range(NC)
    ]


SWAP = [(0, 1), (1, 0)]


def local(activations, student_out, teacher_out, weight):
    x, zh, c, y = (lax.axis_index(n) for n in ("x", "zh", "core", "outc"))
    zl = lax.axis_index("inc")
    d = 1 - 2 * c
    own = weight[0]
    mb = activations.shape[0]

    def step_x(value, way=1):
        return lax.ppermute(value, ("x", "core"), by_core(NX, way, False))

    def step_y(value, way=1):
        return lax.ppermute(value, ("core", "outc"), by_core(NY, way, True))

    def swap_zh(value):
        return lax.ppermute(value, "zh", SWAP)

    def swap_core(value):
        return lax.ppermute(value, "core", SWAP)

    def neighbours(piece):
        return lax.ppermute(piece, "x", by_x(1)), lax.ppermute(piece, "x", by_x(-1))

    def pick(below, above):
        return jnp.where(c == 0, below, above)

    ways = (2, -d, d, 0)
    at_o = jnp.stack([*(((x + k) & (NX - 1)) * NZ + zh for k in ways), c, zl])
    at_p = jnp.stack([*(((x + k) & (NX - 1)) * NZ + 1 - zh for k in ways), c, zl])

    def place_of(z, h):
        away = (2 * z + h - y) & (NY - 1)
        beside = jnp.where(away == (d & (NY - 1)), 2, 1)
        return jnp.where(away == 2, 0, jnp.where(away == 0, 3, beside))

    at_y = jnp.stack([place_of(z, h) for z in (zl, 1 - zl) for h in range(2)])

    act_send = other_columns(activations, c)
    student_out = after(student_out, act_send)
    diff = (student_out.astype(F32) - teacher_out.astype(F32)).astype(BF16)
    diff_z = lax.ppermute(diff, "inc", SWAP)
    near_o = neighbours(own)
    w_z = swap_zh(own)
    act_got = swap_core(act_send)
    diff_c = swap_core(diff)
    w_o = (own, *near_o, step_x(pick(*near_o)))
    near_p = neighbours(w_z)
    diff_z = after(diff_z, w_z)
    diffs = (diff, diff_z, diff_c, swap_core(diff_z))

    def later(*others):
        return (after(diff, *others), *diffs[1:])

    def add(*terms):
        total = terms[0].astype(F32)
        for t in terms[1:]:
            total = total + t.astype(F32)
        return total

    def ring(step, terms, *first):
        far, back, ahead, here = terms
        far, back = after(step(far), *first), step(back, -1)
        return add(here, back, step(add(ahead, far).astype(BF16)))

    terms = dx_terms(at_y, diffs, w_o)
    terms_p = dw_terms(at_p, activations, act_got, later(*terms))
    terms_o = dw_terms(at_o, activations, act_got, later(*terms_p))
    far_p = step_x(pick(after(near_p[0], terms_p[0]), near_p[1]))
    w_p = (w_z, *near_p, far_p)
    dx_o = ring(step_y, terms, terms_p[0]).astype(BF16)
    cross = swap_zh(ring(step_x, terms_p).astype(BF16))
    weight_grad = ring(step_x, terms_o) + cross.astype(F32)
    dx_p = ring(step_y, dx_terms(at_y, later(*terms_o), w_p)).astype(BF16)

    half = dx_o.shape[0] // 2
    got_o, got_p = swap_core(dx_o[half:]), swap_core(dx_p[half:])
    input_grad = place(
        jnp.stack([x, zh, c]), mb, dx_o[:half], got_o, dx_p[:half], got_p
    )
    return input_grad, weight_grad.reshape(weight.shape)


def solution(mesh):
    fine = Mesh(
        mesh.devices.reshape(NX, NZ, NC, NL, NY), ("x", "zh", "core", "inc", "outc")
    )
    tok = ("x", "zh", "core")
    placed = (
        P(None, tok, "inc"),
        P(None, (*tok, "inc"), "outc"),
        P(None, (*tok, "inc"), "outc"),
        P("inc", tok, "outc"),
    )
    return jax.shard_map(
        local,
        mesh=fine,
        in_specs=placed,
        out_specs=(P(None, (*tok, "outc"), "inc"), P("inc", tok, "outc")),
        check_vma=False,
    )
```

time: 119 us -> 196 us (1.65)
  Pallas kernels: 20.5 us -> 92 us
  waiting for transfers between devices: 45 us -> 57.4 us
  local copies, waits for them, and re-layouts: 10.5 us -> 1.11 us
  starting transfers between devices: 31.5 us -> 35.8 us
  other arithmetic: 10.2 us -> 6.47 us
    pallas_call x5, Pallas kernels: 18.9 us -> 90.3 us  [the longest x1 64.7 us: other_columns(): pl.pallas_call(body, out_shape=out, in_specs=[SMEM, HBM], out_specs=HBM,...]
    unnamed x24 -> x32, local copies, waits for them, and re-layouts: 10.3 us -> 0.87 us
    ppermute x6, waiting for transfers between devices: 9.63 us -> 16.9 us  [step_y(): return lax.ppermute(value, ('core', 'outc'), by_core(NY, way, True))]
    ppermute x2, waiting for transfers between devices: 1.33 us -> 6.59 us  [swap_zh(): return lax.ppermute(value, 'zh', SWAP)]
    ppermute x1, waiting for transfers between devices: 6.62 us -> 10.9 us  [local(): diff_z = lax.ppermute(diff, 'inc', SWAP)]
    ppermute x8, waiting for transfers between devices: 14.8 us -> 11.2 us  [step_x(): return lax.ppermute(value, ('x', 'core'), by_core(NX, way, False))]
    ppermute x2, waiting for transfers between devices: 6.72 us -> 3.41 us  [neighbours(): lax.ppermute(piece, 'x', by_x(1))]
    ppermute x6, starting transfers between devices: 9.4 us -> 12.5 us  [step_y(): return lax.ppermute(value, ('core', 'outc'), by_core(NY, way, True))]
  transfers between devices with their start and end apart: 25 -> 26, of which waited for: 11 -> 10; matrix products, arithmetic and copies ran while one was open for 8% -> 3% of each run, Pallas kernels for 17% -> 13%
where the time goes in v5:
time: 196 us; the launch traced here: 194 us
  Pallas kernels  92 us (47%)
  waiting for transfers between devices  57.4 us (29%)
  starting transfers between devices  35.8 us (18%)
  other arithmetic  6.47 us (3%)
    pallas_call x1, Pallas kernels, other_columns(): pl.pallas_call(body, out_shape=out, in_specs=[SMEM, HBM], out_specs=HBM,...  64.7 us
    ppermute x6, waiting for transfers between devices, step_y(): return lax.ppermute(value, ('core', 'outc'), by_core(NY, way, True))  16.9 us
    pallas_call x2, Pallas kernels, dx_terms(): pl.pallas_call(dx_body, out_shape=outs, in_specs=[SMEM, *[HBM] * (4 + NX)...  13.1 us
    pallas_call x2, Pallas kernels, dw_terms(): pl.pallas_call(dw_body, out_shape=outs, in_specs=[SMEM, *[HBM] * 6], out_...  12.5 us
    ppermute x6, starting transfers between devices, step_y(): return lax.ppermute(value, ('core', 'outc'), by_core(NY, way, True))  12.5 us
    ppermute x8, waiting for transfers between devices, step_x(): return lax.ppermute(value, ('x', 'core'), by_core(NX, way, False))  11.2 us
    ppermute x1, waiting for transfers between devices, local(): diff_z = lax.ppermute(diff, 'inc', SWAP)  10.9 us
    ppermute x8, starting transfers between devices, step_x(): return lax.ppermute(value, ('x', 'core'), by_core(NX, way, False))  10.5 us
  transfers between devices with their start and end apart: 26, of which 10 were waited for; matrix products, arithmetic and copies ran while one was open for 3% of the time, Pallas kernels for 13%

profile of v5, /device:TPU:0, one launch (start us, length us, event | category | flops | bytes accessed | tf_op | source)
XLA Modules:
  0.0 193.8 jit_solution(9168816909897701378)
XLA Ops:
  0.7 64.7 %other_columns.1 = bf16[8,2,256,256]{3,2,1,0:T(8,128)(2,1)} custom-call(s32[1]{0:T(128)} %bitcast.2.core, bf16[2,256,4096]{2,1,0:T(8,128)(2,1)} %act.3), custom_call_target="tpu_custom_call" | custom-call | bytes 4194304 | tf_op jit(solution)/shard_map/other_columns/pallas_call | solution.py:57
  65.5 2.9 %collective-permute-start.5 = (bf16[256,1024]{1,0:T(8,128)(2,1)}, bf16[256,1024]{1,0:T(8,128)(2,1)}, u32[]{:S(2)}, u32[]{:S(2)}) collective-permute-start(bf16[256,1024]{1,0:T(8,128)(2,1)} %bitcast.7.refs_4_), channel_id=1, source_target_pairs={{0,96},{32,0},{64,32},{96,64},{1,97},{33,1},{65,33},{97,65},{2,98}... | collective-permute-start | bytes 1572872 | tf_op jit(solution)/shard_map/ppermute | solution.py:260
  68.4 3.9 %collective-permute-start.1 = (bf16[256,1024]{1,0:T(8,128)(2,1)}, bf16[256,1024]{1,0:T(8,128)(2,1)}, u32[]{:S(2)}, u32[]{:S(2)}) collective-permute-start(bf16[256,1024]{1,0:T(8,128)(2,1)} %bitcast.7.refs_4_), channel_id=1, source_target_pairs={{0,16},{16,0},{1,17},{17,1},{2,18},{18,2},{3,19},{19,3},{4,20},{20... | collective-permute-start | bytes 1572872 | tf_op jit(solution)/shard_map/ppermute | solution.py:254
  72.5 1.1 collective-permute-start
  73.6 6.9 %collective-permute-done.5.refs_6_ = bf16[256,1024]{1,0:T(8,128)(2,1)} collective-permute-done((bf16[256,1024]{1,0:T(8,128)(2,1)}, bf16[256,1024]{1,0:T(8,128)(2,1)}, u32[]{:S(2)}, u32[]{:S(2)}) %collective-permute-start.5) | collective-permute-done | bytes 524320 | tf_op jit(solution)/shard_map/ppermute | solution.py:260
  80.5 3.4 %collective-permute-done.4.refs_5_ = bf16[256,1024]{1,0:T(8,128)(2,1)} collective-permute-done((bf16[256,1024]{1,0:T(8,128)(2,1)}, bf16[256,1024]{1,0:T(8,128)(2,1)}, u32[]{:S(2)}, u32[]{:S(2)}) %collective-permute-start.4) | collective-permute-done | bytes 524320 | tf_op jit(solution)/shard_map/ppermute | solution.py:260
  83.9 1.9 broadcast_select_fusion.1
  85.8 10.9 %collective-permute-done.refs_1_ = bf16[2,128,1024]{2,1,0:T(8,128)(2,1)S(1)} collective-permute-done((bf16[2,128,1024]{2,1,0:T(8,128)(2,1)S(1)}, bf16[2,128,1024]{2,1,0:T(8,128)(2,1)S(1)}, u32[]{:S(2)}, u32[]{:S(2)}) %collective-permute-start) | collective-permute-done | bytes 524320 | tf_op jit(solution)/shard_map/ppermute | solution.py:279
  97.3 1.5 collective-permute-done.3.refs_3_
  98.7 6.6 %dx_terms.2 = (bf16[256,1024]{1,0:T(8,128)(2,1)}, bf16[256,1024]{1,0:T(8,128)(2,1)}, f32[256,1024]{1,0:T(8,128)}, f32[256,1024]{1,0:T(8,128)}) custom-call(s32[4]{0:T(128)S(1)} %pad_add_fusion.1.at, bf16[2,128,1024]{2,1,0:T(8,128)(2,1)} %copy-done, bf16[2,128,1024]{2,1,0:T(8,128)(2,1)} %copy-done.1, bf16[2,128,1024]{2,1,0:T(8,128)(2,1)} %collective-permute-done.2.refs_2_, ...), custom_call_target="tpu_custom_call" | custom-call | flops 2147483648 | bytes 7340032 | tf_op jit(solution)/shard_map/dx_terms/pallas_call | solution.py:168
  105.3 1.6 collective-permute-start.8
  106.9 3.0 %collective-permute-start.13 = (bf16[256,1024]{1,0:T(8,128)(2,1)}, bf16[256,1024]{1,0:T(8,128)(2,1)S(1)}, u32[]{:S(2)}, u32[]{:S(2)}) collective-permute-start(bf16[256,1024]{1,0:T(8,128)(2,1)} %collective-permute-done.1.refs_4_), channel_id=1, source_target_pairs={{0,96},{32,0},{64,32},{96,64},{1,97},{33,1},{65,33},{97,65},{2,98}... | collective-permute-start | bytes 1572872 | tf_op jit(solution)/shard_map/ppermute | solution.py:260
  110.1 1.7 collective-permute-start.7
  111.7 6.3 %dw_terms.2 = (bf16[256,1024]{1,0:T(8,128)(2,1)}, bf16[256,1024]{1,0:T(8,128)(2,1)}, f32[256,1024]{1,0:T(8,128)}, f32[256,1024]{1,0:T(8,128)}) custom-call(s32[6]{0:T(128)S(1)} %stack.77.at, bf16[2,256,4096]{2,1,0:T(8,128)(2,1)} %act.3, bf16[8,2,256,256]{3,2,1,0:T(8,128)(2,1)S(1)} %collective-permute-done.9.got, bf16[2,128,1024]{2,1,0:T(8,128)(2,1)} %copy-done, ...), custom_call_target="tpu_custom_call" | custom-call | flops 2147483648 | bytes 7340032 | tf_op jit(solution)/shard_map/dw_terms/pallas_call | solution.py:115
  118.1 6.3 %dw_terms.3 = (bf16[256,1024]{1,0:T(8,128)(2,1)}, bf16[256,1024]{1,0:T(8,128)(2,1)}, f32[256,1024]{1,0:T(8,128)}, f32[256,1024]{1,0:T(8,128)}) custom-call(s32[6]{0:T(128)S(1)} %stack.82.at, bf16[2,256,4096]{2,1,0:T(8,128)(2,1)} %act.3, bf16[8,2,256,256]{3,2,1,0:T(8,128)(2,1)S(1)} %collective-permute-done.9.got, bf16[2,128,1024]{2,1,0:T(8,128)(2,1)} %copy-done, ...), custom_call_target="tpu_custom_call" | custom-call | flops 2147483648 | bytes 7340032 | tf_op jit(solution)/shard_map/dw_terms/pallas_call | solution.py:115
  125.0 1.6 broadcast_select_fusion
  126.6 3.1 %collective-permute-start.14 = (bf16[256,1024]{1,0:T(8,128)(2,1)S(1)}, bf16[256,1024]{1,0:T(8,128)(2,1)S(1)}, u32[]{:S(2)}, u32[]{:S(2)}) collective-permute-start(bf16[256,1024]{1,0:T(8,128)(2,1)S(1)} %broadcast_select_fusion), channel_id=1, source_target_pairs={{0,32},{8,104},{32,64},{40,8},{64,96},{72,40},{96,0},{104,72},{1,3... | collective-permute-start | bytes 1572872 | tf_op jit(solution)/shard_map/ppermute | solution.py:248
  129.9 1.8 collective-permute-start.10
  131.8 0.8 collective-permute-start.22
  132.5 3.8 %collective-permute-done.20 = bf16[256,1024]{1,0:T(8,128)(2,1)S(1)} collective-permute-done((bf16[256,1024]{1,0:T(8,128)(2,1)}, bf16[256,1024]{1,0:T(8,128)(2,1)S(1)}, u32[]{:S(2)}, u32[]{:S(2)}) %collective-permute-start.20) | collective-permute-done | bytes 524320 | tf_op jit(solution)/shard_map/ppermute | solution.py:248
  136.4 4.1 %collective-permute-start.19 = (bf16[256,1024]{1,0:T(8,128)(2,1)S(1)}, bf16[256,1024]{1,0:T(8,128)(2,1)S(1)}, u32[]{:S(2)}, u32[]{:S(2)}) collective-permute-start(bf16[256,1024]{1,0:T(8,128)(2,1)S(1)} %copy-done.13), channel_id=1, source_target_pairs={{0,96},{8,40},{32,0},{40,72},{64,32},{72,104},{96,64},{104,8},{1,9... | collective-permute-start | bytes 1572872 | tf_op jit(solution)/shard_map/ppermute | solution.py:248
  140.6 7.0 %collective-permute-done.14.refs_7_ = bf16[256,1024]{1,0:T(8,128)(2,1)S(1)} collective-permute-done((bf16[256,1024]{1,0:T(8,128)(2,1)S(1)}, bf16[256,1024]{1,0:T(8,128)(2,1)S(1)}, u32[]{:S(2)}, u32[]{:S(2)}) %collective-permute-start.14) | collective-permute-done | bytes 524320 | tf_op jit(solution)/shard_map/ppermute | solution.py:248
  147.6 0.8 copy-done.15
  148.4 6.6 %dx_terms.3 = (bf16[256,1024]{1,0:T(8,128)(2,1)}, bf16[256,1024]{1,0:T(8,128)(2,1)}, f32[256,1024]{1,0:T(8,128)}, f32[256,1024]{1,0:T(8,128)}) custom-call(s32[4]{0:T(128)S(1)} %pad_add_fusion.1.at, bf16[2,128,1024]{2,1,0:T(8,128)(2,1)} %copy-done, bf16[2,128,1024]{2,1,0:T(8,128)(2,1)} %copy-done.1, bf16[2,128,1024]{2,1,0:T(8,128)(2,1)} %collective-permute-done.2.refs_2_, ...), custom_call_target="tpu_custom_call" | custom-call | flops 2147483648 | bytes 7340032 | tf_op jit(solution)/shard_map/dx_terms/pallas_call | solution.py:168
  155.0 7.3 %collective-permute-start.15 = (bf16[256,1024]{1,0:T(8,128)(2,1)}, bf16[256,1024]{1,0:T(8,128)(2,1)S(1)}, u32[]{:S(2)}, u32[]{:S(2)}) collective-permute-start(bf16[256,1024]{1,0:T(8,128)(2,1)} %get-tuple-element.45), channel_id=1, source_target_pairs={{0,3},{8,9},{1,0},{9,10},{2,1},{10,11},{3,2},{11,8},{4,7},{12,13},... | collective-permute-start | bytes 1572872 | tf_op jit(solution)/shard_map/ppermute | solution.py:251
  162.7 10.2 %collective-permute-done.16 = bf16[256,1024]{1,0:T(8,128)(2,1)S(1)} collective-permute-done((bf16[256,1024]{1,0:T(8,128)(2,1)}, bf16[256,1024]{1,0:T(8,128)(2,1)S(1)}, u32[]{:S(2)}, u32[]{:S(2)}) %collective-permute-start.16) | collective-permute-done | bytes 524320 | tf_op jit(solution)/shard_map/ppermute | solution.py:251
  173.3 2.0 %collective-permute-start.21 = (bf16[256,1024]{1,0:T(8,128)(2,1)S(1)}, bf16[256,1024]{1,0:T(8,128)(2,1)S(1)}, u32[]{:S(2)}, u32[]{:S(2)}) collective-permute-start(bf16[256,1024]{1,0:T(8,128)(2,1)S(1)} %add_convert_fusion.2), channel_id=1, source_target_pairs={{0,32},{8,104},{32,64},{40,8},{64,96},{72,40},{96,0},{104,72},{1,3... | collective-permute-start | bytes 1572872 | tf_op jit(solution)/shard_map/ppermute | solution.py:248
  175.5 1.3 collective-permute-start.25
  176.8 6.7 %collective-permute-done.17 = bf16[256,1024]{1,0:T(8,128)(2,1)S(1)} collective-permute-done((bf16[256,1024]{1,0:T(8,128)(2,1)S(1)}, bf16[256,1024]{1,0:T(8,128)(2,1)S(1)}, u32[]{:S(2)}, u32[]{:S(2)}) %collective-permute-start.17) | collective-permute-done | bytes 524320 | tf_op jit(solution)/shard_map/ppermute | solution.py:251
  184.3 6.6 %collective-permute-done.25 = bf16[256,1024]{1,0:T(8,128)(2,1)S(1)} collective-permute-done((bf16[256,1024]{1,0:T(8,128)(2,1)S(1)}, bf16[256,1024]{1,0:T(8,128)(2,1)S(1)}, u32[]{:S(2)}, u32[]{:S(2)}) %collective-permute-start.25) | collective-permute-done | bytes 524320 | tf_op jit(solution)/shard_map/ppermute | solution.py:254
  190.9 1.3 add_bitcast_fusion
  192.2 1.7 place.1
  (75 shorter events, 3.9 us)
Async XLA Ops:
  0.6 71.6 %copy-start.10 = (bf16[2,128,1024]{2,1,0:T(8,128)(2,1)S(1)}, bf16[2,128,1024]{2,1,0:T(8,128)(2,1)}, u32[]{:S(2)}) copy-start(bf16[2,128,1024]{2,1,0:T(8,128)(2,1)} %param.6) | copy-start | bytes 1572868
  0.6 71.6 %copy-start.11 = (bf16[2,128,1024]{2,1,0:T(8,128)(2,1)S(1)}, bf16[2,128,1024]{2,1,0:T(8,128)(2,1)}, u32[]{:S(2)}) copy-start(bf16[2,128,1024]{2,1,0:T(8,128)(2,1)} %param.5) | copy-start | bytes 1572868
  65.4 46.4 %collective-permute-start.9 = (bf16[8,2,256,256]{3,2,1,0:T(8,128)(2,1)}, bf16[8,2,256,256]{3,2,1,0:T(8,128)(2,1)S(1)}, u32[]{:S(2)}, u32[]{:S(2)}) collective-permute-start(bf16[8,2,256,256]{3,2,1,0:T(8,128)(2,1)} %other_columns.1), channel_id=1, source_target_pairs={{0,8},{8,0},{1,9},{9,1},{2,10},{10,2},{3,11},{11,3},{4,12},{12,4},... | collective-permute-start | bytes 6291464 | tf_op jit(solution)/shard_map/ppermute | solution.py:257
  65.5 15.0 %collective-permute-start.5 = (bf16[256,1024]{1,0:T(8,128)(2,1)}, bf16[256,1024]{1,0:T(8,128)(2,1)}, u32[]{:S(2)}, u32[]{:S(2)}) collective-permute-start(bf16[256,1024]{1,0:T(8,128)(2,1)} %bitcast.7.refs_4_), channel_id=1, source_target_pairs={{0,96},{32,0},{64,32},{96,64},{1,97},{33,1},{65,33},{97,65},{2,98}... | collective-permute-start | bytes 1572872 | tf_op jit(solution)/shard_map/ppermute | solution.py:260
  68.4 15.5 %collective-permute-start.4 = (bf16[256,1024]{1,0:T(8,128)(2,1)}, bf16[256,1024]{1,0:T(8,128)(2,1)}, u32[]{:S(2)}, u32[]{:S(2)}) collective-permute-start(bf16[256,1024]{1,0:T(8,128)(2,1)} %bitcast.7.refs_4_), channel_id=1, source_target_pairs={{0,32},{32,64},{64,96},{96,0},{1,33},{33,65},{65,97},{97,1},{2,34}... | collective-permute-start | bytes 1572872 | tf_op jit(solution)/shard_map/ppermute | solution.py:260
  68.4 17.4 %collective-permute-start.1 = (bf16[256,1024]{1,0:T(8,128)(2,1)}, bf16[256,1024]{1,0:T(8,128)(2,1)}, u32[]{:S(2)}, u32[]{:S(2)}) collective-permute-start(bf16[256,1024]{1,0:T(8,128)(2,1)} %bitcast.7.refs_4_), channel_id=1, source_target_pairs={{0,16},{16,0},{1,17},{17,1},{2,18},{18,2},{3,19},{19,3},{4,20},{20... | collective-permute-start | bytes 1572872 | tf_op jit(solution)/shard_map/ppermute | solution.py:254
  72.5 26.3 %copy-start = (bf16[2,128,1024]{2,1,0:T(8,128)(2,1)}, bf16[2,128,1024]{2,1,0:T(8,128)(2,1)S(1)}, u32[]{:S(2)}) copy-start(bf16[2,128,1024]{2,1,0:T(8,128)(2,1)S(1)} %subtract_convert_fusion.refs_0_) | copy-start | bytes 1572868
  72.5 24.2 %collective-permute-start = (bf16[2,128,1024]{2,1,0:T(8,128)(2,1)S(1)}, bf16[2,128,1024]{2,1,0:T(8,128)(2,1)S(1)}, u32[]{:S(2)}, u32[]{:S(2)}) collective-permute-start(bf16[2,128,1024]{2,1,0:T(8,128)(2,1)S(1)} %subtract_convert_fusion.refs_0_), channel_id=1, source_target_pairs={{0,4},{4,0},{1,5},{5,1},{2,6},{6,2},{3,7},{7,3},{8,12},{12,8},{9,1... | collective-permute-start | bytes 1572872 | tf_op jit(solution)/shard_map/ppermute | solution.py:279
  80.5 16.8 %collective-permute-start.2 = (bf16[2,128,1024]{2,1,0:T(8,128)(2,1)S(1)}, bf16[2,128,1024]{2,1,0:T(8,128)(2,1)}, u32[]{:S(2)}, u32[]{:S(2)}) collective-permute-start(bf16[2,128,1024]{2,1,0:T(8,128)(2,1)S(1)} %subtract_convert_fusion.refs_0_), channel_id=1, source_target_pairs={{0,8},{8,0},{1,9},{9,1},{2,10},{10,2},{3,11},{11,3},{4,12},{12,4},... | collective-permute-start | bytes 1572872 | tf_op jit(solution)/shard_map/ppermute | solution.py:257
  85.8 11.5 %collective-permute-start.6 = (bf16[256,1024]{1,0:T(8,128)(2,1)}, bf16[256,1024]{1,0:T(8,128)(2,1)}, u32[]{:S(2)}, u32[]{:S(2)}) collective-permute-start(bf16[256,1024]{1,0:T(8,128)(2,1)} %broadcast_select_fusion.1), channel_id=1, source_target_pairs={{0,32},{8,104},{32,64},{40,8},{64,96},{72,40},{96,0},{104,72},{1,3... | collective-permute-start | bytes 1572872 | tf_op jit(solution)/shard_map/ppermute | solution.py:248
  96.7 2.0 %collective-permute-start.3 = (bf16[2,128,1024]{2,1,0:T(8,128)(2,1)S(1)}, bf16[2,128,1024]{2,1,0:T(8,128)(2,1)}, u32[]{:S(2)}, u32[]{:S(2)}) collective-permute-start(bf16[2,128,1024]{2,1,0:T(8,128)(2,1)S(1)} %collective-permute-done.refs_1_), channel_id=1, source_target_pairs={{0,8},{8,0},{1,9},{9,1},{2,10},{10,2},{3,11},{11,3},{4,12},{12,4},... | collective-permute-start | bytes 1572872 | tf_op jit(solution)/shard_map/ppermute | solution.py:257
  96.8 21.3 %collective-permute-start.12 = (bf16[256,1024]{1,0:T(8,128)(2,1)}, bf16[256,1024]{1,0:T(8,128)(2,1)}, u32[]{:S(2)}, u32[]{:S(2)}) collective-permute-start(bf16[256,1024]{1,0:T(8,128)(2,1)} %collective-permute-done.1.refs_4_), channel_id=1, source_target_pairs={{0,32},{32,64},{64,96},{96,0},{1,33},{33,65},{65,97},{97,1},{2,34}... | collective-permute-start | bytes 1572872 | tf_op jit(solution)/shard_map/ppermute | solution.py:260
  105.3 12.8 %collective-permute-start.8 = (bf16[256,1024]{1,0:T(8,128)(2,1)}, bf16[256,1024]{1,0:T(8,128)(2,1)S(1)}, u32[]{:S(2)}, u32[]{:S(2)}) collective-permute-start(bf16[256,1024]{1,0:T(8,128)(2,1)} %get-tuple-element.30), channel_id=1, source_target_pairs={{0,1},{8,11},{1,2},{9,8},{2,3},{10,9},{3,0},{11,10},{4,5},{12,15},... | collective-permute-start | bytes 1572872 | tf_op jit(solution)/shard_map/ppermute | solution.py:251
  106.9 18.1 %collective-permute-start.13 = (bf16[256,1024]{1,0:T(8,128)(2,1)}, bf16[256,1024]{1,0:T(8,128)(2,1)S(1)}, u32[]{:S(2)}, u32[]{:S(2)}) collective-permute-start(bf16[256,1024]{1,0:T(8,128)(2,1)} %collective-permute-done.1.refs_4_), channel_id=1, source_target_pairs={{0,96},{32,0},{64,32},{96,64},{1,97},{33,1},{65,33},{97,65},{2,98}... | collective-permute-start | bytes 1572872 | tf_op jit(solution)/shard_map/ppermute | solution.py:260
  110.1 44.9 %collective-permute-start.7 = (bf16[256,1024]{1,0:T(8,128)(2,1)}, bf16[256,1024]{1,0:T(8,128)(2,1)S(1)}, u32[]{:S(2)}, u32[]{:S(2)}) collective-permute-start(bf16[256,1024]{1,0:T(8,128)(2,1)} %get-tuple-element.28), channel_id=1, source_target_pairs={{0,3},{8,9},{1,0},{9,10},{2,1},{10,11},{3,2},{11,8},{4,7},{12,13},... | collective-permute-start | bytes 1572872 | tf_op jit(solution)/shard_map/ppermute | solution.py:251
  118.0 13.8 %collective-permute-start.23 = (bf16[256,1024]{1,0:T(8,128)(2,1)}, bf16[256,1024]{1,0:T(8,128)(2,1)S(1)}, u32[]{:S(2)}, u32[]{:S(2)}) collective-permute-start(bf16[256,1024]{1,0:T(8,128)(2,1)} %get-tuple-element.32), channel_id=1, source_target_pairs={{0,32},{8,104},{32,64},{40,8},{64,96},{72,40},{96,0},{104,72},{1,3... | collective-permute-start | bytes 1572872 | tf_op jit(solution)/shard_map/ppermute | solution.py:248
  124.4 16.0 %copy-start.8 = (f32[256,1024]{1,0:T(8,128)S(1)}, f32[256,1024]{1,0:T(8,128)}, u32[]{:S(2)}) copy-start(f32[256,1024]{1,0:T(8,128)} %get-tuple-element.35) | copy-start | bytes 3145732
  124.4 11.9 %collective-permute-start.20 = (bf16[256,1024]{1,0:T(8,128)(2,1)}, bf16[256,1024]{1,0:T(8,128)(2,1)S(1)}, u32[]{:S(2)}, u32[]{:S(2)}) collective-permute-start(bf16[256,1024]{1,0:T(8,128)(2,1)} %get-tuple-element.38), channel_id=1, source_target_pairs={{0,32},{8,104},{32,64},{40,8},{64,96},{72,40},{96,0},{104,72},{1,3... | collective-permute-start | bytes 1572872 | tf_op jit(solution)/shard_map/ppermute | solution.py:248
  125.0 15.6 %copy-start.12 = (bf16[256,1024]{1,0:T(8,128)(2,1)}, bf16[256,1024]{1,0:T(8,128)(2,1)S(1)}, u32[]{:S(2)}) copy-start(bf16[256,1024]{1,0:T(8,128)(2,1)S(1)} %collective-permute-done.13.refs_6_) | copy-start | bytes 1572868
  126.6 21.0 %collective-permute-start.14 = (bf16[256,1024]{1,0:T(8,128)(2,1)S(1)}, bf16[256,1024]{1,0:T(8,128)(2,1)S(1)}, u32[]{:S(2)}, u32[]{:S(2)}) collective-permute-start(bf16[256,1024]{1,0:T(8,128)(2,1)S(1)} %broadcast_select_fusion), channel_id=1, source_target_pairs={{0,32},{8,104},{32,64},{40,8},{64,96},{72,40},{96,0},{104,72},{1,3... | collective-permute-start | bytes 1572872 | tf_op jit(solution)/shard_map/ppermute | solution.py:248
  129.9 32.4 %collective-permute-start.10 = (bf16[256,1024]{1,0:T(8,128)(2,1)S(1)}, bf16[256,1024]{1,0:T(8,128)(2,1)S(1)}, u32[]{:S(2)}, u32[]{:S(2)}) collective-permute-start(bf16[256,1024]{1,0:T(8,128)(2,1)S(1)} %add_convert_fusion.6), channel_id=1, source_target_pairs={{0,1},{8,11},{1,2},{9,8},{2,3},{10,9},{3,0},{11,10},{4,5},{12,15},... | collective-permute-start | bytes 1572872 | tf_op jit(solution)/shard_map/ppermute | solution.py:251
  131.8 41.4 %collective-permute-start.22 = (bf16[256,1024]{1,0:T(8,128)(2,1)S(1)}, bf16[256,1024]{1,0:T(8,128)(2,1)S(1)}, u32[]{:S(2)}, u32[]{:S(2)}) collective-permute-start(bf16[256,1024]{1,0:T(8,128)(2,1)S(1)} %copy-done.14), channel_id=1, source_target_pairs={{0,96},{8,40},{32,0},{40,72},{64,32},{72,104},{96,64},{104,8},{1,9... | collective-permute-start | bytes 1572872 | tf_op jit(solution)/shard_map/ppermute | solution.py:248
  136.4 47.5 %collective-permute-start.19 = (bf16[256,1024]{1,0:T(8,128)(2,1)S(1)}, bf16[256,1024]{1,0:T(8,128)(2,1)S(1)}, u32[]{:S(2)}, u32[]{:S(2)}) collective-permute-start(bf16[256,1024]{1,0:T(8,128)(2,1)S(1)} %copy-done.13), channel_id=1, source_target_pairs={{0,96},{8,40},{32,0},{40,72},{64,32},{72,104},{96,64},{104,8},{1,9... | collective-permute-start | bytes 1572872 | tf_op jit(solution)/shard_map/ppermute | solution.py:248
  140.6 21.7 %copy-start.3 = (f32[256,1024]{1,0:T(8,128)S(1)}, f32[256,1024]{1,0:T(8,128)}, u32[]{:S(2)}) copy-start(f32[256,1024]{1,0:T(8,128)} %get-tuple-element.27) | copy-start | bytes 3145732
  147.6 25.7 %collective-permute-start.24 = (bf16[256,1024]{1,0:T(8,128)(2,1)S(1)}, bf16[256,1024]{1,0:T(8,128)(2,1)S(1)}, u32[]{:S(2)}, u32[]{:S(2)}) collective-permute-start(bf16[256,1024]{1,0:T(8,128)(2,1)S(1)} %add_convert_fusion.1), channel_id=1, source_target_pairs={{0,32},{8,104},{32,64},{40,8},{64,96},{72,40},{96,0},{104,72},{1,3... | collective-permute-start | bytes 1572872 | tf_op jit(solution)/shard_map/ppermute | solution.py:248
  155.0 20.5 %collective-permute-start.15 = (bf16[256,1024]{1,0:T(8,128)(2,1)}, bf16[256,1024]{1,0:T(8,128)(2,1)S(1)}, u32[]{:S(2)}, u32[]{:S(2)}) collective-permute-start(bf16[256,1024]{1,0:T(8,128)(2,1)} %get-tuple-element.45), channel_id=1, source_target_pairs={{0,3},{8,9},{1,0},{9,10},{2,1},{10,11},{3,2},{11,8},{4,7},{12,13},... | collective-permute-start | bytes 1572872 | tf_op jit(solution)/shard_map/ppermute | solution.py:251
  162.3 10.6 %collective-permute-start.16 = (bf16[256,1024]{1,0:T(8,128)(2,1)}, bf16[256,1024]{1,0:T(8,128)(2,1)S(1)}, u32[]{:S(2)}, u32[]{:S(2)}) collective-permute-start(bf16[256,1024]{1,0:T(8,128)(2,1)} %get-tuple-element.47), channel_id=1, source_target_pairs={{0,1},{8,11},{1,2},{9,8},{2,3},{10,9},{3,0},{11,10},{4,5},{12,15},... | collective-permute-start | bytes 1572872 | tf_op jit(solution)/shard_map/ppermute | solution.py:251
  173.0 10.5 %collective-permute-start.17 = (bf16[256,1024]{1,0:T(8,128)(2,1)S(1)}, bf16[256,1024]{1,0:T(8,128)(2,1)S(1)}, u32[]{:S(2)}, u32[]{:S(2)}) collective-permute-start(bf16[256,1024]{1,0:T(8,128)(2,1)S(1)} %add_convert_fusion.4), channel_id=1, source_target_pairs={{0,1},{8,11},{1,2},{9,8},{2,3},{10,9},{3,0},{11,10},{4,5},{12,15},... | collective-permute-start | bytes 1572872 | tf_op jit(solution)/shard_map/ppermute | solution.py:251
  173.2 19.0 %collective-permute-start.11 = (bf16[128,1024]{1,0:T(8,128)(2,1)S(1)}, bf16[128,1024]{1,0:T(8,128)(2,1)S(1)}, u32[]{:S(2)}, u32[]{:S(2)}) collective-permute-start(bf16[128,1024]{1,0:T(8,128)(2,1)S(1)} %get-tuple-element.50), channel_id=1, source_target_pairs={{0,8},{8,0},{1,9},{9,1},{2,10},{10,2},{3,11},{11,3},{4,12},{12,4},... | collective-permute-start | bytes 786440 | tf_op jit(solution)/shard_map/ppermute | solution.py:257
  173.3 11.0 %collective-permute-start.21 = (bf16[256,1024]{1,0:T(8,128)(2,1)S(1)}, bf16[256,1024]{1,0:T(8,128)(2,1)S(1)}, u32[]{:S(2)}, u32[]{:S(2)}) collective-permute-start(bf16[256,1024]{1,0:T(8,128)(2,1)S(1)} %add_convert_fusion.2), channel_id=1, source_target_pairs={{0,32},{8,104},{32,64},{40,8},{64,96},{72,40},{96,0},{104,72},{1,3... | collective-permute-start | bytes 1572872 | tf_op jit(solution)/shard_map/ppermute | solution.py:248
  175.5 15.3 %collective-permute-start.25 = (bf16[256,1024]{1,0:T(8,128)(2,1)S(1)}, bf16[256,1024]{1,0:T(8,128)(2,1)S(1)}, u32[]{:S(2)}, u32[]{:S(2)}) collective-permute-start(bf16[256,1024]{1,0:T(8,128)(2,1)S(1)} %add_convert_fusion), channel_id=1, source_target_pairs={{0,16},{16,0},{1,17},{17,1},{2,18},{18,2},{3,19},{19,3},{4,20},{20... | collective-permute-start | bytes 1572872 | tf_op jit(solution)/shard_map/ppermute | solution.py:254
  183.8 8.3 %collective-permute-start.18 = (bf16[128,1024]{1,0:T(8,128)(2,1)S(1)}, bf16[128,1024]{1,0:T(8,128)(2,1)S(1)}, u32[]{:S(2)}, u32[]{:S(2)}) collective-permute-start(bf16[128,1024]{1,0:T(8,128)(2,1)S(1)} %get-tuple-element.48), channel_id=1, source_target_pairs={{0,8},{8,0},{1,9},{9,1},{2,10},{10,2},{3,11},{11,3},{4,12},{12,4},... | collective-permute-start | bytes 786440 | tf_op jit(solution)/shard_map/ppermute | solution.py:257
  (10 other events, 84.1 us)

commit v6 on v5

--- a/solution.py
+++ b/solution.py
@@ -46,22 +46,19 @@
     n = NX * NZ
     rows = width // (n * NC)
 
-    def body(core, act_ref, out_ref, sems):
-        pairs = []
-        for k in range(n):
-            start = pl.multiple_of((k * NC + 1 - core[0]) * rows, rows)
-            pairs.append((act_ref.at[:, :, pl.ds(start, rows)], out_ref.at[k]))
-        wait_all(start_all(pairs, sems))
+    def body(core, act_ref, out_ref):
+        pick = core[0] == 0
+        out_ref[0] = jnp.where(pick, act_ref[:, :, rows:], act_ref[:, :, :rows])
 
     out = pltpu.HBM((n, mb, toks, rows), act.dtype)
     return pl.pallas_call(
         body,
         out_shape=out,
-        in_specs=[SMEM, HBM],
-        out_specs=HBM,
-        scratch_shapes=[pltpu.SemaphoreType.DMA((n,))],
-        compiler_params=pltpu.CompilerParams(vmem_limit_bytes=1 << 20),
-        cost_estimate=cost(0, out, out),
+        grid=(n,),
+        in_specs=[SMEM, pl.BlockSpec((mb, toks, NC * rows), lambda k: (0, 0, k))],
+        out_specs=pl.BlockSpec((1, mb, toks, rows), lambda k: (k, 0, 0, 0)),
+        compiler_params=pltpu.CompilerParams(vmem_limit_bytes=8 << 20),
+        cost_estimate=cost(0, act, out),
         name="other_columns",
     )(c.reshape(1), in_hbm(act))
 
@@ -127,7 +124,7 @@
         compiler_params=pltpu.CompilerParams(vmem_limit_bytes=20 << 20),
         cost_estimate=cost(16 * NC * mb * toks * rows * cols // 2, *outs, *diffs, got),
         name="dw_terms",
-    )(at, in_hbm(act), got, *map(in_hbm, diffs))
+    )(at, in_hbm(act), got, *diffs)
 
 
 def dx_body(at, *refs):
@@ -180,7 +177,7 @@
         compiler_params=pltpu.CompilerParams(vmem_limit_bytes=20 << 20),
         cost_estimate=cost(8 * math.prod(outs[0].shape) * cols, *outs, *diffs, *pieces),
         name="dx_terms",
-    )(at, *map(in_hbm, (*diffs, *pieces)))
+    )(at, *diffs, *map(in_hbm, pieces))
 
 
 def place_body(at, keep_o, got_o, keep_p, got_p, out_ref):
@@ -273,17 +270,16 @@
 
     at_y = jnp.stack([place_of(z, h) for z in (zl, 1 - zl) for h in range(2)])
 
-    act_send = other_columns(activations, c)
-    student_out = after(student_out, act_send)
     diff = (student_out.astype(F32) - teacher_out.astype(F32)).astype(BF16)
     diff_z = lax.ppermute(diff, "inc", SWAP)
-    near_o = neighbours(own)
-    w_z = swap_zh(own)
-    act_got = swap_core(act_send)
+    own_late = after(own, diff)
+    near_o = neighbours(own_late)
+    w_z = swap_zh(own_late)
     diff_c = swap_core(diff)
-    w_o = (own, *near_o, step_x(pick(*near_o)))
     near_p = neighbours(w_z)
-    diff_z = after(diff_z, w_z)
+    far_o = step_x(pick(*near_o))
+    diff_z = after(diff_z, w_z, diff_c, far_o)
+    act_got = swap_core(other_columns(after(activations, diff_z), c))
     diffs = (diff, diff_z, diff_c, swap_core(diff_z))
 
     def later(*others):
@@ -297,18 +293,19 @@
 
     def ring(step, terms, *first):
         far, back, ahead, here = terms
-        far, back = after(step(far), *first), step(back, -1)
+        far, back = lax.optimization_barrier((step(far), step(back, -1), *first))[:2]
         return add(here, back, step(add(ahead, far).astype(BF16)))
 
-    terms = dx_terms(at_y, diffs, w_o)
-    terms_p = dw_terms(at_p, activations, act_got, later(*terms))
-    terms_o = dw_terms(at_o, activations, act_got, later(*terms_p))
-    far_p = step_x(pick(after(near_p[0], terms_p[0]), near_p[1]))
-    w_p = (w_z, *near_p, far_p)
-    dx_o = ring(step_y, terms, terms_p[0]).astype(BF16)
-    cross = swap_zh(ring(step_x, terms_p).astype(BF16))
-    weight_grad = ring(step_x, terms_o) + cross.astype(F32)
-    dx_p = ring(step_y, dx_terms(at_y, later(*terms_o), w_p)).astype(BF16)
+    terms_o = dx_terms(at_y, diffs, (own, *near_o, far_o))
+    forward_p = pick(after(near_p[0], terms_o[0]), near_p[1])
+    sums_p = dw_terms(at_p, activations, act_got, later(forward_p))
+    w_p = (w_z, *near_p, step_x(forward_p))
+    terms_p = dx_terms(at_y, later(*sums_p), w_p)
+    sums_o = dw_terms(at_o, activations, act_got, later(*terms_p))
+    dx_o = ring(step_y, terms_o, sums_p[0]).astype(BF16)
+    cross = swap_zh(ring(step_x, sums_p).astype(BF16))
+    dx_p = ring(step_y, terms_p).astype(BF16)
+    weight_grad = ring(step_x, sums_o) + cross.astype(F32)
 
     half = dx_o.shape[0] // 2
     got_o, got_p = swap_core(dx_o[half:]), swap_core(dx_p[half:])

time: 196 us -> 129 us (0.66)
  Pallas kernels: 92 us -> 33.5 us
  starting transfers between devices: 35.8 us -> 28.8 us
  other arithmetic: 6.47 us -> 10.2 us
  waiting for transfers between devices: 57.4 us -> 54.2 us
    pallas_call x1, Pallas kernels: 64.7 us -> 6.09 us  [other_columns(): pl.pallas_call(body, out_shape=out, grid=(n,), in_specs=[SMEM, pl.BlockSp...]
    ppermute x6, waiting for transfers between devices: 16.9 us -> 2.73 us  [step_y(): return lax.ppermute(value, ('core', 'outc'), by_core(NY, way, True))]
    ppermute x8, waiting for transfers between devices: 11.2 us -> 19.3 us  [step_x(): return lax.ppermute(value, ('x', 'core'), by_core(NX, way, False))]
    ppermute x6, starting transfers between devices: 12.5 us -> 8.04 us  [step_y(): return lax.ppermute(value, ('core', 'outc'), by_core(NY, way, True))]
    ppermute x8, starting transfers between devices: 10.5 us -> 7.82 us  [step_x(): return lax.ppermute(value, ('x', 'core'), by_core(NX, way, False))]
    convert_element_type x3, other arithmetic: 0.73 us -> 2.95 us  [the longest x1 1.44 us: local(): dx_o = ring(step_y, terms_o, sums_p[0]).astype(BF16)]
  transfers between devices with their start and end apart: 26 -> 26, of which waited for: 10 -> 12; matrix products, arithmetic and copies ran while one was open for 3% -> 6% of each run, Pallas kernels for 13% -> 21%
where the time goes in v6:
time: 129 us
  waiting for transfers between devices  54.2 us (42%)
  Pallas kernels  33.5 us (26%)
  starting transfers between devices  28.8 us (22%)
  other arithmetic  10.2 us (8%)
    ppermute x8, waiting for transfers between devices, step_x(): return lax.ppermute(value, ('x', 'core'), by_core(NX, way, False))  19.3 us
    pallas_call x2, Pallas kernels, dx_terms(): pl.pallas_call(dx_body, out_shape=outs, in_specs=[SMEM, *[HBM] * (4 + NX)...  13.8 us
    pallas_call x2, Pallas kernels, dw_terms(): pl.pallas_call(dw_body, out_shape=outs, in_specs=[SMEM, *[HBM] * 6], out_...  12 us
    ppermute x1, waiting for transfers between devices, local(): diff_z = lax.ppermute(diff, 'inc', SWAP)  10.9 us
    ppermute x6, starting transfers between devices, step_y(): return lax.ppermute(value, ('core', 'outc'), by_core(NY, way, True))  8.04 us
    ppermute x2, waiting for transfers between devices, swap_zh(): return lax.ppermute(value, 'zh', SWAP)  7.97 us
    ppermute x8, starting transfers between devices, step_x(): return lax.ppermute(value, ('x', 'core'), by_core(NX, way, False))  7.82 us
    ppermute x2, waiting for transfers between devices, neighbours(): lax.ppermute(piece, 'x', by_x(-1))  6.6 us
  transfers between devices with their start and end apart: 26, of which 12 were waited for; matrix products, arithmetic and copies ran while one was open for 6% of the time, Pallas kernels for 21%

profile of v6, /device:TPU:0, one launch (start us, length us, event | category | flops | bytes accessed | tf_op | source)
XLA Modules:
  0.0 128.7 jit_solution(11224256951966942520)
XLA Ops:
  0.6 1.4 %subtract_convert_fusion.refs_0_ = bf16[2,128,1024]{2,1,0:T(8,128)(2,1)S(1)} fusion(bf16[2,128,1024]{2,1,0:T(8,128)(2,1)} %param.6, bf16[2,128,1024]{2,1,0:T(8,128)(2,1)} %param.5), kind=kLoop, calls=%fused_computation.8 | loop fusion | flops 1048576 | bytes 1572864 | tf_op jit(solution)/shard_map/convert_element_type | solution.py:273
  2.0 2.9 %collective-permute-start.4 = (bf16[256,1024]{1,0:T(8,128)(2,1)}, bf16[256,1024]{1,0:T(8,128)(2,1)S(1)}, u32[]{:S(2)}, u32[]{:S(2)}) collective-permute-start(bf16[256,1024]{1,0:T(8,128)(2,1)} %bitcast.19), channel_id=1, source_target_pairs={{0,96},{32,0},{64,32},{96,64},{1,97},{33,1},{65,33},{97,65},{2,98}... | collective-permute-start | bytes 1572872 | tf_op jit(solution)/shard_map/ppermute | solution.py:257
  4.9 3.9 %collective-permute-start.1 = (bf16[256,1024]{1,0:T(8,128)(2,1)}, bf16[256,1024]{1,0:T(8,128)(2,1)S(1)}, u32[]{:S(2)}, u32[]{:S(2)}) collective-permute-start(bf16[256,1024]{1,0:T(8,128)(2,1)} %bitcast.21), channel_id=1, source_target_pairs={{0,16},{16,0},{1,17},{17,1},{2,18},{18,2},{3,19},{19,3},{4,20},{20... | collective-permute-start | bytes 1572872 | tf_op jit(solution)/shard_map/ppermute | solution.py:251
  9.8 6.6 %collective-permute-done.4.refs_6_ = bf16[256,1024]{1,0:T(8,128)(2,1)S(1)} collective-permute-done((bf16[256,1024]{1,0:T(8,128)(2,1)}, bf16[256,1024]{1,0:T(8,128)(2,1)S(1)}, u32[]{:S(2)}, u32[]{:S(2)}) %collective-permute-start.4) | collective-permute-done | bytes 524320 | tf_op jit(solution)/shard_map/ppermute | solution.py:257
  16.4 3.3 %collective-permute-done.3.refs_5_ = bf16[256,1024]{1,0:T(8,128)(2,1)S(1)} collective-permute-done((bf16[256,1024]{1,0:T(8,128)(2,1)}, bf16[256,1024]{1,0:T(8,128)(2,1)S(1)}, u32[]{:S(2)}, u32[]{:S(2)}) %collective-permute-start.3) | collective-permute-done | bytes 524320 | tf_op jit(solution)/shard_map/ppermute | solution.py:257
  19.9 2.0 %collective-permute-done.1.refs_4_ = bf16[256,1024]{1,0:T(8,128)(2,1)S(1)} collective-permute-done((bf16[256,1024]{1,0:T(8,128)(2,1)}, bf16[256,1024]{1,0:T(8,128)(2,1)S(1)}, u32[]{:S(2)}, u32[]{:S(2)}) %collective-permute-start.1) | collective-permute-done | bytes 524320 | tf_op jit(solution)/shard_map/ppermute | solution.py:251
  21.9 10.9 %collective-permute-done.refs_1_ = bf16[2,128,1024]{2,1,0:T(8,128)(2,1)} collective-permute-done((bf16[2,128,1024]{2,1,0:T(8,128)(2,1)S(1)}, bf16[2,128,1024]{2,1,0:T(8,128)(2,1)}, u32[]{:S(2)}, u32[]{:S(2)}) %collective-permute-start) | collective-permute-done | bytes 524320 | tf_op jit(solution)/shard_map/ppermute | solution.py:274
  33.6 6.1 %other_columns.1 = bf16[8,2,256,256]{3,2,1,0:T(8,128)(2,1)} custom-call(s32[1]{0:T(128)} %bitcast.2.core, bf16[2,256,4096]{2,1,0:T(8,128)(2,1)} %act.3), custom_call_target="tpu_custom_call" | custom-call | bytes 6291456 | tf_op jit(solution)/shard_map/other_columns/pallas_call | solution.py:54
  40.6 2.8 %collective-permute-start.11 = (bf16[256,1024]{1,0:T(8,128)(2,1)}, bf16[256,1024]{1,0:T(8,128)(2,1)}, u32[]{:S(2)}, u32[]{:S(2)}) collective-permute-start(bf16[256,1024]{1,0:T(8,128)(2,1)} %copy-done.10), channel_id=1, source_target_pairs={{0,96},{32,0},{64,32},{96,64},{1,97},{33,1},{65,33},{97,65},{2,98}... | collective-permute-start | bytes 1572872 | tf_op jit(solution)/shard_map/ppermute | solution.py:257
  44.5 6.9 %dx_terms.2 = (bf16[256,1024]{1,0:T(8,128)(2,1)}, bf16[256,1024]{1,0:T(8,128)(2,1)}, f32[256,1024]{1,0:T(8,128)}, f32[256,1024]{1,0:T(8,128)}) custom-call(s32[4]{0:T(128)S(1)} %pad_add_fusion.1.at, bf16[2,128,1024]{2,1,0:T(8,128)(2,1)S(1)} %subtract_convert_fusion.refs_0_, bf16[2,128,1024]{2,1,0:T(8,128)(2,1)} %collective-permute-done.refs_1_, ...), custom_call_target="tpu_custom_call" | custom-call | flops 2147483648 | bytes 7340032 | tf_op jit(solution)/shard_map/dx_terms/pallas_call | solution.py:165
  51.4 3.1 %collective-permute-start.8 = (bf16[256,1024]{1,0:T(8,128)(2,1)}, bf16[256,1024]{1,0:T(8,128)(2,1)}, u32[]{:S(2)}, u32[]{:S(2)}) collective-permute-start(bf16[256,1024]{1,0:T(8,128)(2,1)} %get-tuple-element.37), channel_id=1, source_target_pairs={{0,3},{8,9},{1,0},{9,10},{2,1},{10,11},{3,2},{11,8},{4,7},{12,13},... | collective-permute-start | bytes 1572872 | tf_op jit(solution)/shard_map/ppermute | solution.py:248
  55.5 1.9 %broadcast_select_fusion = bf16[256,1024]{1,0:T(8,128)(2,1)} fusion(bf16[256,1024]{1,0:T(8,128)(2,1)} %collective-permute-done.10.refs_5_, bf16[256,1024]{1,0:T(8,128)(2,1)} %collective-permute-done.11.refs_6_, pred[]{:T(512)S(6)} %eq.52), kind=kLoop, calls=%fused_computation.9 | loop fusion | flops 262144 | bytes 1572865 | tf_op jit(solution)/shard_map/jit(_where)/select_n | solution.py:260
  57.4 1.2 collective-permute-start.14
  58.6 6.0 %dw_terms.2 = (bf16[256,1024]{1,0:T(8,128)(2,1)}, bf16[256,1024]{1,0:T(8,128)(2,1)}, f32[256,1024]{1,0:T(8,128)}, f32[256,1024]{1,0:T(8,128)}) custom-call(s32[6]{0:T(128)S(1)} %stack.77.at, bf16[2,256,4096]{2,1,0:T(8,128)(2,1)} %act.3, bf16[8,2,256,256]{3,2,1,0:T(8,128)(2,1)S(1)} %collective-permute-done.9.got, ...), custom_call_target="tpu_custom_call" | custom-call | flops 2147483648 | bytes 7340032 | tf_op jit(solution)/shard_map/dw_terms/pallas_call | solution.py:112
  64.6 2.1 %collective-permute-done.8 = bf16[256,1024]{1,0:T(8,128)(2,1)} collective-permute-done((bf16[256,1024]{1,0:T(8,128)(2,1)}, bf16[256,1024]{1,0:T(8,128)(2,1)}, u32[]{:S(2)}, u32[]{:S(2)}) %collective-permute-start.8) | collective-permute-done | bytes 524320 | tf_op jit(solution)/shard_map/ppermute | solution.py:248
  67.3 2.0 %add_convert_fusion.6 = bf16[256,1024]{1,0:T(8,128)(2,1)} fusion(f32[256,1024]{1,0:T(8,128)S(1)} %copy-done.5, bf16[256,1024]{1,0:T(8,128)(2,1)} %collective-permute-done.7), kind=kLoop, calls=%fused_computation.7 | loop fusion | flops 786432 | bytes 2097152 | tf_op jit(solution)/shard_map/convert_element_type | solution.py:297
  69.6 3.0 %collective-permute-start.23 = (bf16[256,1024]{1,0:T(8,128)(2,1)}, bf16[256,1024]{1,0:T(8,128)(2,1)}, u32[]{:S(2)}, u32[]{:S(2)}) collective-permute-start(bf16[256,1024]{1,0:T(8,128)(2,1)} %get-tuple-element.45), channel_id=1, source_target_pairs={{0,96},{8,40},{32,0},{40,72},{64,32},{72,104},{96,64},{104,8},{1,9... | collective-permute-start | bytes 1572872 | tf_op jit(solution)/shard_map/ppermute | solution.py:245
  72.8 6.9 %dx_terms.3 = (bf16[256,1024]{1,0:T(8,128)(2,1)}, bf16[256,1024]{1,0:T(8,128)(2,1)}, f32[256,1024]{1,0:T(8,128)}, f32[256,1024]{1,0:T(8,128)}) custom-call(s32[4]{0:T(128)S(1)} %pad_add_fusion.1.at, bf16[2,128,1024]{2,1,0:T(8,128)(2,1)S(1)} %subtract_convert_fusion.refs_0_, bf16[2,128,1024]{2,1,0:T(8,128)(2,1)} %collective-permute-done.refs_1_, ...), custom_call_target="tpu_custom_call" | custom-call | flops 2147483648 | bytes 7340032 | tf_op jit(solution)/shard_map/dx_terms/pallas_call | solution.py:165
  79.8 1.9 %collective-permute-start.15 = (bf16[256,1024]{1,0:T(8,128)(2,1)}, bf16[256,1024]{1,0:T(8,128)(2,1)S(1)}, u32[]{:S(2)}, u32[]{:S(2)}) collective-permute-start(bf16[256,1024]{1,0:T(8,128)(2,1)} %get-tuple-element.50), channel_id=1, source_target_pairs={{0,1},{8,11},{1,2},{9,8},{2,3},{10,9},{3,0},{11,10},{4,5},{12,15},... | collective-permute-start | bytes 1572872 | tf_op jit(solution)/shard_map/ppermute | solution.py:248
  81.7 1.4 %collective-permute-start.16 = (bf16[256,1024]{1,0:T(8,128)(2,1)}, bf16[256,1024]{1,0:T(8,128)(2,1)S(1)}, u32[]{:S(2)}, u32[]{:S(2)}) collective-permute-start(bf16[256,1024]{1,0:T(8,128)(2,1)} %get-tuple-element.51), channel_id=1, source_target_pairs={{0,3},{8,9},{1,0},{9,10},{2,1},{10,11},{3,2},{11,8},{4,7},{12,13},... | collective-permute-start | bytes 1572872 | tf_op jit(solution)/shard_map/ppermute | solution.py:248
  83.1 6.0 %dw_terms.3 = (bf16[256,1024]{1,0:T(8,128)(2,1)}, bf16[256,1024]{1,0:T(8,128)(2,1)}, f32[256,1024]{1,0:T(8,128)}, f32[256,1024]{1,0:T(8,128)}) custom-call(s32[6]{0:T(128)S(1)} %stack.82.at, bf16[2,256,4096]{2,1,0:T(8,128)(2,1)} %act.3, bf16[8,2,256,256]{3,2,1,0:T(8,128)(2,1)S(1)} %collective-permute-done.9.got, ...), custom_call_target="tpu_custom_call" | custom-call | flops 2147483648 | bytes 7340032 | tf_op jit(solution)/shard_map/dw_terms/pallas_call | solution.py:112
  89.2 3.3 %collective-permute-start.20 = (bf16[256,1024]{1,0:T(8,128)(2,1)}, bf16[256,1024]{1,0:T(8,128)(2,1)S(1)}, u32[]{:S(2)}, u32[]{:S(2)}) collective-permute-start(bf16[256,1024]{1,0:T(8,128)(2,1)} %get-tuple-element.58), channel_id=1, source_target_pairs={{0,96},{8,40},{32,0},{40,72},{64,32},{72,104},{96,64},{104,8},{1,9... | collective-permute-start | bytes 1572872 | tf_op jit(solution)/shard_map/ppermute | solution.py:245
  92.5 1.4 %add_convert_fusion.5 = bf16[256,1024]{1,0:T(8,128)(2,1)S(1)} fusion(bf16[256,1024]{1,0:T(8,128)(2,1)} %collective-permute-done.12, f32[256,1024]{1,0:T(8,128)S(1)} %copy-done.1, bf16[256,1024]{1,0:T(8,128)(2,1)} %collective-permute-done.8), kind=kLoop, calls=%fused_computation.6 | loop fusion | flops 1310720 | bytes 2621440 | tf_op jit(solution)/shard_map/convert_element_type | solution.py:305
  94.2 10.7 %collective-permute-done.19 = bf16[256,1024]{1,0:T(8,128)(2,1)S(1)} collective-permute-done((bf16[256,1024]{1,0:T(8,128)(2,1)}, bf16[256,1024]{1,0:T(8,128)(2,1)S(1)}, u32[]{:S(2)}, u32[]{:S(2)}) %collective-permute-start.19) | collective-permute-done | bytes 524320 | tf_op jit(solution)/shard_map/ppermute | solution.py:245
  105.1 1.4 %collective-permute-start.17 = (bf16[256,1024]{1,0:T(8,128)(2,1)S(1)}, bf16[256,1024]{1,0:T(8,128)(2,1)S(1)}, u32[]{:S(2)}, u32[]{:S(2)}) collective-permute-start(bf16[256,1024]{1,0:T(8,128)(2,1)S(1)} %add_convert_fusion.4), channel_id=1, source_target_pairs={{0,1},{8,11},{1,2},{9,8},{2,3},{10,9},{3,0},{11,10},{4,5},{12,15},... | collective-permute-start | bytes 1572872 | tf_op jit(solution)/shard_map/ppermute | solution.py:248
  106.7 8.6 %collective-permute-done.24 = bf16[256,1024]{1,0:T(8,128)(2,1)S(1)} collective-permute-done((bf16[256,1024]{1,0:T(8,128)(2,1)S(1)}, bf16[256,1024]{1,0:T(8,128)(2,1)S(1)}, u32[]{:S(2)}, u32[]{:S(2)}) %collective-permute-start.24) | collective-permute-done | bytes 524320 | tf_op jit(solution)/shard_map/ppermute | solution.py:245
  115.3 1.3 add_convert_fusion
  116.6 1.2 collective-permute-start.25
  118.3 1.4 %collective-permute-done.18.got_p = bf16[128,1024]{1,0:T(8,128)(2,1)S(1)} collective-permute-done((bf16[128,1024]{1,0:T(8,128)(2,1)S(1)}, bf16[128,1024]{1,0:T(8,128)(2,1)S(1)}, u32[]{:S(2)}, u32[]{:S(2)}) %collective-permute-start.18) | collective-permute-done | bytes 262176 | tf_op jit(solution)/shard_map/ppermute | solution.py:254
  119.7 1.7 %place.1 = bf16[2,64,4096]{2,1,0:T(8,128)(2,1)} custom-call(s32[3]{0:T(128)S(1)} %pad_add_fusion.at, bf16[128,1024]{1,0:T(8,128)(2,1)S(1)} %get-tuple-element.67.keep_o, bf16[128,1024]{1,0:T(8,128)(2,1)S(1)} %collective-permute-done.13.got_o, bf16[128,1024]{1,0:T(8,128)(2,1)S(1)} %get-tuple-element.65.keep_p, bf16[128,1024]{1,0:T(8,128)(2,1)S(1)} %collective-permute-done.18.got_p), custom_call_target="tpu_custom_call" | custom-call | bytes 2097152 | tf_op jit(solution)/shard_map/place/pallas_call | solution.py:206
  121.4 6.0 %collective-permute-done.25 = bf16[256,1024]{1,0:T(8,128)(2,1)S(1)} collective-permute-done((bf16[256,1024]{1,0:T(8,128)(2,1)S(1)}, bf16[256,1024]{1,0:T(8,128)(2,1)S(1)}, u32[]{:S(2)}, u32[]{:S(2)}) %collective-permute-start.25) | collective-permute-done | bytes 524320 | tf_op jit(solution)/shard_map/ppermute | solution.py:251
  127.4 1.3 %add_bitcast_fusion = f32[1,256,1024]{2,1,0:T(8,128)} fusion(bf16[256,1024]{1,0:T(8,128)(2,1)S(1)} %collective-permute-done.25, bf16[256,1024]{1,0:T(8,128)(2,1)S(1)} %collective-permute-done.21, f32[256,1024]{1,0:T(8,128)S(1)} %copy-done, bf16[256,1024]{1,0:T(8,128)(2,1)S(1)} %collective-permute-done.20), kind=kLoop, calls=%fused_computation | loop fusion | flops 1572864 | bytes 3670016 | tf_op jit(solution)/shard_map/reshape | solution.py:315
  (67 shorter events, 7.5 us)
Async XLA Ops:
  2.0 14.4 %collective-permute-start.4 = (bf16[256,1024]{1,0:T(8,128)(2,1)}, bf16[256,1024]{1,0:T(8,128)(2,1)S(1)}, u32[]{:S(2)}, u32[]{:S(2)}) collective-permute-start(bf16[256,1024]{1,0:T(8,128)(2,1)} %bitcast.19), channel_id=1, source_target_pairs={{0,96},{32,0},{64,32},{96,64},{1,97},{33,1},{65,33},{97,65},{2,98}... | collective-permute-start | bytes 1572872 | tf_op jit(solution)/shard_map/ppermute | solution.py:257
  4.9 14.8 %collective-permute-start.3 = (bf16[256,1024]{1,0:T(8,128)(2,1)}, bf16[256,1024]{1,0:T(8,128)(2,1)S(1)}, u32[]{:S(2)}, u32[]{:S(2)}) collective-permute-start(bf16[256,1024]{1,0:T(8,128)(2,1)} %bitcast.20), channel_id=1, source_target_pairs={{0,32},{32,64},{64,96},{96,0},{1,33},{33,65},{65,97},{97,1},{2,34}... | collective-permute-start | bytes 1572872 | tf_op jit(solution)/shard_map/ppermute | solution.py:257
  4.9 16.9 %collective-permute-start.1 = (bf16[256,1024]{1,0:T(8,128)(2,1)}, bf16[256,1024]{1,0:T(8,128)(2,1)S(1)}, u32[]{:S(2)}, u32[]{:S(2)}) collective-permute-start(bf16[256,1024]{1,0:T(8,128)(2,1)} %bitcast.21), channel_id=1, source_target_pairs={{0,16},{16,0},{1,17},{17,1},{2,18},{18,2},{3,19},{19,3},{4,20},{20... | collective-permute-start | bytes 1572872 | tf_op jit(solution)/shard_map/ppermute | solution.py:251
  8.8 13.1 %collective-permute-start.2 = (bf16[2,128,1024]{2,1,0:T(8,128)(2,1)S(1)}, bf16[2,128,1024]{2,1,0:T(8,128)(2,1)S(1)}, u32[]{:S(2)}, u32[]{:S(2)}) collective-permute-start(bf16[2,128,1024]{2,1,0:T(8,128)(2,1)S(1)} %subtract_convert_fusion.refs_0_), channel_id=1, source_target_pairs={{0,8},{8,0},{1,9},{9,1},{2,10},{10,2},{3,11},{11,3},{4,12},{12,4},... | collective-permute-start | bytes 1572872 | tf_op jit(solution)/shard_map/ppermute | solution.py:254
  8.8 23.9 %collective-permute-start = (bf16[2,128,1024]{2,1,0:T(8,128)(2,1)S(1)}, bf16[2,128,1024]{2,1,0:T(8,128)(2,1)}, u32[]{:S(2)}, u32[]{:S(2)}) collective-permute-start(bf16[2,128,1024]{2,1,0:T(8,128)(2,1)S(1)} %subtract_convert_fusion.refs_0_), channel_id=1, source_target_pairs={{0,4},{4,0},{1,5},{5,1},{2,6},{6,2},{3,7},{7,3},{8,12},{12,8},{9,1... | collective-permute-start | bytes 1572872 | tf_op jit(solution)/shard_map/ppermute | solution.py:274
  16.4 16.3 %copy-start.8 = (bf16[256,1024]{1,0:T(8,128)(2,1)}, bf16[256,1024]{1,0:T(8,128)(2,1)S(1)}, u32[]{:S(2)}) copy-start(bf16[256,1024]{1,0:T(8,128)(2,1)S(1)} %collective-permute-done.4.refs_6_) | copy-start | bytes 1572868
  19.7 13.8 %copy-start.9 = (bf16[256,1024]{1,0:T(8,128)(2,1)}, bf16[256,1024]{1,0:T(8,128)(2,1)S(1)}, u32[]{:S(2)}) copy-start(bf16[256,1024]{1,0:T(8,128)(2,1)S(1)} %collective-permute-done.3.refs_5_) | copy-start | bytes 1572868
  19.8 12.9 %collective-permute-start.5 = (bf16[256,1024]{1,0:T(8,128)(2,1)S(1)}, bf16[256,1024]{1,0:T(8,128)(2,1)S(1)}, u32[]{:S(2)}, u32[]{:S(2)}) collective-permute-start(bf16[256,1024]{1,0:T(8,128)(2,1)S(1)} %broadcast_select_fusion.1), channel_id=1, source_target_pairs={{0,32},{8,104},{32,64},{40,8},{64,96},{72,40},{96,0},{104,72},{1,3... | collective-permute-start | bytes 1572872 | tf_op jit(solution)/shard_map/ppermute | solution.py:245
  21.9 11.7 %copy-start.10 = (bf16[256,1024]{1,0:T(8,128)(2,1)}, bf16[256,1024]{1,0:T(8,128)(2,1)S(1)}, u32[]{:S(2)}) copy-start(bf16[256,1024]{1,0:T(8,128)(2,1)S(1)} %collective-permute-done.1.refs_4_) | copy-start | bytes 1572868
  39.6 18.9 %collective-permute-start.9 = (bf16[8,2,256,256]{3,2,1,0:T(8,128)(2,1)}, bf16[8,2,256,256]{3,2,1,0:T(8,128)(2,1)S(1)}, u32[]{:S(2)}, u32[]{:S(2)}) collective-permute-start(bf16[8,2,256,256]{3,2,1,0:T(8,128)(2,1)} %other_columns.1), channel_id=1, source_target_pairs={{0,8},{8,0},{1,9},{9,1},{2,10},{10,2},{3,11},{11,3},{4,12},{12,4},... | collective-permute-start | bytes 6291464 | tf_op jit(solution)/shard_map/ppermute | solution.py:254
  39.6 4.9 %collective-permute-start.6 = (bf16[2,128,1024]{2,1,0:T(8,128)(2,1)}, bf16[2,128,1024]{2,1,0:T(8,128)(2,1)}, u32[]{:S(2)}, u32[]{:S(2)}) collective-permute-start(bf16[2,128,1024]{2,1,0:T(8,128)(2,1)} %collective-permute-done.refs_1_), channel_id=1, source_target_pairs={{0,8},{8,0},{1,9},{9,1},{2,10},{10,2},{3,11},{11,3},{4,12},{12,4},... | collective-permute-start | bytes 1572872 | tf_op jit(solution)/shard_map/ppermute | solution.py:254
  40.2 15.4 %collective-permute-start.10 = (bf16[256,1024]{1,0:T(8,128)(2,1)}, bf16[256,1024]{1,0:T(8,128)(2,1)}, u32[]{:S(2)}, u32[]{:S(2)}) collective-permute-start(bf16[256,1024]{1,0:T(8,128)(2,1)} %copy-done.10), channel_id=1, source_target_pairs={{0,32},{32,64},{64,96},{96,0},{1,33},{33,65},{65,97},{97,1},{2,34}... | collective-permute-start | bytes 1572872 | tf_op jit(solution)/shard_map/ppermute | solution.py:257
  40.6 14.9 %collective-permute-start.11 = (bf16[256,1024]{1,0:T(8,128)(2,1)}, bf16[256,1024]{1,0:T(8,128)(2,1)}, u32[]{:S(2)}, u32[]{:S(2)}) collective-permute-start(bf16[256,1024]{1,0:T(8,128)(2,1)} %copy-done.10), channel_id=1, source_target_pairs={{0,96},{32,0},{64,32},{96,64},{1,97},{33,1},{65,33},{97,65},{2,98}... | collective-permute-start | bytes 1572872 | tf_op jit(solution)/shard_map/ppermute | solution.py:257
  51.4 15.2 %collective-permute-start.8 = (bf16[256,1024]{1,0:T(8,128)(2,1)}, bf16[256,1024]{1,0:T(8,128)(2,1)}, u32[]{:S(2)}, u32[]{:S(2)}) collective-permute-start(bf16[256,1024]{1,0:T(8,128)(2,1)} %get-tuple-element.37), channel_id=1, source_target_pairs={{0,3},{8,9},{1,0},{9,10},{2,1},{10,11},{3,2},{11,8},{4,7},{12,13},... | collective-permute-start | bytes 1572872 | tf_op jit(solution)/shard_map/ppermute | solution.py:248
  54.5 12.8 %collective-permute-start.7 = (bf16[256,1024]{1,0:T(8,128)(2,1)}, bf16[256,1024]{1,0:T(8,128)(2,1)}, u32[]{:S(2)}, u32[]{:S(2)}) collective-permute-start(bf16[256,1024]{1,0:T(8,128)(2,1)} %get-tuple-element.36), channel_id=1, source_target_pairs={{0,1},{8,11},{1,2},{9,8},{2,3},{10,9},{3,0},{11,10},{4,5},{12,15},... | collective-permute-start | bytes 1572872 | tf_op jit(solution)/shard_map/ppermute | solution.py:248
  57.4 15.4 %collective-permute-start.14 = (bf16[256,1024]{1,0:T(8,128)(2,1)}, bf16[256,1024]{1,0:T(8,128)(2,1)}, u32[]{:S(2)}, u32[]{:S(2)}) collective-permute-start(bf16[256,1024]{1,0:T(8,128)(2,1)} %broadcast_select_fusion), channel_id=1, source_target_pairs={{0,32},{8,104},{32,64},{40,8},{64,96},{72,40},{96,0},{104,72},{1,3... | collective-permute-start | bytes 1572872 | tf_op jit(solution)/shard_map/ppermute | solution.py:245
  69.3 19.8 %collective-permute-start.12 = (bf16[256,1024]{1,0:T(8,128)(2,1)}, bf16[256,1024]{1,0:T(8,128)(2,1)}, u32[]{:S(2)}, u32[]{:S(2)}) collective-permute-start(bf16[256,1024]{1,0:T(8,128)(2,1)} %add_convert_fusion.6), channel_id=1, source_target_pairs={{0,1},{8,11},{1,2},{9,8},{2,3},{10,9},{3,0},{11,10},{4,5},{12,15},... | collective-permute-start | bytes 1572872 | tf_op jit(solution)/shard_map/ppermute | solution.py:248
  69.6 19.6 %collective-permute-start.23 = (bf16[256,1024]{1,0:T(8,128)(2,1)}, bf16[256,1024]{1,0:T(8,128)(2,1)}, u32[]{:S(2)}, u32[]{:S(2)}) collective-permute-start(bf16[256,1024]{1,0:T(8,128)(2,1)} %get-tuple-element.45), channel_id=1, source_target_pairs={{0,96},{8,40},{32,0},{40,72},{64,32},{72,104},{96,64},{104,8},{1,9... | collective-permute-start | bytes 1572872 | tf_op jit(solution)/shard_map/ppermute | solution.py:245
  72.6 21.3 %collective-permute-start.22 = (bf16[256,1024]{1,0:T(8,128)(2,1)}, bf16[256,1024]{1,0:T(8,128)(2,1)S(1)}, u32[]{:S(2)}, u32[]{:S(2)}) collective-permute-start(bf16[256,1024]{1,0:T(8,128)(2,1)} %get-tuple-element.41), channel_id=1, source_target_pairs={{0,32},{8,104},{32,64},{40,8},{64,96},{72,40},{96,0},{104,72},{1,3... | collective-permute-start | bytes 1572872 | tf_op jit(solution)/shard_map/ppermute | solution.py:245
  79.8 25.2 %collective-permute-start.15 = (bf16[256,1024]{1,0:T(8,128)(2,1)}, bf16[256,1024]{1,0:T(8,128)(2,1)S(1)}, u32[]{:S(2)}, u32[]{:S(2)}) collective-permute-start(bf16[256,1024]{1,0:T(8,128)(2,1)} %get-tuple-element.50), channel_id=1, source_target_pairs={{0,1},{8,11},{1,2},{9,8},{2,3},{10,9},{3,0},{11,10},{4,5},{12,15},... | collective-permute-start | bytes 1572872 | tf_op jit(solution)/shard_map/ppermute | solution.py:248
  81.7 23.2 %collective-permute-start.16 = (bf16[256,1024]{1,0:T(8,128)(2,1)}, bf16[256,1024]{1,0:T(8,128)(2,1)S(1)}, u32[]{:S(2)}, u32[]{:S(2)}) collective-permute-start(bf16[256,1024]{1,0:T(8,128)(2,1)} %get-tuple-element.51), channel_id=1, source_target_pairs={{0,3},{8,9},{1,0},{9,10},{2,1},{10,11},{3,2},{11,8},{4,7},{12,13},... | collective-permute-start | bytes 1572872 | tf_op jit(solution)/shard_map/ppermute | solution.py:248
  89.1 15.8 %collective-permute-start.19 = (bf16[256,1024]{1,0:T(8,128)(2,1)}, bf16[256,1024]{1,0:T(8,128)(2,1)S(1)}, u32[]{:S(2)}, u32[]{:S(2)}) collective-permute-start(bf16[256,1024]{1,0:T(8,128)(2,1)} %get-tuple-element.57), channel_id=1, source_target_pairs={{0,32},{8,104},{32,64},{40,8},{64,96},{72,40},{96,0},{104,72},{1,3... | collective-permute-start | bytes 1572872 | tf_op jit(solution)/shard_map/ppermute | solution.py:245
  89.2 15.7 %collective-permute-start.20 = (bf16[256,1024]{1,0:T(8,128)(2,1)}, bf16[256,1024]{1,0:T(8,128)(2,1)S(1)}, u32[]{:S(2)}, u32[]{:S(2)}) collective-permute-start(bf16[256,1024]{1,0:T(8,128)(2,1)} %get-tuple-element.58), channel_id=1, source_target_pairs={{0,96},{8,40},{32,0},{40,72},{64,32},{72,104},{96,64},{104,8},{1,9... | collective-permute-start | bytes 1572872 | tf_op jit(solution)/shard_map/ppermute | solution.py:245
  94.0 12.5 %copy-start.7 = (f32[256,1024]{1,0:T(8,128)S(1)}, f32[256,1024]{1,0:T(8,128)}, u32[]{:S(2)}) copy-start(f32[256,1024]{1,0:T(8,128)} %get-tuple-element.60) | copy-start | bytes 3145732
  94.0 24.3 %collective-permute-start.13 = (bf16[128,1024]{1,0:T(8,128)(2,1)S(1)}, bf16[128,1024]{1,0:T(8,128)(2,1)S(1)}, u32[]{:S(2)}, u32[]{:S(2)}) collective-permute-start(bf16[128,1024]{1,0:T(8,128)(2,1)S(1)} %get-tuple-element.66), channel_id=1, source_target_pairs={{0,8},{8,0},{1,9},{9,1},{2,10},{10,2},{3,11},{11,3},{4,12},{12,4},... | collective-permute-start | bytes 786440 | tf_op jit(solution)/shard_map/ppermute | solution.py:254
  94.2 21.1 %copy-start.2 = (f32[256,1024]{1,0:T(8,128)S(1)}, f32[256,1024]{1,0:T(8,128)}, u32[]{:S(2)}) copy-start(f32[256,1024]{1,0:T(8,128)} %get-tuple-element.47) | copy-start | bytes 3145732
  104.9 10.4 %collective-permute-start.24 = (bf16[256,1024]{1,0:T(8,128)(2,1)S(1)}, bf16[256,1024]{1,0:T(8,128)(2,1)S(1)}, u32[]{:S(2)}, u32[]{:S(2)}) collective-permute-start(bf16[256,1024]{1,0:T(8,128)(2,1)S(1)} %add_convert_fusion.1), channel_id=1, source_target_pairs={{0,32},{8,104},{32,64},{40,8},{64,96},{72,40},{96,0},{104,72},{1,3... | collective-permute-start | bytes 1572872 | tf_op jit(solution)/shard_map/ppermute | solution.py:245
  105.1 12.7 %collective-permute-start.17 = (bf16[256,1024]{1,0:T(8,128)(2,1)S(1)}, bf16[256,1024]{1,0:T(8,128)(2,1)S(1)}, u32[]{:S(2)}, u32[]{:S(2)}) collective-permute-start(bf16[256,1024]{1,0:T(8,128)(2,1)S(1)} %add_convert_fusion.4), channel_id=1, source_target_pairs={{0,1},{8,11},{1,2},{9,8},{2,3},{10,9},{3,0},{11,10},{4,5},{12,15},... | collective-permute-start | bytes 1572872 | tf_op jit(solution)/shard_map/ppermute | solution.py:248
  106.5 11.3 %copy-start.3 = (f32[256,1024]{1,0:T(8,128)S(1)}, f32[256,1024]{1,0:T(8,128)}, u32[]{:S(2)}) copy-start(f32[256,1024]{1,0:T(8,128)} %get-tuple-element.49) | copy-start | bytes 3145732
  106.6 14.8 %collective-permute-start.21 = (bf16[256,1024]{1,0:T(8,128)(2,1)S(1)}, bf16[256,1024]{1,0:T(8,128)(2,1)S(1)}, u32[]{:S(2)}, u32[]{:S(2)}) collective-permute-start(bf16[256,1024]{1,0:T(8,128)(2,1)S(1)} %add_convert_fusion.2), channel_id=1, source_target_pairs={{0,32},{8,104},{32,64},{40,8},{64,96},{72,40},{96,0},{104,72},{1,3... | collective-permute-start | bytes 1572872 | tf_op jit(solution)/shard_map/ppermute | solution.py:245
  116.6 10.8 %collective-permute-start.25 = (bf16[256,1024]{1,0:T(8,128)(2,1)S(1)}, bf16[256,1024]{1,0:T(8,128)(2,1)S(1)}, u32[]{:S(2)}, u32[]{:S(2)}) collective-permute-start(bf16[256,1024]{1,0:T(8,128)(2,1)S(1)} %add_convert_fusion), channel_id=1, source_target_pairs={{0,16},{16,0},{1,17},{17,1},{2,18},{18,2},{3,19},{19,3},{4,20},{20... | collective-permute-start | bytes 1572872 | tf_op jit(solution)/shard_map/ppermute | solution.py:251
  118.1 1.6 %collective-permute-start.18 = (bf16[128,1024]{1,0:T(8,128)(2,1)S(1)}, bf16[128,1024]{1,0:T(8,128)(2,1)S(1)}, u32[]{:S(2)}, u32[]{:S(2)}) collective-permute-start(bf16[128,1024]{1,0:T(8,128)(2,1)S(1)} %get-tuple-element.64), channel_id=1, source_target_pairs={{0,8},{8,0},{1,9},{9,1},{2,10},{10,2},{3,11},{11,3},{4,12},{12,4},... | collective-permute-start | bytes 786440 | tf_op jit(solution)/shard_map/ppermute | solution.py:254
  (6 other events, 45.4 us)

commit v7 on v6

--- a/solution.py
+++ b/solution.py
@@ -46,18 +46,28 @@
     n = NX * NZ
     rows = width // (n * NC)
 
-    def body(core, act_ref, out_ref):
-        pick = core[0] == 0
-        out_ref[0] = jnp.where(pick, act_ref[:, :, rows:], act_ref[:, :, :rows])
+    def body(core, act_ref, out_ref, held, sems):
+        loads = []
+        for k in range(n):
+            start = pl.multiple_of((k * NC + 1 - core[0]) * rows, rows)
+            loads.append((act_ref.at[:, :, pl.ds(start, rows)], held.at[k]))
+        stores = []
+        for k, load in enumerate(start_all(loads, sems)):
+            load.wait()
+            stores += start_all([(held.at[k], out_ref.at[k])], sems, n + k)
+        wait_all(stores)
 
     out = pltpu.HBM((n, mb, toks, rows), act.dtype)
     return pl.pallas_call(
         body,
         out_shape=out,
-        grid=(n,),
-        in_specs=[SMEM, pl.BlockSpec((mb, toks, NC * rows), lambda k: (0, 0, k))],
-        out_specs=pl.BlockSpec((1, mb, toks, rows), lambda k: (k, 0, 0, 0)),
-        compiler_params=pltpu.CompilerParams(vmem_limit_bytes=8 << 20),
+        in_specs=[SMEM, HBM],
+        out_specs=HBM,
+        scratch_shapes=[
+            pltpu.VMEM((n, mb, toks, rows), act.dtype),
+            pltpu.SemaphoreType.DMA((2 * n,)),
+        ],
+        compiler_params=pltpu.CompilerParams(vmem_limit_bytes=4 << 20),
         cost_estimate=cost(0, act, out),
         name="other_columns",
     )(c.reshape(1), in_hbm(act))
@@ -121,10 +131,10 @@
             pltpu.VMEM((2, rows, cols), F32),
             pltpu.SemaphoreType.DMA((16,)),
         ],
-        compiler_params=pltpu.CompilerParams(vmem_limit_bytes=20 << 20),
-        cost_estimate=cost(16 * NC * mb * toks * rows * cols // 2, *outs, *diffs, got),
+        compiler_params=pltpu.CompilerParams(vmem_limit_bytes=16 << 20),
+        cost_estimate=cost(8 * NC * mb * toks * rows * cols, *outs, *diffs, got),
         name="dw_terms",
-    )(at, in_hbm(act), got, *diffs)
+    )(at, *map(in_hbm, (act, got, *diffs)))
 
 
 def dx_body(at, *refs):
@@ -133,27 +143,33 @@
     mb, toks, cols = diffs[0].shape
     part = toks // 2
     rows = pieces[0].shape[0]
-    loads = [(piece, rhs.at[p]) for p, piece in enumerate(pieces)]
+    loads = []
     for j, diff in enumerate(diffs):
         for h in range(2):
             k = at[j % 2 * 2 + h]
             for m in range(mb):
                 src = diff.at[m, h * part : (h + 1) * part]
                 loads.append((src, lhs.at[k, j // 2, m]))
-    wait_all(start_all(loads, sems))
+    first = len(loads)
+    loads += [(piece, rhs.at[p]) for p, piece in enumerate(pieces)]
+    loads = start_all(loads, sems)
+    wait_all(loads[:first])
     each = NC * mb * part
+    left = lhs[...].reshape(4 * each, cols)
     stores = []
-    for g, held in enumerate((narrow, wide)):
-        left = lhs[2 * g : 2 * g + 2].reshape(2 * each, cols)
-        for p in range(NX):
-            got = lax.dot_general(
-                left, rhs[p], (((1,), (1,)), ((), ())), preferred_element_type=F32
-            )
-            for k in range(2):
-                term = got[k * each : (k + 1) * each]
-                held[k, :, p * rows : (p + 1) * rows] = term.astype(held.dtype)
-        pairs = [(held.at[k], outs[2 * g + k]) for k in range(2)]
-        stores += start_all(pairs, sems, len(loads) + 2 * g)
+    for p in range(NX):
+        loads[first + p].wait()
+        got = lax.dot_general(
+            left, rhs[p], (((1,), (1,)), ((), ())), preferred_element_type=F32
+        )
+        pairs = []
+        for k, out in enumerate(outs):
+            held = narrow if k < 2 else wide
+            at_p = slice(p * rows, (p + 1) * rows)
+            term = got[k * each : (k + 1) * each]
+            held[k % 2, :, at_p] = term.astype(held.dtype)
+            pairs.append((held.at[k % 2, :, at_p], out.at[:, at_p]))
+        stores += start_all(pairs, sems, len(loads) + 4 * p)
     wait_all(stores)
 
 
@@ -172,12 +188,12 @@
             pltpu.VMEM((NX, rows, cols), BF16),
             pltpu.VMEM((2, NC * mb * part, NX * rows), BF16),
             pltpu.VMEM((2, NC * mb * part, NX * rows), F32),
-            pltpu.SemaphoreType.DMA((NX + 16 + 4,)),
+            pltpu.SemaphoreType.DMA((8 * mb + 5 * NX,)),
         ],
-        compiler_params=pltpu.CompilerParams(vmem_limit_bytes=20 << 20),
+        compiler_params=pltpu.CompilerParams(vmem_limit_bytes=16 << 20),
         cost_estimate=cost(8 * math.prod(outs[0].shape) * cols, *outs, *diffs, *pieces),
         name="dx_terms",
-    )(at, *diffs, *map(in_hbm, pieces))
+    )(at, *map(in_hbm, (*diffs, *pieces)))
 
 
 def place_body(at, keep_o, got_o, keep_p, got_p, out_ref):
@@ -272,15 +288,13 @@
 
     diff = (student_out.astype(F32) - teacher_out.astype(F32)).astype(BF16)
     diff_z = lax.ppermute(diff, "inc", SWAP)
-    own_late = after(own, diff)
-    near_o = neighbours(own_late)
-    w_z = swap_zh(own_late)
     diff_c = swap_core(diff)
-    near_p = neighbours(w_z)
+    near_o = neighbours(after(own, diff))
     far_o = step_x(pick(*near_o))
-    diff_z = after(diff_z, w_z, diff_c, far_o)
+    w_z = swap_zh(after(own, diff_z))
+    diff_z = after(diff_z, diff_c, *near_o)
+    diffs = (diff, diff_z, diff_c, swap_core(diff_z))
     act_got = swap_core(other_columns(after(activations, diff_z), c))
-    diffs = (diff, diff_z, diff_c, swap_core(diff_z))
 
     def later(*others):
         return (after(diff, *others), *diffs[1:])
@@ -297,15 +311,15 @@
         return add(here, back, step(add(ahead, far).astype(BF16)))
 
     terms_o = dx_terms(at_y, diffs, (own, *near_o, far_o))
-    forward_p = pick(after(near_p[0], terms_o[0]), near_p[1])
-    sums_p = dw_terms(at_p, activations, act_got, later(forward_p))
-    w_p = (w_z, *near_p, step_x(forward_p))
-    terms_p = dx_terms(at_y, later(*sums_p), w_p)
-    sums_o = dw_terms(at_o, activations, act_got, later(*terms_p))
+    near_p = neighbours(after(w_z, terms_o[0]))
+    sums_p = dw_terms(at_p, activations, act_got, later(*terms_o))
+    forward_p = pick(after(near_p[0], sums_p[0]), near_p[1])
+    sums_o = dw_terms(at_o, activations, act_got, later(forward_p))
+    terms_p = dx_terms(at_y, later(*sums_o), (w_z, *near_p, step_x(forward_p)))
     dx_o = ring(step_y, terms_o, sums_p[0]).astype(BF16)
     cross = swap_zh(ring(step_x, sums_p).astype(BF16))
+    weight_grad = ring(step_x, sums_o) + cross.astype(F32)
     dx_p = ring(step_y, terms_p).astype(BF16)
-    weight_grad = ring(step_x, sums_o) + cross.astype(F32)
 
     half = dx_o.shape[0] // 2
     got_o, got_p = swap_core(dx_o[half:]), swap_core(dx_p[half:])

time: 129 us -> 124 us (0.961)
  waiting for transfers between devices: 54.2 us -> 44.9 us
  starting transfers between devices: 28.8 us -> 32.6 us
  other arithmetic: 10.2 us -> 7.13 us
  local copies, waits for them, and re-layouts: 1.08 us -> 4.03 us
    ppermute x1, waiting for transfers between devices: 10.9 us -> 0.01 us  [local(): diff_z = lax.ppermute(diff, 'inc', SWAP)]
    ppermute x6, waiting for transfers between devices: 2.73 us -> 10.7 us  [step_y(): return lax.ppermute(value, ('core', 'outc'), by_core(NY, way, True))]
    ppermute x8, waiting for transfers between devices: 19.3 us -> 11.6 us  [step_x(): return lax.ppermute(value, ('x', 'core'), by_core(NX, way, False))]
    ppermute x2, waiting for transfers between devices: 6.6 us -> 11.8 us  [neighbours(): lax.ppermute(piece, 'x', by_x(-1))]
    pallas_call x1, Pallas kernels: 6.09 us -> 2.43 us  [other_columns(): pl.pallas_call(body, out_shape=out, in_specs=[SMEM, HBM], out_specs=HBM,...]
    pallas_call x2, Pallas kernels: 13.8 us -> 17 us  [dx_terms(): pl.pallas_call(dx_body, out_shape=outs, in_specs=[SMEM, *[HBM] * (4 + NX)...]
    unnamed x24 -> x32, local copies, waits for them, and re-layouts: 0.84 us -> 3.79 us
    ppermute x5, waiting for transfers between devices: 2.5 us -> 0.01 us  [swap_core(): return lax.ppermute(value, 'core', SWAP)]
  transfers between devices with their start and end apart: 26 -> 26, of which waited for: 12 -> 10; matrix products, arithmetic and copies ran while one was open for 6% -> 5% of each run, Pallas kernels for 21% -> 24%
where the time goes in v7:
time: 124 us; the launch traced here: 123 us
  waiting for transfers between devices  44.9 us (36%)
  Pallas kernels  33.8 us (27%)
  starting transfers between devices  32.6 us (26%)
  other arithmetic  7.13 us (6%)
  local copies, waits for them, and re-layouts  4.03 us (3%)
    pallas_call x2, Pallas kernels, dx_terms(): pl.pallas_call(dx_body, out_shape=outs, in_specs=[SMEM, *[HBM] * (4 + NX)...  17 us
    pallas_call x2, Pallas kernels, dw_terms(): pl.pallas_call(dw_body, out_shape=outs, in_specs=[SMEM, *[HBM] * 6], out_...  12.6 us
    ppermute x2, waiting for transfers between devices, neighbours(): lax.ppermute(piece, 'x', by_x(-1))  11.8 us
    ppermute x8, waiting for transfers between devices, step_x(): return lax.ppermute(value, ('x', 'core'), by_core(NX, way, False))  11.6 us
    ppermute x6, waiting for transfers between devices, step_y(): return lax.ppermute(value, ('core', 'outc'), by_core(NY, way, True))  10.7 us
    ppermute x8, starting transfers between devices, step_x(): return lax.ppermute(value, ('x', 'core'), by_core(NX, way, False))  7.79 us
    ppermute x2, waiting for transfers between devices, swap_zh(): return lax.ppermute(value, 'zh', SWAP)  7.41 us
    ppermute x2, starting transfers between devices, swap_zh(): return lax.ppermute(value, 'zh', SWAP)  7.33 us
  transfers between devices with their start and end apart: 26, of which 10 were waited for; matrix products, arithmetic and copies ran while one was open for 5% of the time, Pallas kernels for 24%

profile of v7, /device:TPU:0, one launch (start us, length us, event | category | flops | bytes accessed | tf_op | source)
XLA Modules:
  0.0 123.4 jit_solution(12558161606100457187)
XLA Ops:
  0.6 1.4 %subtract_convert_fusion.refs_0_ = bf16[2,128,1024]{2,1,0:T(8,128)(2,1)S(1)} fusion(bf16[2,128,1024]{2,1,0:T(8,128)(2,1)} %param.6, bf16[2,128,1024]{2,1,0:T(8,128)(2,1)} %param.5), kind=kLoop, calls=%fused_computation.8 | loop fusion | flops 1048576 | bytes 1572864 | tf_op jit(solution)/shard_map/convert_element_type | solution.py:289
  2.0 2.9 %collective-permute-start.3 = (bf16[256,1024]{1,0:T(8,128)(2,1)}, bf16[256,1024]{1,0:T(8,128)(2,1)S(1)}, u32[]{:S(2)}, u32[]{:S(2)}) collective-permute-start(bf16[256,1024]{1,0:T(8,128)(2,1)} %bitcast.19), channel_id=1, source_target_pairs={{0,96},{32,0},{64,32},{96,64},{1,97},{33,1},{65,33},{97,65},{2,98}... | collective-permute-start | bytes 1572872 | tf_op jit(solution)/shard_map/ppermute | solution.py:273
  5.0 1.9 %collective-permute-start = (bf16[2,128,1024]{2,1,0:T(8,128)(2,1)S(1)}, bf16[2,128,1024]{2,1,0:T(8,128)(2,1)S(1)}, u32[]{:S(2)}, u32[]{:S(2)}) collective-permute-start(bf16[2,128,1024]{2,1,0:T(8,128)(2,1)S(1)} %subtract_convert_fusion.refs_0_), channel_id=1, source_target_pairs={{0,4},{4,0},{1,5},{5,1},{2,6},{6,2},{3,7},{7,3},{8,12},{12,8},{9,1... | collective-permute-start | bytes 1572872 | tf_op jit(solution)/shard_map/ppermute | solution.py:290
  6.9 9.6 %collective-permute-done.3.refs_6_ = bf16[256,1024]{1,0:T(8,128)(2,1)S(1)} collective-permute-done((bf16[256,1024]{1,0:T(8,128)(2,1)}, bf16[256,1024]{1,0:T(8,128)(2,1)S(1)}, u32[]{:S(2)}, u32[]{:S(2)}) %collective-permute-start.3) | collective-permute-done | bytes 524320 | tf_op jit(solution)/shard_map/ppermute | solution.py:273
  16.4 3.3 %collective-permute-done.2.refs_5_ = bf16[256,1024]{1,0:T(8,128)(2,1)S(1)} collective-permute-done((bf16[256,1024]{1,0:T(8,128)(2,1)}, bf16[256,1024]{1,0:T(8,128)(2,1)S(1)}, u32[]{:S(2)}, u32[]{:S(2)}) %collective-permute-start.2) | collective-permute-done | bytes 524320 | tf_op jit(solution)/shard_map/ppermute | solution.py:273
  21.4 2.4 %other_columns.1 = bf16[8,2,256,256]{3,2,1,0:T(8,128)(2,1)} custom-call(s32[1]{0:T(128)} %bitcast.2.core, bf16[2,256,4096]{2,1,0:T(8,128)(2,1)} %act.3), custom_call_target="tpu_custom_call" | custom-call | bytes 6291456 | tf_op jit(solution)/shard_map/other_columns/pallas_call | solution.py:61
  25.1 2.3 %collective-permute-start.4 = (bf16[2,128,1024]{2,1,0:T(8,128)(2,1)}, bf16[2,128,1024]{2,1,0:T(8,128)(2,1)S(1)}, u32[]{:S(2)}, u32[]{:S(2)}) collective-permute-start(bf16[2,128,1024]{2,1,0:T(8,128)(2,1)} %copy-done.3), channel_id=1, source_target_pairs={{0,8},{8,0},{1,9},{9,1},{2,10},{10,2},{3,11},{11,3},{4,12},{12,4},... | collective-permute-start | bytes 1572872 | tf_op jit(solution)/shard_map/ppermute | solution.py:270
  27.4 3.7 %collective-permute-start.11 = (bf16[256,1024]{1,0:T(8,128)(2,1)}, bf16[256,1024]{1,0:T(8,128)(2,1)}, u32[]{:S(2)}, u32[]{:S(2)}) collective-permute-start(bf16[256,1024]{1,0:T(8,128)(2,1)} %bitcast.21), channel_id=1, source_target_pairs={{0,16},{16,0},{1,17},{17,1},{2,18},{18,2},{3,19},{19,3},{4,20},{20... | collective-permute-start | bytes 1572872 | tf_op jit(solution)/shard_map/ppermute | solution.py:267
  31.2 4.4 %collective-permute-done.5.refs_7_ = bf16[256,1024]{1,0:T(8,128)(2,1)} collective-permute-done((bf16[256,1024]{1,0:T(8,128)(2,1)S(1)}, bf16[256,1024]{1,0:T(8,128)(2,1)}, u32[]{:S(2)}, u32[]{:S(2)}) %collective-permute-start.5) | collective-permute-done | bytes 524320 | tf_op jit(solution)/shard_map/ppermute | solution.py:261
  36.4 8.5 %dx_terms.2 = (bf16[256,1024]{1,0:T(8,128)(2,1)}, bf16[256,1024]{1,0:T(8,128)(2,1)}, f32[256,1024]{1,0:T(8,128)}, f32[256,1024]{1,0:T(8,128)}) custom-call(s32[4]{0:T(128)S(1)} %pad_add_fusion.1.at, bf16[2,128,1024]{2,1,0:T(8,128)(2,1)} %copy-done.1, bf16[2,128,1024]{2,1,0:T(8,128)(2,1)} %copy-done.3, bf16[2,128,1024]{2,1,0:T(8,128)(2,1)} %copy-done.2, ...), custom_call_target="tpu_custom_call" | custom-call | flops 2147483648 | bytes 7340032 | tf_op jit(solution)/shard_map/dx_terms/pallas_call | solution.py:181
  45.0 3.1 %collective-permute-start.7 = (bf16[256,1024]{1,0:T(8,128)(2,1)}, bf16[256,1024]{1,0:T(8,128)(2,1)S(1)}, u32[]{:S(2)}, u32[]{:S(2)}) collective-permute-start(bf16[256,1024]{1,0:T(8,128)(2,1)} %get-tuple-element.39), channel_id=1, source_target_pairs={{0,3},{8,9},{1,0},{9,10},{2,1},{10,11},{3,2},{11,8},{4,7},{12,13},... | collective-permute-start | bytes 1572872 | tf_op jit(solution)/shard_map/ppermute | solution.py:264
  48.1 3.2 %collective-permute-start.13 = (bf16[256,1024]{1,0:T(8,128)(2,1)}, bf16[256,1024]{1,0:T(8,128)(2,1)}, u32[]{:S(2)}, u32[]{:S(2)}) collective-permute-start(bf16[256,1024]{1,0:T(8,128)(2,1)} %collective-permute-done.11.refs_4_), channel_id=1, source_target_pairs={{0,96},{32,0},{64,32},{96,64},{1,97},{33,1},{65,33},{97,65},{2,98}... | collective-permute-start | bytes 1572872 | tf_op jit(solution)/shard_map/ppermute | solution.py:273
  51.3 1.3 %copy-done = bf16[8,2,256,256]{3,2,1,0:T(8,128)(2,1)} copy-done((bf16[8,2,256,256]{3,2,1,0:T(8,128)(2,1)}, bf16[8,2,256,256]{3,2,1,0:T(8,128)(2,1)S(1)}, u32[]{:S(2)}) %copy-start) | copy-done | bytes 2097176
  52.7 6.3 %dw_terms.2 = (bf16[256,1024]{1,0:T(8,128)(2,1)}, bf16[256,1024]{1,0:T(8,128)(2,1)}, f32[256,1024]{1,0:T(8,128)}, f32[256,1024]{1,0:T(8,128)}) custom-call(s32[6]{0:T(128)S(1)} %stack.77.at, bf16[2,256,4096]{2,1,0:T(8,128)(2,1)} %act.3, bf16[8,2,256,256]{3,2,1,0:T(8,128)(2,1)} %copy-done, bf16[2,128,1024]{2,1,0:T(8,128)(2,1)} %copy-done.1, ...), custom_call_target="tpu_custom_call" | custom-call | flops 2147483648 | bytes 7340032 | tf_op jit(solution)/shard_map/dw_terms/pallas_call | solution.py:122
  59.1 2.3 %collective-permute-done.13.refs_6_ = bf16[256,1024]{1,0:T(8,128)(2,1)} collective-permute-done((bf16[256,1024]{1,0:T(8,128)(2,1)}, bf16[256,1024]{1,0:T(8,128)(2,1)}, u32[]{:S(2)}, u32[]{:S(2)}) %collective-permute-start.13) | collective-permute-done | bytes 524320 | tf_op jit(solution)/shard_map/ppermute | solution.py:273
  61.4 1.8 %collective-permute-start.14 = (bf16[256,1024]{1,0:T(8,128)(2,1)S(1)}, bf16[256,1024]{1,0:T(8,128)(2,1)}, u32[]{:S(2)}, u32[]{:S(2)}) collective-permute-start(bf16[256,1024]{1,0:T(8,128)(2,1)S(1)} %broadcast_select_fusion), channel_id=1, source_target_pairs={{0,32},{8,104},{32,64},{40,8},{64,96},{72,40},{96,0},{104,72},{1,3... | collective-permute-start | bytes 1572872 | tf_op jit(solution)/shard_map/ppermute | solution.py:261
  63.2 2.0 %add_convert_fusion.6 = bf16[256,1024]{1,0:T(8,128)(2,1)} fusion(f32[256,1024]{1,0:T(8,128)S(1)} %copy-done.9, bf16[256,1024]{1,0:T(8,128)(2,1)} %collective-permute-done.6), kind=kLoop, calls=%fused_computation.7 | loop fusion | flops 786432 | bytes 2097152 | tf_op jit(solution)/shard_map/convert_element_type | solution.py:311
  65.5 1.9 %collective-permute-start.23 = (bf16[256,1024]{1,0:T(8,128)(2,1)}, bf16[256,1024]{1,0:T(8,128)(2,1)S(1)}, u32[]{:S(2)}, u32[]{:S(2)}) collective-permute-start(bf16[256,1024]{1,0:T(8,128)(2,1)} %get-tuple-element.64), channel_id=1, source_target_pairs={{0,96},{8,40},{32,0},{40,72},{64,32},{72,104},{96,64},{104,8},{1,9... | collective-permute-start | bytes 1572872 | tf_op jit(solution)/shard_map/ppermute | solution.py:261
  67.8 6.3 %dw_terms.3 = (bf16[256,1024]{1,0:T(8,128)(2,1)}, bf16[256,1024]{1,0:T(8,128)(2,1)}, f32[256,1024]{1,0:T(8,128)}, f32[256,1024]{1,0:T(8,128)}) custom-call(s32[6]{0:T(128)S(1)} %stack.82.at, bf16[2,256,4096]{2,1,0:T(8,128)(2,1)} %act.3, bf16[8,2,256,256]{3,2,1,0:T(8,128)(2,1)} %copy-done, bf16[2,128,1024]{2,1,0:T(8,128)(2,1)} %copy-done.1, ...), custom_call_target="tpu_custom_call" | custom-call | flops 2147483648 | bytes 7340032 | tf_op jit(solution)/shard_map/dw_terms/pallas_call | solution.py:122
  74.2 1.8 %collective-permute-start.19 = (bf16[256,1024]{1,0:T(8,128)(2,1)}, bf16[256,1024]{1,0:T(8,128)(2,1)S(1)}, u32[]{:S(2)}, u32[]{:S(2)}) collective-permute-start(bf16[256,1024]{1,0:T(8,128)(2,1)} %get-tuple-element.50), channel_id=1, source_target_pairs={{0,32},{8,104},{32,64},{40,8},{64,96},{72,40},{96,0},{104,72},{1,3... | collective-permute-start | bytes 1572872 | tf_op jit(solution)/shard_map/ppermute | solution.py:261
  76.0 1.5 %collective-permute-start.20 = (bf16[256,1024]{1,0:T(8,128)(2,1)}, bf16[256,1024]{1,0:T(8,128)(2,1)S(1)}, u32[]{:S(2)}, u32[]{:S(2)}) collective-permute-start(bf16[256,1024]{1,0:T(8,128)(2,1)} %get-tuple-element.51), channel_id=1, source_target_pairs={{0,96},{8,40},{32,0},{40,72},{64,32},{72,104},{96,64},{104,8},{1,9... | collective-permute-start | bytes 1572872 | tf_op jit(solution)/shard_map/ppermute | solution.py:261
  77.5 8.5 %dx_terms.3 = (bf16[256,1024]{1,0:T(8,128)(2,1)}, bf16[256,1024]{1,0:T(8,128)(2,1)}, f32[256,1024]{1,0:T(8,128)}, f32[256,1024]{1,0:T(8,128)}) custom-call(s32[4]{0:T(128)S(1)} %pad_add_fusion.1.at, bf16[2,128,1024]{2,1,0:T(8,128)(2,1)} %copy-done.1, bf16[2,128,1024]{2,1,0:T(8,128)(2,1)} %copy-done.3, bf16[2,128,1024]{2,1,0:T(8,128)(2,1)} %copy-done.2, ...), custom_call_target="tpu_custom_call" | custom-call | flops 2147483648 | bytes 7340032 | tf_op jit(solution)/shard_map/dx_terms/pallas_call | solution.py:181
  86.1 1.6 %collective-permute-start.15 = (bf16[256,1024]{1,0:T(8,128)(2,1)}, bf16[256,1024]{1,0:T(8,128)(2,1)S(1)}, u32[]{:S(2)}, u32[]{:S(2)}) collective-permute-start(bf16[256,1024]{1,0:T(8,128)(2,1)} %get-tuple-element.56), channel_id=1, source_target_pairs={{0,1},{8,11},{1,2},{9,8},{2,3},{10,9},{3,0},{11,10},{4,5},{12,15},... | collective-permute-start | bytes 1572872 | tf_op jit(solution)/shard_map/ppermute | solution.py:264
  87.7 1.7 %collective-permute-start.16 = (bf16[256,1024]{1,0:T(8,128)(2,1)}, bf16[256,1024]{1,0:T(8,128)(2,1)S(1)}, u32[]{:S(2)}, u32[]{:S(2)}) collective-permute-start(bf16[256,1024]{1,0:T(8,128)(2,1)} %get-tuple-element.57), channel_id=1, source_target_pairs={{0,3},{8,9},{1,0},{9,10},{2,1},{10,11},{3,2},{11,8},{4,7},{12,13},... | collective-permute-start | bytes 1572872 | tf_op jit(solution)/shard_map/ppermute | solution.py:264
  90.0 4.8 %collective-permute-done.19 = bf16[256,1024]{1,0:T(8,128)(2,1)S(1)} collective-permute-done((bf16[256,1024]{1,0:T(8,128)(2,1)}, bf16[256,1024]{1,0:T(8,128)(2,1)S(1)}, u32[]{:S(2)}, u32[]{:S(2)}) %collective-permute-start.19) | collective-permute-done | bytes 524320 | tf_op jit(solution)/shard_map/ppermute | solution.py:261
  94.8 7.1 %collective-permute-done.15 = bf16[256,1024]{1,0:T(8,128)(2,1)S(1)} collective-permute-done((bf16[256,1024]{1,0:T(8,128)(2,1)}, bf16[256,1024]{1,0:T(8,128)(2,1)S(1)}, u32[]{:S(2)}, u32[]{:S(2)}) %collective-permute-start.15) | collective-permute-done | bytes 524320 | tf_op jit(solution)/shard_map/ppermute | solution.py:264
  102.8 2.4 %collective-permute-done.24 = bf16[256,1024]{1,0:T(8,128)(2,1)S(1)} collective-permute-done((bf16[256,1024]{1,0:T(8,128)(2,1)S(1)}, bf16[256,1024]{1,0:T(8,128)(2,1)S(1)}, u32[]{:S(2)}, u32[]{:S(2)}) %collective-permute-start.24) | collective-permute-done | bytes 524320 | tf_op jit(solution)/shard_map/ppermute | solution.py:261
  105.4 3.6 %collective-permute-start.25 = (bf16[256,1024]{1,0:T(8,128)(2,1)S(1)}, bf16[256,1024]{1,0:T(8,128)(2,1)S(1)}, u32[]{:S(2)}, u32[]{:S(2)}) collective-permute-start(bf16[256,1024]{1,0:T(8,128)(2,1)S(1)} %add_convert_fusion), channel_id=1, source_target_pairs={{0,16},{16,0},{1,17},{17,1},{2,18},{18,2},{3,19},{19,3},{4,20},{20... | collective-permute-start | bytes 1572872 | tf_op jit(solution)/shard_map/ppermute | solution.py:267
  109.1 3.5 %collective-permute-done.17 = bf16[256,1024]{1,0:T(8,128)(2,1)S(1)} collective-permute-done((bf16[256,1024]{1,0:T(8,128)(2,1)S(1)}, bf16[256,1024]{1,0:T(8,128)(2,1)S(1)}, u32[]{:S(2)}, u32[]{:S(2)}) %collective-permute-start.17) | collective-permute-done | bytes 524320 | tf_op jit(solution)/shard_map/ppermute | solution.py:264
  113.0 7.4 %collective-permute-done.25 = bf16[256,1024]{1,0:T(8,128)(2,1)S(1)} collective-permute-done((bf16[256,1024]{1,0:T(8,128)(2,1)S(1)}, bf16[256,1024]{1,0:T(8,128)(2,1)S(1)}, u32[]{:S(2)}, u32[]{:S(2)}) %collective-permute-start.25) | collective-permute-done | bytes 524320 | tf_op jit(solution)/shard_map/ppermute | solution.py:267
  120.4 1.3 %add_bitcast_fusion = f32[1,256,1024]{2,1,0:T(8,128)} fusion(bf16[256,1024]{1,0:T(8,128)(2,1)S(1)} %collective-permute-done.25, bf16[256,1024]{1,0:T(8,128)(2,1)S(1)} %collective-permute-done.21, f32[256,1024]{1,0:T(8,128)S(1)} %copy-done.5, bf16[256,1024]{1,0:T(8,128)(2,1)S(1)} %collective-permute-done.20), kind=kLoop, calls=%fused_computation | loop fusion | flops 1572864 | bytes 3670016 | tf_op jit(solution)/shard_map/reshape | solution.py:329
  121.7 1.7 %place.1 = bf16[2,64,4096]{2,1,0:T(8,128)(2,1)} custom-call(s32[3]{0:T(128)S(1)} %pad_add_fusion.at, bf16[128,1024]{1,0:T(8,128)(2,1)S(1)} %get-tuple-element.71.keep_o, bf16[128,1024]{1,0:T(8,128)(2,1)S(1)} %collective-permute-done.10.got_o, bf16[128,1024]{1,0:T(8,128)(2,1)S(1)} %get-tuple-element.69.keep_p, bf16[128,1024]{1,0:T(8,128)(2,1)S(1)} %collective-permute-done.18.got_p), custom_call_target="tpu_custom_call" | custom-call | bytes 2097152 | tf_op jit(solution)/shard_map/place/pallas_call | solution.py:222
  (75 shorter events, 6.8 us)
Async XLA Ops:
  2.0 21.8 %copy-start.1 = (bf16[2,128,1024]{2,1,0:T(8,128)(2,1)}, bf16[2,128,1024]{2,1,0:T(8,128)(2,1)S(1)}, u32[]{:S(2)}) copy-start(bf16[2,128,1024]{2,1,0:T(8,128)(2,1)S(1)} %subtract_convert_fusion.refs_0_) | copy-start | bytes 1572868
  2.0 14.4 %collective-permute-start.3 = (bf16[256,1024]{1,0:T(8,128)(2,1)}, bf16[256,1024]{1,0:T(8,128)(2,1)S(1)}, u32[]{:S(2)}, u32[]{:S(2)}) collective-permute-start(bf16[256,1024]{1,0:T(8,128)(2,1)} %bitcast.19), channel_id=1, source_target_pairs={{0,96},{32,0},{64,32},{96,64},{1,97},{33,1},{65,33},{97,65},{2,98}... | collective-permute-start | bytes 1572872 | tf_op jit(solution)/shard_map/ppermute | solution.py:273
  4.9 14.8 %collective-permute-start.2 = (bf16[256,1024]{1,0:T(8,128)(2,1)}, bf16[256,1024]{1,0:T(8,128)(2,1)S(1)}, u32[]{:S(2)}, u32[]{:S(2)}) collective-permute-start(bf16[256,1024]{1,0:T(8,128)(2,1)} %bitcast.20), channel_id=1, source_target_pairs={{0,32},{32,64},{64,96},{96,0},{1,33},{33,65},{65,97},{97,1},{2,34}... | collective-permute-start | bytes 1572872 | tf_op jit(solution)/shard_map/ppermute | solution.py:273
  5.0 14.8 %collective-permute-start.1 = (bf16[2,128,1024]{2,1,0:T(8,128)(2,1)S(1)}, bf16[2,128,1024]{2,1,0:T(8,128)(2,1)S(1)}, u32[]{:S(2)}, u32[]{:S(2)}) collective-permute-start(bf16[2,128,1024]{2,1,0:T(8,128)(2,1)S(1)} %subtract_convert_fusion.refs_0_), channel_id=1, source_target_pairs={{0,8},{8,0},{1,9},{9,1},{2,10},{10,2},{3,11},{11,3},{4,12},{12,4},... | collective-permute-start | bytes 1572872 | tf_op jit(solution)/shard_map/ppermute | solution.py:270
  5.0 14.8 %collective-permute-start = (bf16[2,128,1024]{2,1,0:T(8,128)(2,1)S(1)}, bf16[2,128,1024]{2,1,0:T(8,128)(2,1)S(1)}, u32[]{:S(2)}, u32[]{:S(2)}) collective-permute-start(bf16[2,128,1024]{2,1,0:T(8,128)(2,1)S(1)} %subtract_convert_fusion.refs_0_), channel_id=1, source_target_pairs={{0,4},{4,0},{1,5},{5,1},{2,6},{6,2},{3,7},{7,3},{8,12},{12,8},{9,1... | collective-permute-start | bytes 1572872 | tf_op jit(solution)/shard_map/ppermute | solution.py:290
  23.8 27.5 %collective-permute-start.8 = (bf16[8,2,256,256]{3,2,1,0:T(8,128)(2,1)}, bf16[8,2,256,256]{3,2,1,0:T(8,128)(2,1)S(1)}, u32[]{:S(2)}, u32[]{:S(2)}) collective-permute-start(bf16[8,2,256,256]{3,2,1,0:T(8,128)(2,1)} %other_columns.1), channel_id=1, source_target_pairs={{0,8},{8,0},{1,9},{9,1},{2,10},{10,2},{3,11},{11,3},{4,12},{12,4},... | collective-permute-start | bytes 6291464 | tf_op jit(solution)/shard_map/ppermute | solution.py:270
  25.0 10.6 %collective-permute-start.5 = (bf16[256,1024]{1,0:T(8,128)(2,1)S(1)}, bf16[256,1024]{1,0:T(8,128)(2,1)}, u32[]{:S(2)}, u32[]{:S(2)}) collective-permute-start(bf16[256,1024]{1,0:T(8,128)(2,1)S(1)} %broadcast_select_fusion.1), channel_id=1, source_target_pairs={{0,32},{8,104},{32,64},{40,8},{64,96},{72,40},{96,0},{104,72},{1,3... | collective-permute-start | bytes 1572872 | tf_op jit(solution)/shard_map/ppermute | solution.py:261
  25.1 10.5 %collective-permute-start.4 = (bf16[2,128,1024]{2,1,0:T(8,128)(2,1)}, bf16[2,128,1024]{2,1,0:T(8,128)(2,1)S(1)}, u32[]{:S(2)}, u32[]{:S(2)}) collective-permute-start(bf16[2,128,1024]{2,1,0:T(8,128)(2,1)} %copy-done.3), channel_id=1, source_target_pairs={{0,8},{8,0},{1,9},{9,1},{2,10},{10,2},{3,11},{11,3},{4,12},{12,4},... | collective-permute-start | bytes 1572872 | tf_op jit(solution)/shard_map/ppermute | solution.py:270
  27.4 17.5 %collective-permute-start.11 = (bf16[256,1024]{1,0:T(8,128)(2,1)}, bf16[256,1024]{1,0:T(8,128)(2,1)}, u32[]{:S(2)}, u32[]{:S(2)}) collective-permute-start(bf16[256,1024]{1,0:T(8,128)(2,1)} %bitcast.21), channel_id=1, source_target_pairs={{0,16},{16,0},{1,17},{17,1},{2,18},{18,2},{3,19},{19,3},{4,20},{20... | collective-permute-start | bytes 1572872 | tf_op jit(solution)/shard_map/ppermute | solution.py:267
  44.9 14.1 %collective-permute-start.12 = (bf16[256,1024]{1,0:T(8,128)(2,1)}, bf16[256,1024]{1,0:T(8,128)(2,1)S(1)}, u32[]{:S(2)}, u32[]{:S(2)}) collective-permute-start(bf16[256,1024]{1,0:T(8,128)(2,1)} %collective-permute-done.11.refs_4_), channel_id=1, source_target_pairs={{0,32},{32,64},{64,96},{96,0},{1,33},{33,65},{65,97},{97,1},{2,34}... | collective-permute-start | bytes 1572872 | tf_op jit(solution)/shard_map/ppermute | solution.py:273
  45.0 14.1 %collective-permute-start.7 = (bf16[256,1024]{1,0:T(8,128)(2,1)}, bf16[256,1024]{1,0:T(8,128)(2,1)S(1)}, u32[]{:S(2)}, u32[]{:S(2)}) collective-permute-start(bf16[256,1024]{1,0:T(8,128)(2,1)} %get-tuple-element.39), channel_id=1, source_target_pairs={{0,3},{8,9},{1,0},{9,10},{2,1},{10,11},{3,2},{11,8},{4,7},{12,13},... | collective-permute-start | bytes 1572872 | tf_op jit(solution)/shard_map/ppermute | solution.py:264
  48.1 11.0 %collective-permute-start.6 = (bf16[256,1024]{1,0:T(8,128)(2,1)}, bf16[256,1024]{1,0:T(8,128)(2,1)}, u32[]{:S(2)}, u32[]{:S(2)}) collective-permute-start(bf16[256,1024]{1,0:T(8,128)(2,1)} %get-tuple-element.38), channel_id=1, source_target_pairs={{0,1},{8,11},{1,2},{9,8},{2,3},{10,9},{3,0},{11,10},{4,5},{12,15},... | collective-permute-start | bytes 1572872 | tf_op jit(solution)/shard_map/ppermute | solution.py:264
  48.1 13.2 %collective-permute-start.13 = (bf16[256,1024]{1,0:T(8,128)(2,1)}, bf16[256,1024]{1,0:T(8,128)(2,1)}, u32[]{:S(2)}, u32[]{:S(2)}) collective-permute-start(bf16[256,1024]{1,0:T(8,128)(2,1)} %collective-permute-done.11.refs_4_), channel_id=1, source_target_pairs={{0,96},{32,0},{64,32},{96,64},{1,97},{33,1},{65,33},{97,65},{2,98}... | collective-permute-start | bytes 1572872 | tf_op jit(solution)/shard_map/ppermute | solution.py:273
  59.1 15.1 %copy-start.13 = (bf16[256,1024]{1,0:T(8,128)(2,1)}, bf16[256,1024]{1,0:T(8,128)(2,1)S(1)}, u32[]{:S(2)}) copy-start(bf16[256,1024]{1,0:T(8,128)(2,1)S(1)} %collective-permute-done.12.refs_5_) | copy-start | bytes 1572868
  61.4 14.6 %collective-permute-start.14 = (bf16[256,1024]{1,0:T(8,128)(2,1)S(1)}, bf16[256,1024]{1,0:T(8,128)(2,1)}, u32[]{:S(2)}, u32[]{:S(2)}) collective-permute-start(bf16[256,1024]{1,0:T(8,128)(2,1)S(1)} %broadcast_select_fusion), channel_id=1, source_target_pairs={{0,32},{8,104},{32,64},{40,8},{64,96},{72,40},{96,0},{104,72},{1,3... | collective-permute-start | bytes 1572872 | tf_op jit(solution)/shard_map/ppermute | solution.py:261
  65.2 20.9 %collective-permute-start.9 = (bf16[256,1024]{1,0:T(8,128)(2,1)}, bf16[256,1024]{1,0:T(8,128)(2,1)S(1)}, u32[]{:S(2)}, u32[]{:S(2)}) collective-permute-start(bf16[256,1024]{1,0:T(8,128)(2,1)} %add_convert_fusion.6), channel_id=1, source_target_pairs={{0,1},{8,11},{1,2},{9,8},{2,3},{10,9},{3,0},{11,10},{4,5},{12,15},... | collective-permute-start | bytes 1572872 | tf_op jit(solution)/shard_map/ppermute | solution.py:264
  65.5 22.3 %collective-permute-start.23 = (bf16[256,1024]{1,0:T(8,128)(2,1)}, bf16[256,1024]{1,0:T(8,128)(2,1)S(1)}, u32[]{:S(2)}, u32[]{:S(2)}) collective-permute-start(bf16[256,1024]{1,0:T(8,128)(2,1)} %get-tuple-element.64), channel_id=1, source_target_pairs={{0,96},{8,40},{32,0},{40,72},{64,32},{72,104},{96,64},{104,8},{1,9... | collective-permute-start | bytes 1572872 | tf_op jit(solution)/shard_map/ppermute | solution.py:261
  67.6 22.2 %collective-permute-start.22 = (bf16[256,1024]{1,0:T(8,128)(2,1)}, bf16[256,1024]{1,0:T(8,128)(2,1)S(1)}, u32[]{:S(2)}, u32[]{:S(2)}) collective-permute-start(bf16[256,1024]{1,0:T(8,128)(2,1)} %get-tuple-element.43), channel_id=1, source_target_pairs={{0,32},{8,104},{32,64},{40,8},{64,96},{72,40},{96,0},{104,72},{1,3... | collective-permute-start | bytes 1572872 | tf_op jit(solution)/shard_map/ppermute | solution.py:261
  74.2 20.6 %collective-permute-start.19 = (bf16[256,1024]{1,0:T(8,128)(2,1)}, bf16[256,1024]{1,0:T(8,128)(2,1)S(1)}, u32[]{:S(2)}, u32[]{:S(2)}) collective-permute-start(bf16[256,1024]{1,0:T(8,128)(2,1)} %get-tuple-element.50), channel_id=1, source_target_pairs={{0,32},{8,104},{32,64},{40,8},{64,96},{72,40},{96,0},{104,72},{1,3... | collective-permute-start | bytes 1572872 | tf_op jit(solution)/shard_map/ppermute | solution.py:261
  76.0 13.4 %copy-start.6 = (f32[256,1024]{1,0:T(8,128)S(1)}, f32[256,1024]{1,0:T(8,128)}, u32[]{:S(2)}) copy-start(f32[256,1024]{1,0:T(8,128)} %get-tuple-element.37) | copy-start | bytes 3145732
  76.0 18.8 %collective-permute-start.20 = (bf16[256,1024]{1,0:T(8,128)(2,1)}, bf16[256,1024]{1,0:T(8,128)(2,1)S(1)}, u32[]{:S(2)}, u32[]{:S(2)}) collective-permute-start(bf16[256,1024]{1,0:T(8,128)(2,1)} %get-tuple-element.51), channel_id=1, source_target_pairs={{0,96},{8,40},{32,0},{40,72},{64,32},{72,104},{96,64},{104,8},{1,9... | collective-permute-start | bytes 1572872 | tf_op jit(solution)/shard_map/ppermute | solution.py:261
  86.1 15.9 %collective-permute-start.15 = (bf16[256,1024]{1,0:T(8,128)(2,1)}, bf16[256,1024]{1,0:T(8,128)(2,1)S(1)}, u32[]{:S(2)}, u32[]{:S(2)}) collective-permute-start(bf16[256,1024]{1,0:T(8,128)(2,1)} %get-tuple-element.56), channel_id=1, source_target_pairs={{0,1},{8,11},{1,2},{9,8},{2,3},{10,9},{3,0},{11,10},{4,5},{12,15},... | collective-permute-start | bytes 1572872 | tf_op jit(solution)/shard_map/ppermute | solution.py:264
  87.7 14.3 %collective-permute-start.16 = (bf16[256,1024]{1,0:T(8,128)(2,1)}, bf16[256,1024]{1,0:T(8,128)(2,1)S(1)}, u32[]{:S(2)}, u32[]{:S(2)}) collective-permute-start(bf16[256,1024]{1,0:T(8,128)(2,1)} %get-tuple-element.57), channel_id=1, source_target_pairs={{0,3},{8,9},{1,0},{9,10},{2,1},{10,11},{3,2},{11,8},{4,7},{12,13},... | collective-permute-start | bytes 1572872 | tf_op jit(solution)/shard_map/ppermute | solution.py:264
  89.6 12.3 %copy-start.12 = (f32[256,1024]{1,0:T(8,128)S(1)}, f32[256,1024]{1,0:T(8,128)}, u32[]{:S(2)}) copy-start(f32[256,1024]{1,0:T(8,128)} %get-tuple-element.59) | copy-start | bytes 3145732
  89.7 32.0 %collective-permute-start.10 = (bf16[128,1024]{1,0:T(8,128)(2,1)S(1)}, bf16[128,1024]{1,0:T(8,128)(2,1)S(1)}, u32[]{:S(2)}, u32[]{:S(2)}) collective-permute-start(bf16[128,1024]{1,0:T(8,128)(2,1)S(1)} %get-tuple-element.70), channel_id=1, source_target_pairs={{0,8},{8,0},{1,9},{9,1},{2,10},{10,2},{3,11},{11,3},{4,12},{12,4},... | collective-permute-start | bytes 786440 | tf_op jit(solution)/shard_map/ppermute | solution.py:270
  89.8 12.5 %copy-start.11 = (f32[256,1024]{1,0:T(8,128)S(1)}, f32[256,1024]{1,0:T(8,128)}, u32[]{:S(2)}) copy-start(f32[256,1024]{1,0:T(8,128)} %get-tuple-element.52) | copy-start | bytes 3145732
  94.8 10.4 %collective-permute-start.24 = (bf16[256,1024]{1,0:T(8,128)(2,1)S(1)}, bf16[256,1024]{1,0:T(8,128)(2,1)S(1)}, u32[]{:S(2)}, u32[]{:S(2)}) collective-permute-start(bf16[256,1024]{1,0:T(8,128)(2,1)S(1)} %add_convert_fusion.1), channel_id=1, source_target_pairs={{0,32},{8,104},{32,64},{40,8},{64,96},{72,40},{96,0},{104,72},{1,3... | collective-permute-start | bytes 1572872 | tf_op jit(solution)/shard_map/ppermute | solution.py:261
  102.1 10.5 %collective-permute-start.17 = (bf16[256,1024]{1,0:T(8,128)(2,1)S(1)}, bf16[256,1024]{1,0:T(8,128)(2,1)S(1)}, u32[]{:S(2)}, u32[]{:S(2)}) collective-permute-start(bf16[256,1024]{1,0:T(8,128)(2,1)S(1)} %add_convert_fusion.4), channel_id=1, source_target_pairs={{0,1},{8,11},{1,2},{9,8},{2,3},{10,9},{3,0},{11,10},{4,5},{12,15},... | collective-permute-start | bytes 1572872 | tf_op jit(solution)/shard_map/ppermute | solution.py:264
  102.4 10.6 %collective-permute-start.21 = (bf16[256,1024]{1,0:T(8,128)(2,1)S(1)}, bf16[256,1024]{1,0:T(8,128)(2,1)S(1)}, u32[]{:S(2)}, u32[]{:S(2)}) collective-permute-start(bf16[256,1024]{1,0:T(8,128)(2,1)S(1)} %add_convert_fusion.2), channel_id=1, source_target_pairs={{0,32},{8,104},{32,64},{40,8},{64,96},{72,40},{96,0},{104,72},{1,3... | collective-permute-start | bytes 1572872 | tf_op jit(solution)/shard_map/ppermute | solution.py:261
  105.4 15.0 %copy-start.5 = (f32[256,1024]{1,0:T(8,128)S(1)}, f32[256,1024]{1,0:T(8,128)}, u32[]{:S(2)}) copy-start(f32[256,1024]{1,0:T(8,128)} %get-tuple-element.53) | copy-start | bytes 3145732
  105.4 15.0 %collective-permute-start.25 = (bf16[256,1024]{1,0:T(8,128)(2,1)S(1)}, bf16[256,1024]{1,0:T(8,128)(2,1)S(1)}, u32[]{:S(2)}, u32[]{:S(2)}) collective-permute-start(bf16[256,1024]{1,0:T(8,128)(2,1)S(1)} %add_convert_fusion), channel_id=1, source_target_pairs={{0,16},{16,0},{1,17},{17,1},{2,18},{18,2},{3,19},{19,3},{4,20},{20... | collective-permute-start | bytes 1572872 | tf_op jit(solution)/shard_map/ppermute | solution.py:267
  112.9 8.8 %collective-permute-start.18 = (bf16[128,1024]{1,0:T(8,128)(2,1)S(1)}, bf16[128,1024]{1,0:T(8,128)(2,1)S(1)}, u32[]{:S(2)}, u32[]{:S(2)}) collective-permute-start(bf16[128,1024]{1,0:T(8,128)(2,1)S(1)} %get-tuple-element.68), channel_id=1, source_target_pairs={{0,8},{8,0},{1,9},{9,1},{2,10},{10,2},{3,11},{11,3},{4,12},{12,4},... | collective-permute-start | bytes 786440 | tf_op jit(solution)/shard_map/ppermute | solution.py:270
  (10 other events, 32.7 us)

commit v8 on v7

--- a/solution.py
+++ b/solution.py
@@ -134,42 +134,38 @@
         compiler_params=pltpu.CompilerParams(vmem_limit_bytes=16 << 20),
         cost_estimate=cost(8 * NC * mb * toks * rows * cols, *outs, *diffs, got),
         name="dw_terms",
-    )(at, *map(in_hbm, (act, got, *diffs)))
+    )(at, in_hbm(act), got, *map(in_hbm, diffs))
 
 
 def dx_body(at, *refs):
     diffs, pieces, outs = refs[:4], refs[4:8], refs[8:12]
-    lhs, rhs, narrow, wide, sems = refs[12:]
+    held, lhs, rhs, narrow, wide, sems = refs[12:]
     mb, toks, cols = diffs[0].shape
     part = toks // 2
     rows = pieces[0].shape[0]
-    loads = []
-    for j, diff in enumerate(diffs):
+    loads = [(diff, held.at[j]) for j, diff in enumerate(diffs)]
+    loads += [(piece, rhs.at[p]) for p, piece in enumerate(pieces)]
+    loads = start_all(loads, sems)
+    for j in range(4):
+        loads[j].wait()
         for h in range(2):
             k = at[j % 2 * 2 + h]
             for m in range(mb):
-                src = diff.at[m, h * part : (h + 1) * part]
-                loads.append((src, lhs.at[k, j // 2, m]))
-    first = len(loads)
-    loads += [(piece, rhs.at[p]) for p, piece in enumerate(pieces)]
-    loads = start_all(loads, sems)
-    wait_all(loads[:first])
+                lhs[k, j // 2, m] = held[j, m, h * part : (h + 1) * part]
+    wait_all(loads[4:])
     each = NC * mb * part
-    left = lhs[...].reshape(4 * each, cols)
     stores = []
-    for p in range(NX):
-        loads[first + p].wait()
-        got = lax.dot_general(
-            left, rhs[p], (((1,), (1,)), ((), ())), preferred_element_type=F32
-        )
-        pairs = []
-        for k, out in enumerate(outs):
-            held = narrow if k < 2 else wide
-            at_p = slice(p * rows, (p + 1) * rows)
-            term = got[k * each : (k + 1) * each]
-            held[k % 2, :, at_p] = term.astype(held.dtype)
-            pairs.append((held.at[k % 2, :, at_p], out.at[:, at_p]))
-        stores += start_all(pairs, sems, len(loads) + 4 * p)
+    for g, terms in enumerate((narrow, wide)):
+        left = lhs[2 * g : 2 * g + 2].reshape(2 * each, cols)
+        for p in range(NX):
+            got = lax.dot_general(
+                left, rhs[p], (((1,), (1,)), ((), ())), preferred_element_type=F32
+            )
+            for k in range(2):
+                term = got[k * each : (k + 1) * each]
+                terms[k, :, p * rows : (p + 1) * rows] = term.astype(terms.dtype)
+        pairs = [(terms.at[k], outs[2 * g + k]) for k in range(2)]
+        stores += start_all(pairs, sems, len(loads) + 2 * g)
     wait_all(stores)
 
 
@@ -184,11 +180,12 @@
         in_specs=[SMEM, *([HBM] * (4 + NX))],
         out_specs=[HBM] * 4,
         scratch_shapes=[
+            pltpu.VMEM((4, mb, toks, cols), BF16),
             pltpu.VMEM((4, NC, mb, part, cols), BF16),
             pltpu.VMEM((NX, rows, cols), BF16),
             pltpu.VMEM((2, NC * mb * part, NX * rows), BF16),
             pltpu.VMEM((2, NC * mb * part, NX * rows), F32),
-            pltpu.SemaphoreType.DMA((8 * mb + 5 * NX,)),
+            pltpu.SemaphoreType.DMA((12,)),
         ],
         compiler_params=pltpu.CompilerParams(vmem_limit_bytes=16 << 20),
         cost_estimate=cost(8 * math.prod(outs[0].shape) * cols, *outs, *diffs, *pieces),
@@ -290,11 +287,12 @@
     diff_z = lax.ppermute(diff, "inc", SWAP)
     diff_c = swap_core(diff)
     near_o = neighbours(after(own, diff))
-    far_o = step_x(pick(*near_o))
+    forward_o = pick(*near_o)
+    far_o = step_x(forward_o)
     w_z = swap_zh(after(own, diff_z))
-    diff_z = after(diff_z, diff_c, *near_o)
+    diff_z = after(diff_z, diff_c, forward_o)
     diffs = (diff, diff_z, diff_c, swap_core(diff_z))
-    act_got = swap_core(other_columns(after(activations, diff_z), c))
+    act_got = swap_core(other_columns(after(activations, diff_z, far_o), c))
 
     def later(*others):
         return (after(diff, *others), *diffs[1:])
@@ -305,21 +303,27 @@
             total = total + t.astype(F32)
         return total
 
-    def ring(step, terms, *first):
-        far, back, ahead, here = terms
+    def nearer(step, terms, *first):
+        far, back, ahead, _ = terms
         far, back = lax.optimization_barrier((step(far), step(back, -1), *first))[:2]
-        return add(here, back, step(add(ahead, far).astype(BF16)))
+        return add(ahead, far).astype(BF16), back
 
     terms_o = dx_terms(at_y, diffs, (own, *near_o, far_o))
     near_p = neighbours(after(w_z, terms_o[0]))
     sums_p = dw_terms(at_p, activations, act_got, later(*terms_o))
+    next_dx_o, back_dx_o = nearer(step_y, terms_o, sums_p[0])
     forward_p = pick(after(near_p[0], sums_p[0]), near_p[1])
-    sums_o = dw_terms(at_o, activations, act_got, later(forward_p))
-    terms_p = dx_terms(at_y, later(*sums_o), (w_z, *near_p, step_x(forward_p)))
-    dx_o = ring(step_y, terms_o, sums_p[0]).astype(BF16)
-    cross = swap_zh(ring(step_x, sums_p).astype(BF16))
-    weight_grad = ring(step_x, sums_o) + cross.astype(F32)
-    dx_p = ring(step_y, terms_p).astype(BF16)
+    sums_o = dw_terms(at_o, activations, act_got, later(forward_p, next_dx_o))
+    next_p, back_p = nearer(step_x, sums_p, sums_o[0])
+    far_p = step_x(forward_p)
+    terms_p = dx_terms(at_y, later(*sums_o, next_p), (w_z, *near_p, far_p))
+    dx_o = add(terms_o[3], back_dx_o, step_y(next_dx_o)).astype(BF16)
+    whole_p = add(sums_p[3], back_p, step_x(next_p)).astype(BF16)
+    next_o, back_o = nearer(step_x, sums_o, terms_p[0], whole_p)
+    cross = swap_zh(whole_p)
+    next_dx_p, back_dx_p = nearer(step_y, terms_p)
+    dx_p = add(terms_p[3], back_dx_p, step_y(next_dx_p)).astype(BF16)
+    weight_grad = add(sums_o[3], back_o, step_x(next_o), cross)
 
     half = dx_o.shape[0] // 2
     got_o, got_p = swap_core(dx_o[half:]), swap_core(dx_p[half:])

time: 124 us -> 131 us (1.056)
  waiting for transfers between devices: 44.9 us -> 61.7 us
  Pallas kernels: 33.8 us -> 29.6 us
  other arithmetic: 7.13 us -> 4.23 us
  starting transfers between devices: 32.6 us -> 30.7 us
  local copies, waits for them, and re-layouts: 4.03 us -> 2.7 us
    ppermute x6, waiting for transfers between devices: 10.7 us -> 18.7 us  [step_y(): return lax.ppermute(value, ('core', 'outc'), by_core(NY, way, True))]
    ppermute x8, waiting for transfers between devices: 11.6 us -> 17.5 us  [step_x(): return lax.ppermute(value, ('x', 'core'), by_core(NX, way, False))]
    pallas_call x2, Pallas kernels: 17 us -> 12.9 us  [dx_terms(): pl.pallas_call(dx_body, out_shape=outs, in_specs=[SMEM, *[HBM] * (4 + NX)...]
    ppermute x2, waiting for transfers between devices: 7.41 us -> 10.2 us  [swap_zh(): return lax.ppermute(value, 'zh', SWAP)]
    ppermute x2, waiting for transfers between devices: 11.8 us -> 9.58 us  [neighbours(): lax.ppermute(piece, 'x', by_x(-1))]
    ppermute x5, starting transfers between devices: 2.59 us -> 0.67 us  [swap_core(): return lax.ppermute(value, 'core', SWAP)]
    convert_element_type x7, other arithmetic: 3.14 us -> 1.29 us  [the longest x4 0.56 us: nearer(): return (add(ahead, far).astype(BF16), back)]
    ppermute x2, waiting for transfers between devices: 3.37 us -> 5.04 us  [neighbours(): lax.ppermute(piece, 'x', by_x(1))]
  transfers between devices with their start and end apart: 26 -> 26, of which waited for: 10 -> 13; matrix products, arithmetic and copies ran while one was open for 5% -> 2% of each run, Pallas kernels for 24% -> 20%
where the time goes in v8:
time: 131 us; the launch traced here: 130 us
  waiting for transfers between devices  61.7 us (47%)
  starting transfers between devices  30.7 us (23%)
  Pallas kernels  29.6 us (23%)
  other arithmetic  4.23 us (3%)
  local copies, waits for them, and re-layouts  2.7 us (2%)
    ppermute x6, waiting for transfers between devices, step_y(): return lax.ppermute(value, ('core', 'outc'), by_core(NY, way, True))  18.7 us
    ppermute x8, waiting for transfers between devices, step_x(): return lax.ppermute(value, ('x', 'core'), by_core(NX, way, False))  17.5 us
    pallas_call x2, Pallas kernels, dx_terms(): pl.pallas_call(dx_body, out_shape=outs, in_specs=[SMEM, *[HBM] * (4 + NX)...  12.9 us
    pallas_call x2, Pallas kernels, dw_terms(): pl.pallas_call(dw_body, out_shape=outs, in_specs=[SMEM, *[HBM] * 6], out_...  12.5 us
    ppermute x2, waiting for transfers between devices, swap_zh(): return lax.ppermute(value, 'zh', SWAP)  10.2 us
    ppermute x2, waiting for transfers between devices, neighbours(): lax.ppermute(piece, 'x', by_x(-1))  9.58 us
    ppermute x6, starting transfers between devices, step_y(): return lax.ppermute(value, ('core', 'outc'), by_core(NY, way, True))  7.8 us
    ppermute x2, starting transfers between devices, swap_zh(): return lax.ppermute(value, 'zh', SWAP)  7.8 us
  transfers between devices with their start and end apart: 26, of which 13 were waited for; matrix products, arithmetic and copies ran while one was open for 2% of the time, Pallas kernels for 20%

profile of v8, /device:TPU:0, one launch (start us, length us, event | category | flops | bytes accessed | tf_op | source)
XLA Modules:
  0.0 129.9 jit_solution(2367878522911504172)
XLA Ops:
  0.6 1.4 %subtract_convert_fusion.refs_0_ = bf16[2,128,1024]{2,1,0:T(8,128)(2,1)S(1)} fusion(bf16[2,128,1024]{2,1,0:T(8,128)(2,1)} %param.6, bf16[2,128,1024]{2,1,0:T(8,128)(2,1)} %param.5), kind=kLoop, calls=%fused_computation.8 | loop fusion | flops 1048576 | bytes 1572864 | tf_op jit(solution)/shard_map/convert_element_type | solution.py:286
  2.0 2.9 %collective-permute-start.3 = (bf16[256,1024]{1,0:T(8,128)(2,1)}, bf16[256,1024]{1,0:T(8,128)(2,1)S(1)}, u32[]{:S(2)}, u32[]{:S(2)}) collective-permute-start(bf16[256,1024]{1,0:T(8,128)(2,1)} %bitcast.7.refs_4_), channel_id=1, source_target_pairs={{0,96},{32,0},{64,32},{96,64},{1,97},{33,1},{65,33},{97,65},{2,98}... | collective-permute-start | bytes 1572872 | tf_op jit(solution)/shard_map/ppermute | solution.py:270
  5.0 1.9 %collective-permute-start = (bf16[2,128,1024]{2,1,0:T(8,128)(2,1)S(1)}, bf16[2,128,1024]{2,1,0:T(8,128)(2,1)}, u32[]{:S(2)}, u32[]{:S(2)}) collective-permute-start(bf16[2,128,1024]{2,1,0:T(8,128)(2,1)S(1)} %subtract_convert_fusion.refs_0_), channel_id=1, source_target_pairs={{0,4},{4,0},{1,5},{5,1},{2,6},{6,2},{3,7},{7,3},{8,12},{12,8},{9,1... | collective-permute-start | bytes 1572872 | tf_op jit(solution)/shard_map/ppermute | solution.py:287
  6.9 9.6 %collective-permute-done.3.refs_6_ = bf16[256,1024]{1,0:T(8,128)(2,1)S(1)} collective-permute-done((bf16[256,1024]{1,0:T(8,128)(2,1)}, bf16[256,1024]{1,0:T(8,128)(2,1)S(1)}, u32[]{:S(2)}, u32[]{:S(2)}) %collective-permute-start.3) | collective-permute-done | bytes 524320 | tf_op jit(solution)/shard_map/ppermute | solution.py:270
  16.4 3.3 %collective-permute-done.2.refs_5_ = bf16[256,1024]{1,0:T(8,128)(2,1)S(1)} collective-permute-done((bf16[256,1024]{1,0:T(8,128)(2,1)}, bf16[256,1024]{1,0:T(8,128)(2,1)S(1)}, u32[]{:S(2)}, u32[]{:S(2)}) %collective-permute-start.2) | collective-permute-done | bytes 524320 | tf_op jit(solution)/shard_map/ppermute | solution.py:270
  19.9 10.3 %collective-permute-done.5.refs_7_ = bf16[256,1024]{1,0:T(8,128)(2,1)S(1)} collective-permute-done((bf16[256,1024]{1,0:T(8,128)(2,1)S(1)}, bf16[256,1024]{1,0:T(8,128)(2,1)S(1)}, u32[]{:S(2)}, u32[]{:S(2)}) %collective-permute-start.5) | collective-permute-done | bytes 524320 | tf_op jit(solution)/shard_map/ppermute | solution.py:258
  31.1 2.4 %other_columns.1 = bf16[8,2,256,256]{3,2,1,0:T(8,128)(2,1)} custom-call(s32[1]{0:T(128)} %bitcast.2.core, bf16[2,256,4096]{2,1,0:T(8,128)(2,1)} %act.3), custom_call_target="tpu_custom_call" | custom-call | bytes 6291456 | tf_op jit(solution)/shard_map/other_columns/pallas_call | solution.py:61
  34.1 3.9 %collective-permute-start.11 = (bf16[256,1024]{1,0:T(8,128)(2,1)}, bf16[256,1024]{1,0:T(8,128)(2,1)}, u32[]{:S(2)}, u32[]{:S(2)}) collective-permute-start(bf16[256,1024]{1,0:T(8,128)(2,1)} %bitcast.7.refs_4_), channel_id=1, source_target_pairs={{0,16},{16,0},{1,17},{17,1},{2,18},{18,2},{3,19},{19,3},{4,20},{20... | collective-permute-start | bytes 1572872 | tf_op jit(solution)/shard_map/ppermute | solution.py:264
  39.5 6.5 %dx_terms.2 = (bf16[256,1024]{1,0:T(8,128)(2,1)}, bf16[256,1024]{1,0:T(8,128)(2,1)}, f32[256,1024]{1,0:T(8,128)}, f32[256,1024]{1,0:T(8,128)}) custom-call(s32[4]{0:T(128)S(1)} %pad_add_fusion.1.at, bf16[2,128,1024]{2,1,0:T(8,128)(2,1)} %copy-done, bf16[2,128,1024]{2,1,0:T(8,128)(2,1)} %collective-permute-done.refs_1_, bf16[2,128,1024]{2,1,0:T(8,128)(2,1)} %copy-done.1, ...), custom_call_target="tpu_custom_call" | custom-call | flops 2147483648 | bytes 7340032 | tf_op jit(solution)/shard_map/dx_terms/pallas_call | solution.py:177
  46.0 4.5 %collective-permute-done.11.refs_4_ = bf16[256,1024]{1,0:T(8,128)(2,1)} collective-permute-done((bf16[256,1024]{1,0:T(8,128)(2,1)}, bf16[256,1024]{1,0:T(8,128)(2,1)}, u32[]{:S(2)}, u32[]{:S(2)}) %collective-permute-start.11) | collective-permute-done | bytes 524320 | tf_op jit(solution)/shard_map/ppermute | solution.py:264
  50.5 3.2 %collective-permute-start.13 = (bf16[256,1024]{1,0:T(8,128)(2,1)}, bf16[256,1024]{1,0:T(8,128)(2,1)S(1)}, u32[]{:S(2)}, u32[]{:S(2)}) collective-permute-start(bf16[256,1024]{1,0:T(8,128)(2,1)} %collective-permute-done.11.refs_4_), channel_id=1, source_target_pairs={{0,96},{32,0},{64,32},{96,64},{1,97},{33,1},{65,33},{97,65},{2,98}... | collective-permute-start | bytes 1572872 | tf_op jit(solution)/shard_map/ppermute | solution.py:270
  53.9 1.6 %collective-permute-start.6 = (bf16[256,1024]{1,0:T(8,128)(2,1)}, bf16[256,1024]{1,0:T(8,128)(2,1)S(1)}, u32[]{:S(2)}, u32[]{:S(2)}) collective-permute-start(bf16[256,1024]{1,0:T(8,128)(2,1)} %get-tuple-element.38), channel_id=1, source_target_pairs={{0,1},{8,11},{1,2},{9,8},{2,3},{10,9},{3,0},{11,10},{4,5},{12,15},... | collective-permute-start | bytes 1572872 | tf_op jit(solution)/shard_map/ppermute | solution.py:261
  55.5 1.7 %collective-permute-start.7 = (bf16[256,1024]{1,0:T(8,128)(2,1)}, bf16[256,1024]{1,0:T(8,128)(2,1)S(1)}, u32[]{:S(2)}, u32[]{:S(2)}) collective-permute-start(bf16[256,1024]{1,0:T(8,128)(2,1)} %get-tuple-element.39), channel_id=1, source_target_pairs={{0,3},{8,9},{1,0},{9,10},{2,1},{10,11},{3,2},{11,8},{4,7},{12,13},... | collective-permute-start | bytes 1572872 | tf_op jit(solution)/shard_map/ppermute | solution.py:261
  57.2 6.3 %dw_terms.2 = (bf16[256,1024]{1,0:T(8,128)(2,1)}, bf16[256,1024]{1,0:T(8,128)(2,1)}, f32[256,1024]{1,0:T(8,128)}, f32[256,1024]{1,0:T(8,128)}) custom-call(s32[6]{0:T(128)S(1)} %stack.77.at, bf16[2,256,4096]{2,1,0:T(8,128)(2,1)} %act.3, bf16[8,2,256,256]{3,2,1,0:T(8,128)(2,1)S(1)} %collective-permute-done.8.got, bf16[2,128,1024]{2,1,0:T(8,128)(2,1)} %copy-done, ...), custom_call_target="tpu_custom_call" | custom-call | flops 2147483648 | bytes 7340032 | tf_op jit(solution)/shard_map/dw_terms/pallas_call | solution.py:122
  63.6 1.7 %collective-permute-done.12.refs_5_ = bf16[256,1024]{1,0:T(8,128)(2,1)S(1)} collective-permute-done((bf16[256,1024]{1,0:T(8,128)(2,1)}, bf16[256,1024]{1,0:T(8,128)(2,1)S(1)}, u32[]{:S(2)}, u32[]{:S(2)}) %collective-permute-start.12) | collective-permute-done | bytes 524320 | tf_op jit(solution)/shard_map/ppermute | solution.py:270
  65.3 1.5 %collective-permute-start.15 = (bf16[256,1024]{1,0:T(8,128)(2,1)}, bf16[256,1024]{1,0:T(8,128)(2,1)S(1)}, u32[]{:S(2)}, u32[]{:S(2)}) collective-permute-start(bf16[256,1024]{1,0:T(8,128)(2,1)} %get-tuple-element.55), channel_id=1, source_target_pairs={{0,96},{8,40},{32,0},{40,72},{64,32},{72,104},{96,64},{104,8},{1,9... | collective-permute-start | bytes 1572872 | tf_op jit(solution)/shard_map/ppermute | solution.py:258
  67.6 1.8 %collective-permute-done.6 = bf16[256,1024]{1,0:T(8,128)(2,1)S(1)} collective-permute-done((bf16[256,1024]{1,0:T(8,128)(2,1)}, bf16[256,1024]{1,0:T(8,128)(2,1)S(1)}, u32[]{:S(2)}, u32[]{:S(2)}) %collective-permute-start.6) | collective-permute-done | bytes 524320 | tf_op jit(solution)/shard_map/ppermute | solution.py:261
  69.5 0.9 collective-permute-start.9
  70.4 6.3 %dw_terms.3 = (bf16[256,1024]{1,0:T(8,128)(2,1)}, bf16[256,1024]{1,0:T(8,128)(2,1)}, f32[256,1024]{1,0:T(8,128)}, f32[256,1024]{1,0:T(8,128)}) custom-call(s32[6]{0:T(128)S(1)} %stack.82.at, bf16[2,256,4096]{2,1,0:T(8,128)(2,1)} %act.3, bf16[8,2,256,256]{3,2,1,0:T(8,128)(2,1)S(1)} %collective-permute-done.8.got, bf16[2,128,1024]{2,1,0:T(8,128)(2,1)} %copy-done, ...), custom_call_target="tpu_custom_call" | custom-call | flops 2147483648 | bytes 7340032 | tf_op jit(solution)/shard_map/dw_terms/pallas_call | solution.py:122
  76.7 3.3 %collective-permute-start.22 = (bf16[256,1024]{1,0:T(8,128)(2,1)}, bf16[256,1024]{1,0:T(8,128)(2,1)S(1)}, u32[]{:S(2)}, u32[]{:S(2)}) collective-permute-start(bf16[256,1024]{1,0:T(8,128)(2,1)} %get-tuple-element.51), channel_id=1, source_target_pairs={{0,96},{8,40},{32,0},{40,72},{64,32},{72,104},{96,64},{104,8},{1,9... | collective-permute-start | bytes 1572872 | tf_op jit(solution)/shard_map/ppermute | solution.py:258
  80.2 1.4 %collective-permute-start.23 = (bf16[256,1024]{1,0:T(8,128)(2,1)S(1)}, bf16[256,1024]{1,0:T(8,128)(2,1)S(1)}, u32[]{:S(2)}, u32[]{:S(2)}) collective-permute-start(bf16[256,1024]{1,0:T(8,128)(2,1)S(1)} %add_convert_fusion.4), channel_id=1, source_target_pairs={{0,32},{8,104},{32,64},{40,8},{64,96},{72,40},{96,0},{104,72},{1,3... | collective-permute-start | bytes 1572872 | tf_op jit(solution)/shard_map/ppermute | solution.py:258
  81.5 7.1 %collective-permute-done.16.refs_7_ = bf16[256,1024]{1,0:T(8,128)(2,1)S(1)} collective-permute-done((bf16[256,1024]{1,0:T(8,128)(2,1)S(1)}, bf16[256,1024]{1,0:T(8,128)(2,1)S(1)}, u32[]{:S(2)}, u32[]{:S(2)}) %collective-permute-start.16) | collective-permute-done | bytes 524320 | tf_op jit(solution)/shard_map/ppermute | solution.py:258
  88.7 0.8 copy-done.16
  89.5 6.5 %dx_terms.3 = (bf16[256,1024]{1,0:T(8,128)(2,1)}, bf16[256,1024]{1,0:T(8,128)(2,1)}, f32[256,1024]{1,0:T(8,128)}, f32[256,1024]{1,0:T(8,128)}) custom-call(s32[4]{0:T(128)S(1)} %pad_add_fusion.1.at, bf16[2,128,1024]{2,1,0:T(8,128)(2,1)} %copy-done, bf16[2,128,1024]{2,1,0:T(8,128)(2,1)} %collective-permute-done.refs_1_, bf16[2,128,1024]{2,1,0:T(8,128)(2,1)} %copy-done.1, ...), custom_call_target="tpu_custom_call" | custom-call | flops 2147483648 | bytes 7340032 | tf_op jit(solution)/shard_map/dx_terms/pallas_call | solution.py:177
  96.0 3.6 %collective-permute-start.18 = (bf16[256,1024]{1,0:T(8,128)(2,1)}, bf16[256,1024]{1,0:T(8,128)(2,1)S(1)}, u32[]{:S(2)}, u32[]{:S(2)}) collective-permute-start(bf16[256,1024]{1,0:T(8,128)(2,1)} %get-tuple-element.60), channel_id=1, source_target_pairs={{0,3},{8,9},{1,0},{9,10},{2,1},{10,11},{3,2},{11,8},{4,7},{12,13},... | collective-permute-start | bytes 1572872 | tf_op jit(solution)/shard_map/ppermute | solution.py:261
  99.9 6.7 %collective-permute-done.18 = bf16[256,1024]{1,0:T(8,128)(2,1)S(1)} collective-permute-done((bf16[256,1024]{1,0:T(8,128)(2,1)}, bf16[256,1024]{1,0:T(8,128)(2,1)S(1)}, u32[]{:S(2)}, u32[]{:S(2)}) %collective-permute-start.18) | collective-permute-done | bytes 524320 | tf_op jit(solution)/shard_map/ppermute | solution.py:261
  106.6 3.6 %collective-permute-done.17 = bf16[256,1024]{1,0:T(8,128)(2,1)S(1)} collective-permute-done((bf16[256,1024]{1,0:T(8,128)(2,1)}, bf16[256,1024]{1,0:T(8,128)(2,1)S(1)}, u32[]{:S(2)}, u32[]{:S(2)}) %collective-permute-start.17) | collective-permute-done | bytes 524320 | tf_op jit(solution)/shard_map/ppermute | solution.py:261
  110.7 3.9 %collective-permute-start.25 = (bf16[256,1024]{1,0:T(8,128)(2,1)S(1)}, bf16[256,1024]{1,0:T(8,128)(2,1)S(1)}, u32[]{:S(2)}, u32[]{:S(2)}) collective-permute-start(bf16[256,1024]{1,0:T(8,128)(2,1)S(1)} %add_convert_fusion.1), channel_id=1, source_target_pairs={{0,16},{16,0},{1,17},{17,1},{2,18},{18,2},{3,19},{19,3},{4,20},{20... | collective-permute-start | bytes 1572872 | tf_op jit(solution)/shard_map/ppermute | solution.py:264
  114.9 5.9 %collective-permute-done.19 = bf16[256,1024]{1,0:T(8,128)(2,1)S(1)} collective-permute-done((bf16[256,1024]{1,0:T(8,128)(2,1)S(1)}, bf16[256,1024]{1,0:T(8,128)(2,1)S(1)}, u32[]{:S(2)}, u32[]{:S(2)}) %collective-permute-start.19) | collective-permute-done | bytes 524320 | tf_op jit(solution)/shard_map/ppermute | solution.py:261
  121.2 5.7 %collective-permute-done.25 = bf16[256,1024]{1,0:T(8,128)(2,1)S(1)} collective-permute-done((bf16[256,1024]{1,0:T(8,128)(2,1)S(1)}, bf16[256,1024]{1,0:T(8,128)(2,1)S(1)}, u32[]{:S(2)}, u32[]{:S(2)}) %collective-permute-start.25) | collective-permute-done | bytes 524320 | tf_op jit(solution)/shard_map/ppermute | solution.py:264
  126.9 1.3 add_bitcast_fusion
  128.2 1.7 %place.1 = bf16[2,64,4096]{2,1,0:T(8,128)(2,1)} custom-call(s32[3]{0:T(128)S(1)} %pad_add_fusion.at, bf16[128,1024]{1,0:T(8,128)(2,1)S(1)} %get-tuple-element.71.keep_o, bf16[128,1024]{1,0:T(8,128)(2,1)S(1)} %collective-permute-done.10.got_o, bf16[128,1024]{1,0:T(8,128)(2,1)S(1)} %get-tuple-element.69.keep_p, bf16[128,1024]{1,0:T(8,128)(2,1)S(1)} %collective-permute-done.20.got_p), custom_call_target="tpu_custom_call" | custom-call | bytes 2097152 | tf_op jit(solution)/shard_map/place/pallas_call | solution.py:219
  (77 shorter events, 5.8 us)
Async XLA Ops:
  2.0 31.5 %copy-start = (bf16[2,128,1024]{2,1,0:T(8,128)(2,1)}, bf16[2,128,1024]{2,1,0:T(8,128)(2,1)S(1)}, u32[]{:S(2)}) copy-start(bf16[2,128,1024]{2,1,0:T(8,128)(2,1)S(1)} %subtract_convert_fusion.refs_0_) | copy-start | bytes 1572868
  2.0 14.4 %collective-permute-start.3 = (bf16[256,1024]{1,0:T(8,128)(2,1)}, bf16[256,1024]{1,0:T(8,128)(2,1)S(1)}, u32[]{:S(2)}, u32[]{:S(2)}) collective-permute-start(bf16[256,1024]{1,0:T(8,128)(2,1)} %bitcast.7.refs_4_), channel_id=1, source_target_pairs={{0,96},{32,0},{64,32},{96,64},{1,97},{33,1},{65,33},{97,65},{2,98}... | collective-permute-start | bytes 1572872 | tf_op jit(solution)/shard_map/ppermute | solution.py:270
  4.9 14.8 %collective-permute-start.2 = (bf16[256,1024]{1,0:T(8,128)(2,1)}, bf16[256,1024]{1,0:T(8,128)(2,1)S(1)}, u32[]{:S(2)}, u32[]{:S(2)}) collective-permute-start(bf16[256,1024]{1,0:T(8,128)(2,1)} %bitcast.7.refs_4_), channel_id=1, source_target_pairs={{0,32},{32,64},{64,96},{96,0},{1,33},{33,65},{65,97},{97,1},{2,34}... | collective-permute-start | bytes 1572872 | tf_op jit(solution)/shard_map/ppermute | solution.py:270
  5.0 14.9 %collective-permute-start.1 = (bf16[2,128,1024]{2,1,0:T(8,128)(2,1)S(1)}, bf16[2,128,1024]{2,1,0:T(8,128)(2,1)S(1)}, u32[]{:S(2)}, u32[]{:S(2)}) collective-permute-start(bf16[2,128,1024]{2,1,0:T(8,128)(2,1)S(1)} %subtract_convert_fusion.refs_0_), channel_id=1, source_target_pairs={{0,8},{8,0},{1,9},{9,1},{2,10},{10,2},{3,11},{11,3},{4,12},{12,4},... | collective-permute-start | bytes 1572872 | tf_op jit(solution)/shard_map/ppermute | solution.py:267
  5.0 15.0 %collective-permute-start = (bf16[2,128,1024]{2,1,0:T(8,128)(2,1)S(1)}, bf16[2,128,1024]{2,1,0:T(8,128)(2,1)}, u32[]{:S(2)}, u32[]{:S(2)}) collective-permute-start(bf16[2,128,1024]{2,1,0:T(8,128)(2,1)S(1)} %subtract_convert_fusion.refs_0_), channel_id=1, source_target_pairs={{0,4},{4,0},{1,5},{5,1},{2,6},{6,2},{3,7},{7,3},{8,12},{12,8},{9,1... | collective-permute-start | bytes 1572872 | tf_op jit(solution)/shard_map/ppermute | solution.py:287
  19.8 10.5 %collective-permute-start.5 = (bf16[256,1024]{1,0:T(8,128)(2,1)S(1)}, bf16[256,1024]{1,0:T(8,128)(2,1)S(1)}, u32[]{:S(2)}, u32[]{:S(2)}) collective-permute-start(bf16[256,1024]{1,0:T(8,128)(2,1)S(1)} %broadcast_select_fusion.1), channel_id=1, source_target_pairs={{0,32},{8,104},{32,64},{40,8},{64,96},{72,40},{96,0},{104,72},{1,3... | collective-permute-start | bytes 1572872 | tf_op jit(solution)/shard_map/ppermute | solution.py:258
  19.9 13.6 %copy-start.1 = (bf16[2,128,1024]{2,1,0:T(8,128)(2,1)}, bf16[2,128,1024]{2,1,0:T(8,128)(2,1)S(1)}, u32[]{:S(2)}) copy-start(bf16[2,128,1024]{2,1,0:T(8,128)(2,1)S(1)} %collective-permute-done.1.refs_2_) | copy-start | bytes 1572868
  33.5 23.7 %collective-permute-start.8 = (bf16[8,2,256,256]{3,2,1,0:T(8,128)(2,1)}, bf16[8,2,256,256]{3,2,1,0:T(8,128)(2,1)S(1)}, u32[]{:S(2)}, u32[]{:S(2)}) collective-permute-start(bf16[8,2,256,256]{3,2,1,0:T(8,128)(2,1)} %other_columns.1), channel_id=1, source_target_pairs={{0,8},{8,0},{1,9},{9,1},{2,10},{10,2},{3,11},{11,3},{4,12},{12,4},... | collective-permute-start | bytes 6291464 | tf_op jit(solution)/shard_map/ppermute | solution.py:267
  33.6 5.1 %collective-permute-start.4 = (bf16[2,128,1024]{2,1,0:T(8,128)(2,1)}, bf16[2,128,1024]{2,1,0:T(8,128)(2,1)S(1)}, u32[]{:S(2)}, u32[]{:S(2)}) collective-permute-start(bf16[2,128,1024]{2,1,0:T(8,128)(2,1)} %collective-permute-done.refs_1_), channel_id=1, source_target_pairs={{0,8},{8,0},{1,9},{9,1},{2,10},{10,2},{3,11},{11,3},{4,12},{12,4},... | collective-permute-start | bytes 1572872 | tf_op jit(solution)/shard_map/ppermute | solution.py:267
  34.1 16.4 %collective-permute-start.11 = (bf16[256,1024]{1,0:T(8,128)(2,1)}, bf16[256,1024]{1,0:T(8,128)(2,1)}, u32[]{:S(2)}, u32[]{:S(2)}) collective-permute-start(bf16[256,1024]{1,0:T(8,128)(2,1)} %bitcast.7.refs_4_), channel_id=1, source_target_pairs={{0,16},{16,0},{1,17},{17,1},{2,18},{18,2},{3,19},{19,3},{4,20},{20... | collective-permute-start | bytes 1572872 | tf_op jit(solution)/shard_map/ppermute | solution.py:264
  50.5 14.8 %collective-permute-start.12 = (bf16[256,1024]{1,0:T(8,128)(2,1)}, bf16[256,1024]{1,0:T(8,128)(2,1)S(1)}, u32[]{:S(2)}, u32[]{:S(2)}) collective-permute-start(bf16[256,1024]{1,0:T(8,128)(2,1)} %collective-permute-done.11.refs_4_), channel_id=1, source_target_pairs={{0,32},{32,64},{64,96},{96,0},{1,33},{33,65},{65,97},{97,1},{2,34}... | collective-permute-start | bytes 1572872 | tf_op jit(solution)/shard_map/ppermute | solution.py:270
  50.5 16.3 %collective-permute-start.13 = (bf16[256,1024]{1,0:T(8,128)(2,1)}, bf16[256,1024]{1,0:T(8,128)(2,1)S(1)}, u32[]{:S(2)}, u32[]{:S(2)}) collective-permute-start(bf16[256,1024]{1,0:T(8,128)(2,1)} %collective-permute-done.11.refs_4_), channel_id=1, source_target_pairs={{0,96},{32,0},{64,32},{96,64},{1,97},{33,1},{65,33},{97,65},{2,98}... | collective-permute-start | bytes 1572872 | tf_op jit(solution)/shard_map/ppermute | solution.py:270
  53.9 15.5 %collective-permute-start.6 = (bf16[256,1024]{1,0:T(8,128)(2,1)}, bf16[256,1024]{1,0:T(8,128)(2,1)S(1)}, u32[]{:S(2)}, u32[]{:S(2)}) collective-permute-start(bf16[256,1024]{1,0:T(8,128)(2,1)} %get-tuple-element.38), channel_id=1, source_target_pairs={{0,1},{8,11},{1,2},{9,8},{2,3},{10,9},{3,0},{11,10},{4,5},{12,15},... | collective-permute-start | bytes 1572872 | tf_op jit(solution)/shard_map/ppermute | solution.py:261
  55.5 12.1 %collective-permute-start.7 = (bf16[256,1024]{1,0:T(8,128)(2,1)}, bf16[256,1024]{1,0:T(8,128)(2,1)S(1)}, u32[]{:S(2)}, u32[]{:S(2)}) collective-permute-start(bf16[256,1024]{1,0:T(8,128)(2,1)} %get-tuple-element.39), channel_id=1, source_target_pairs={{0,3},{8,9},{1,0},{9,10},{2,1},{10,11},{3,2},{11,8},{4,7},{12,13},... | collective-permute-start | bytes 1572872 | tf_op jit(solution)/shard_map/ppermute | solution.py:261
  63.5 16.5 %collective-permute-start.14 = (bf16[256,1024]{1,0:T(8,128)(2,1)}, bf16[256,1024]{1,0:T(8,128)(2,1)S(1)}, u32[]{:S(2)}, u32[]{:S(2)}) collective-permute-start(bf16[256,1024]{1,0:T(8,128)(2,1)} %get-tuple-element.43), channel_id=1, source_target_pairs={{0,32},{8,104},{32,64},{40,8},{64,96},{72,40},{96,0},{104,72},{1,3... | collective-permute-start | bytes 1572872 | tf_op jit(solution)/shard_map/ppermute | solution.py:258
  65.3 11.3 %copy-start.11 = (bf16[256,1024]{1,0:T(8,128)(2,1)}, bf16[256,1024]{1,0:T(8,128)(2,1)S(1)}, u32[]{:S(2)}) copy-start(bf16[256,1024]{1,0:T(8,128)(2,1)S(1)} %collective-permute-done.12.refs_5_) | copy-start | bytes 1572868
  65.3 14.7 %collective-permute-start.15 = (bf16[256,1024]{1,0:T(8,128)(2,1)}, bf16[256,1024]{1,0:T(8,128)(2,1)S(1)}, u32[]{:S(2)}, u32[]{:S(2)}) collective-permute-start(bf16[256,1024]{1,0:T(8,128)(2,1)} %get-tuple-element.55), channel_id=1, source_target_pairs={{0,96},{8,40},{32,0},{40,72},{64,32},{72,104},{96,64},{104,8},{1,9... | collective-permute-start | bytes 1572872 | tf_op jit(solution)/shard_map/ppermute | solution.py:258
  69.4 19.3 %collective-permute-start.16 = (bf16[256,1024]{1,0:T(8,128)(2,1)S(1)}, bf16[256,1024]{1,0:T(8,128)(2,1)S(1)}, u32[]{:S(2)}, u32[]{:S(2)}) collective-permute-start(bf16[256,1024]{1,0:T(8,128)(2,1)S(1)} %broadcast_select_fusion), channel_id=1, source_target_pairs={{0,32},{8,104},{32,64},{40,8},{64,96},{72,40},{96,0},{104,72},{1,3... | collective-permute-start | bytes 1572872 | tf_op jit(solution)/shard_map/ppermute | solution.py:258
  69.5 30.1 %collective-permute-start.9 = (bf16[256,1024]{1,0:T(8,128)(2,1)S(1)}, bf16[256,1024]{1,0:T(8,128)(2,1)S(1)}, u32[]{:S(2)}, u32[]{:S(2)}) collective-permute-start(bf16[256,1024]{1,0:T(8,128)(2,1)S(1)} %add_convert_fusion.6), channel_id=1, source_target_pairs={{0,1},{8,11},{1,2},{9,8},{2,3},{10,9},{3,0},{11,10},{4,5},{12,15},... | collective-permute-start | bytes 1572872 | tf_op jit(solution)/shard_map/ppermute | solution.py:261
  76.7 38.0 %collective-permute-start.22 = (bf16[256,1024]{1,0:T(8,128)(2,1)}, bf16[256,1024]{1,0:T(8,128)(2,1)S(1)}, u32[]{:S(2)}, u32[]{:S(2)}) collective-permute-start(bf16[256,1024]{1,0:T(8,128)(2,1)} %get-tuple-element.51), channel_id=1, source_target_pairs={{0,96},{8,40},{32,0},{40,72},{64,32},{72,104},{96,64},{104,8},{1,9... | collective-permute-start | bytes 1572872 | tf_op jit(solution)/shard_map/ppermute | solution.py:258
  80.0 34.7 %collective-permute-start.21 = (bf16[256,1024]{1,0:T(8,128)(2,1)}, bf16[256,1024]{1,0:T(8,128)(2,1)S(1)}, u32[]{:S(2)}, u32[]{:S(2)}) collective-permute-start(bf16[256,1024]{1,0:T(8,128)(2,1)} %get-tuple-element.50), channel_id=1, source_target_pairs={{0,32},{8,104},{32,64},{40,8},{64,96},{72,40},{96,0},{104,72},{1,3... | collective-permute-start | bytes 1572872 | tf_op jit(solution)/shard_map/ppermute | solution.py:258
  80.2 30.3 %collective-permute-start.23 = (bf16[256,1024]{1,0:T(8,128)(2,1)S(1)}, bf16[256,1024]{1,0:T(8,128)(2,1)S(1)}, u32[]{:S(2)}, u32[]{:S(2)}) collective-permute-start(bf16[256,1024]{1,0:T(8,128)(2,1)S(1)} %add_convert_fusion.4), channel_id=1, source_target_pairs={{0,32},{8,104},{32,64},{40,8},{64,96},{72,40},{96,0},{104,72},{1,3... | collective-permute-start | bytes 1572872 | tf_op jit(solution)/shard_map/ppermute | solution.py:258
  81.5 18.1 %copy-start.4 = (f32[256,1024]{1,0:T(8,128)S(1)}, f32[256,1024]{1,0:T(8,128)}, u32[]{:S(2)}) copy-start(f32[256,1024]{1,0:T(8,128)} %get-tuple-element.37) | copy-start | bytes 3145732
  96.0 14.3 %copy-start.10 = (f32[256,1024]{1,0:T(8,128)S(1)}, f32[256,1024]{1,0:T(8,128)}, u32[]{:S(2)}) copy-start(f32[256,1024]{1,0:T(8,128)} %get-tuple-element.62) | copy-start | bytes 3145732
  96.0 10.6 %collective-permute-start.18 = (bf16[256,1024]{1,0:T(8,128)(2,1)}, bf16[256,1024]{1,0:T(8,128)(2,1)S(1)}, u32[]{:S(2)}, u32[]{:S(2)}) collective-permute-start(bf16[256,1024]{1,0:T(8,128)(2,1)} %get-tuple-element.60), channel_id=1, source_target_pairs={{0,3},{8,9},{1,0},{9,10},{2,1},{10,11},{3,2},{11,8},{4,7},{12,13},... | collective-permute-start | bytes 1572872 | tf_op jit(solution)/shard_map/ppermute | solution.py:261
  99.6 10.6 %collective-permute-start.17 = (bf16[256,1024]{1,0:T(8,128)(2,1)}, bf16[256,1024]{1,0:T(8,128)(2,1)S(1)}, u32[]{:S(2)}, u32[]{:S(2)}) collective-permute-start(bf16[256,1024]{1,0:T(8,128)(2,1)} %get-tuple-element.59), channel_id=1, source_target_pairs={{0,1},{8,11},{1,2},{9,8},{2,3},{10,9},{3,0},{11,10},{4,5},{12,15},... | collective-permute-start | bytes 1572872 | tf_op jit(solution)/shard_map/ppermute | solution.py:261
  106.6 21.6 %collective-permute-start.10 = (bf16[128,1024]{1,0:T(8,128)(2,1)S(1)}, bf16[128,1024]{1,0:T(8,128)(2,1)S(1)}, u32[]{:S(2)}, u32[]{:S(2)}) collective-permute-start(bf16[128,1024]{1,0:T(8,128)(2,1)S(1)} %get-tuple-element.70), channel_id=1, source_target_pairs={{0,8},{8,0},{1,9},{9,1},{2,10},{10,2},{3,11},{11,3},{4,12},{12,4},... | collective-permute-start | bytes 786440 | tf_op jit(solution)/shard_map/ppermute | solution.py:267
  110.4 10.5 %collective-permute-start.19 = (bf16[256,1024]{1,0:T(8,128)(2,1)S(1)}, bf16[256,1024]{1,0:T(8,128)(2,1)S(1)}, u32[]{:S(2)}, u32[]{:S(2)}) collective-permute-start(bf16[256,1024]{1,0:T(8,128)(2,1)S(1)} %add_convert_fusion.3), channel_id=1, source_target_pairs={{0,1},{8,11},{1,2},{9,8},{2,3},{10,9},{3,0},{11,10},{4,5},{12,15},... | collective-permute-start | bytes 1572872 | tf_op jit(solution)/shard_map/ppermute | solution.py:261
  110.7 16.2 %collective-permute-start.25 = (bf16[256,1024]{1,0:T(8,128)(2,1)S(1)}, bf16[256,1024]{1,0:T(8,128)(2,1)S(1)}, u32[]{:S(2)}, u32[]{:S(2)}) collective-permute-start(bf16[256,1024]{1,0:T(8,128)(2,1)S(1)} %add_convert_fusion.1), channel_id=1, source_target_pairs={{0,16},{16,0},{1,17},{17,1},{2,18},{18,2},{3,19},{19,3},{4,20},{20... | collective-permute-start | bytes 1572872 | tf_op jit(solution)/shard_map/ppermute | solution.py:264
  114.8 12.1 %copy-start.3 = (f32[256,1024]{1,0:T(8,128)S(1)}, f32[256,1024]{1,0:T(8,128)}, u32[]{:S(2)}) copy-start(f32[256,1024]{1,0:T(8,128)} %get-tuple-element.53) | copy-start | bytes 3145732
  114.8 12.1 %collective-permute-start.24 = (bf16[256,1024]{1,0:T(8,128)(2,1)S(1)}, bf16[256,1024]{1,0:T(8,128)(2,1)S(1)}, u32[]{:S(2)}, u32[]{:S(2)}) collective-permute-start(bf16[256,1024]{1,0:T(8,128)(2,1)S(1)} %add_convert_fusion), channel_id=1, source_target_pairs={{0,32},{8,104},{32,64},{40,8},{64,96},{72,40},{96,0},{104,72},{1,3... | collective-permute-start | bytes 1572872 | tf_op jit(solution)/shard_map/ppermute | solution.py:258
  121.1 7.1 %collective-permute-start.20 = (bf16[128,1024]{1,0:T(8,128)(2,1)S(1)}, bf16[128,1024]{1,0:T(8,128)(2,1)S(1)}, u32[]{:S(2)}, u32[]{:S(2)}) collective-permute-start(bf16[128,1024]{1,0:T(8,128)(2,1)S(1)} %get-tuple-element.68), channel_id=1, source_target_pairs={{0,8},{8,0},{1,9},{9,1},{2,10},{10,2},{3,11},{11,3},{4,12},{12,4},... | collective-permute-start | bytes 786440 | tf_op jit(solution)/shard_map/ppermute | solution.py:267
  (11 other events, 68.0 us)

commit v9 on v4

--- a/solution.py
+++ b/solution.py
@@ -1,3 +1,5 @@
+import math
+
 import jax
 import jax.numpy as jnp
 from jax import lax
@@ -12,8 +14,31 @@
 
 
 def cost(flops, *arrays):
-    moved = sum(a.size * a.dtype.itemsize for a in arrays)
+    moved = sum(math.prod(a.shape) * jnp.dtype(a.dtype).itemsize for a in arrays)
     return pl.CostEstimate(flops=flops, bytes_accessed=moved, transcendentals=0)
+
+
+HBM = pl.BlockSpec(memory_space=pltpu.HBM)
+SMEM = pl.BlockSpec(memory_space=pltpu.SMEM)
+
+
+def in_hbm(array):
+    return pltpu.with_memory_space_constraint(array, pltpu.HBM)
+
+
+def start_all(pairs, sems, first=0):
+    copies = [
+        pltpu.make_async_copy(src, dst, sems.at[first + k])
+        for k, (src, dst) in enumerate(pairs)
+    ]
+    for copy in copies:
+        copy.start()
+    return copies
+
+
+def wait_all(copies):
+    for copy in copies:
+        copy.wait()
 
 
 def other_columns(act, c):
@@ -21,49 +46,62 @@
     n = NX * NZ
     rows = width // (n * NC)
 
-    def body(core, a_ref, out_ref):
-        pick = core[0] == 0
-        out_ref[0] = jnp.where(pick, a_ref[:, :, rows:], a_ref[:, :, :rows])
-
-    out = jax.ShapeDtypeStruct((n, mb, toks, rows), act.dtype)
+    def body(core, act_ref, out_ref, held, sems):
+        loads = []
+        for k in range(n):
+            start = pl.multiple_of((k * NC + 1 - core[0]) * rows, rows)
+            loads.append((act_ref.at[:, :, pl.ds(start, rows)], held.at[k]))
+        stores = []
+        for k, load in enumerate(start_all(loads, sems)):
+            load.wait()
+            stores += start_all([(held.at[k], out_ref.at[k])], sems, n + k)
+        wait_all(stores)
+
+    out = pltpu.HBM((n, mb, toks, rows), act.dtype)
     return pl.pallas_call(
         body,
         out_shape=out,
-        grid_spec=pltpu.PrefetchScalarGridSpec(
-            num_scalar_prefetch=1,
-            grid=(n,),
-            in_specs=[pl.BlockSpec((mb, toks, NC * rows), lambda k, core: (0, 0, k))],
-            out_specs=pl.BlockSpec((1, mb, toks, rows), lambda k, core: (k, 0, 0, 0)),
-        ),
-        compiler_params=pltpu.CompilerParams(vmem_limit_bytes=8 << 20),
+        in_specs=[SMEM, HBM],
+        out_specs=HBM,
+        scratch_shapes=[
+            pltpu.VMEM((n, mb, toks, rows), act.dtype),
+            pltpu.SemaphoreType.DMA((2 * n,)),
+        ],
+        compiler_params=pltpu.CompilerParams(vmem_limit_bytes=4 << 20),
         cost_estimate=cost(0, act, out),
         name="other_columns",
-    )(c.reshape(1), act)
+    )(c.reshape(1), in_hbm(act))
 
 
 def four_terms(rows, cols):
-    return [jax.ShapeDtypeStruct((rows, cols), t) for t in (BF16, BF16, F32, F32)]
-
-
-def dw_body(at, act, got, mine, theirs, *outs):
+    return [jax.ShapeDtypeStruct((rows, cols), BF16) for _ in range(4)]
+
+
+def dw_body(at, act, got, mine, theirs, *refs):
+    outs, held, sems = refs[:4], refs[4], refs[5]
     mb, toks, cols = mine.shape
     rows = got.shape[-1]
-    wide = cols // 2
+    step = cols // 2
+    loads = []
+    for k in range(4):
+        start = pl.multiple_of((at[k] * NC + at[4]) * rows, rows)
+        loads.append((act.at[:, :, pl.ds(start, rows)], held.at[k]))
+    loads = start_all(loads, sems)
+
+    def term(left, diff, j):
+        return lax.dot_general(
+            left.reshape(mb * toks, rows),
+            diff[:, :, j : j + step].reshape(mb * toks, step),
+            (((0,), (0,)), ((), ())),
+            preferred_element_type=F32,
+        )
+
     for k, out in enumerate(outs):
-        lanes = pl.ds(pl.multiple_of((at[k] * NC + at[len(outs)]) * rows, rows), rows)
-        a = act[:, :, lanes].reshape(mb * toks, rows)
-        b = got[at[k]].reshape(mb * toks, rows)
-        for j in range(0, cols, wide):
-            total = None
-            for lhs, diff in ((a, mine), (b, theirs)):
-                term = lax.dot_general(
-                    lhs,
-                    diff[:, :, j : j + wide].reshape(mb * toks, wide),
-                    (((0,), (0,)), ((), ())),
-                    preferred_element_type=F32,
-                )
-                total = term if total is None else total + term
-            out[:, j : j + wide] = total.astype(out.dtype)
+        for j in range(0, cols, step):
+            total = term(got[at[k]], theirs, j)
+            if j == 0:
+                loads[k].wait()
+            out[:, j : j + step] = (total + term(held[k], mine, j)).astype(out.dtype)
 
 
 def dw_terms(at, act, got, mine, theirs):
@@ -72,12 +110,16 @@
     return pl.pallas_call(
         dw_body,
         out_shape=outs,
-        in_specs=[pl.BlockSpec(memory_space=pltpu.SMEM), *([vmem] * 4)],
+        in_specs=[SMEM, HBM, *([vmem] * 3)],
         out_specs=[vmem] * 4,
+        scratch_shapes=[
+            pltpu.VMEM((4, *got.shape[1:]), BF16),
+            pltpu.SemaphoreType.DMA((4,)),
+        ],
         compiler_params=pltpu.CompilerParams(vmem_limit_bytes=6 << 20),
         cost_estimate=cost(16 * mine.size * got.shape[-1], *outs, mine, theirs, got),
         name="dw_terms",
-    )(at, act, got, mine, theirs)
+    )(at, in_hbm(act), got, mine, theirs)
 
 
 def dx_body(at, mine, theirs, *refs):
@@ -113,7 +155,7 @@
         out_specs=[vmem] * 4,
         scratch_shapes=[pltpu.VMEM((4, NC, mb, part, cols), BF16)],
         compiler_params=pltpu.CompilerParams(vmem_limit_bytes=8 << 20),
-        cost_estimate=cost(8 * outs[0].size * cols, *outs, mine, theirs, *pieces),
+        cost_estimate=cost(8 * math.prod(outs[0].shape) * cols, *outs, mine, theirs, *pieces),
         name="dx_terms",
     )(at, mine, theirs, *pieces)
 
@@ -202,16 +244,16 @@
     at_o = jnp.stack([*(((x + k) & (NX - 1)) * NZ + zh for k in ways), c])
     at_p = jnp.stack([*(((x + k) & (NX - 1)) * NZ + 1 - zh for k in ways), c])
 
+    act_send = other_columns(activations, c)
+    act_got = swap_core(act_send)
+    student_out = after(student_out, act_send)
     diff = (student_out.astype(F32) - teacher_out.astype(F32)).astype(BF16)
     diff_z = lax.ppermute(diff, "inc", SWAP)
     near_o = neighbours(own)
-    w_z = swap_zh(own)
-    act_send = other_columns(after(activations, *near_o), c)
-    act_got = swap_core(act_send)
-    w_o = (own, *near_o, step_x(pick(*near_o)))
-    near_p = neighbours(w_z)
-    w_p = (w_z, *near_p, step_x(pick(*near_p)))
-    diff_z = after(diff_z, w_z, act_send, w_o[3])
+    forward_o = pick(*near_o)
+    far_o = step_x(forward_o)
+    w_z = swap_zh(after(own, diff_z))
+    diff_z = after(diff_z, forward_o)
     mine = jnp.where(
         zl == 0,
         jnp.concatenate([diff, diff_z], axis=1),
@@ -225,19 +267,27 @@
             total = total + t.astype(F32)
         return total
 
-    def ring(step, terms):
-        far, back, ahead, here = terms
-        far, back = step(far), step(back, -1)
-        return add(here, back, step(add(ahead, far).astype(BF16)))
-
-    terms = dx_terms(at_y, mine, theirs, w_o)
-    theirs_w = after(theirs, *terms)
-    dx_o = ring(step_y, terms).astype(BF16)
-    terms_p = dw_terms(at_p, activations, act_got, mine, theirs_w)
-    terms_o = dw_terms(at_o, activations, act_got, mine, after(theirs_w, *terms_p))
-    cross = swap_zh(ring(step_x, terms_p).astype(BF16))
-    weight_grad = ring(step_x, terms_o) + cross.astype(F32)
-    dx_p = ring(step_y, dx_terms(at_y, mine, after(theirs, *terms_o), w_p)).astype(BF16)
+    def nearer(step, terms, *first):
+        far, back, ahead, _ = terms
+        far, back = lax.optimization_barrier((step(far), step(back, -1), *first))[:2]
+        return add(ahead, far).astype(BF16), back
+
+    terms_o = dx_terms(at_y, mine, theirs, (own, *near_o, far_o))
+    near_p = neighbours(after(w_z, terms_o[0]))
+    sums_p = dw_terms(at_p, activations, act_got, mine, after(theirs, *terms_o))
+    next_dx_o, back_dx_o = nearer(step_y, terms_o, sums_p[0])
+    forward_p = pick(after(near_p[0], sums_p[0]), near_p[1])
+    sums_o = dw_terms(at_o, activations, act_got, mine, after(theirs, forward_p, next_dx_o))
+    next_p, back_p = nearer(step_x, sums_p, sums_o[0])
+    far_p = step_x(forward_p)
+    terms_p = dx_terms(at_y, mine, after(theirs, *sums_o, next_p), (w_z, *near_p, far_p))
+    dx_o = add(terms_o[3], back_dx_o, step_y(next_dx_o)).astype(BF16)
+    whole_p = add(sums_p[3], back_p, step_x(next_p)).astype(BF16)
+    next_o, back_o = nearer(step_x, sums_o, terms_p[0], whole_p)
+    cross = swap_zh(whole_p)
+    next_dx_p, back_dx_p = nearer(step_y, terms_p)
+    dx_p = add(terms_p[3], back_dx_p, step_y(next_dx_p)).astype(BF16)
+    weight_grad = add(sums_o[3], back_o, step_x(next_o), cross)
 
     half = dx_o.shape[0] // 2
     got_o, got_p = swap_core(dx_o[half:]), swap_core(dx_p[half:])

time: 119 us -> 121 us (1.017)
  waiting for transfers between devices: 45 us -> 53 us
  local copies, waits for them, and re-layouts: 10.5 us -> 4.04 us
  Pallas kernels: 20.5 us -> 23.6 us
  starting transfers between devices: 31.5 us -> 29 us
    ppermute x8, waiting for transfers between devices: 14.8 us -> 23.7 us  [step_x(): return lax.ppermute(value, ('x', 'core'), by_core(NX, way, False))]
    unnamed x24 -> x20, local copies, waits for them, and re-layouts: 10.3 us -> 3.8 us
    ppermute x2, waiting for transfers between devices: 1.33 us -> 7.47 us  [swap_zh(): return lax.ppermute(value, 'zh', SWAP)]
    ppermute x8, starting transfers between devices: 9.81 us -> 5.37 us  [step_x(): return lax.ppermute(value, ('x', 'core'), by_core(NX, way, False))]
    ppermute x2, waiting for transfers between devices: 4.44 us -> 0.19 us  [neighbours(): lax.ppermute(piece, 'x', by_x(-1))]
    pallas_call x3, Pallas kernels: 10.4 us -> 13.3 us  [the longest x2 10.7 us: dw_terms(): pl.pallas_call(dw_body, out_shape=outs, in_specs=[SMEM, HBM, *[vmem] * 3]...]
    ppermute x6, starting transfers between devices: 9.4 us -> 6.87 us  [step_y(): return lax.ppermute(value, ('core', 'outc'), by_core(NY, way, True))]
    ppermute x2, starting transfers between devices: 5.11 us -> 7.49 us  [swap_zh(): return lax.ppermute(value, 'zh', SWAP)]
  transfers between devices with their start and end apart: 25 -> 25, of which waited for: 11 -> 13; matrix products, arithmetic and copies ran while one was open for 8% -> 9% of each run, Pallas kernels for 17% -> 18%
where the time goes in v9:
time: 121 us
  waiting for transfers between devices  53 us (44%)
  starting transfers between devices  29 us (24%)
  Pallas kernels  23.6 us (20%)
  other arithmetic  10.2 us (8%)
  local copies, waits for them, and re-layouts  4.04 us (3%)
    ppermute x8, waiting for transfers between devices, step_x(): return lax.ppermute(value, ('x', 'core'), by_core(NX, way, False))  23.7 us
    pallas_call x2, Pallas kernels, dw_terms(): pl.pallas_call(dw_body, out_shape=outs, in_specs=[SMEM, HBM, *[vmem] * 3]...  10.7 us
    ppermute x6, waiting for transfers between devices, step_y(): return lax.ppermute(value, ('core', 'outc'), by_core(NY, way, True))  9.52 us
    pallas_call x2, Pallas kernels, dx_terms(): pl.pallas_call(dx_body, out_shape=outs, in_specs=[pl.BlockSpec(memory_spa...  8.7 us
    ppermute x2, waiting for transfers between devices, neighbours(): lax.ppermute(piece, 'x', by_x(1))  7.76 us
    ppermute x2, starting transfers between devices, swap_zh(): return lax.ppermute(value, 'zh', SWAP)  7.49 us
    ppermute x2, waiting for transfers between devices, swap_zh(): return lax.ppermute(value, 'zh', SWAP)  7.47 us
    ppermute x6, starting transfers between devices, step_y(): return lax.ppermute(value, ('core', 'outc'), by_core(NY, way, True))  6.87 us
  transfers between devices with their start and end apart: 25, of which 13 were waited for; matrix products, arithmetic and copies ran while one was open for 9% of the time, Pallas kernels for 18%

profile of v9, /device:TPU:0, one launch (start us, length us, event | category | flops | bytes accessed | tf_op | source)
XLA Modules:
  0.0 120.8 jit_solution(12722928949910390316)
XLA Ops:
  0.6 1.6 %collective-permute-start.1 = (bf16[256,1024]{1,0:T(8,128)(2,1)}, bf16[256,1024]{1,0:T(8,128)(2,1)S(1)}, u32[]{:S(2)}, u32[]{:S(2)}) collective-permute-start(bf16[256,1024]{1,0:T(8,128)(2,1)} %bitcast.7.refs_0_), channel_id=1, source_target_pairs={{0,32},{32,64},{64,96},{96,0},{1,33},{33,65},{65,97},{97,1},{2,34}... | collective-permute-start | bytes 1572872 | tf_op jit(solution)/shard_map/ppermute | solution.py:237
  2.3 1.7 %collective-permute-start.2 = (bf16[256,1024]{1,0:T(8,128)(2,1)}, bf16[256,1024]{1,0:T(8,128)(2,1)S(1)}, u32[]{:S(2)}, u32[]{:S(2)}) collective-permute-start(bf16[256,1024]{1,0:T(8,128)(2,1)} %bitcast.7.refs_0_), channel_id=1, source_target_pairs={{0,96},{32,0},{64,32},{96,64},{1,97},{33,1},{65,33},{97,65},{2,98}... | collective-permute-start | bytes 1572872 | tf_op jit(solution)/shard_map/ppermute | solution.py:237
  3.9 2.5 %other_columns.1 = bf16[8,2,256,256]{3,2,1,0:T(8,128)(2,1)} custom-call(s32[1]{0:T(128)} %bitcast.2.core, bf16[2,256,4096]{2,1,0:T(8,128)(2,1)} %act.3), custom_call_target="tpu_custom_call" | custom-call | bytes 6291456 | tf_op jit(solution)/shard_map/other_columns/pallas_call | solution.py:61
  7.5 2.0 %collective-permute-start = (bf16[2,128,1024]{2,1,0:T(8,128)(2,1)}, bf16[2,128,1024]{2,1,0:T(8,128)(2,1)}, u32[]{:S(2)}, u32[]{:S(2)}) collective-permute-start(bf16[2,128,1024]{2,1,0:T(8,128)(2,1)} %subtract_convert_fusion), channel_id=1, source_target_pairs={{0,4},{4,0},{1,5},{5,1},{2,6},{6,2},{3,7},{7,3},{8,12},{12,8},{9,1... | collective-permute-start | bytes 1572872 | tf_op jit(solution)/shard_map/ppermute | solution.py:251
  9.5 6.2 %collective-permute-done.1.refs_1_ = bf16[256,1024]{1,0:T(8,128)(2,1)S(1)} collective-permute-done((bf16[256,1024]{1,0:T(8,128)(2,1)}, bf16[256,1024]{1,0:T(8,128)(2,1)S(1)}, u32[]{:S(2)}, u32[]{:S(2)}) %collective-permute-start.1) | collective-permute-done | bytes 524320 | tf_op jit(solution)/shard_map/ppermute | solution.py:237
  16.9 4.3 %collective-permute-done = bf16[2,128,1024]{2,1,0:T(8,128)(2,1)} collective-permute-done((bf16[2,128,1024]{2,1,0:T(8,128)(2,1)}, bf16[2,128,1024]{2,1,0:T(8,128)(2,1)}, u32[]{:S(2)}, u32[]{:S(2)}) %collective-permute-start) | collective-permute-done | bytes 524320 | tf_op jit(solution)/shard_map/ppermute | solution.py:251
  21.2 2.1 %maximum_select_fusion.mine = bf16[2,256,1024]{2,1,0:T(8,128)(2,1)S(1)} fusion(bf16[2,128,1024]{2,1,0:T(8,128)(2,1)} %collective-permute-done, bf16[2,128,1024]{2,1,0:T(8,128)(2,1)} %subtract_convert_fusion, pred[]{:T(512)S(6)} %eq.7), kind=kLoop, calls=%fused_computation | loop fusion | flops 4718592 | bytes 2097153 | tf_op jit(solution)/shard_map/jit(_where)/select_n | solution.py:257
  23.7 3.7 %collective-permute-start.10 = (bf16[256,1024]{1,0:T(8,128)(2,1)}, bf16[256,1024]{1,0:T(8,128)(2,1)}, u32[]{:S(2)}, u32[]{:S(2)}) collective-permute-start(bf16[256,1024]{1,0:T(8,128)(2,1)} %bitcast.7.refs_0_), channel_id=1, source_target_pairs={{0,16},{16,0},{1,17},{17,1},{2,18},{18,2},{3,19},{19,3},{4,20},{20... | collective-permute-start | bytes 1572872 | tf_op jit(solution)/shard_map/ppermute | solution.py:231
  27.5 6.6 %collective-permute-done.4.refs_3_ = bf16[256,1024]{1,0:T(8,128)(2,1)} collective-permute-done((bf16[256,1024]{1,0:T(8,128)(2,1)}, bf16[256,1024]{1,0:T(8,128)(2,1)}, u32[]{:S(2)}, u32[]{:S(2)}) %collective-permute-start.4) | collective-permute-done | bytes 524320 | tf_op jit(solution)/shard_map/ppermute | solution.py:225
  36.2 4.7 %dx_terms.2 = (bf16[256,1024]{1,0:T(8,128)(2,1)}, bf16[256,1024]{1,0:T(8,128)(2,1)}, bf16[256,1024]{1,0:T(8,128)(2,1)S(1)}, bf16[256,1024]{1,0:T(8,128)(2,1)S(1)}) custom-call(s32[4]{0:T(128)S(1)} %pad_add_fusion.1.at, bf16[2,256,1024]{2,1,0:T(8,128)(2,1)S(1)} %maximum_select_fusion.mine, bf16[2,256,1024]{2,1,0:T(8,128)(2,1)} %collective-permute-done.3.theirs, ...), custom_call_target="tpu_custom_call" | custom-call | flops 2147483648 | bytes 6291456 | tf_op jit(solution)/shard_map/dx_terms/pallas_call | solution.py:151
  42.5 3.2 %collective-permute-start.12 = (bf16[256,1024]{1,0:T(8,128)(2,1)}, bf16[256,1024]{1,0:T(8,128)(2,1)}, u32[]{:S(2)}, u32[]{:S(2)}) collective-permute-start(bf16[256,1024]{1,0:T(8,128)(2,1)} %collective-permute-done.10.refs_0_), channel_id=1, source_target_pairs={{0,96},{32,0},{64,32},{96,64},{1,97},{33,1},{65,33},{97,65},{2,98}... | collective-permute-start | bytes 1572872 | tf_op jit(solution)/shard_map/ppermute | solution.py:237
  45.7 1.6 %collective-permute-start.5 = (bf16[256,1024]{1,0:T(8,128)(2,1)}, bf16[256,1024]{1,0:T(8,128)(2,1)}, u32[]{:S(2)}, u32[]{:S(2)}) collective-permute-start(bf16[256,1024]{1,0:T(8,128)(2,1)} %get-tuple-element.37), channel_id=1, source_target_pairs={{0,1},{8,11},{1,2},{9,8},{2,3},{10,9},{3,0},{11,10},{4,5},{12,15},... | collective-permute-start | bytes 1572872 | tf_op jit(solution)/shard_map/ppermute | solution.py:228
  47.3 1.7 %collective-permute-start.6 = (bf16[256,1024]{1,0:T(8,128)(2,1)}, bf16[256,1024]{1,0:T(8,128)(2,1)}, u32[]{:S(2)}, u32[]{:S(2)}) collective-permute-start(bf16[256,1024]{1,0:T(8,128)(2,1)} %get-tuple-element.38), channel_id=1, source_target_pairs={{0,3},{8,9},{1,0},{9,10},{2,1},{10,11},{3,2},{11,8},{4,7},{12,13},... | collective-permute-start | bytes 1572872 | tf_op jit(solution)/shard_map/ppermute | solution.py:228
  49.1 5.4 %dw_terms.2 = (bf16[256,1024]{1,0:T(8,128)(2,1)S(1)}, bf16[256,1024]{1,0:T(8,128)(2,1)S(1)}, bf16[256,1024]{1,0:T(8,128)(2,1)S(1)}, bf16[256,1024]{1,0:T(8,128)(2,1)S(1)}) custom-call(s32[5]{0:T(128)S(1)} %stack.72.at, bf16[2,256,4096]{2,1,0:T(8,128)(2,1)} %act.3, bf16[8,2,256,256]{3,2,1,0:T(8,128)(2,1)S(1)} %collective-permute-done.7.got, ...), custom_call_target="tpu_custom_call" | custom-call | flops 2147483648 | bytes 6291456 | tf_op jit(solution)/shard_map/dw_terms/pallas_call | solution.py:110
  54.6 1.6 %collective-permute-done.11.refs_1_ = bf16[256,1024]{1,0:T(8,128)(2,1)} collective-permute-done((bf16[256,1024]{1,0:T(8,128)(2,1)}, bf16[256,1024]{1,0:T(8,128)(2,1)}, u32[]{:S(2)}, u32[]{:S(2)}) %collective-permute-start.11) | collective-permute-done | bytes 524320 | tf_op jit(solution)/shard_map/ppermute | solution.py:237
  56.2 1.6 %collective-permute-start.14 = (bf16[256,1024]{1,0:T(8,128)(2,1)S(1)}, bf16[256,1024]{1,0:T(8,128)(2,1)S(1)}, u32[]{:S(2)}, u32[]{:S(2)}) collective-permute-start(bf16[256,1024]{1,0:T(8,128)(2,1)S(1)} %get-tuple-element.53), channel_id=1, source_target_pairs={{0,96},{8,40},{32,0},{40,72},{64,32},{72,104},{96,64},{104,8},{1,9... | collective-permute-start | bytes 1572872 | tf_op jit(solution)/shard_map/ppermute | solution.py:225
  59.0 2.7 %collective-permute-done.5 = bf16[256,1024]{1,0:T(8,128)(2,1)} collective-permute-done((bf16[256,1024]{1,0:T(8,128)(2,1)}, bf16[256,1024]{1,0:T(8,128)(2,1)}, u32[]{:S(2)}, u32[]{:S(2)}) %collective-permute-start.5) | collective-permute-done | bytes 524320 | tf_op jit(solution)/shard_map/ppermute | solution.py:228
  63.2 5.3 %dw_terms.3 = (bf16[256,1024]{1,0:T(8,128)(2,1)S(1)}, bf16[256,1024]{1,0:T(8,128)(2,1)S(1)}, bf16[256,1024]{1,0:T(8,128)(2,1)S(1)}, bf16[256,1024]{1,0:T(8,128)(2,1)S(1)}) custom-call(s32[5]{0:T(128)S(1)} %stack.77.at, bf16[2,256,4096]{2,1,0:T(8,128)(2,1)} %act.3, bf16[8,2,256,256]{3,2,1,0:T(8,128)(2,1)S(1)} %collective-permute-done.7.got, ...), custom_call_target="tpu_custom_call" | custom-call | flops 2147483648 | bytes 6291456 | tf_op jit(solution)/shard_map/dw_terms/pallas_call | solution.py:110
  68.5 1.3 %collective-permute-done.13 = bf16[256,1024]{1,0:T(8,128)(2,1)S(1)} collective-permute-done((bf16[256,1024]{1,0:T(8,128)(2,1)S(1)}, bf16[256,1024]{1,0:T(8,128)(2,1)S(1)}, u32[]{:S(2)}, u32[]{:S(2)}) %collective-permute-start.13) | collective-permute-done | bytes 524320 | tf_op jit(solution)/shard_map/ppermute | solution.py:225
  70.4 5.0 %collective-permute-done.15.refs_3_ = bf16[256,1024]{1,0:T(8,128)(2,1)S(1)} collective-permute-done((bf16[256,1024]{1,0:T(8,128)(2,1)S(1)}, bf16[256,1024]{1,0:T(8,128)(2,1)S(1)}, u32[]{:S(2)}, u32[]{:S(2)}) %collective-permute-start.15) | collective-permute-done | bytes 524320 | tf_op jit(solution)/shard_map/ppermute | solution.py:225
  75.4 4.0 %dx_terms.3 = (bf16[256,1024]{1,0:T(8,128)(2,1)S(1)}, bf16[256,1024]{1,0:T(8,128)(2,1)S(1)}, bf16[256,1024]{1,0:T(8,128)(2,1)S(1)}, bf16[256,1024]{1,0:T(8,128)(2,1)S(1)}) custom-call(s32[4]{0:T(128)S(1)} %pad_add_fusion.1.at, bf16[2,256,1024]{2,1,0:T(8,128)(2,1)S(1)} %maximum_select_fusion.mine, bf16[2,256,1024]{2,1,0:T(8,128)(2,1)} %collective-permute-done.3.theirs, ...), custom_call_target="tpu_custom_call" | custom-call | flops 2147483648 | bytes 6291456 | tf_op jit(solution)/shard_map/dx_terms/pallas_call | solution.py:151
  79.5 1.3 %collective-permute-start.16 = (bf16[256,1024]{1,0:T(8,128)(2,1)S(1)}, bf16[256,1024]{1,0:T(8,128)(2,1)S(1)}, u32[]{:S(2)}, u32[]{:S(2)}) collective-permute-start(bf16[256,1024]{1,0:T(8,128)(2,1)S(1)} %get-tuple-element.57), channel_id=1, source_target_pairs={{0,1},{8,11},{1,2},{9,8},{2,3},{10,9},{3,0},{11,10},{4,5},{12,15},... | collective-permute-start | bytes 1572872 | tf_op jit(solution)/shard_map/ppermute | solution.py:228
  80.7 2.0 %collective-permute-start.17 = (bf16[256,1024]{1,0:T(8,128)(2,1)S(1)}, bf16[256,1024]{1,0:T(8,128)(2,1)S(1)}, u32[]{:S(2)}, u32[]{:S(2)}) collective-permute-start(bf16[256,1024]{1,0:T(8,128)(2,1)S(1)} %get-tuple-element.58), channel_id=1, source_target_pairs={{0,3},{8,9},{1,0},{9,10},{2,1},{10,11},{3,2},{11,8},{4,7},{12,13},... | collective-permute-start | bytes 1572872 | tf_op jit(solution)/shard_map/ppermute | solution.py:228
  82.9 3.2 %collective-permute-start.21 = (bf16[256,1024]{1,0:T(8,128)(2,1)S(1)}, bf16[256,1024]{1,0:T(8,128)(2,1)S(1)}, u32[]{:S(2)}, u32[]{:S(2)}) collective-permute-start(bf16[256,1024]{1,0:T(8,128)(2,1)S(1)} %get-tuple-element.49), channel_id=1, source_target_pairs={{0,96},{8,40},{32,0},{40,72},{64,32},{72,104},{96,64},{104,8},{1,9... | collective-permute-start | bytes 1572872 | tf_op jit(solution)/shard_map/ppermute | solution.py:225
  86.1 1.3 %add_convert_fusion.5 = bf16[256,1024]{1,0:T(8,128)(2,1)S(1)} fusion(bf16[256,1024]{1,0:T(8,128)(2,1)S(1)} %collective-permute-done.8, bf16[256,1024]{1,0:T(8,128)(2,1)} %collective-permute-done.6, bf16[256,1024]{1,0:T(8,128)(2,1)S(1)} %copy-done.7), kind=kLoop, calls=%fused_computation.7 | loop fusion | flops 1572864 | bytes 2097152 | tf_op jit(solution)/shard_map/convert_element_type | solution.py:284
  87.4 6.8 %collective-permute-done.16 = bf16[256,1024]{1,0:T(8,128)(2,1)S(1)} collective-permute-done((bf16[256,1024]{1,0:T(8,128)(2,1)S(1)}, bf16[256,1024]{1,0:T(8,128)(2,1)S(1)}, u32[]{:S(2)}, u32[]{:S(2)}) %collective-permute-start.16) | collective-permute-done | bytes 524320 | tf_op jit(solution)/shard_map/ppermute | solution.py:228
  94.5 8.5 %collective-permute-done.22 = bf16[256,1024]{1,0:T(8,128)(2,1)S(1)} collective-permute-done((bf16[256,1024]{1,0:T(8,128)(2,1)S(1)}, bf16[256,1024]{1,0:T(8,128)(2,1)S(1)}, u32[]{:S(2)}, u32[]{:S(2)}) %collective-permute-start.22) | collective-permute-done | bytes 524320 | tf_op jit(solution)/shard_map/ppermute | solution.py:225
  103.3 3.8 %collective-permute-start.24 = (bf16[256,1024]{1,0:T(8,128)(2,1)S(1)}, bf16[256,1024]{1,0:T(8,128)(2,1)S(1)}, u32[]{:S(2)}, u32[]{:S(2)}) collective-permute-start(bf16[256,1024]{1,0:T(8,128)(2,1)S(1)} %add_convert_fusion.1), channel_id=1, source_target_pairs={{0,16},{16,0},{1,17},{17,1},{2,18},{18,2},{3,19},{19,3},{4,20},{20... | collective-permute-start | bytes 1572872 | tf_op jit(solution)/shard_map/ppermute | solution.py:231
  108.4 7.5 %collective-permute-done.24 = bf16[256,1024]{1,0:T(8,128)(2,1)S(1)} collective-permute-done((bf16[256,1024]{1,0:T(8,128)(2,1)S(1)}, bf16[256,1024]{1,0:T(8,128)(2,1)S(1)}, u32[]{:S(2)}, u32[]{:S(2)}) %collective-permute-start.24) | collective-permute-done | bytes 524320 | tf_op jit(solution)/shard_map/ppermute | solution.py:231
  115.9 1.9 %collective-permute-done.23 = bf16[256,1024]{1,0:T(8,128)(2,1)S(1)} collective-permute-done((bf16[256,1024]{1,0:T(8,128)(2,1)S(1)}, bf16[256,1024]{1,0:T(8,128)(2,1)S(1)}, u32[]{:S(2)}, u32[]{:S(2)}) %collective-permute-start.23) | collective-permute-done | bytes 524320 | tf_op jit(solution)/shard_map/ppermute | solution.py:225
  117.8 1.3 %add_bitcast_fusion = f32[1,256,1024]{2,1,0:T(8,128)} fusion(bf16[256,1024]{1,0:T(8,128)(2,1)S(1)} %collective-permute-done.24, bf16[256,1024]{1,0:T(8,128)(2,1)S(1)} %collective-permute-done.23, bf16[256,1024]{1,0:T(8,128)(2,1)S(1)} %collective-permute-done.21, bf16[256,1024]{1,0:T(8,128)(2,1)S(1)} %get-tuple-element.51), kind=kLoop, calls=%fused_computation.1 | loop fusion | flops 1835008 | bytes 3145728 | tf_op jit(solution)/shard_map/reshape | solution.py:297
  119.1 1.7 %place.1 = bf16[2,64,4096]{2,1,0:T(8,128)(2,1)} custom-call(s32[3]{0:T(128)S(1)} %pad_add_fusion.at, bf16[128,1024]{1,0:T(8,128)(2,1)S(1)} %get-tuple-element.69.keep_o, bf16[128,1024]{1,0:T(8,128)(2,1)S(1)} %collective-permute-done.9.got_o, bf16[128,1024]{1,0:T(8,128)(2,1)S(1)} %get-tuple-element.67.keep_p, bf16[128,1024]{1,0:T(8,128)(2,1)S(1)} %collective-permute-done.19.got_p), custom_call_target="tpu_custom_call" | custom-call | bytes 2097152 | tf_op jit(solution)/shard_map/place/pallas_call | solution.py:186
  (62 shorter events, 11.8 us)
Async XLA Ops:
  0.6 15.0 %collective-permute-start.1 = (bf16[256,1024]{1,0:T(8,128)(2,1)}, bf16[256,1024]{1,0:T(8,128)(2,1)S(1)}, u32[]{:S(2)}, u32[]{:S(2)}) collective-permute-start(bf16[256,1024]{1,0:T(8,128)(2,1)} %bitcast.7.refs_0_), channel_id=1, source_target_pairs={{0,32},{32,64},{64,96},{96,0},{1,33},{33,65},{65,97},{97,1},{2,34}... | collective-permute-start | bytes 1572872 | tf_op jit(solution)/shard_map/ppermute | solution.py:237
  2.3 13.6 %collective-permute-start.2 = (bf16[256,1024]{1,0:T(8,128)(2,1)}, bf16[256,1024]{1,0:T(8,128)(2,1)S(1)}, u32[]{:S(2)}, u32[]{:S(2)}) collective-permute-start(bf16[256,1024]{1,0:T(8,128)(2,1)} %bitcast.7.refs_0_), channel_id=1, source_target_pairs={{0,96},{32,0},{64,32},{96,64},{1,97},{33,1},{65,33},{97,65},{2,98}... | collective-permute-start | bytes 1572872 | tf_op jit(solution)/shard_map/ppermute | solution.py:237
  3.9 2.6 %copy-start.8 = (bf16[2,128,1024]{2,1,0:T(8,128)(2,1)S(1)}, bf16[2,128,1024]{2,1,0:T(8,128)(2,1)}, u32[]{:S(2)}) copy-start(bf16[2,128,1024]{2,1,0:T(8,128)(2,1)} %param.6) | copy-start | bytes 1572868
  3.9 2.6 %copy-start.9 = (bf16[2,128,1024]{2,1,0:T(8,128)(2,1)S(1)}, bf16[2,128,1024]{2,1,0:T(8,128)(2,1)}, u32[]{:S(2)}) copy-start(bf16[2,128,1024]{2,1,0:T(8,128)(2,1)} %param.5) | copy-start | bytes 1572868
  7.5 13.7 %collective-permute-start = (bf16[2,128,1024]{2,1,0:T(8,128)(2,1)}, bf16[2,128,1024]{2,1,0:T(8,128)(2,1)}, u32[]{:S(2)}, u32[]{:S(2)}) collective-permute-start(bf16[2,128,1024]{2,1,0:T(8,128)(2,1)} %subtract_convert_fusion), channel_id=1, source_target_pairs={{0,4},{4,0},{1,5},{5,1},{2,6},{6,2},{3,7},{7,3},{8,12},{12,8},{9,1... | collective-permute-start | bytes 1572872 | tf_op jit(solution)/shard_map/ppermute | solution.py:251
  9.5 39.6 %collective-permute-start.7 = (bf16[8,2,256,256]{3,2,1,0:T(8,128)(2,1)}, bf16[8,2,256,256]{3,2,1,0:T(8,128)(2,1)S(1)}, u32[]{:S(2)}, u32[]{:S(2)}) collective-permute-start(bf16[8,2,256,256]{3,2,1,0:T(8,128)(2,1)} %other_columns.1), channel_id=1, source_target_pairs={{0,8},{8,0},{1,9},{9,1},{2,10},{10,2},{3,11},{11,3},{4,12},{12,4},... | collective-permute-start | bytes 6291464 | tf_op jit(solution)/shard_map/ppermute | solution.py:234
  15.7 1.1 copy-start.2
  23.3 10.9 %collective-permute-start.3 = (bf16[2,256,1024]{2,1,0:T(8,128)(2,1)S(1)}, bf16[2,256,1024]{2,1,0:T(8,128)(2,1)}, u32[]{:S(2)}, u32[]{:S(2)}) collective-permute-start(bf16[2,256,1024]{2,1,0:T(8,128)(2,1)S(1)} %maximum_select_fusion.mine), channel_id=1, source_target_pairs={{0,8},{8,0},{1,9},{9,1},{2,10},{10,2},{3,11},{11,3},{4,12},{12,4},... | collective-permute-start | bytes 3145736 | tf_op jit(solution)/shard_map/ppermute | solution.py:234
  23.4 10.8 %collective-permute-start.4 = (bf16[256,1024]{1,0:T(8,128)(2,1)}, bf16[256,1024]{1,0:T(8,128)(2,1)}, u32[]{:S(2)}, u32[]{:S(2)}) collective-permute-start(bf16[256,1024]{1,0:T(8,128)(2,1)} %broadcast_select_fusion.1), channel_id=1, source_target_pairs={{0,32},{8,104},{32,64},{40,8},{64,96},{72,40},{96,0},{104,72},{1,3... | collective-permute-start | bytes 1572872 | tf_op jit(solution)/shard_map/ppermute | solution.py:225
  23.7 18.8 %collective-permute-start.10 = (bf16[256,1024]{1,0:T(8,128)(2,1)}, bf16[256,1024]{1,0:T(8,128)(2,1)}, u32[]{:S(2)}, u32[]{:S(2)}) collective-permute-start(bf16[256,1024]{1,0:T(8,128)(2,1)} %bitcast.7.refs_0_), channel_id=1, source_target_pairs={{0,16},{16,0},{1,17},{17,1},{2,18},{18,2},{3,19},{19,3},{4,20},{20... | collective-permute-start | bytes 1572872 | tf_op jit(solution)/shard_map/ppermute | solution.py:231
  34.1 1.0 copy-start.3
  35.2 1.0 copy-start.5
  42.5 13.7 %collective-permute-start.11 = (bf16[256,1024]{1,0:T(8,128)(2,1)}, bf16[256,1024]{1,0:T(8,128)(2,1)}, u32[]{:S(2)}, u32[]{:S(2)}) collective-permute-start(bf16[256,1024]{1,0:T(8,128)(2,1)} %collective-permute-done.10.refs_0_), channel_id=1, source_target_pairs={{0,32},{32,64},{64,96},{96,0},{1,33},{33,65},{65,97},{97,1},{2,34}... | collective-permute-start | bytes 1572872 | tf_op jit(solution)/shard_map/ppermute | solution.py:237
  42.5 15.4 %collective-permute-start.12 = (bf16[256,1024]{1,0:T(8,128)(2,1)}, bf16[256,1024]{1,0:T(8,128)(2,1)}, u32[]{:S(2)}, u32[]{:S(2)}) collective-permute-start(bf16[256,1024]{1,0:T(8,128)(2,1)} %collective-permute-done.10.refs_0_), channel_id=1, source_target_pairs={{0,96},{32,0},{64,32},{96,64},{1,97},{33,1},{65,33},{97,65},{2,98}... | collective-permute-start | bytes 1572872 | tf_op jit(solution)/shard_map/ppermute | solution.py:237
  45.7 15.9 %collective-permute-start.5 = (bf16[256,1024]{1,0:T(8,128)(2,1)}, bf16[256,1024]{1,0:T(8,128)(2,1)}, u32[]{:S(2)}, u32[]{:S(2)}) collective-permute-start(bf16[256,1024]{1,0:T(8,128)(2,1)} %get-tuple-element.37), channel_id=1, source_target_pairs={{0,1},{8,11},{1,2},{9,8},{2,3},{10,9},{3,0},{11,10},{4,5},{12,15},... | collective-permute-start | bytes 1572872 | tf_op jit(solution)/shard_map/ppermute | solution.py:228
  47.3 14.3 %collective-permute-start.6 = (bf16[256,1024]{1,0:T(8,128)(2,1)}, bf16[256,1024]{1,0:T(8,128)(2,1)}, u32[]{:S(2)}, u32[]{:S(2)}) collective-permute-start(bf16[256,1024]{1,0:T(8,128)(2,1)} %get-tuple-element.38), channel_id=1, source_target_pairs={{0,3},{8,9},{1,0},{9,10},{2,1},{10,11},{3,2},{11,8},{4,7},{12,13},... | collective-permute-start | bytes 1572872 | tf_op jit(solution)/shard_map/ppermute | solution.py:228
  49.1 12.5 %copy-start.1 = (bf16[256,1024]{1,0:T(8,128)(2,1)S(1)}, bf16[256,1024]{1,0:T(8,128)(2,1)}, u32[]{:S(2)}) copy-start(bf16[256,1024]{1,0:T(8,128)(2,1)} %copy-done) | copy-start | bytes 1572868
  54.5 15.2 %collective-permute-start.13 = (bf16[256,1024]{1,0:T(8,128)(2,1)S(1)}, bf16[256,1024]{1,0:T(8,128)(2,1)S(1)}, u32[]{:S(2)}, u32[]{:S(2)}) collective-permute-start(bf16[256,1024]{1,0:T(8,128)(2,1)S(1)} %get-tuple-element.41), channel_id=1, source_target_pairs={{0,32},{8,104},{32,64},{40,8},{64,96},{72,40},{96,0},{104,72},{1,3... | collective-permute-start | bytes 1572872 | tf_op jit(solution)/shard_map/ppermute | solution.py:225
  56.2 14.0 %collective-permute-start.14 = (bf16[256,1024]{1,0:T(8,128)(2,1)S(1)}, bf16[256,1024]{1,0:T(8,128)(2,1)S(1)}, u32[]{:S(2)}, u32[]{:S(2)}) collective-permute-start(bf16[256,1024]{1,0:T(8,128)(2,1)S(1)} %get-tuple-element.53), channel_id=1, source_target_pairs={{0,96},{8,40},{32,0},{40,72},{64,32},{72,104},{96,64},{104,8},{1,9... | collective-permute-start | bytes 1572872 | tf_op jit(solution)/shard_map/ppermute | solution.py:225
  61.6 13.8 %collective-permute-start.15 = (bf16[256,1024]{1,0:T(8,128)(2,1)S(1)}, bf16[256,1024]{1,0:T(8,128)(2,1)S(1)}, u32[]{:S(2)}, u32[]{:S(2)}) collective-permute-start(bf16[256,1024]{1,0:T(8,128)(2,1)S(1)} %broadcast_select_fusion), channel_id=1, source_target_pairs={{0,32},{8,104},{32,64},{40,8},{64,96},{72,40},{96,0},{104,72},{1,3... | collective-permute-start | bytes 1572872 | tf_op jit(solution)/shard_map/ppermute | solution.py:225
  62.9 23.2 %collective-permute-start.8 = (bf16[256,1024]{1,0:T(8,128)(2,1)S(1)}, bf16[256,1024]{1,0:T(8,128)(2,1)S(1)}, u32[]{:S(2)}, u32[]{:S(2)}) collective-permute-start(bf16[256,1024]{1,0:T(8,128)(2,1)S(1)} %add_convert_fusion.6), channel_id=1, source_target_pairs={{0,1},{8,11},{1,2},{9,8},{2,3},{10,9},{3,0},{11,10},{4,5},{12,15},... | collective-permute-start | bytes 1572872 | tf_op jit(solution)/shard_map/ppermute | solution.py:228
  70.4 15.7 %copy-start.7 = (bf16[256,1024]{1,0:T(8,128)(2,1)S(1)}, bf16[256,1024]{1,0:T(8,128)(2,1)}, u32[]{:S(2)}) copy-start(bf16[256,1024]{1,0:T(8,128)(2,1)} %copy-done.6) | copy-start | bytes 1572868
  79.5 14.8 %collective-permute-start.16 = (bf16[256,1024]{1,0:T(8,128)(2,1)S(1)}, bf16[256,1024]{1,0:T(8,128)(2,1)S(1)}, u32[]{:S(2)}, u32[]{:S(2)}) collective-permute-start(bf16[256,1024]{1,0:T(8,128)(2,1)S(1)} %get-tuple-element.57), channel_id=1, source_target_pairs={{0,1},{8,11},{1,2},{9,8},{2,3},{10,9},{3,0},{11,10},{4,5},{12,15},... | collective-permute-start | bytes 1572872 | tf_op jit(solution)/shard_map/ppermute | solution.py:228
  80.7 13.5 %collective-permute-start.17 = (bf16[256,1024]{1,0:T(8,128)(2,1)S(1)}, bf16[256,1024]{1,0:T(8,128)(2,1)S(1)}, u32[]{:S(2)}, u32[]{:S(2)}) collective-permute-start(bf16[256,1024]{1,0:T(8,128)(2,1)S(1)} %get-tuple-element.58), channel_id=1, source_target_pairs={{0,3},{8,9},{1,0},{9,10},{2,1},{10,11},{3,2},{11,8},{4,7},{12,13},... | collective-permute-start | bytes 1572872 | tf_op jit(solution)/shard_map/ppermute | solution.py:228
  82.8 24.3 %collective-permute-start.20 = (bf16[256,1024]{1,0:T(8,128)(2,1)S(1)}, bf16[256,1024]{1,0:T(8,128)(2,1)S(1)}, u32[]{:S(2)}, u32[]{:S(2)}) collective-permute-start(bf16[256,1024]{1,0:T(8,128)(2,1)S(1)} %get-tuple-element.48), channel_id=1, source_target_pairs={{0,32},{8,104},{32,64},{40,8},{64,96},{72,40},{96,0},{104,72},{1,3... | collective-permute-start | bytes 1572872 | tf_op jit(solution)/shard_map/ppermute | solution.py:225
  82.9 24.3 %collective-permute-start.21 = (bf16[256,1024]{1,0:T(8,128)(2,1)S(1)}, bf16[256,1024]{1,0:T(8,128)(2,1)S(1)}, u32[]{:S(2)}, u32[]{:S(2)}) collective-permute-start(bf16[256,1024]{1,0:T(8,128)(2,1)S(1)} %get-tuple-element.49), channel_id=1, source_target_pairs={{0,96},{8,40},{32,0},{40,72},{64,32},{72,104},{96,64},{104,8},{1,9... | collective-permute-start | bytes 1572872 | tf_op jit(solution)/shard_map/ppermute | solution.py:225
  86.1 17.0 %collective-permute-start.22 = (bf16[256,1024]{1,0:T(8,128)(2,1)S(1)}, bf16[256,1024]{1,0:T(8,128)(2,1)S(1)}, u32[]{:S(2)}, u32[]{:S(2)}) collective-permute-start(bf16[256,1024]{1,0:T(8,128)(2,1)S(1)} %add_convert_fusion.4), channel_id=1, source_target_pairs={{0,32},{8,104},{32,64},{40,8},{64,96},{72,40},{96,0},{104,72},{1,3... | collective-permute-start | bytes 1572872 | tf_op jit(solution)/shard_map/ppermute | solution.py:225
  94.4 13.1 %collective-permute-start.18 = (bf16[256,1024]{1,0:T(8,128)(2,1)S(1)}, bf16[256,1024]{1,0:T(8,128)(2,1)S(1)}, u32[]{:S(2)}, u32[]{:S(2)}) collective-permute-start(bf16[256,1024]{1,0:T(8,128)(2,1)S(1)} %add_convert_fusion.3), channel_id=1, source_target_pairs={{0,1},{8,11},{1,2},{9,8},{2,3},{10,9},{3,0},{11,10},{4,5},{12,15},... | collective-permute-start | bytes 1572872 | tf_op jit(solution)/shard_map/ppermute | solution.py:228
  103.3 12.6 %collective-permute-start.24 = (bf16[256,1024]{1,0:T(8,128)(2,1)S(1)}, bf16[256,1024]{1,0:T(8,128)(2,1)S(1)}, u32[]{:S(2)}, u32[]{:S(2)}) collective-permute-start(bf16[256,1024]{1,0:T(8,128)(2,1)S(1)} %add_convert_fusion.1), channel_id=1, source_target_pairs={{0,16},{16,0},{1,17},{17,1},{2,18},{18,2},{3,19},{19,3},{4,20},{20... | collective-permute-start | bytes 1572872 | tf_op jit(solution)/shard_map/ppermute | solution.py:231
  107.3 10.5 %collective-permute-start.23 = (bf16[256,1024]{1,0:T(8,128)(2,1)S(1)}, bf16[256,1024]{1,0:T(8,128)(2,1)S(1)}, u32[]{:S(2)}, u32[]{:S(2)}) collective-permute-start(bf16[256,1024]{1,0:T(8,128)(2,1)S(1)} %add_convert_fusion), channel_id=1, source_target_pairs={{0,32},{8,104},{32,64},{40,8},{64,96},{72,40},{96,0},{104,72},{1,3... | collective-permute-start | bytes 1572872 | tf_op jit(solution)/shard_map/ppermute | solution.py:225
  107.5 11.6 %collective-permute-start.9 = (bf16[128,1024]{1,0:T(8,128)(2,1)S(1)}, bf16[128,1024]{1,0:T(8,128)(2,1)S(1)}, u32[]{:S(2)}, u32[]{:S(2)}) collective-permute-start(bf16[128,1024]{1,0:T(8,128)(2,1)S(1)} %get-tuple-element.68), channel_id=1, source_target_pairs={{0,8},{8,0},{1,9},{9,1},{2,10},{10,2},{3,11},{11,3},{4,12},{12,4},... | collective-permute-start | bytes 786440 | tf_op jit(solution)/shard_map/ppermute | solution.py:234
  107.9 11.2 %collective-permute-start.19 = (bf16[128,1024]{1,0:T(8,128)(2,1)S(1)}, bf16[128,1024]{1,0:T(8,128)(2,1)S(1)}, u32[]{:S(2)}, u32[]{:S(2)}) collective-permute-start(bf16[128,1024]{1,0:T(8,128)(2,1)S(1)} %get-tuple-element.66), channel_id=1, source_target_pairs={{0,8},{8,0},{1,9},{9,1},{2,10},{10,2},{3,11},{11,3},{4,12},{12,4},... | collective-permute-start | bytes 786440 | tf_op jit(solution)/shard_map/ppermute | solution.py:234
  (3 other events, 2.6 us)

commit v10 on v9

--- a/solution.py
+++ b/solution.py
@@ -280,14 +280,17 @@
     sums_o = dw_terms(at_o, activations, act_got, mine, after(theirs, forward_p, next_dx_o))
     next_p, back_p = nearer(step_x, sums_p, sums_o[0])
     far_p = step_x(forward_p)
-    terms_p = dx_terms(at_y, mine, after(theirs, *sums_o, next_p), (w_z, *near_p, far_p))
     dx_o = add(terms_o[3], back_dx_o, step_y(next_dx_o)).astype(BF16)
+    terms_p = dx_terms(
+        at_y, mine, after(theirs, *sums_o, next_p, dx_o), (w_z, *near_p, far_p)
+    )
     whole_p = add(sums_p[3], back_p, step_x(next_p)).astype(BF16)
-    next_o, back_o = nearer(step_x, sums_o, terms_p[0], whole_p)
+    next_o, back_o = nearer(step_x, sums_o, whole_p)
     cross = swap_zh(whole_p)
-    next_dx_p, back_dx_p = nearer(step_y, terms_p)
-    dx_p = add(terms_p[3], back_dx_p, step_y(next_dx_p)).astype(BF16)
+    next_dx_p, back_dx_p = nearer(step_y, terms_p, next_o, whole_p)
     weight_grad = add(sums_o[3], back_o, step_x(next_o), cross)
+    last = after(step_y(next_dx_p), weight_grad)
+    dx_p = add(terms_p[3], back_dx_p, last).astype(BF16)
 
     half = dx_o.shape[0] // 2
     got_o, got_p = swap_core(dx_o[half:]), swap_core(dx_p[half:])

time: 121 us -> 114 us (0.942); the launches traced: 121 us -> 113 us
  waiting for transfers between devices: 53 us -> 43.9 us
    ppermute x2, waiting for transfers between devices: 7.47 us -> 1.07 us  [swap_zh(): return lax.ppermute(value, 'zh', SWAP)]
    ppermute x8, waiting for transfers between devices: 23.7 us -> 20.6 us  [step_x(): return lax.ppermute(value, ('x', 'core'), by_core(NX, way, False))]
    ppermute x2, waiting for transfers between devices: 7.76 us -> 6.18 us  [neighbours(): lax.ppermute(piece, 'x', by_x(1))]
    ppermute x4, waiting for transfers between devices: 0.01 us -> 1.45 us  [swap_core(): return lax.ppermute(value, 'core', SWAP)]
    reshape x1 -> x0, other arithmetic: 1.3 us -> none  [local(): return (input_grad, weight_grad.reshape(weight.shape))]
    add x0 -> x1, other arithmetic: none -> 1.3 us  [add(): total = total + t.astype(F32)]
    unnamed x20 -> x22, local copies, waits for them, and re-layouts: 3.8 us -> 4.81 us
  transfers between devices with their start and end apart: 25 -> 25, of which waited for: 13 -> 14; matrix products, arithmetic and copies ran while one was open for 9% -> 9% of each run, Pallas kernels for 18% -> 19%
where the time goes in v10:
time: 114 us; the launch traced here: 113 us
  waiting for transfers between devices  43.9 us (39%)
  starting transfers between devices  29.1 us (26%)
  Pallas kernels  23.4 us (21%)
  other arithmetic  10.1 us (9%)
  local copies, waits for them, and re-layouts  5.05 us (4%)
    ppermute x8, waiting for transfers between devices, step_x(): return lax.ppermute(value, ('x', 'core'), by_core(NX, way, False))  20.6 us
    pallas_call x2, Pallas kernels, dw_terms(): pl.pallas_call(dw_body, out_shape=outs, in_specs=[SMEM, HBM, *[vmem] * 3]...  10.7 us
    ppermute x6, waiting for transfers between devices, step_y(): return lax.ppermute(value, ('core', 'outc'), by_core(NY, way, True))  9.05 us
    pallas_call x2, Pallas kernels, dx_terms(): pl.pallas_call(dx_body, out_shape=outs, in_specs=[pl.BlockSpec(memory_spa...  8.54 us
    ppermute x2, starting transfers between devices, swap_zh(): return lax.ppermute(value, 'zh', SWAP)  7.53 us
    ppermute x6, starting transfers between devices, step_y(): return lax.ppermute(value, ('core', 'outc'), by_core(NY, way, True))  7.32 us
    ppermute x2, waiting for transfers between devices, neighbours(): lax.ppermute(piece, 'x', by_x(1))  6.18 us
    ppermute x2, starting transfers between devices, neighbours(): lax.ppermute(piece, 'x', by_x(-1))  4.9 us
  transfers between devices with their start and end apart: 25, of which 14 were waited for; matrix products, arithmetic and copies ran while one was open for 9% of the time, Pallas kernels for 19%

profile of v10, /device:TPU:0, one launch (start us, length us, event | category | flops | bytes accessed | tf_op | source)
XLA Modules:
  0.0 112.5 jit_solution(3142616756581229797)
XLA Ops:
  0.6 1.6 %collective-permute-start.1 = (bf16[256,1024]{1,0:T(8,128)(2,1)}, bf16[256,1024]{1,0:T(8,128)(2,1)S(1)}, u32[]{:S(2)}, u32[]{:S(2)}) collective-permute-start(bf16[256,1024]{1,0:T(8,128)(2,1)} %bitcast.17), channel_id=1, source_target_pairs={{0,32},{32,64},{64,96},{96,0},{1,33},{33,65},{65,97},{97,1},{2,34}... | collective-permute-start | bytes 1572872 | tf_op jit(solution)/shard_map/ppermute | solution.py:237
  2.3 1.7 %collective-permute-start.2 = (bf16[256,1024]{1,0:T(8,128)(2,1)}, bf16[256,1024]{1,0:T(8,128)(2,1)S(1)}, u32[]{:S(2)}, u32[]{:S(2)}) collective-permute-start(bf16[256,1024]{1,0:T(8,128)(2,1)} %bitcast.18), channel_id=1, source_target_pairs={{0,96},{32,0},{64,32},{96,64},{1,97},{33,1},{65,33},{97,65},{2,98}... | collective-permute-start | bytes 1572872 | tf_op jit(solution)/shard_map/ppermute | solution.py:237
  3.9 2.5 %other_columns.1 = bf16[8,2,256,256]{3,2,1,0:T(8,128)(2,1)} custom-call(s32[1]{0:T(128)} %bitcast.2.core, bf16[2,256,4096]{2,1,0:T(8,128)(2,1)} %act.3), custom_call_target="tpu_custom_call" | custom-call | bytes 6291456 | tf_op jit(solution)/shard_map/other_columns/pallas_call | solution.py:61
  7.5 2.0 %collective-permute-start = (bf16[2,128,1024]{2,1,0:T(8,128)(2,1)}, bf16[2,128,1024]{2,1,0:T(8,128)(2,1)}, u32[]{:S(2)}, u32[]{:S(2)}) collective-permute-start(bf16[2,128,1024]{2,1,0:T(8,128)(2,1)} %subtract_convert_fusion), channel_id=1, source_target_pairs={{0,4},{4,0},{1,5},{5,1},{2,6},{6,2},{3,7},{7,3},{8,12},{12,8},{9,1... | collective-permute-start | bytes 1572872 | tf_op jit(solution)/shard_map/ppermute | solution.py:251
  9.5 6.2 %collective-permute-done.1.refs_1_ = bf16[256,1024]{1,0:T(8,128)(2,1)S(1)} collective-permute-done((bf16[256,1024]{1,0:T(8,128)(2,1)}, bf16[256,1024]{1,0:T(8,128)(2,1)S(1)}, u32[]{:S(2)}, u32[]{:S(2)}) %collective-permute-start.1) | collective-permute-done | bytes 524320 | tf_op jit(solution)/shard_map/ppermute | solution.py:237
  16.8 4.3 %collective-permute-done = bf16[2,128,1024]{2,1,0:T(8,128)(2,1)} collective-permute-done((bf16[2,128,1024]{2,1,0:T(8,128)(2,1)}, bf16[2,128,1024]{2,1,0:T(8,128)(2,1)}, u32[]{:S(2)}, u32[]{:S(2)}) %collective-permute-start) | collective-permute-done | bytes 524320 | tf_op jit(solution)/shard_map/ppermute | solution.py:251
  21.2 2.0 %maximum_select_fusion.mine = bf16[2,256,1024]{2,1,0:T(8,128)(2,1)S(1)} fusion(bf16[2,128,1024]{2,1,0:T(8,128)(2,1)} %collective-permute-done, bf16[2,128,1024]{2,1,0:T(8,128)(2,1)} %subtract_convert_fusion, pred[]{:T(512)S(6)} %eq.7), kind=kLoop, calls=%fused_computation | loop fusion | flops 4718592 | bytes 2097153 | tf_op jit(solution)/shard_map/jit(_where)/select_n | solution.py:257
  23.7 3.7 %collective-permute-start.10 = (bf16[256,1024]{1,0:T(8,128)(2,1)}, bf16[256,1024]{1,0:T(8,128)(2,1)}, u32[]{:S(2)}, u32[]{:S(2)}) collective-permute-start(bf16[256,1024]{1,0:T(8,128)(2,1)} %bitcast.19), channel_id=1, source_target_pairs={{0,16},{16,0},{1,17},{17,1},{2,18},{18,2},{3,19},{19,3},{4,20},{20... | collective-permute-start | bytes 1572872 | tf_op jit(solution)/shard_map/ppermute | solution.py:231
  27.4 6.6 %collective-permute-done.4.refs_3_ = bf16[256,1024]{1,0:T(8,128)(2,1)} collective-permute-done((bf16[256,1024]{1,0:T(8,128)(2,1)}, bf16[256,1024]{1,0:T(8,128)(2,1)}, u32[]{:S(2)}, u32[]{:S(2)}) %collective-permute-start.4) | collective-permute-done | bytes 524320 | tf_op jit(solution)/shard_map/ppermute | solution.py:225
  37.2 4.5 %dx_terms.2 = (bf16[256,1024]{1,0:T(8,128)(2,1)}, bf16[256,1024]{1,0:T(8,128)(2,1)}, bf16[256,1024]{1,0:T(8,128)(2,1)S(1)}, bf16[256,1024]{1,0:T(8,128)(2,1)S(1)}) custom-call(s32[4]{0:T(128)S(1)} %pad_add_fusion.1.at, bf16[2,256,1024]{2,1,0:T(8,128)(2,1)S(1)} %maximum_select_fusion.mine, bf16[2,256,1024]{2,1,0:T(8,128)(2,1)} %collective-permute-done.3.theirs, ...), custom_call_target="tpu_custom_call" | custom-call | flops 2147483648 | bytes 6291456 | tf_op jit(solution)/shard_map/dx_terms/pallas_call | solution.py:151
  43.3 1.6 %collective-permute-start.5 = (bf16[256,1024]{1,0:T(8,128)(2,1)}, bf16[256,1024]{1,0:T(8,128)(2,1)}, u32[]{:S(2)}, u32[]{:S(2)}) collective-permute-start(bf16[256,1024]{1,0:T(8,128)(2,1)} %get-tuple-element.38), channel_id=1, source_target_pairs={{0,1},{8,11},{1,2},{9,8},{2,3},{10,9},{3,0},{11,10},{4,5},{12,15},... | collective-permute-start | bytes 1572872 | tf_op jit(solution)/shard_map/ppermute | solution.py:228
  44.9 1.7 %collective-permute-start.6 = (bf16[256,1024]{1,0:T(8,128)(2,1)}, bf16[256,1024]{1,0:T(8,128)(2,1)}, u32[]{:S(2)}, u32[]{:S(2)}) collective-permute-start(bf16[256,1024]{1,0:T(8,128)(2,1)} %get-tuple-element.39), channel_id=1, source_target_pairs={{0,3},{8,9},{1,0},{9,10},{2,1},{10,11},{3,2},{11,8},{4,7},{12,13},... | collective-permute-start | bytes 1572872 | tf_op jit(solution)/shard_map/ppermute | solution.py:228
  46.6 3.2 %collective-permute-start.12 = (bf16[256,1024]{1,0:T(8,128)(2,1)}, bf16[256,1024]{1,0:T(8,128)(2,1)}, u32[]{:S(2)}, u32[]{:S(2)}) collective-permute-start(bf16[256,1024]{1,0:T(8,128)(2,1)} %collective-permute-done.10.refs_0_), channel_id=1, source_target_pairs={{0,96},{32,0},{64,32},{96,64},{1,97},{33,1},{65,33},{97,65},{2,98}... | collective-permute-start | bytes 1572872 | tf_op jit(solution)/shard_map/ppermute | solution.py:237
  50.0 5.4 %dw_terms.2 = (bf16[256,1024]{1,0:T(8,128)(2,1)S(1)}, bf16[256,1024]{1,0:T(8,128)(2,1)S(1)}, bf16[256,1024]{1,0:T(8,128)(2,1)S(1)}, bf16[256,1024]{1,0:T(8,128)(2,1)S(1)}) custom-call(s32[5]{0:T(128)S(1)} %stack.72.at, bf16[2,256,4096]{2,1,0:T(8,128)(2,1)} %act.3, bf16[8,2,256,256]{3,2,1,0:T(8,128)(2,1)S(1)} %collective-permute-done.7.got, ...), custom_call_target="tpu_custom_call" | custom-call | flops 2147483648 | bytes 6291456 | tf_op jit(solution)/shard_map/dw_terms/pallas_call | solution.py:110
  55.4 4.1 %collective-permute-done.5 = bf16[256,1024]{1,0:T(8,128)(2,1)} collective-permute-done((bf16[256,1024]{1,0:T(8,128)(2,1)}, bf16[256,1024]{1,0:T(8,128)(2,1)}, u32[]{:S(2)}, u32[]{:S(2)}) %collective-permute-start.5) | collective-permute-done | bytes 524320 | tf_op jit(solution)/shard_map/ppermute | solution.py:228
  59.5 1.2 %add_convert_fusion.6 = bf16[256,1024]{1,0:T(8,128)(2,1)S(1)} fusion(bf16[256,1024]{1,0:T(8,128)(2,1)} %collective-permute-done.5, bf16[256,1024]{1,0:T(8,128)(2,1)S(1)} %copy-done.1), kind=kLoop, calls=%fused_computation.8 | loop fusion | flops 1048576 | bytes 1572864 | tf_op jit(solution)/shard_map/convert_element_type | solution.py:273
  64.3 5.3 %dw_terms.3 = (bf16[256,1024]{1,0:T(8,128)(2,1)S(1)}, bf16[256,1024]{1,0:T(8,128)(2,1)S(1)}, bf16[256,1024]{1,0:T(8,128)(2,1)S(1)}, bf16[256,1024]{1,0:T(8,128)(2,1)S(1)}) custom-call(s32[5]{0:T(128)S(1)} %stack.77.at, bf16[2,256,4096]{2,1,0:T(8,128)(2,1)} %act.3, bf16[8,2,256,256]{3,2,1,0:T(8,128)(2,1)S(1)} %collective-permute-done.7.got, ...), custom_call_target="tpu_custom_call" | custom-call | flops 2147483648 | bytes 6291456 | tf_op jit(solution)/shard_map/dw_terms/pallas_call | solution.py:110
  69.6 4.8 %collective-permute-done.14 = bf16[256,1024]{1,0:T(8,128)(2,1)S(1)} collective-permute-done((bf16[256,1024]{1,0:T(8,128)(2,1)S(1)}, bf16[256,1024]{1,0:T(8,128)(2,1)S(1)}, u32[]{:S(2)}, u32[]{:S(2)}) %collective-permute-start.14) | collective-permute-done | bytes 524320 | tf_op jit(solution)/shard_map/ppermute | solution.py:225
  74.7 1.1 %collective-permute-start.18 = (bf16[256,1024]{1,0:T(8,128)(2,1)S(1)}, bf16[256,1024]{1,0:T(8,128)(2,1)S(1)}, u32[]{:S(2)}, u32[]{:S(2)}) collective-permute-start(bf16[256,1024]{1,0:T(8,128)(2,1)S(1)} %get-tuple-element.49), channel_id=1, source_target_pairs={{0,32},{8,104},{32,64},{40,8},{64,96},{72,40},{96,0},{104,72},{1,3... | collective-permute-start | bytes 1572872 | tf_op jit(solution)/shard_map/ppermute | solution.py:225
  75.8 2.2 %collective-permute-start.19 = (bf16[256,1024]{1,0:T(8,128)(2,1)S(1)}, bf16[256,1024]{1,0:T(8,128)(2,1)S(1)}, u32[]{:S(2)}, u32[]{:S(2)}) collective-permute-start(bf16[256,1024]{1,0:T(8,128)(2,1)S(1)} %get-tuple-element.50), channel_id=1, source_target_pairs={{0,96},{8,40},{32,0},{40,72},{64,32},{72,104},{96,64},{104,8},{1,9... | collective-permute-start | bytes 1572872 | tf_op jit(solution)/shard_map/ppermute | solution.py:225
  78.0 1.3 %add_convert_fusion.5 = bf16[256,1024]{1,0:T(8,128)(2,1)S(1)} fusion(bf16[256,1024]{1,0:T(8,128)(2,1)S(1)} %collective-permute-done.8, bf16[256,1024]{1,0:T(8,128)(2,1)} %collective-permute-done.6, bf16[256,1024]{1,0:T(8,128)(2,1)S(1)} %copy-done.7), kind=kLoop, calls=%fused_computation.7 | loop fusion | flops 1572864 | bytes 2097152 | tf_op jit(solution)/shard_map/convert_element_type | solution.py:283
  79.3 4.0 %dx_terms.3 = (bf16[256,1024]{1,0:T(8,128)(2,1)S(1)}, bf16[256,1024]{1,0:T(8,128)(2,1)S(1)}, bf16[256,1024]{1,0:T(8,128)(2,1)S(1)}, bf16[256,1024]{1,0:T(8,128)(2,1)S(1)}) custom-call(s32[4]{0:T(128)S(1)} %pad_add_fusion.1.at, bf16[2,256,1024]{2,1,0:T(8,128)(2,1)S(1)} %maximum_select_fusion.mine, bf16[2,256,1024]{2,1,0:T(8,128)(2,1)} %collective-permute-done.3.theirs, ...), custom_call_target="tpu_custom_call" | custom-call | flops 2147483648 | bytes 6291456 | tf_op jit(solution)/shard_map/dx_terms/pallas_call | solution.py:151
  83.4 3.2 %collective-permute-start.17 = (bf16[256,1024]{1,0:T(8,128)(2,1)S(1)}, bf16[256,1024]{1,0:T(8,128)(2,1)S(1)}, u32[]{:S(2)}, u32[]{:S(2)}) collective-permute-start(bf16[256,1024]{1,0:T(8,128)(2,1)S(1)} %get-tuple-element.59), channel_id=1, source_target_pairs={{0,3},{8,9},{1,0},{9,10},{2,1},{10,11},{3,2},{11,8},{4,7},{12,13},... | collective-permute-start | bytes 1572872 | tf_op jit(solution)/shard_map/ppermute | solution.py:228
  86.7 2.7 %collective-permute-done.20 = bf16[256,1024]{1,0:T(8,128)(2,1)S(1)} collective-permute-done((bf16[256,1024]{1,0:T(8,128)(2,1)S(1)}, bf16[256,1024]{1,0:T(8,128)(2,1)S(1)}, u32[]{:S(2)}, u32[]{:S(2)}) %collective-permute-start.20) | collective-permute-done | bytes 524320 | tf_op jit(solution)/shard_map/ppermute | solution.py:225
  89.6 3.8 %collective-permute-start.23 = (bf16[256,1024]{1,0:T(8,128)(2,1)S(1)}, bf16[256,1024]{1,0:T(8,128)(2,1)S(1)}, u32[]{:S(2)}, u32[]{:S(2)}) collective-permute-start(bf16[256,1024]{1,0:T(8,128)(2,1)S(1)} %add_convert_fusion.3), channel_id=1, source_target_pairs={{0,16},{16,0},{1,17},{17,1},{2,18},{18,2},{3,19},{19,3},{4,20},{20... | collective-permute-start | bytes 1572872 | tf_op jit(solution)/shard_map/ppermute | solution.py:231
  93.4 1.5 %collective-permute-done.18 = bf16[256,1024]{1,0:T(8,128)(2,1)S(1)} collective-permute-done((bf16[256,1024]{1,0:T(8,128)(2,1)S(1)}, bf16[256,1024]{1,0:T(8,128)(2,1)S(1)}, u32[]{:S(2)}, u32[]{:S(2)}) %collective-permute-start.18) | collective-permute-done | bytes 524320 | tf_op jit(solution)/shard_map/ppermute | solution.py:225
  95.3 2.9 %collective-permute-done.16 = bf16[256,1024]{1,0:T(8,128)(2,1)S(1)} collective-permute-done((bf16[256,1024]{1,0:T(8,128)(2,1)S(1)}, bf16[256,1024]{1,0:T(8,128)(2,1)S(1)}, u32[]{:S(2)}, u32[]{:S(2)}) %collective-permute-start.16) | collective-permute-done | bytes 524320 | tf_op jit(solution)/shard_map/ppermute | solution.py:228
  100.6 5.0 %collective-permute-done.22 = bf16[256,1024]{1,0:T(8,128)(2,1)S(1)} collective-permute-done((bf16[256,1024]{1,0:T(8,128)(2,1)S(1)}, bf16[256,1024]{1,0:T(8,128)(2,1)S(1)}, u32[]{:S(2)}, u32[]{:S(2)}) %collective-permute-start.22) | collective-permute-done | bytes 524320 | tf_op jit(solution)/shard_map/ppermute | solution.py:225
  105.6 1.3 %convert_add_fusion = f32[256,1024]{1,0:T(8,128)} fusion(bf16[256,1024]{1,0:T(8,128)(2,1)S(1)} %collective-permute-done.23, bf16[256,1024]{1,0:T(8,128)(2,1)S(1)} %collective-permute-done.22, bf16[256,1024]{1,0:T(8,128)(2,1)S(1)} %collective-permute-done.19, bf16[256,1024]{1,0:T(8,128)(2,1)S(1)} %get-tuple-element.52), kind=kLoop, calls=%fused_computation.2 | loop fusion | flops 1835008 | bytes 3145728 | tf_op jit(solution)/shard_map/add | solution.py:267
  106.9 2.0 %collective-permute-done.21 = bf16[256,1024]{1,0:T(8,128)(2,1)S(1)} collective-permute-done((bf16[256,1024]{1,0:T(8,128)(2,1)S(1)}, bf16[256,1024]{1,0:T(8,128)(2,1)S(1)}, u32[]{:S(2)}, u32[]{:S(2)}) %collective-permute-start.21) | collective-permute-done | bytes 524320 | tf_op jit(solution)/shard_map/ppermute | solution.py:228
  109.4 1.4 %collective-permute-done.24.got_p = bf16[128,1024]{1,0:T(8,128)(2,1)S(1)} collective-permute-done((bf16[128,1024]{1,0:T(8,128)(2,1)S(1)}, bf16[128,1024]{1,0:T(8,128)(2,1)S(1)}, u32[]{:S(2)}, u32[]{:S(2)}) %collective-permute-start.24) | collective-permute-done | bytes 262176 | tf_op jit(solution)/shard_map/ppermute | solution.py:234
  110.9 1.7 %place.1 = bf16[2,64,4096]{2,1,0:T(8,128)(2,1)} custom-call(s32[3]{0:T(128)S(1)} %pad_add_fusion.at, bf16[128,1024]{1,0:T(8,128)(2,1)S(1)} %get-tuple-element.71.keep_o, bf16[128,1024]{1,0:T(8,128)(2,1)S(1)} %collective-permute-done.9.got_o, bf16[128,1024]{1,0:T(8,128)(2,1)S(1)} %get-tuple-element.69.keep_p, bf16[128,1024]{1,0:T(8,128)(2,1)S(1)} %collective-permute-done.24.got_p), custom_call_target="tpu_custom_call" | custom-call | bytes 2097152 | tf_op jit(solution)/shard_map/place/pallas_call | solution.py:186
  (64 shorter events, 14.9 us)
Async XLA Ops:
  0.6 15.0 %collective-permute-start.1 = (bf16[256,1024]{1,0:T(8,128)(2,1)}, bf16[256,1024]{1,0:T(8,128)(2,1)S(1)}, u32[]{:S(2)}, u32[]{:S(2)}) collective-permute-start(bf16[256,1024]{1,0:T(8,128)(2,1)} %bitcast.17), channel_id=1, source_target_pairs={{0,32},{32,64},{64,96},{96,0},{1,33},{33,65},{65,97},{97,1},{2,34}... | collective-permute-start | bytes 1572872 | tf_op jit(solution)/shard_map/ppermute | solution.py:237
  2.3 13.6 %collective-permute-start.2 = (bf16[256,1024]{1,0:T(8,128)(2,1)}, bf16[256,1024]{1,0:T(8,128)(2,1)S(1)}, u32[]{:S(2)}, u32[]{:S(2)}) collective-permute-start(bf16[256,1024]{1,0:T(8,128)(2,1)} %bitcast.18), channel_id=1, source_target_pairs={{0,96},{32,0},{64,32},{96,64},{1,97},{33,1},{65,33},{97,65},{2,98}... | collective-permute-start | bytes 1572872 | tf_op jit(solution)/shard_map/ppermute | solution.py:237
  3.9 2.5 %copy-start.9 = (bf16[2,128,1024]{2,1,0:T(8,128)(2,1)S(1)}, bf16[2,128,1024]{2,1,0:T(8,128)(2,1)}, u32[]{:S(2)}) copy-start(bf16[2,128,1024]{2,1,0:T(8,128)(2,1)} %param.6) | copy-start | bytes 1572868
  3.9 2.6 %copy-start.10 = (bf16[2,128,1024]{2,1,0:T(8,128)(2,1)S(1)}, bf16[2,128,1024]{2,1,0:T(8,128)(2,1)}, u32[]{:S(2)}) copy-start(bf16[2,128,1024]{2,1,0:T(8,128)(2,1)} %param.5) | copy-start | bytes 1572868
  7.5 13.7 %collective-permute-start = (bf16[2,128,1024]{2,1,0:T(8,128)(2,1)}, bf16[2,128,1024]{2,1,0:T(8,128)(2,1)}, u32[]{:S(2)}, u32[]{:S(2)}) collective-permute-start(bf16[2,128,1024]{2,1,0:T(8,128)(2,1)} %subtract_convert_fusion), channel_id=1, source_target_pairs={{0,4},{4,0},{1,5},{5,1},{2,6},{6,2},{3,7},{7,3},{8,12},{12,8},{9,1... | collective-permute-start | bytes 1572872 | tf_op jit(solution)/shard_map/ppermute | solution.py:251
  9.5 40.5 %collective-permute-start.7 = (bf16[8,2,256,256]{3,2,1,0:T(8,128)(2,1)}, bf16[8,2,256,256]{3,2,1,0:T(8,128)(2,1)S(1)}, u32[]{:S(2)}, u32[]{:S(2)}) collective-permute-start(bf16[8,2,256,256]{3,2,1,0:T(8,128)(2,1)} %other_columns.1), channel_id=1, source_target_pairs={{0,8},{8,0},{1,9},{9,1},{2,10},{10,2},{3,11},{11,3},{4,12},{12,4},... | collective-permute-start | bytes 6291464 | tf_op jit(solution)/shard_map/ppermute | solution.py:234
  15.7 1.1 copy-start.2
  23.2 10.9 %collective-permute-start.3 = (bf16[2,256,1024]{2,1,0:T(8,128)(2,1)S(1)}, bf16[2,256,1024]{2,1,0:T(8,128)(2,1)}, u32[]{:S(2)}, u32[]{:S(2)}) collective-permute-start(bf16[2,256,1024]{2,1,0:T(8,128)(2,1)S(1)} %maximum_select_fusion.mine), channel_id=1, source_target_pairs={{0,8},{8,0},{1,9},{9,1},{2,10},{10,2},{3,11},{11,3},{4,12},{12,4},... | collective-permute-start | bytes 3145736 | tf_op jit(solution)/shard_map/ppermute | solution.py:234
  23.3 10.8 %collective-permute-start.4 = (bf16[256,1024]{1,0:T(8,128)(2,1)}, bf16[256,1024]{1,0:T(8,128)(2,1)}, u32[]{:S(2)}, u32[]{:S(2)}) collective-permute-start(bf16[256,1024]{1,0:T(8,128)(2,1)} %broadcast_select_fusion.1), channel_id=1, source_target_pairs={{0,32},{8,104},{32,64},{40,8},{64,96},{72,40},{96,0},{104,72},{1,3... | collective-permute-start | bytes 1572872 | tf_op jit(solution)/shard_map/ppermute | solution.py:225
  23.7 22.9 %collective-permute-start.10 = (bf16[256,1024]{1,0:T(8,128)(2,1)}, bf16[256,1024]{1,0:T(8,128)(2,1)}, u32[]{:S(2)}, u32[]{:S(2)}) collective-permute-start(bf16[256,1024]{1,0:T(8,128)(2,1)} %bitcast.19), channel_id=1, source_target_pairs={{0,16},{16,0},{1,17},{17,1},{2,18},{18,2},{3,19},{19,3},{4,20},{20... | collective-permute-start | bytes 1572872 | tf_op jit(solution)/shard_map/ppermute | solution.py:231
  34.1 1.0 copy-start.3
  35.1 1.0 copy-start.5
  43.3 16.2 %collective-permute-start.5 = (bf16[256,1024]{1,0:T(8,128)(2,1)}, bf16[256,1024]{1,0:T(8,128)(2,1)}, u32[]{:S(2)}, u32[]{:S(2)}) collective-permute-start(bf16[256,1024]{1,0:T(8,128)(2,1)} %get-tuple-element.38), channel_id=1, source_target_pairs={{0,1},{8,11},{1,2},{9,8},{2,3},{10,9},{3,0},{11,10},{4,5},{12,15},... | collective-permute-start | bytes 1572872 | tf_op jit(solution)/shard_map/ppermute | solution.py:228
  44.9 14.6 %collective-permute-start.6 = (bf16[256,1024]{1,0:T(8,128)(2,1)}, bf16[256,1024]{1,0:T(8,128)(2,1)}, u32[]{:S(2)}, u32[]{:S(2)}) collective-permute-start(bf16[256,1024]{1,0:T(8,128)(2,1)} %get-tuple-element.39), channel_id=1, source_target_pairs={{0,3},{8,9},{1,0},{9,10},{2,1},{10,11},{3,2},{11,8},{4,7},{12,13},... | collective-permute-start | bytes 1572872 | tf_op jit(solution)/shard_map/ppermute | solution.py:228
  46.6 14.9 %collective-permute-start.11 = (bf16[256,1024]{1,0:T(8,128)(2,1)}, bf16[256,1024]{1,0:T(8,128)(2,1)}, u32[]{:S(2)}, u32[]{:S(2)}) collective-permute-start(bf16[256,1024]{1,0:T(8,128)(2,1)} %collective-permute-done.10.refs_0_), channel_id=1, source_target_pairs={{0,32},{32,64},{64,96},{96,0},{1,33},{33,65},{65,97},{97,1},{2,34}... | collective-permute-start | bytes 1572872 | tf_op jit(solution)/shard_map/ppermute | solution.py:237
  46.6 15.9 %collective-permute-start.12 = (bf16[256,1024]{1,0:T(8,128)(2,1)}, bf16[256,1024]{1,0:T(8,128)(2,1)}, u32[]{:S(2)}, u32[]{:S(2)}) collective-permute-start(bf16[256,1024]{1,0:T(8,128)(2,1)} %collective-permute-done.10.refs_0_), channel_id=1, source_target_pairs={{0,96},{32,0},{64,32},{96,64},{1,97},{33,1},{65,33},{97,65},{2,98}... | collective-permute-start | bytes 1572872 | tf_op jit(solution)/shard_map/ppermute | solution.py:237
  50.0 9.6 %copy-start.1 = (bf16[256,1024]{1,0:T(8,128)(2,1)S(1)}, bf16[256,1024]{1,0:T(8,128)(2,1)}, u32[]{:S(2)}) copy-start(bf16[256,1024]{1,0:T(8,128)(2,1)} %copy-done) | copy-start | bytes 1572868
  55.4 14.2 %collective-permute-start.13 = (bf16[256,1024]{1,0:T(8,128)(2,1)S(1)}, bf16[256,1024]{1,0:T(8,128)(2,1)S(1)}, u32[]{:S(2)}, u32[]{:S(2)}) collective-permute-start(bf16[256,1024]{1,0:T(8,128)(2,1)S(1)} %get-tuple-element.42), channel_id=1, source_target_pairs={{0,32},{8,104},{32,64},{40,8},{64,96},{72,40},{96,0},{104,72},{1,3... | collective-permute-start | bytes 1572872 | tf_op jit(solution)/shard_map/ppermute | solution.py:225
  59.5 14.9 %collective-permute-start.14 = (bf16[256,1024]{1,0:T(8,128)(2,1)S(1)}, bf16[256,1024]{1,0:T(8,128)(2,1)S(1)}, u32[]{:S(2)}, u32[]{:S(2)}) collective-permute-start(bf16[256,1024]{1,0:T(8,128)(2,1)S(1)} %get-tuple-element.54), channel_id=1, source_target_pairs={{0,96},{8,40},{32,0},{40,72},{64,32},{72,104},{96,64},{104,8},{1,9... | collective-permute-start | bytes 1572872 | tf_op jit(solution)/shard_map/ppermute | solution.py:225
  60.8 17.2 %collective-permute-start.8 = (bf16[256,1024]{1,0:T(8,128)(2,1)S(1)}, bf16[256,1024]{1,0:T(8,128)(2,1)S(1)}, u32[]{:S(2)}, u32[]{:S(2)}) collective-permute-start(bf16[256,1024]{1,0:T(8,128)(2,1)S(1)} %add_convert_fusion.6), channel_id=1, source_target_pairs={{0,1},{8,11},{1,2},{9,8},{2,3},{10,9},{3,0},{11,10},{4,5},{12,15},... | collective-permute-start | bytes 1572872 | tf_op jit(solution)/shard_map/ppermute | solution.py:228
  63.6 14.4 %copy-start.7 = (bf16[256,1024]{1,0:T(8,128)(2,1)S(1)}, bf16[256,1024]{1,0:T(8,128)(2,1)}, u32[]{:S(2)}) copy-start(bf16[256,1024]{1,0:T(8,128)(2,1)} %copy-done.6) | copy-start | bytes 1572868
  63.6 15.7 %collective-permute-start.15 = (bf16[256,1024]{1,0:T(8,128)(2,1)S(1)}, bf16[256,1024]{1,0:T(8,128)(2,1)S(1)}, u32[]{:S(2)}, u32[]{:S(2)}) collective-permute-start(bf16[256,1024]{1,0:T(8,128)(2,1)S(1)} %broadcast_select_fusion), channel_id=1, source_target_pairs={{0,32},{8,104},{32,64},{40,8},{64,96},{72,40},{96,0},{104,72},{1,3... | collective-permute-start | bytes 1572872 | tf_op jit(solution)/shard_map/ppermute | solution.py:225
  74.6 14.7 %collective-permute-start.20 = (bf16[256,1024]{1,0:T(8,128)(2,1)S(1)}, bf16[256,1024]{1,0:T(8,128)(2,1)S(1)}, u32[]{:S(2)}, u32[]{:S(2)}) collective-permute-start(bf16[256,1024]{1,0:T(8,128)(2,1)S(1)} %add_convert_fusion.4), channel_id=1, source_target_pairs={{0,32},{8,104},{32,64},{40,8},{64,96},{72,40},{96,0},{104,72},{1,3... | collective-permute-start | bytes 1572872 | tf_op jit(solution)/shard_map/ppermute | solution.py:225
  74.7 20.3 %collective-permute-start.18 = (bf16[256,1024]{1,0:T(8,128)(2,1)S(1)}, bf16[256,1024]{1,0:T(8,128)(2,1)S(1)}, u32[]{:S(2)}, u32[]{:S(2)}) collective-permute-start(bf16[256,1024]{1,0:T(8,128)(2,1)S(1)} %get-tuple-element.49), channel_id=1, source_target_pairs={{0,32},{8,104},{32,64},{40,8},{64,96},{72,40},{96,0},{104,72},{1,3... | collective-permute-start | bytes 1572872 | tf_op jit(solution)/shard_map/ppermute | solution.py:225
  75.8 19.1 %collective-permute-start.19 = (bf16[256,1024]{1,0:T(8,128)(2,1)S(1)}, bf16[256,1024]{1,0:T(8,128)(2,1)S(1)}, u32[]{:S(2)}, u32[]{:S(2)}) collective-permute-start(bf16[256,1024]{1,0:T(8,128)(2,1)S(1)} %get-tuple-element.50), channel_id=1, source_target_pairs={{0,96},{8,40},{32,0},{40,72},{64,32},{72,104},{96,64},{104,8},{1,9... | collective-permute-start | bytes 1572872 | tf_op jit(solution)/shard_map/ppermute | solution.py:225
  83.3 14.9 %collective-permute-start.16 = (bf16[256,1024]{1,0:T(8,128)(2,1)S(1)}, bf16[256,1024]{1,0:T(8,128)(2,1)S(1)}, u32[]{:S(2)}, u32[]{:S(2)}) collective-permute-start(bf16[256,1024]{1,0:T(8,128)(2,1)S(1)} %get-tuple-element.58), channel_id=1, source_target_pairs={{0,1},{8,11},{1,2},{9,8},{2,3},{10,9},{3,0},{11,10},{4,5},{12,15},... | collective-permute-start | bytes 1572872 | tf_op jit(solution)/shard_map/ppermute | solution.py:228
  83.4 14.8 %collective-permute-start.17 = (bf16[256,1024]{1,0:T(8,128)(2,1)S(1)}, bf16[256,1024]{1,0:T(8,128)(2,1)S(1)}, u32[]{:S(2)}, u32[]{:S(2)}) collective-permute-start(bf16[256,1024]{1,0:T(8,128)(2,1)S(1)} %get-tuple-element.59), channel_id=1, source_target_pairs={{0,3},{8,9},{1,0},{9,10},{2,1},{10,11},{3,2},{11,8},{4,7},{12,13},... | collective-permute-start | bytes 1572872 | tf_op jit(solution)/shard_map/ppermute | solution.py:228
  89.6 11.0 %collective-permute-start.23 = (bf16[256,1024]{1,0:T(8,128)(2,1)S(1)}, bf16[256,1024]{1,0:T(8,128)(2,1)S(1)}, u32[]{:S(2)}, u32[]{:S(2)}) collective-permute-start(bf16[256,1024]{1,0:T(8,128)(2,1)S(1)} %add_convert_fusion.3), channel_id=1, source_target_pairs={{0,16},{16,0},{1,17},{17,1},{2,18},{18,2},{3,19},{19,3},{4,20},{20... | collective-permute-start | bytes 1572872 | tf_op jit(solution)/shard_map/ppermute | solution.py:231
  95.1 10.5 %collective-permute-start.22 = (bf16[256,1024]{1,0:T(8,128)(2,1)S(1)}, bf16[256,1024]{1,0:T(8,128)(2,1)S(1)}, u32[]{:S(2)}, u32[]{:S(2)}) collective-permute-start(bf16[256,1024]{1,0:T(8,128)(2,1)S(1)} %add_convert_fusion.2), channel_id=1, source_target_pairs={{0,32},{8,104},{32,64},{40,8},{64,96},{72,40},{96,0},{104,72},{1,3... | collective-permute-start | bytes 1572872 | tf_op jit(solution)/shard_map/ppermute | solution.py:225
  98.5 10.5 %collective-permute-start.21 = (bf16[256,1024]{1,0:T(8,128)(2,1)S(1)}, bf16[256,1024]{1,0:T(8,128)(2,1)S(1)}, u32[]{:S(2)}, u32[]{:S(2)}) collective-permute-start(bf16[256,1024]{1,0:T(8,128)(2,1)S(1)} %add_convert_fusion.1), channel_id=1, source_target_pairs={{0,1},{8,11},{1,2},{9,8},{2,3},{10,9},{3,0},{11,10},{4,5},{12,15},... | collective-permute-start | bytes 1572872 | tf_op jit(solution)/shard_map/ppermute | solution.py:228
  98.6 10.8 %collective-permute-start.9 = (bf16[128,1024]{1,0:T(8,128)(2,1)S(1)}, bf16[128,1024]{1,0:T(8,128)(2,1)S(1)}, u32[]{:S(2)}, u32[]{:S(2)}) collective-permute-start(bf16[128,1024]{1,0:T(8,128)(2,1)S(1)} %get-tuple-element.70), channel_id=1, source_target_pairs={{0,8},{8,0},{1,9},{9,1},{2,10},{10,2},{3,11},{11,3},{4,12},{12,4},... | collective-permute-start | bytes 786440 | tf_op jit(solution)/shard_map/ppermute | solution.py:234
  109.3 1.6 %collective-permute-start.24 = (bf16[128,1024]{1,0:T(8,128)(2,1)S(1)}, bf16[128,1024]{1,0:T(8,128)(2,1)S(1)}, u32[]{:S(2)}, u32[]{:S(2)}) collective-permute-start(bf16[128,1024]{1,0:T(8,128)(2,1)S(1)} %get-tuple-element.68), channel_id=1, source_target_pairs={{0,8},{8,0},{1,9},{9,1},{2,10},{10,2},{3,11},{11,3},{4,12},{12,4},... | collective-permute-start | bytes 786440 | tf_op jit(solution)/shard_map/ppermute | solution.py:234
  (4 other events, 3.6 us)

commit v11 on v10

--- a/solution.py
+++ b/solution.py
@@ -123,7 +123,8 @@
 
 
 def dx_body(at, mine, theirs, *refs):
-    pieces, outs, lhs = refs[:NX], refs[NX : NX + 4], refs[NX + 4]
+    pieces, outs, lhs, rhs, sems = refs[:NX], refs[NX : NX + 4], *refs[NX + 4 :]
+    loads = start_all([(piece, rhs.at[p]) for p, piece in enumerate(pieces)], sems)
     mb, toks, cols = mine.shape
     part = toks // NY
     rows = pieces[0].shape[0]
@@ -134,9 +135,10 @@
                 lhs[k, n, m] = diff[m, pl.ds(start, part)]
     each = NC * mb * part
     left = lhs[...].reshape(4 * each, cols)
-    for p, piece in enumerate(pieces):
+    for p, load in enumerate(loads):
+        load.wait()
         got = lax.dot_general(
-            left, piece[...], (((1,), (1,)), ((), ())), preferred_element_type=F32
+            left, rhs[p], (((1,), (1,)), ((), ())), preferred_element_type=F32
         )
         for k, out in enumerate(outs):
             term = got[k * each : (k + 1) * each]
@@ -151,13 +153,17 @@
     return pl.pallas_call(
         dx_body,
         out_shape=outs,
-        in_specs=[pl.BlockSpec(memory_space=pltpu.SMEM), *([vmem] * (2 + NX))],
+        in_specs=[SMEM, vmem, vmem, *([HBM] * NX)],
         out_specs=[vmem] * 4,
-        scratch_shapes=[pltpu.VMEM((4, NC, mb, part, cols), BF16)],
-        compiler_params=pltpu.CompilerParams(vmem_limit_bytes=8 << 20),
+        scratch_shapes=[
+            pltpu.VMEM((4, NC, mb, part, cols), BF16),
+            pltpu.VMEM((NX, *pieces[0].shape), BF16),
+            pltpu.SemaphoreType.DMA((NX,)),
+        ],
+        compiler_params=pltpu.CompilerParams(vmem_limit_bytes=10 << 20),
         cost_estimate=cost(8 * math.prod(outs[0].shape) * cols, *outs, mine, theirs, *pieces),
         name="dx_terms",
-    )(at, mine, theirs, *pieces)
+    )(at, mine, theirs, *map(in_hbm, pieces))
 
 
 def place_body(at, keep_o, got_o, keep_p, got_p, out_ref):
@@ -253,7 +259,7 @@
     forward_o = pick(*near_o)
     far_o = step_x(forward_o)
     w_z = swap_zh(after(own, diff_z))
-    diff_z = after(diff_z, forward_o)
+    diff_z = after(diff_z, far_o)
     mine = jnp.where(
         zl == 0,
         jnp.concatenate([diff, diff_z], axis=1),

time: 114 us -> 119 us (1.044)
  Pallas kernels: 23.4 us -> 30.4 us
  starting transfers between devices: 29.1 us -> 33 us
  waiting for transfers between devices: 43.9 us -> 40.5 us
  local copies, waits for them, and re-layouts: 5.05 us -> 3.47 us
    ppermute x8, waiting for transfers between devices: 20.6 us -> 13.3 us  [step_x(): return lax.ppermute(value, ('x', 'core'), by_core(NX, way, False))]
    ppermute x6, waiting for transfers between devices: 9.05 us -> 16.3 us  [step_y(): return lax.ppermute(value, ('core', 'outc'), by_core(NY, way, True))]
    pallas_call x2, Pallas kernels: 8.54 us -> 15.5 us  [dx_terms(): pl.pallas_call(dx_body, out_shape=outs, in_specs=[SMEM, vmem, vmem, *[HBM...]
    ppermute x8, starting transfers between devices: 4.67 us -> 7.96 us  [step_x(): return lax.ppermute(value, ('x', 'core'), by_core(NX, way, False))]
    ppermute x1, waiting for transfers between devices: 4.32 us -> 1.8 us  [local(): diff_z = lax.ppermute(diff, 'inc', SWAP)]
    unnamed x22, local copies, waits for them, and re-layouts: 4.81 us -> 3.23 us
  transfers between devices with their start and end apart: 25 -> 25, of which waited for: 14 -> 14; matrix products, arithmetic and copies ran while one was open for 9% -> 8% of each run, Pallas kernels for 19% -> 24%
where the time goes in v11:
time: 119 us; the launch traced here: 118 us
  waiting for transfers between devices  40.5 us (34%)
  starting transfers between devices  33 us (28%)
  Pallas kernels  30.4 us (26%)
  other arithmetic  9.59 us (8%)
  local copies, waits for them, and re-layouts  3.47 us (3%)
    ppermute x6, waiting for transfers between devices, step_y(): return lax.ppermute(value, ('core', 'outc'), by_core(NY, way, True))  16.3 us
    pallas_call x2, Pallas kernels, dx_terms(): pl.pallas_call(dx_body, out_shape=outs, in_specs=[SMEM, vmem, vmem, *[HBM...  15.5 us
    ppermute x8, waiting for transfers between devices, step_x(): return lax.ppermute(value, ('x', 'core'), by_core(NX, way, False))  13.3 us
    pallas_call x2, Pallas kernels, dw_terms(): pl.pallas_call(dw_body, out_shape=outs, in_specs=[SMEM, HBM, *[vmem] * 3]...  10.7 us
    ppermute x6, starting transfers between devices, step_y(): return lax.ppermute(value, ('core', 'outc'), by_core(NY, way, True))  8.46 us
    ppermute x8, starting transfers between devices, step_x(): return lax.ppermute(value, ('x', 'core'), by_core(NX, way, False))  7.96 us
    ppermute x2, starting transfers between devices, swap_zh(): return lax.ppermute(value, 'zh', SWAP)  7.22 us
    ppermute x2, waiting for transfers between devices, neighbours(): lax.ppermute(piece, 'x', by_x(1))  6.88 us
  transfers between devices with their start and end apart: 25, of which 14 were waited for; matrix products, arithmetic and copies ran while one was open for 8% of the time, Pallas kernels for 24%

profile of v11, /device:TPU:0, one launch (start us, length us, event | category | flops | bytes accessed | tf_op | source)
XLA Modules:
  0.0 117.8 jit_solution(14785904431314222396)
XLA Ops:
  0.6 1.6 %collective-permute-start.1 = (bf16[256,1024]{1,0:T(8,128)(2,1)}, bf16[256,1024]{1,0:T(8,128)(2,1)S(1)}, u32[]{:S(2)}, u32[]{:S(2)}) collective-permute-start(bf16[256,1024]{1,0:T(8,128)(2,1)} %bitcast.18), channel_id=1, source_target_pairs={{0,32},{32,64},{64,96},{96,0},{1,33},{33,65},{65,97},{97,1},{2,34}... | collective-permute-start | bytes 1572872 | tf_op jit(solution)/shard_map/ppermute | solution.py:243
  2.3 1.7 %collective-permute-start.2 = (bf16[256,1024]{1,0:T(8,128)(2,1)}, bf16[256,1024]{1,0:T(8,128)(2,1)S(1)}, u32[]{:S(2)}, u32[]{:S(2)}) collective-permute-start(bf16[256,1024]{1,0:T(8,128)(2,1)} %bitcast.19), channel_id=1, source_target_pairs={{0,96},{32,0},{64,32},{96,64},{1,97},{33,1},{65,33},{97,65},{2,98}... | collective-permute-start | bytes 1572872 | tf_op jit(solution)/shard_map/ppermute | solution.py:243
  3.9 2.5 %other_columns.1 = bf16[8,2,256,256]{3,2,1,0:T(8,128)(2,1)} custom-call(s32[1]{0:T(128)} %bitcast.2.core, bf16[2,256,4096]{2,1,0:T(8,128)(2,1)} %act.3), custom_call_target="tpu_custom_call" | custom-call | bytes 6291456 | tf_op jit(solution)/shard_map/other_columns/pallas_call | solution.py:61
  6.7 2.1 %collective-permute-start = (bf16[2,128,1024]{2,1,0:T(8,128)(2,1)S(1)}, bf16[2,128,1024]{2,1,0:T(8,128)(2,1)S(1)}, u32[]{:S(2)}, u32[]{:S(2)}) collective-permute-start(bf16[2,128,1024]{2,1,0:T(8,128)(2,1)S(1)} %subtract_convert_fusion), channel_id=1, source_target_pairs={{0,4},{4,0},{1,5},{5,1},{2,6},{6,2},{3,7},{7,3},{8,12},{12,8},{9,1... | collective-permute-start | bytes 1572872 | tf_op jit(solution)/shard_map/ppermute | solution.py:257
  8.8 6.9 %collective-permute-done.1.refs_1_ = bf16[256,1024]{1,0:T(8,128)(2,1)S(1)} collective-permute-done((bf16[256,1024]{1,0:T(8,128)(2,1)}, bf16[256,1024]{1,0:T(8,128)(2,1)S(1)}, u32[]{:S(2)}, u32[]{:S(2)}) %collective-permute-start.1) | collective-permute-done | bytes 524320 | tf_op jit(solution)/shard_map/ppermute | solution.py:243
  16.9 1.5 %collective-permute-start.3 = (bf16[256,1024]{1,0:T(8,128)(2,1)}, bf16[256,1024]{1,0:T(8,128)(2,1)}, u32[]{:S(2)}, u32[]{:S(2)}) collective-permute-start(bf16[256,1024]{1,0:T(8,128)(2,1)} %broadcast_select_fusion.1), channel_id=1, source_target_pairs={{0,32},{8,104},{32,64},{40,8},{64,96},{72,40},{96,0},{104,72},{1,3... | collective-permute-start | bytes 1572872 | tf_op jit(solution)/shard_map/ppermute | solution.py:231
  18.4 1.8 %collective-permute-done = bf16[2,128,1024]{2,1,0:T(8,128)(2,1)S(1)} collective-permute-done((bf16[2,128,1024]{2,1,0:T(8,128)(2,1)S(1)}, bf16[2,128,1024]{2,1,0:T(8,128)(2,1)S(1)}, u32[]{:S(2)}, u32[]{:S(2)}) %collective-permute-start) | collective-permute-done | bytes 524320 | tf_op jit(solution)/shard_map/ppermute | solution.py:257
  21.0 6.6 %collective-permute-done.3.refs_3_ = bf16[256,1024]{1,0:T(8,128)(2,1)} collective-permute-done((bf16[256,1024]{1,0:T(8,128)(2,1)}, bf16[256,1024]{1,0:T(8,128)(2,1)}, u32[]{:S(2)}, u32[]{:S(2)}) %collective-permute-start.3) | collective-permute-done | bytes 524320 | tf_op jit(solution)/shard_map/ppermute | solution.py:231
  27.6 2.2 %maximum_select_fusion.mine = bf16[2,256,1024]{2,1,0:T(8,128)(2,1)S(1)} fusion(bf16[2,128,1024]{2,1,0:T(8,128)(2,1)} %copy-done.7, bf16[2,128,1024]{2,1,0:T(8,128)(2,1)} %copy-done.4, pred[]{:T(512)S(6)} %eq.7), kind=kLoop, calls=%fused_computation | loop fusion | flops 4718592 | bytes 2097153 | tf_op jit(solution)/shard_map/jit(_where)/select_n | solution.py:263
  29.9 4.1 %collective-permute-start.10 = (bf16[256,1024]{1,0:T(8,128)(2,1)}, bf16[256,1024]{1,0:T(8,128)(2,1)}, u32[]{:S(2)}, u32[]{:S(2)}) collective-permute-start(bf16[256,1024]{1,0:T(8,128)(2,1)} %bitcast.20), channel_id=1, source_target_pairs={{0,16},{16,0},{1,17},{17,1},{2,18},{18,2},{3,19},{19,3},{4,20},{20... | collective-permute-start | bytes 1572872 | tf_op jit(solution)/shard_map/ppermute | solution.py:237
  34.1 8.1 %dx_terms.2 = (bf16[256,1024]{1,0:T(8,128)(2,1)}, bf16[256,1024]{1,0:T(8,128)(2,1)}, bf16[256,1024]{1,0:T(8,128)(2,1)S(1)}, bf16[256,1024]{1,0:T(8,128)(2,1)S(1)}) custom-call(s32[4]{0:T(128)S(1)} %pad_add_fusion.1.at, bf16[2,256,1024]{2,1,0:T(8,128)(2,1)S(1)} %maximum_select_fusion.mine, bf16[2,256,1024]{2,1,0:T(8,128)(2,1)} %collective-permute-done.4.theirs, ...), custom_call_target="tpu_custom_call" | custom-call | flops 2147483648 | bytes 6291456 | tf_op jit(solution)/shard_map/dx_terms/pallas_call | solution.py:153
  43.9 1.6 %collective-permute-start.5 = (bf16[256,1024]{1,0:T(8,128)(2,1)}, bf16[256,1024]{1,0:T(8,128)(2,1)}, u32[]{:S(2)}, u32[]{:S(2)}) collective-permute-start(bf16[256,1024]{1,0:T(8,128)(2,1)} %get-tuple-element.38), channel_id=1, source_target_pairs={{0,1},{8,11},{1,2},{9,8},{2,3},{10,9},{3,0},{11,10},{4,5},{12,15},... | collective-permute-start | bytes 1572872 | tf_op jit(solution)/shard_map/ppermute | solution.py:234
  45.5 1.7 %collective-permute-start.6 = (bf16[256,1024]{1,0:T(8,128)(2,1)}, bf16[256,1024]{1,0:T(8,128)(2,1)}, u32[]{:S(2)}, u32[]{:S(2)}) collective-permute-start(bf16[256,1024]{1,0:T(8,128)(2,1)} %get-tuple-element.39), channel_id=1, source_target_pairs={{0,3},{8,9},{1,0},{9,10},{2,1},{10,11},{3,2},{11,8},{4,7},{12,13},... | collective-permute-start | bytes 1572872 | tf_op jit(solution)/shard_map/ppermute | solution.py:234
  47.2 3.1 %collective-permute-start.12 = (bf16[256,1024]{1,0:T(8,128)(2,1)}, bf16[256,1024]{1,0:T(8,128)(2,1)}, u32[]{:S(2)}, u32[]{:S(2)}) collective-permute-start(bf16[256,1024]{1,0:T(8,128)(2,1)} %collective-permute-done.10.refs_0_), channel_id=1, source_target_pairs={{0,96},{32,0},{64,32},{96,64},{1,97},{33,1},{65,33},{97,65},{2,98}... | collective-permute-start | bytes 1572872 | tf_op jit(solution)/shard_map/ppermute | solution.py:243
  50.5 5.4 %dw_terms.2 = (bf16[256,1024]{1,0:T(8,128)(2,1)S(1)}, bf16[256,1024]{1,0:T(8,128)(2,1)S(1)}, bf16[256,1024]{1,0:T(8,128)(2,1)S(1)}, bf16[256,1024]{1,0:T(8,128)(2,1)S(1)}) custom-call(s32[5]{0:T(128)S(1)} %stack.72.at, bf16[2,256,4096]{2,1,0:T(8,128)(2,1)} %act.3, bf16[8,2,256,256]{3,2,1,0:T(8,128)(2,1)S(1)} %collective-permute-done.7.got, ...), custom_call_target="tpu_custom_call" | custom-call | flops 2147483648 | bytes 6291456 | tf_op jit(solution)/shard_map/dw_terms/pallas_call | solution.py:110
  56.0 2.2 %collective-permute-done.5 = bf16[256,1024]{1,0:T(8,128)(2,1)} collective-permute-done((bf16[256,1024]{1,0:T(8,128)(2,1)}, bf16[256,1024]{1,0:T(8,128)(2,1)}, u32[]{:S(2)}, u32[]{:S(2)}) %collective-permute-start.5) | collective-permute-done | bytes 524320 | tf_op jit(solution)/shard_map/ppermute | solution.py:234
  58.2 1.6 %collective-permute-start.14 = (bf16[256,1024]{1,0:T(8,128)(2,1)S(1)}, bf16[256,1024]{1,0:T(8,128)(2,1)S(1)}, u32[]{:S(2)}, u32[]{:S(2)}) collective-permute-start(bf16[256,1024]{1,0:T(8,128)(2,1)S(1)} %get-tuple-element.54), channel_id=1, source_target_pairs={{0,96},{8,40},{32,0},{40,72},{64,32},{72,104},{96,64},{104,8},{1,9... | collective-permute-start | bytes 1572872 | tf_op jit(solution)/shard_map/ppermute | solution.py:231
  61.1 1.8 %collective-permute-start.8 = (bf16[256,1024]{1,0:T(8,128)(2,1)S(1)}, bf16[256,1024]{1,0:T(8,128)(2,1)S(1)}, u32[]{:S(2)}, u32[]{:S(2)}) collective-permute-start(bf16[256,1024]{1,0:T(8,128)(2,1)S(1)} %add_convert_fusion.6), channel_id=1, source_target_pairs={{0,1},{8,11},{1,2},{9,8},{2,3},{10,9},{3,0},{11,10},{4,5},{12,15},... | collective-permute-start | bytes 1572872 | tf_op jit(solution)/shard_map/ppermute | solution.py:234
  65.0 5.3 %dw_terms.3 = (bf16[256,1024]{1,0:T(8,128)(2,1)S(1)}, bf16[256,1024]{1,0:T(8,128)(2,1)S(1)}, bf16[256,1024]{1,0:T(8,128)(2,1)S(1)}, bf16[256,1024]{1,0:T(8,128)(2,1)S(1)}) custom-call(s32[5]{0:T(128)S(1)} %stack.77.at, bf16[2,256,4096]{2,1,0:T(8,128)(2,1)} %act.3, bf16[8,2,256,256]{3,2,1,0:T(8,128)(2,1)S(1)} %collective-permute-done.7.got, ...), custom_call_target="tpu_custom_call" | custom-call | flops 2147483648 | bytes 6291456 | tf_op jit(solution)/shard_map/dw_terms/pallas_call | solution.py:110
  70.3 2.9 %collective-permute-done.13 = bf16[256,1024]{1,0:T(8,128)(2,1)S(1)} collective-permute-done((bf16[256,1024]{1,0:T(8,128)(2,1)S(1)}, bf16[256,1024]{1,0:T(8,128)(2,1)S(1)}, u32[]{:S(2)}, u32[]{:S(2)}) %collective-permute-start.13) | collective-permute-done | bytes 524320 | tf_op jit(solution)/shard_map/ppermute | solution.py:231
  75.0 1.7 %collective-permute-start.18 = (bf16[256,1024]{1,0:T(8,128)(2,1)S(1)}, bf16[256,1024]{1,0:T(8,128)(2,1)S(1)}, u32[]{:S(2)}, u32[]{:S(2)}) collective-permute-start(bf16[256,1024]{1,0:T(8,128)(2,1)S(1)} %get-tuple-element.49), channel_id=1, source_target_pairs={{0,32},{8,104},{32,64},{40,8},{64,96},{72,40},{96,0},{104,72},{1,3... | collective-permute-start | bytes 1572872 | tf_op jit(solution)/shard_map/ppermute | solution.py:231
  76.7 1.6 %collective-permute-start.19 = (bf16[256,1024]{1,0:T(8,128)(2,1)S(1)}, bf16[256,1024]{1,0:T(8,128)(2,1)S(1)}, u32[]{:S(2)}, u32[]{:S(2)}) collective-permute-start(bf16[256,1024]{1,0:T(8,128)(2,1)S(1)} %get-tuple-element.50), channel_id=1, source_target_pairs={{0,96},{8,40},{32,0},{40,72},{64,32},{72,104},{96,64},{104,8},{1,9... | collective-permute-start | bytes 1572872 | tf_op jit(solution)/shard_map/ppermute | solution.py:231
  78.3 1.3 %add_convert_fusion.5 = bf16[256,1024]{1,0:T(8,128)(2,1)S(1)} fusion(bf16[256,1024]{1,0:T(8,128)(2,1)S(1)} %collective-permute-done.8, bf16[256,1024]{1,0:T(8,128)(2,1)} %collective-permute-done.6, bf16[256,1024]{1,0:T(8,128)(2,1)S(1)} %copy-done.3), kind=kLoop, calls=%fused_computation.7 | loop fusion | flops 1572864 | bytes 2097152 | tf_op jit(solution)/shard_map/convert_element_type | solution.py:289
  80.4 7.4 %dx_terms.3 = (bf16[256,1024]{1,0:T(8,128)(2,1)S(1)}, bf16[256,1024]{1,0:T(8,128)(2,1)S(1)}, bf16[256,1024]{1,0:T(8,128)(2,1)S(1)}, bf16[256,1024]{1,0:T(8,128)(2,1)S(1)}) custom-call(s32[4]{0:T(128)S(1)} %pad_add_fusion.1.at, bf16[2,256,1024]{2,1,0:T(8,128)(2,1)S(1)} %maximum_select_fusion.mine, bf16[2,256,1024]{2,1,0:T(8,128)(2,1)} %collective-permute-done.4.theirs, ...), custom_call_target="tpu_custom_call" | custom-call | flops 2147483648 | bytes 6291456 | tf_op jit(solution)/shard_map/dx_terms/pallas_call | solution.py:153
  87.8 1.4 %collective-permute-start.16 = (bf16[256,1024]{1,0:T(8,128)(2,1)S(1)}, bf16[256,1024]{1,0:T(8,128)(2,1)S(1)}, u32[]{:S(2)}, u32[]{:S(2)}) collective-permute-start(bf16[256,1024]{1,0:T(8,128)(2,1)S(1)} %get-tuple-element.58), channel_id=1, source_target_pairs={{0,1},{8,11},{1,2},{9,8},{2,3},{10,9},{3,0},{11,10},{4,5},{12,15},... | collective-permute-start | bytes 1572872 | tf_op jit(solution)/shard_map/ppermute | solution.py:234
  89.2 1.9 %collective-permute-start.17 = (bf16[256,1024]{1,0:T(8,128)(2,1)S(1)}, bf16[256,1024]{1,0:T(8,128)(2,1)S(1)}, u32[]{:S(2)}, u32[]{:S(2)}) collective-permute-start(bf16[256,1024]{1,0:T(8,128)(2,1)S(1)} %get-tuple-element.59), channel_id=1, source_target_pairs={{0,3},{8,9},{1,0},{9,10},{2,1},{10,11},{3,2},{11,8},{4,7},{12,13},... | collective-permute-start | bytes 1572872 | tf_op jit(solution)/shard_map/ppermute | solution.py:234
  91.4 3.1 %collective-permute-start.23 = (bf16[256,1024]{1,0:T(8,128)(2,1)S(1)}, bf16[256,1024]{1,0:T(8,128)(2,1)S(1)}, u32[]{:S(2)}, u32[]{:S(2)}) collective-permute-start(bf16[256,1024]{1,0:T(8,128)(2,1)S(1)} %add_convert_fusion.3), channel_id=1, source_target_pairs={{0,16},{16,0},{1,17},{17,1},{2,18},{18,2},{3,19},{19,3},{4,20},{20... | collective-permute-start | bytes 1572872 | tf_op jit(solution)/shard_map/ppermute | solution.py:237
  96.0 7.5 %collective-permute-done.16 = bf16[256,1024]{1,0:T(8,128)(2,1)S(1)} collective-permute-done((bf16[256,1024]{1,0:T(8,128)(2,1)S(1)}, bf16[256,1024]{1,0:T(8,128)(2,1)S(1)}, u32[]{:S(2)}, u32[]{:S(2)}) %collective-permute-start.16) | collective-permute-done | bytes 524320 | tf_op jit(solution)/shard_map/ppermute | solution.py:234
  104.9 1.5 %collective-permute-done.22 = bf16[256,1024]{1,0:T(8,128)(2,1)S(1)} collective-permute-done((bf16[256,1024]{1,0:T(8,128)(2,1)S(1)}, bf16[256,1024]{1,0:T(8,128)(2,1)S(1)}, u32[]{:S(2)}, u32[]{:S(2)}) %collective-permute-start.22) | collective-permute-done | bytes 524320 | tf_op jit(solution)/shard_map/ppermute | solution.py:231
  107.7 6.5 %collective-permute-done.21 = bf16[256,1024]{1,0:T(8,128)(2,1)S(1)} collective-permute-done((bf16[256,1024]{1,0:T(8,128)(2,1)S(1)}, bf16[256,1024]{1,0:T(8,128)(2,1)S(1)}, u32[]{:S(2)}, u32[]{:S(2)}) %collective-permute-start.21) | collective-permute-done | bytes 524320 | tf_op jit(solution)/shard_map/ppermute | solution.py:234
  114.7 1.4 %collective-permute-done.24.got_p = bf16[128,1024]{1,0:T(8,128)(2,1)S(1)} collective-permute-done((bf16[128,1024]{1,0:T(8,128)(2,1)S(1)}, bf16[128,1024]{1,0:T(8,128)(2,1)S(1)}, u32[]{:S(2)}, u32[]{:S(2)}) %collective-permute-start.24) | collective-permute-done | bytes 262176 | tf_op jit(solution)/shard_map/ppermute | solution.py:240
  116.2 1.7 %place.1 = bf16[2,64,4096]{2,1,0:T(8,128)(2,1)} custom-call(s32[3]{0:T(128)S(1)} %pad_add_fusion.at, bf16[128,1024]{1,0:T(8,128)(2,1)S(1)} %get-tuple-element.71.keep_o, bf16[128,1024]{1,0:T(8,128)(2,1)S(1)} %collective-permute-done.9.got_o, bf16[128,1024]{1,0:T(8,128)(2,1)S(1)} %get-tuple-element.69.keep_p, bf16[128,1024]{1,0:T(8,128)(2,1)S(1)} %collective-permute-done.24.got_p), custom_call_target="tpu_custom_call" | custom-call | bytes 2097152 | tf_op jit(solution)/shard_map/place/pallas_call | solution.py:192
  (64 shorter events, 15.0 us)
Async XLA Ops:
  0.6 15.0 %collective-permute-start.1 = (bf16[256,1024]{1,0:T(8,128)(2,1)}, bf16[256,1024]{1,0:T(8,128)(2,1)S(1)}, u32[]{:S(2)}, u32[]{:S(2)}) collective-permute-start(bf16[256,1024]{1,0:T(8,128)(2,1)} %bitcast.18), channel_id=1, source_target_pairs={{0,32},{32,64},{64,96},{96,0},{1,33},{33,65},{65,97},{97,1},{2,34}... | collective-permute-start | bytes 1572872 | tf_op jit(solution)/shard_map/ppermute | solution.py:243
  2.3 13.6 %collective-permute-start.2 = (bf16[256,1024]{1,0:T(8,128)(2,1)}, bf16[256,1024]{1,0:T(8,128)(2,1)S(1)}, u32[]{:S(2)}, u32[]{:S(2)}) collective-permute-start(bf16[256,1024]{1,0:T(8,128)(2,1)} %bitcast.19), channel_id=1, source_target_pairs={{0,96},{32,0},{64,32},{96,64},{1,97},{33,1},{65,33},{97,65},{2,98}... | collective-permute-start | bytes 1572872 | tf_op jit(solution)/shard_map/ppermute | solution.py:243
  3.9 2.5 %copy-start.5 = (bf16[2,128,1024]{2,1,0:T(8,128)(2,1)S(1)}, bf16[2,128,1024]{2,1,0:T(8,128)(2,1)}, u32[]{:S(2)}) copy-start(bf16[2,128,1024]{2,1,0:T(8,128)(2,1)} %param.6) | copy-start | bytes 1572868
  3.9 2.6 %copy-start.6 = (bf16[2,128,1024]{2,1,0:T(8,128)(2,1)S(1)}, bf16[2,128,1024]{2,1,0:T(8,128)(2,1)}, u32[]{:S(2)}) copy-start(bf16[2,128,1024]{2,1,0:T(8,128)(2,1)} %param.5) | copy-start | bytes 1572868
  6.7 13.5 %copy-start.4 = (bf16[2,128,1024]{2,1,0:T(8,128)(2,1)}, bf16[2,128,1024]{2,1,0:T(8,128)(2,1)S(1)}, u32[]{:S(2)}) copy-start(bf16[2,128,1024]{2,1,0:T(8,128)(2,1)S(1)} %subtract_convert_fusion) | copy-start | bytes 1572868
  6.7 13.4 %collective-permute-start = (bf16[2,128,1024]{2,1,0:T(8,128)(2,1)S(1)}, bf16[2,128,1024]{2,1,0:T(8,128)(2,1)S(1)}, u32[]{:S(2)}, u32[]{:S(2)}) collective-permute-start(bf16[2,128,1024]{2,1,0:T(8,128)(2,1)S(1)} %subtract_convert_fusion), channel_id=1, source_target_pairs={{0,4},{4,0},{1,5},{5,1},{2,6},{6,2},{3,7},{7,3},{8,12},{12,8},{9,1... | collective-permute-start | bytes 1572872 | tf_op jit(solution)/shard_map/ppermute | solution.py:257
  15.7 1.2 copy-start.8
  15.9 1.0 copy-start.9
  16.9 10.7 %collective-permute-start.3 = (bf16[256,1024]{1,0:T(8,128)(2,1)}, bf16[256,1024]{1,0:T(8,128)(2,1)}, u32[]{:S(2)}, u32[]{:S(2)}) collective-permute-start(bf16[256,1024]{1,0:T(8,128)(2,1)} %broadcast_select_fusion.1), channel_id=1, source_target_pairs={{0,32},{8,104},{32,64},{40,8},{64,96},{72,40},{96,0},{104,72},{1,3... | collective-permute-start | bytes 1572872 | tf_op jit(solution)/shard_map/ppermute | solution.py:231
  18.4 32.2 %collective-permute-start.7 = (bf16[8,2,256,256]{3,2,1,0:T(8,128)(2,1)}, bf16[8,2,256,256]{3,2,1,0:T(8,128)(2,1)S(1)}, u32[]{:S(2)}, u32[]{:S(2)}) collective-permute-start(bf16[8,2,256,256]{3,2,1,0:T(8,128)(2,1)} %other_columns.1), channel_id=1, source_target_pairs={{0,8},{8,0},{1,9},{9,1},{2,10},{10,2},{3,11},{11,3},{4,12},{12,4},... | collective-permute-start | bytes 6291464 | tf_op jit(solution)/shard_map/ppermute | solution.py:240
  29.8 4.3 %collective-permute-start.4 = (bf16[2,256,1024]{2,1,0:T(8,128)(2,1)S(1)}, bf16[2,256,1024]{2,1,0:T(8,128)(2,1)}, u32[]{:S(2)}, u32[]{:S(2)}) collective-permute-start(bf16[2,256,1024]{2,1,0:T(8,128)(2,1)S(1)} %maximum_select_fusion.mine), channel_id=1, source_target_pairs={{0,8},{8,0},{1,9},{9,1},{2,10},{10,2},{3,11},{11,3},{4,12},{12,4},... | collective-permute-start | bytes 3145736 | tf_op jit(solution)/shard_map/ppermute | solution.py:240
  29.9 17.2 %collective-permute-start.10 = (bf16[256,1024]{1,0:T(8,128)(2,1)}, bf16[256,1024]{1,0:T(8,128)(2,1)}, u32[]{:S(2)}, u32[]{:S(2)}) collective-permute-start(bf16[256,1024]{1,0:T(8,128)(2,1)} %bitcast.20), channel_id=1, source_target_pairs={{0,16},{16,0},{1,17},{17,1},{2,18},{18,2},{3,19},{19,3},{4,20},{20... | collective-permute-start | bytes 1572872 | tf_op jit(solution)/shard_map/ppermute | solution.py:237
  43.9 14.3 %collective-permute-start.5 = (bf16[256,1024]{1,0:T(8,128)(2,1)}, bf16[256,1024]{1,0:T(8,128)(2,1)}, u32[]{:S(2)}, u32[]{:S(2)}) collective-permute-start(bf16[256,1024]{1,0:T(8,128)(2,1)} %get-tuple-element.38), channel_id=1, source_target_pairs={{0,1},{8,11},{1,2},{9,8},{2,3},{10,9},{3,0},{11,10},{4,5},{12,15},... | collective-permute-start | bytes 1572872 | tf_op jit(solution)/shard_map/ppermute | solution.py:234
  45.5 14.3 %collective-permute-start.6 = (bf16[256,1024]{1,0:T(8,128)(2,1)}, bf16[256,1024]{1,0:T(8,128)(2,1)}, u32[]{:S(2)}, u32[]{:S(2)}) collective-permute-start(bf16[256,1024]{1,0:T(8,128)(2,1)} %get-tuple-element.39), channel_id=1, source_target_pairs={{0,3},{8,9},{1,0},{9,10},{2,1},{10,11},{3,2},{11,8},{4,7},{12,13},... | collective-permute-start | bytes 1572872 | tf_op jit(solution)/shard_map/ppermute | solution.py:234
  47.1 15.8 %collective-permute-start.11 = (bf16[256,1024]{1,0:T(8,128)(2,1)}, bf16[256,1024]{1,0:T(8,128)(2,1)}, u32[]{:S(2)}, u32[]{:S(2)}) collective-permute-start(bf16[256,1024]{1,0:T(8,128)(2,1)} %collective-permute-done.10.refs_0_), channel_id=1, source_target_pairs={{0,32},{32,64},{64,96},{96,0},{1,33},{33,65},{65,97},{97,1},{2,34}... | collective-permute-start | bytes 1572872 | tf_op jit(solution)/shard_map/ppermute | solution.py:243
  47.2 15.8 %collective-permute-start.12 = (bf16[256,1024]{1,0:T(8,128)(2,1)}, bf16[256,1024]{1,0:T(8,128)(2,1)}, u32[]{:S(2)}, u32[]{:S(2)}) collective-permute-start(bf16[256,1024]{1,0:T(8,128)(2,1)} %collective-permute-done.10.refs_0_), channel_id=1, source_target_pairs={{0,96},{32,0},{64,32},{96,64},{1,97},{33,1},{65,33},{97,65},{2,98}... | collective-permute-start | bytes 1572872 | tf_op jit(solution)/shard_map/ppermute | solution.py:243
  50.5 9.3 %copy-start.1 = (bf16[256,1024]{1,0:T(8,128)(2,1)S(1)}, bf16[256,1024]{1,0:T(8,128)(2,1)}, u32[]{:S(2)}) copy-start(bf16[256,1024]{1,0:T(8,128)(2,1)} %copy-done) | copy-start | bytes 1572868
  56.0 17.3 %collective-permute-start.13 = (bf16[256,1024]{1,0:T(8,128)(2,1)S(1)}, bf16[256,1024]{1,0:T(8,128)(2,1)S(1)}, u32[]{:S(2)}, u32[]{:S(2)}) collective-permute-start(bf16[256,1024]{1,0:T(8,128)(2,1)S(1)} %get-tuple-element.42), channel_id=1, source_target_pairs={{0,32},{8,104},{32,64},{40,8},{64,96},{72,40},{96,0},{104,72},{1,3... | collective-permute-start | bytes 1572872 | tf_op jit(solution)/shard_map/ppermute | solution.py:231
  58.2 16.0 %collective-permute-start.14 = (bf16[256,1024]{1,0:T(8,128)(2,1)S(1)}, bf16[256,1024]{1,0:T(8,128)(2,1)S(1)}, u32[]{:S(2)}, u32[]{:S(2)}) collective-permute-start(bf16[256,1024]{1,0:T(8,128)(2,1)S(1)} %get-tuple-element.54), channel_id=1, source_target_pairs={{0,96},{8,40},{32,0},{40,72},{64,32},{72,104},{96,64},{104,8},{1,9... | collective-permute-start | bytes 1572872 | tf_op jit(solution)/shard_map/ppermute | solution.py:231
  61.1 17.3 %collective-permute-start.8 = (bf16[256,1024]{1,0:T(8,128)(2,1)S(1)}, bf16[256,1024]{1,0:T(8,128)(2,1)S(1)}, u32[]{:S(2)}, u32[]{:S(2)}) collective-permute-start(bf16[256,1024]{1,0:T(8,128)(2,1)S(1)} %add_convert_fusion.6), channel_id=1, source_target_pairs={{0,1},{8,11},{1,2},{9,8},{2,3},{10,9},{3,0},{11,10},{4,5},{12,15},... | collective-permute-start | bytes 1572872 | tf_op jit(solution)/shard_map/ppermute | solution.py:234
  64.2 14.2 %copy-start.3 = (bf16[256,1024]{1,0:T(8,128)(2,1)S(1)}, bf16[256,1024]{1,0:T(8,128)(2,1)}, u32[]{:S(2)}) copy-start(bf16[256,1024]{1,0:T(8,128)(2,1)} %copy-done.2) | copy-start | bytes 1572868
  64.2 15.5 %collective-permute-start.15 = (bf16[256,1024]{1,0:T(8,128)(2,1)S(1)}, bf16[256,1024]{1,0:T(8,128)(2,1)S(1)}, u32[]{:S(2)}, u32[]{:S(2)}) collective-permute-start(bf16[256,1024]{1,0:T(8,128)(2,1)S(1)} %broadcast_select_fusion), channel_id=1, source_target_pairs={{0,32},{8,104},{32,64},{40,8},{64,96},{72,40},{96,0},{104,72},{1,3... | collective-permute-start | bytes 1572872 | tf_op jit(solution)/shard_map/ppermute | solution.py:231
  74.4 16.7 %collective-permute-start.20 = (bf16[256,1024]{1,0:T(8,128)(2,1)S(1)}, bf16[256,1024]{1,0:T(8,128)(2,1)S(1)}, u32[]{:S(2)}, u32[]{:S(2)}) collective-permute-start(bf16[256,1024]{1,0:T(8,128)(2,1)S(1)} %add_convert_fusion.4), channel_id=1, source_target_pairs={{0,32},{8,104},{32,64},{40,8},{64,96},{72,40},{96,0},{104,72},{1,3... | collective-permute-start | bytes 1572872 | tf_op jit(solution)/shard_map/ppermute | solution.py:231
  75.0 20.7 %collective-permute-start.18 = (bf16[256,1024]{1,0:T(8,128)(2,1)S(1)}, bf16[256,1024]{1,0:T(8,128)(2,1)S(1)}, u32[]{:S(2)}, u32[]{:S(2)}) collective-permute-start(bf16[256,1024]{1,0:T(8,128)(2,1)S(1)} %get-tuple-element.49), channel_id=1, source_target_pairs={{0,32},{8,104},{32,64},{40,8},{64,96},{72,40},{96,0},{104,72},{1,3... | collective-permute-start | bytes 1572872 | tf_op jit(solution)/shard_map/ppermute | solution.py:231
  76.7 19.0 %collective-permute-start.19 = (bf16[256,1024]{1,0:T(8,128)(2,1)S(1)}, bf16[256,1024]{1,0:T(8,128)(2,1)S(1)}, u32[]{:S(2)}, u32[]{:S(2)}) collective-permute-start(bf16[256,1024]{1,0:T(8,128)(2,1)S(1)} %get-tuple-element.50), channel_id=1, source_target_pairs={{0,96},{8,40},{32,0},{40,72},{64,32},{72,104},{96,64},{104,8},{1,9... | collective-permute-start | bytes 1572872 | tf_op jit(solution)/shard_map/ppermute | solution.py:231
  87.8 15.8 %collective-permute-start.16 = (bf16[256,1024]{1,0:T(8,128)(2,1)S(1)}, bf16[256,1024]{1,0:T(8,128)(2,1)S(1)}, u32[]{:S(2)}, u32[]{:S(2)}) collective-permute-start(bf16[256,1024]{1,0:T(8,128)(2,1)S(1)} %get-tuple-element.58), channel_id=1, source_target_pairs={{0,1},{8,11},{1,2},{9,8},{2,3},{10,9},{3,0},{11,10},{4,5},{12,15},... | collective-permute-start | bytes 1572872 | tf_op jit(solution)/shard_map/ppermute | solution.py:234
  89.2 14.4 %collective-permute-start.17 = (bf16[256,1024]{1,0:T(8,128)(2,1)S(1)}, bf16[256,1024]{1,0:T(8,128)(2,1)S(1)}, u32[]{:S(2)}, u32[]{:S(2)}) collective-permute-start(bf16[256,1024]{1,0:T(8,128)(2,1)S(1)} %get-tuple-element.59), channel_id=1, source_target_pairs={{0,3},{8,9},{1,0},{9,10},{2,1},{10,11},{3,2},{11,8},{4,7},{12,13},... | collective-permute-start | bytes 1572872 | tf_op jit(solution)/shard_map/ppermute | solution.py:234
  91.4 13.5 %collective-permute-start.23 = (bf16[256,1024]{1,0:T(8,128)(2,1)S(1)}, bf16[256,1024]{1,0:T(8,128)(2,1)S(1)}, u32[]{:S(2)}, u32[]{:S(2)}) collective-permute-start(bf16[256,1024]{1,0:T(8,128)(2,1)S(1)} %add_convert_fusion.3), channel_id=1, source_target_pairs={{0,16},{16,0},{1,17},{17,1},{2,18},{18,2},{3,19},{19,3},{4,20},{20... | collective-permute-start | bytes 1572872 | tf_op jit(solution)/shard_map/ppermute | solution.py:237
  95.9 10.5 %collective-permute-start.22 = (bf16[256,1024]{1,0:T(8,128)(2,1)S(1)}, bf16[256,1024]{1,0:T(8,128)(2,1)S(1)}, u32[]{:S(2)}, u32[]{:S(2)}) collective-permute-start(bf16[256,1024]{1,0:T(8,128)(2,1)S(1)} %add_convert_fusion.2), channel_id=1, source_target_pairs={{0,32},{8,104},{32,64},{40,8},{64,96},{72,40},{96,0},{104,72},{1,3... | collective-permute-start | bytes 1572872 | tf_op jit(solution)/shard_map/ppermute | solution.py:231
  103.8 10.5 %collective-permute-start.21 = (bf16[256,1024]{1,0:T(8,128)(2,1)S(1)}, bf16[256,1024]{1,0:T(8,128)(2,1)S(1)}, u32[]{:S(2)}, u32[]{:S(2)}) collective-permute-start(bf16[256,1024]{1,0:T(8,128)(2,1)S(1)} %add_convert_fusion.1), channel_id=1, source_target_pairs={{0,1},{8,11},{1,2},{9,8},{2,3},{10,9},{3,0},{11,10},{4,5},{12,15},... | collective-permute-start | bytes 1572872 | tf_op jit(solution)/shard_map/ppermute | solution.py:234
  103.9 10.8 %collective-permute-start.9 = (bf16[128,1024]{1,0:T(8,128)(2,1)S(1)}, bf16[128,1024]{1,0:T(8,128)(2,1)S(1)}, u32[]{:S(2)}, u32[]{:S(2)}) collective-permute-start(bf16[128,1024]{1,0:T(8,128)(2,1)S(1)} %get-tuple-element.70), channel_id=1, source_target_pairs={{0,8},{8,0},{1,9},{9,1},{2,10},{10,2},{3,11},{11,3},{4,12},{12,4},... | collective-permute-start | bytes 786440 | tf_op jit(solution)/shard_map/ppermute | solution.py:240
  114.6 1.6 %collective-permute-start.24 = (bf16[128,1024]{1,0:T(8,128)(2,1)S(1)}, bf16[128,1024]{1,0:T(8,128)(2,1)S(1)}, u32[]{:S(2)}, u32[]{:S(2)}) collective-permute-start(bf16[128,1024]{1,0:T(8,128)(2,1)S(1)} %get-tuple-element.68), channel_id=1, source_target_pairs={{0,8},{8,0},{1,9},{9,1},{2,10},{10,2},{3,11},{11,3},{4,12},{12,4},... | collective-permute-start | bytes 786440 | tf_op jit(solution)/shard_map/ppermute | solution.py:240
  (4 other events, 3.2 us)

commit v12 on v10

--- a/solution.py
+++ b/solution.py
@@ -253,7 +253,7 @@
     forward_o = pick(*near_o)
     far_o = step_x(forward_o)
     w_z = swap_zh(after(own, diff_z))
-    diff_z = after(diff_z, forward_o)
+    diff_z = after(diff_z, far_o)
     mine = jnp.where(
         zl == 0,
         jnp.concatenate([diff, diff_z], axis=1),

time: 114 us -> 115 us (level)
  starting transfers between devices: 29.1 us -> 34.9 us
  waiting for transfers between devices: 43.9 us -> 38.6 us
    ppermute x8, starting transfers between devices: 4.67 us -> 8.3 us  [step_x(): return lax.ppermute(value, ('x', 'core'), by_core(NX, way, False))]
    ppermute x8, waiting for transfers between devices: 20.6 us -> 17.8 us  [step_x(): return lax.ppermute(value, ('x', 'core'), by_core(NX, way, False))]
    ppermute x6, waiting for transfers between devices: 9.05 us -> 7.49 us  [step_y(): return lax.ppermute(value, ('core', 'outc'), by_core(NY, way, True))]
    ppermute x1, waiting for transfers between devices: 4.32 us -> 2.89 us  [local(): diff_z = lax.ppermute(diff, 'inc', SWAP)]
    ppermute x4, starting transfers between devices: 1.08 us -> 2.46 us  [swap_core(): return lax.ppermute(value, 'core', SWAP)]
    ppermute x2, waiting for transfers between devices: 1.07 us -> 2.3 us  [swap_zh(): return lax.ppermute(value, 'zh', SWAP)]
    ppermute x6, starting transfers between devices: 7.32 us -> 8.47 us  [step_y(): return lax.ppermute(value, ('core', 'outc'), by_core(NY, way, True))]
  transfers between devices with their start and end apart: 25 -> 25, of which waited for: 14 -> 16; matrix products, arithmetic and copies ran while one was open for 9% -> 9% of each run, Pallas kernels for 19% -> 19%
where the time goes in v12:
time: 115 us; the launch traced here: 113 us
  waiting for transfers between devices  38.6 us (34%)
  starting transfers between devices  34.9 us (30%)
  Pallas kernels  23.5 us (20%)
  other arithmetic  10.2 us (9%)
  local copies, waits for them, and re-layouts  4.99 us (4%)
    ppermute x8, waiting for transfers between devices, step_x(): return lax.ppermute(value, ('x', 'core'), by_core(NX, way, False))  17.8 us
    pallas_call x2, Pallas kernels, dw_terms(): pl.pallas_call(dw_body, out_shape=outs, in_specs=[SMEM, HBM, *[vmem] * 3]...  10.8 us
    pallas_call x2, Pallas kernels, dx_terms(): pl.pallas_call(dx_body, out_shape=outs, in_specs=[pl.BlockSpec(memory_spa...  8.54 us
    ppermute x6, starting transfers between devices, step_y(): return lax.ppermute(value, ('core', 'outc'), by_core(NY, way, True))  8.47 us
    ppermute x8, starting transfers between devices, step_x(): return lax.ppermute(value, ('x', 'core'), by_core(NX, way, False))  8.3 us
    ppermute x6, waiting for transfers between devices, step_y(): return lax.ppermute(value, ('core', 'outc'), by_core(NY, way, True))  7.49 us
    ppermute x2, starting transfers between devices, swap_zh(): return lax.ppermute(value, 'zh', SWAP)  7.14 us
    ppermute x2, waiting for transfers between devices, neighbours(): lax.ppermute(piece, 'x', by_x(1))  6.48 us
  transfers between devices with their start and end apart: 25, of which 16 were waited for; matrix products, arithmetic and copies ran while one was open for 9% of the time, Pallas kernels for 19%

profile of v12, /device:TPU:0, one launch (start us, length us, event | category | flops | bytes accessed | tf_op | source)
XLA Modules:
  0.0 113.0 jit_solution(14170658419437912413)
XLA Ops:
  0.6 1.6 %collective-permute-start.1 = (bf16[256,1024]{1,0:T(8,128)(2,1)}, bf16[256,1024]{1,0:T(8,128)(2,1)S(1)}, u32[]{:S(2)}, u32[]{:S(2)}) collective-permute-start(bf16[256,1024]{1,0:T(8,128)(2,1)} %bitcast.17), channel_id=1, source_target_pairs={{0,32},{32,64},{64,96},{96,0},{1,33},{33,65},{65,97},{97,1},{2,34}... | collective-permute-start | bytes 1572872 | tf_op jit(solution)/shard_map/ppermute | solution.py:237
  2.3 1.7 %collective-permute-start.2 = (bf16[256,1024]{1,0:T(8,128)(2,1)}, bf16[256,1024]{1,0:T(8,128)(2,1)S(1)}, u32[]{:S(2)}, u32[]{:S(2)}) collective-permute-start(bf16[256,1024]{1,0:T(8,128)(2,1)} %bitcast.18), channel_id=1, source_target_pairs={{0,96},{32,0},{64,32},{96,64},{1,97},{33,1},{65,33},{97,65},{2,98}... | collective-permute-start | bytes 1572872 | tf_op jit(solution)/shard_map/ppermute | solution.py:237
  3.9 2.5 %other_columns.1 = bf16[8,2,256,256]{3,2,1,0:T(8,128)(2,1)} custom-call(s32[1]{0:T(128)} %bitcast.2.core, bf16[2,256,4096]{2,1,0:T(8,128)(2,1)} %act.3), custom_call_target="tpu_custom_call" | custom-call | bytes 6291456 | tf_op jit(solution)/shard_map/other_columns/pallas_call | solution.py:61
  7.5 2.0 %collective-permute-start = (bf16[2,128,1024]{2,1,0:T(8,128)(2,1)}, bf16[2,128,1024]{2,1,0:T(8,128)(2,1)}, u32[]{:S(2)}, u32[]{:S(2)}) collective-permute-start(bf16[2,128,1024]{2,1,0:T(8,128)(2,1)} %subtract_convert_fusion), channel_id=1, source_target_pairs={{0,4},{4,0},{1,5},{5,1},{2,6},{6,2},{3,7},{7,3},{8,12},{12,8},{9,1... | collective-permute-start | bytes 1572872 | tf_op jit(solution)/shard_map/ppermute | solution.py:251
  9.5 6.2 %collective-permute-done.1.refs_1_ = bf16[256,1024]{1,0:T(8,128)(2,1)S(1)} collective-permute-done((bf16[256,1024]{1,0:T(8,128)(2,1)}, bf16[256,1024]{1,0:T(8,128)(2,1)S(1)}, u32[]{:S(2)}, u32[]{:S(2)}) %collective-permute-start.1) | collective-permute-done | bytes 524320 | tf_op jit(solution)/shard_map/ppermute | solution.py:237
  18.3 2.9 %collective-permute-done = bf16[2,128,1024]{2,1,0:T(8,128)(2,1)} collective-permute-done((bf16[2,128,1024]{2,1,0:T(8,128)(2,1)}, bf16[2,128,1024]{2,1,0:T(8,128)(2,1)}, u32[]{:S(2)}, u32[]{:S(2)}) %collective-permute-start) | collective-permute-done | bytes 524320 | tf_op jit(solution)/shard_map/ppermute | solution.py:251
  21.2 6.3 %collective-permute-done.3.refs_3_ = bf16[256,1024]{1,0:T(8,128)(2,1)} collective-permute-done((bf16[256,1024]{1,0:T(8,128)(2,1)}, bf16[256,1024]{1,0:T(8,128)(2,1)}, u32[]{:S(2)}, u32[]{:S(2)}) %collective-permute-start.3) | collective-permute-done | bytes 524320 | tf_op jit(solution)/shard_map/ppermute | solution.py:225
  27.5 2.0 %maximum_select_fusion.mine = bf16[2,256,1024]{2,1,0:T(8,128)(2,1)S(1)} fusion(bf16[2,128,1024]{2,1,0:T(8,128)(2,1)} %collective-permute-done, bf16[2,128,1024]{2,1,0:T(8,128)(2,1)} %subtract_convert_fusion, pred[]{:T(512)S(6)} %eq.7), kind=kLoop, calls=%fused_computation | loop fusion | flops 4718592 | bytes 2097153 | tf_op jit(solution)/shard_map/jit(_where)/select_n | solution.py:257
  29.7 4.0 %collective-permute-start.10 = (bf16[256,1024]{1,0:T(8,128)(2,1)}, bf16[256,1024]{1,0:T(8,128)(2,1)}, u32[]{:S(2)}, u32[]{:S(2)}) collective-permute-start(bf16[256,1024]{1,0:T(8,128)(2,1)} %bitcast.19), channel_id=1, source_target_pairs={{0,16},{16,0},{1,17},{17,1},{2,18},{18,2},{3,19},{19,3},{4,20},{20... | collective-permute-start | bytes 1572872 | tf_op jit(solution)/shard_map/ppermute | solution.py:231
  36.8 4.5 %dx_terms.2 = (bf16[256,1024]{1,0:T(8,128)(2,1)}, bf16[256,1024]{1,0:T(8,128)(2,1)}, bf16[256,1024]{1,0:T(8,128)(2,1)S(1)}, bf16[256,1024]{1,0:T(8,128)(2,1)S(1)}) custom-call(s32[4]{0:T(128)S(1)} %pad_add_fusion.1.at, bf16[2,256,1024]{2,1,0:T(8,128)(2,1)S(1)} %maximum_select_fusion.mine, bf16[2,256,1024]{2,1,0:T(8,128)(2,1)} %collective-permute-done.4.theirs, ...), custom_call_target="tpu_custom_call" | custom-call | flops 2147483648 | bytes 6291456 | tf_op jit(solution)/shard_map/dx_terms/pallas_call | solution.py:151
  42.9 1.6 %collective-permute-start.5 = (bf16[256,1024]{1,0:T(8,128)(2,1)}, bf16[256,1024]{1,0:T(8,128)(2,1)}, u32[]{:S(2)}, u32[]{:S(2)}) collective-permute-start(bf16[256,1024]{1,0:T(8,128)(2,1)} %get-tuple-element.38), channel_id=1, source_target_pairs={{0,1},{8,11},{1,2},{9,8},{2,3},{10,9},{3,0},{11,10},{4,5},{12,15},... | collective-permute-start | bytes 1572872 | tf_op jit(solution)/shard_map/ppermute | solution.py:228
  44.5 1.7 %collective-permute-start.6 = (bf16[256,1024]{1,0:T(8,128)(2,1)}, bf16[256,1024]{1,0:T(8,128)(2,1)}, u32[]{:S(2)}, u32[]{:S(2)}) collective-permute-start(bf16[256,1024]{1,0:T(8,128)(2,1)} %get-tuple-element.39), channel_id=1, source_target_pairs={{0,3},{8,9},{1,0},{9,10},{2,1},{10,11},{3,2},{11,8},{4,7},{12,13},... | collective-permute-start | bytes 1572872 | tf_op jit(solution)/shard_map/ppermute | solution.py:228
  46.7 3.0 %collective-permute-start.12 = (bf16[256,1024]{1,0:T(8,128)(2,1)}, bf16[256,1024]{1,0:T(8,128)(2,1)}, u32[]{:S(2)}, u32[]{:S(2)}) collective-permute-start(bf16[256,1024]{1,0:T(8,128)(2,1)} %collective-permute-done.10.refs_0_), channel_id=1, source_target_pairs={{0,96},{32,0},{64,32},{96,64},{1,97},{33,1},{65,33},{97,65},{2,98}... | collective-permute-start | bytes 1572872 | tf_op jit(solution)/shard_map/ppermute | solution.py:237
  49.8 5.4 %dw_terms.2 = (bf16[256,1024]{1,0:T(8,128)(2,1)S(1)}, bf16[256,1024]{1,0:T(8,128)(2,1)S(1)}, bf16[256,1024]{1,0:T(8,128)(2,1)S(1)}, bf16[256,1024]{1,0:T(8,128)(2,1)S(1)}) custom-call(s32[5]{0:T(128)S(1)} %stack.72.at, bf16[2,256,4096]{2,1,0:T(8,128)(2,1)} %act.3, bf16[8,2,256,256]{3,2,1,0:T(8,128)(2,1)S(1)} %collective-permute-done.7.got, ...), custom_call_target="tpu_custom_call" | custom-call | flops 2147483648 | bytes 6291456 | tf_op jit(solution)/shard_map/dw_terms/pallas_call | solution.py:110
  55.3 1.9 %collective-permute-done.5 = bf16[256,1024]{1,0:T(8,128)(2,1)} collective-permute-done((bf16[256,1024]{1,0:T(8,128)(2,1)}, bf16[256,1024]{1,0:T(8,128)(2,1)}, u32[]{:S(2)}, u32[]{:S(2)}) %collective-permute-start.5) | collective-permute-done | bytes 524320 | tf_op jit(solution)/shard_map/ppermute | solution.py:228
  57.3 1.7 %collective-permute-start.14 = (bf16[256,1024]{1,0:T(8,128)(2,1)S(1)}, bf16[256,1024]{1,0:T(8,128)(2,1)S(1)}, u32[]{:S(2)}, u32[]{:S(2)}) collective-permute-start(bf16[256,1024]{1,0:T(8,128)(2,1)S(1)} %get-tuple-element.54), channel_id=1, source_target_pairs={{0,96},{8,40},{32,0},{40,72},{64,32},{72,104},{96,64},{104,8},{1,9... | collective-permute-start | bytes 1572872 | tf_op jit(solution)/shard_map/ppermute | solution.py:225
  60.2 1.9 %collective-permute-start.8 = (bf16[256,1024]{1,0:T(8,128)(2,1)S(1)}, bf16[256,1024]{1,0:T(8,128)(2,1)S(1)}, u32[]{:S(2)}, u32[]{:S(2)}) collective-permute-start(bf16[256,1024]{1,0:T(8,128)(2,1)S(1)} %add_convert_fusion.6), channel_id=1, source_target_pairs={{0,1},{8,11},{1,2},{9,8},{2,3},{10,9},{3,0},{11,10},{4,5},{12,15},... | collective-permute-start | bytes 1572872 | tf_op jit(solution)/shard_map/ppermute | solution.py:228
  64.4 5.3 %dw_terms.3 = (bf16[256,1024]{1,0:T(8,128)(2,1)S(1)}, bf16[256,1024]{1,0:T(8,128)(2,1)S(1)}, bf16[256,1024]{1,0:T(8,128)(2,1)S(1)}, bf16[256,1024]{1,0:T(8,128)(2,1)S(1)}) custom-call(s32[5]{0:T(128)S(1)} %stack.77.at, bf16[2,256,4096]{2,1,0:T(8,128)(2,1)} %act.3, bf16[8,2,256,256]{3,2,1,0:T(8,128)(2,1)S(1)} %collective-permute-done.7.got, ...), custom_call_target="tpu_custom_call" | custom-call | flops 2147483648 | bytes 6291456 | tf_op jit(solution)/shard_map/dw_terms/pallas_call | solution.py:110
  69.8 3.0 %collective-permute-done.13 = bf16[256,1024]{1,0:T(8,128)(2,1)S(1)} collective-permute-done((bf16[256,1024]{1,0:T(8,128)(2,1)S(1)}, bf16[256,1024]{1,0:T(8,128)(2,1)S(1)}, u32[]{:S(2)}, u32[]{:S(2)}) %collective-permute-start.13) | collective-permute-done | bytes 524320 | tf_op jit(solution)/shard_map/ppermute | solution.py:225
  74.5 1.7 %collective-permute-start.18 = (bf16[256,1024]{1,0:T(8,128)(2,1)S(1)}, bf16[256,1024]{1,0:T(8,128)(2,1)S(1)}, u32[]{:S(2)}, u32[]{:S(2)}) collective-permute-start(bf16[256,1024]{1,0:T(8,128)(2,1)S(1)} %get-tuple-element.49), channel_id=1, source_target_pairs={{0,32},{8,104},{32,64},{40,8},{64,96},{72,40},{96,0},{104,72},{1,3... | collective-permute-start | bytes 1572872 | tf_op jit(solution)/shard_map/ppermute | solution.py:225
  79.0 4.0 %dx_terms.3 = (bf16[256,1024]{1,0:T(8,128)(2,1)S(1)}, bf16[256,1024]{1,0:T(8,128)(2,1)S(1)}, bf16[256,1024]{1,0:T(8,128)(2,1)S(1)}, bf16[256,1024]{1,0:T(8,128)(2,1)S(1)}) custom-call(s32[4]{0:T(128)S(1)} %pad_add_fusion.1.at, bf16[2,256,1024]{2,1,0:T(8,128)(2,1)S(1)} %maximum_select_fusion.mine, bf16[2,256,1024]{2,1,0:T(8,128)(2,1)} %collective-permute-done.4.theirs, ...), custom_call_target="tpu_custom_call" | custom-call | flops 2147483648 | bytes 6291456 | tf_op jit(solution)/shard_map/dx_terms/pallas_call | solution.py:151
  83.1 1.6 %collective-permute-start.16 = (bf16[256,1024]{1,0:T(8,128)(2,1)S(1)}, bf16[256,1024]{1,0:T(8,128)(2,1)S(1)}, u32[]{:S(2)}, u32[]{:S(2)}) collective-permute-start(bf16[256,1024]{1,0:T(8,128)(2,1)S(1)} %get-tuple-element.58), channel_id=1, source_target_pairs={{0,1},{8,11},{1,2},{9,8},{2,3},{10,9},{3,0},{11,10},{4,5},{12,15},... | collective-permute-start | bytes 1572872 | tf_op jit(solution)/shard_map/ppermute | solution.py:228
  84.7 1.7 %collective-permute-start.17 = (bf16[256,1024]{1,0:T(8,128)(2,1)S(1)}, bf16[256,1024]{1,0:T(8,128)(2,1)S(1)}, u32[]{:S(2)}, u32[]{:S(2)}) collective-permute-start(bf16[256,1024]{1,0:T(8,128)(2,1)S(1)} %get-tuple-element.59), channel_id=1, source_target_pairs={{0,3},{8,9},{1,0},{9,10},{2,1},{10,11},{3,2},{11,8},{4,7},{12,13},... | collective-permute-start | bytes 1572872 | tf_op jit(solution)/shard_map/ppermute | solution.py:228
  86.4 3.2 %collective-permute-done.20 = bf16[256,1024]{1,0:T(8,128)(2,1)S(1)} collective-permute-done((bf16[256,1024]{1,0:T(8,128)(2,1)S(1)}, bf16[256,1024]{1,0:T(8,128)(2,1)S(1)}, u32[]{:S(2)}, u32[]{:S(2)}) %collective-permute-start.20) | collective-permute-done | bytes 524320 | tf_op jit(solution)/shard_map/ppermute | solution.py:225
  89.9 3.2 %collective-permute-start.23 = (bf16[256,1024]{1,0:T(8,128)(2,1)S(1)}, bf16[256,1024]{1,0:T(8,128)(2,1)S(1)}, u32[]{:S(2)}, u32[]{:S(2)}) collective-permute-start(bf16[256,1024]{1,0:T(8,128)(2,1)S(1)} %add_convert_fusion.3), channel_id=1, source_target_pairs={{0,16},{16,0},{1,17},{17,1},{2,18},{18,2},{3,19},{19,3},{4,20},{20... | collective-permute-start | bytes 1572872 | tf_op jit(solution)/shard_map/ppermute | solution.py:231
  93.0 2.2 %collective-permute-done.18 = bf16[256,1024]{1,0:T(8,128)(2,1)S(1)} collective-permute-done((bf16[256,1024]{1,0:T(8,128)(2,1)S(1)}, bf16[256,1024]{1,0:T(8,128)(2,1)S(1)}, u32[]{:S(2)}, u32[]{:S(2)}) %collective-permute-start.18) | collective-permute-done | bytes 524320 | tf_op jit(solution)/shard_map/ppermute | solution.py:225
  95.5 3.3 %collective-permute-done.16 = bf16[256,1024]{1,0:T(8,128)(2,1)S(1)} collective-permute-done((bf16[256,1024]{1,0:T(8,128)(2,1)S(1)}, bf16[256,1024]{1,0:T(8,128)(2,1)S(1)}, u32[]{:S(2)}, u32[]{:S(2)}) %collective-permute-start.16) | collective-permute-done | bytes 524320 | tf_op jit(solution)/shard_map/ppermute | solution.py:228
  99.1 2.3 %collective-permute-start.9 = (bf16[128,1024]{1,0:T(8,128)(2,1)S(1)}, bf16[128,1024]{1,0:T(8,128)(2,1)S(1)}, u32[]{:S(2)}, u32[]{:S(2)}) collective-permute-start(bf16[128,1024]{1,0:T(8,128)(2,1)S(1)} %get-tuple-element.70), channel_id=1, source_target_pairs={{0,8},{8,0},{1,9},{9,1},{2,10},{10,2},{3,11},{11,3},{4,12},{12,4},... | collective-permute-start | bytes 786440 | tf_op jit(solution)/shard_map/ppermute | solution.py:234
  101.4 2.0 %collective-permute-done.23 = bf16[256,1024]{1,0:T(8,128)(2,1)S(1)} collective-permute-done((bf16[256,1024]{1,0:T(8,128)(2,1)S(1)}, bf16[256,1024]{1,0:T(8,128)(2,1)S(1)}, u32[]{:S(2)}, u32[]{:S(2)}) %collective-permute-start.23) | collective-permute-done | bytes 524320 | tf_op jit(solution)/shard_map/ppermute | solution.py:231
  103.4 2.4 %collective-permute-done.22 = bf16[256,1024]{1,0:T(8,128)(2,1)S(1)} collective-permute-done((bf16[256,1024]{1,0:T(8,128)(2,1)S(1)}, bf16[256,1024]{1,0:T(8,128)(2,1)S(1)}, u32[]{:S(2)}, u32[]{:S(2)}) %collective-permute-start.22) | collective-permute-done | bytes 524320 | tf_op jit(solution)/shard_map/ppermute | solution.py:225
  107.2 2.3 %collective-permute-done.21 = bf16[256,1024]{1,0:T(8,128)(2,1)S(1)} collective-permute-done((bf16[256,1024]{1,0:T(8,128)(2,1)S(1)}, bf16[256,1024]{1,0:T(8,128)(2,1)S(1)}, u32[]{:S(2)}, u32[]{:S(2)}) %collective-permute-start.21) | collective-permute-done | bytes 524320 | tf_op jit(solution)/shard_map/ppermute | solution.py:228
  111.4 1.7 %place.1 = bf16[2,64,4096]{2,1,0:T(8,128)(2,1)} custom-call(s32[3]{0:T(128)S(1)} %pad_add_fusion.at, bf16[128,1024]{1,0:T(8,128)(2,1)S(1)} %get-tuple-element.71.keep_o, bf16[128,1024]{1,0:T(8,128)(2,1)S(1)} %collective-permute-done.9.got_o, bf16[128,1024]{1,0:T(8,128)(2,1)S(1)} %get-tuple-element.69.keep_p, bf16[128,1024]{1,0:T(8,128)(2,1)S(1)} %collective-permute-done.24.got_p), custom_call_target="tpu_custom_call" | custom-call | bytes 2097152 | tf_op jit(solution)/shard_map/place/pallas_call | solution.py:186
  (64 shorter events, 21.5 us)
Async XLA Ops:
  0.6 15.0 %collective-permute-start.1 = (bf16[256,1024]{1,0:T(8,128)(2,1)}, bf16[256,1024]{1,0:T(8,128)(2,1)S(1)}, u32[]{:S(2)}, u32[]{:S(2)}) collective-permute-start(bf16[256,1024]{1,0:T(8,128)(2,1)} %bitcast.17), channel_id=1, source_target_pairs={{0,32},{32,64},{64,96},{96,0},{1,33},{33,65},{65,97},{97,1},{2,34}... | collective-permute-start | bytes 1572872 | tf_op jit(solution)/shard_map/ppermute | solution.py:237
  2.3 13.6 %collective-permute-start.2 = (bf16[256,1024]{1,0:T(8,128)(2,1)}, bf16[256,1024]{1,0:T(8,128)(2,1)S(1)}, u32[]{:S(2)}, u32[]{:S(2)}) collective-permute-start(bf16[256,1024]{1,0:T(8,128)(2,1)} %bitcast.18), channel_id=1, source_target_pairs={{0,96},{32,0},{64,32},{96,64},{1,97},{33,1},{65,33},{97,65},{2,98}... | collective-permute-start | bytes 1572872 | tf_op jit(solution)/shard_map/ppermute | solution.py:237
  3.9 2.5 %copy-start.9 = (bf16[2,128,1024]{2,1,0:T(8,128)(2,1)S(1)}, bf16[2,128,1024]{2,1,0:T(8,128)(2,1)}, u32[]{:S(2)}) copy-start(bf16[2,128,1024]{2,1,0:T(8,128)(2,1)} %param.6) | copy-start | bytes 1572868
  3.9 2.6 %copy-start.10 = (bf16[2,128,1024]{2,1,0:T(8,128)(2,1)S(1)}, bf16[2,128,1024]{2,1,0:T(8,128)(2,1)}, u32[]{:S(2)}) copy-start(bf16[2,128,1024]{2,1,0:T(8,128)(2,1)} %param.5) | copy-start | bytes 1572868
  7.5 13.7 %collective-permute-start = (bf16[2,128,1024]{2,1,0:T(8,128)(2,1)}, bf16[2,128,1024]{2,1,0:T(8,128)(2,1)}, u32[]{:S(2)}, u32[]{:S(2)}) collective-permute-start(bf16[2,128,1024]{2,1,0:T(8,128)(2,1)} %subtract_convert_fusion), channel_id=1, source_target_pairs={{0,4},{4,0},{1,5},{5,1},{2,6},{6,2},{3,7},{7,3},{8,12},{12,8},{9,1... | collective-permute-start | bytes 1572872 | tf_op jit(solution)/shard_map/ppermute | solution.py:251
  15.7 5.5 %copy-start.2 = (bf16[256,1024]{1,0:T(8,128)(2,1)}, bf16[256,1024]{1,0:T(8,128)(2,1)S(1)}, u32[]{:S(2)}) copy-start(bf16[256,1024]{1,0:T(8,128)(2,1)S(1)} %collective-permute-done.1.refs_1_) | copy-start | bytes 1572868
  15.9 5.3 %copy-start.4 = (bf16[256,1024]{1,0:T(8,128)(2,1)}, bf16[256,1024]{1,0:T(8,128)(2,1)S(1)}, u32[]{:S(2)}) copy-start(bf16[256,1024]{1,0:T(8,128)(2,1)S(1)} %collective-permute-done.2.refs_2_) | copy-start | bytes 1572868
  16.8 10.7 %collective-permute-start.3 = (bf16[256,1024]{1,0:T(8,128)(2,1)}, bf16[256,1024]{1,0:T(8,128)(2,1)}, u32[]{:S(2)}, u32[]{:S(2)}) collective-permute-start(bf16[256,1024]{1,0:T(8,128)(2,1)} %broadcast_select_fusion.1), channel_id=1, source_target_pairs={{0,32},{8,104},{32,64},{40,8},{64,96},{72,40},{96,0},{104,72},{1,3... | collective-permute-start | bytes 1572872 | tf_op jit(solution)/shard_map/ppermute | solution.py:225
  18.3 31.6 %collective-permute-start.7 = (bf16[8,2,256,256]{3,2,1,0:T(8,128)(2,1)}, bf16[8,2,256,256]{3,2,1,0:T(8,128)(2,1)S(1)}, u32[]{:S(2)}, u32[]{:S(2)}) collective-permute-start(bf16[8,2,256,256]{3,2,1,0:T(8,128)(2,1)} %other_columns.1), channel_id=1, source_target_pairs={{0,8},{8,0},{1,9},{9,1},{2,10},{10,2},{3,11},{11,3},{4,12},{12,4},... | collective-permute-start | bytes 6291464 | tf_op jit(solution)/shard_map/ppermute | solution.py:234
  29.5 4.2 %collective-permute-start.4 = (bf16[2,256,1024]{2,1,0:T(8,128)(2,1)S(1)}, bf16[2,256,1024]{2,1,0:T(8,128)(2,1)}, u32[]{:S(2)}, u32[]{:S(2)}) collective-permute-start(bf16[2,256,1024]{2,1,0:T(8,128)(2,1)S(1)} %maximum_select_fusion.mine), channel_id=1, source_target_pairs={{0,8},{8,0},{1,9},{9,1},{2,10},{10,2},{3,11},{11,3},{4,12},{12,4},... | collective-permute-start | bytes 3145736 | tf_op jit(solution)/shard_map/ppermute | solution.py:234
  29.7 16.8 %collective-permute-start.10 = (bf16[256,1024]{1,0:T(8,128)(2,1)}, bf16[256,1024]{1,0:T(8,128)(2,1)}, u32[]{:S(2)}, u32[]{:S(2)}) collective-permute-start(bf16[256,1024]{1,0:T(8,128)(2,1)} %bitcast.19), channel_id=1, source_target_pairs={{0,16},{16,0},{1,17},{17,1},{2,18},{18,2},{3,19},{19,3},{4,20},{20... | collective-permute-start | bytes 1572872 | tf_op jit(solution)/shard_map/ppermute | solution.py:231
  33.7 1.0 copy-start.3
  42.9 14.3 %collective-permute-start.5 = (bf16[256,1024]{1,0:T(8,128)(2,1)}, bf16[256,1024]{1,0:T(8,128)(2,1)}, u32[]{:S(2)}, u32[]{:S(2)}) collective-permute-start(bf16[256,1024]{1,0:T(8,128)(2,1)} %get-tuple-element.38), channel_id=1, source_target_pairs={{0,1},{8,11},{1,2},{9,8},{2,3},{10,9},{3,0},{11,10},{4,5},{12,15},... | collective-permute-start | bytes 1572872 | tf_op jit(solution)/shard_map/ppermute | solution.py:228
  44.5 14.5 %collective-permute-start.6 = (bf16[256,1024]{1,0:T(8,128)(2,1)}, bf16[256,1024]{1,0:T(8,128)(2,1)}, u32[]{:S(2)}, u32[]{:S(2)}) collective-permute-start(bf16[256,1024]{1,0:T(8,128)(2,1)} %get-tuple-element.39), channel_id=1, source_target_pairs={{0,3},{8,9},{1,0},{9,10},{2,1},{10,11},{3,2},{11,8},{4,7},{12,13},... | collective-permute-start | bytes 1572872 | tf_op jit(solution)/shard_map/ppermute | solution.py:228
  46.4 16.0 %collective-permute-start.11 = (bf16[256,1024]{1,0:T(8,128)(2,1)}, bf16[256,1024]{1,0:T(8,128)(2,1)}, u32[]{:S(2)}, u32[]{:S(2)}) collective-permute-start(bf16[256,1024]{1,0:T(8,128)(2,1)} %collective-permute-done.10.refs_0_), channel_id=1, source_target_pairs={{0,32},{32,64},{64,96},{96,0},{1,33},{33,65},{65,97},{97,1},{2,34}... | collective-permute-start | bytes 1572872 | tf_op jit(solution)/shard_map/ppermute | solution.py:237
  46.7 15.7 %collective-permute-start.12 = (bf16[256,1024]{1,0:T(8,128)(2,1)}, bf16[256,1024]{1,0:T(8,128)(2,1)}, u32[]{:S(2)}, u32[]{:S(2)}) collective-permute-start(bf16[256,1024]{1,0:T(8,128)(2,1)} %collective-permute-done.10.refs_0_), channel_id=1, source_target_pairs={{0,96},{32,0},{64,32},{96,64},{1,97},{33,1},{65,33},{97,65},{2,98}... | collective-permute-start | bytes 1572872 | tf_op jit(solution)/shard_map/ppermute | solution.py:237
  49.8 9.2 %copy-start.1 = (bf16[256,1024]{1,0:T(8,128)(2,1)S(1)}, bf16[256,1024]{1,0:T(8,128)(2,1)}, u32[]{:S(2)}) copy-start(bf16[256,1024]{1,0:T(8,128)(2,1)} %copy-done) | copy-start | bytes 1572868
  55.2 17.5 %collective-permute-start.13 = (bf16[256,1024]{1,0:T(8,128)(2,1)S(1)}, bf16[256,1024]{1,0:T(8,128)(2,1)S(1)}, u32[]{:S(2)}, u32[]{:S(2)}) collective-permute-start(bf16[256,1024]{1,0:T(8,128)(2,1)S(1)} %get-tuple-element.42), channel_id=1, source_target_pairs={{0,32},{8,104},{32,64},{40,8},{64,96},{72,40},{96,0},{104,72},{1,3... | collective-permute-start | bytes 1572872 | tf_op jit(solution)/shard_map/ppermute | solution.py:225
  57.3 16.2 %collective-permute-start.14 = (bf16[256,1024]{1,0:T(8,128)(2,1)S(1)}, bf16[256,1024]{1,0:T(8,128)(2,1)S(1)}, u32[]{:S(2)}, u32[]{:S(2)}) collective-permute-start(bf16[256,1024]{1,0:T(8,128)(2,1)S(1)} %get-tuple-element.54), channel_id=1, source_target_pairs={{0,96},{8,40},{32,0},{40,72},{64,32},{72,104},{96,64},{104,8},{1,9... | collective-permute-start | bytes 1572872 | tf_op jit(solution)/shard_map/ppermute | solution.py:225
  60.2 17.4 %collective-permute-start.8 = (bf16[256,1024]{1,0:T(8,128)(2,1)S(1)}, bf16[256,1024]{1,0:T(8,128)(2,1)S(1)}, u32[]{:S(2)}, u32[]{:S(2)}) collective-permute-start(bf16[256,1024]{1,0:T(8,128)(2,1)S(1)} %add_convert_fusion.6), channel_id=1, source_target_pairs={{0,1},{8,11},{1,2},{9,8},{2,3},{10,9},{3,0},{11,10},{4,5},{12,15},... | collective-permute-start | bytes 1572872 | tf_op jit(solution)/shard_map/ppermute | solution.py:228
  63.5 14.2 %copy-start.7 = (bf16[256,1024]{1,0:T(8,128)(2,1)S(1)}, bf16[256,1024]{1,0:T(8,128)(2,1)}, u32[]{:S(2)}) copy-start(bf16[256,1024]{1,0:T(8,128)(2,1)} %copy-done.6) | copy-start | bytes 1572868
  63.5 15.5 %collective-permute-start.15 = (bf16[256,1024]{1,0:T(8,128)(2,1)S(1)}, bf16[256,1024]{1,0:T(8,128)(2,1)S(1)}, u32[]{:S(2)}, u32[]{:S(2)}) collective-permute-start(bf16[256,1024]{1,0:T(8,128)(2,1)S(1)} %broadcast_select_fusion), channel_id=1, source_target_pairs={{0,32},{8,104},{32,64},{40,8},{64,96},{72,40},{96,0},{104,72},{1,3... | collective-permute-start | bytes 1572872 | tf_op jit(solution)/shard_map/ppermute | solution.py:225
  73.7 15.9 %collective-permute-start.20 = (bf16[256,1024]{1,0:T(8,128)(2,1)S(1)}, bf16[256,1024]{1,0:T(8,128)(2,1)S(1)}, u32[]{:S(2)}, u32[]{:S(2)}) collective-permute-start(bf16[256,1024]{1,0:T(8,128)(2,1)S(1)} %add_convert_fusion.4), channel_id=1, source_target_pairs={{0,32},{8,104},{32,64},{40,8},{64,96},{72,40},{96,0},{104,72},{1,3... | collective-permute-start | bytes 1572872 | tf_op jit(solution)/shard_map/ppermute | solution.py:225
  74.5 20.7 %collective-permute-start.18 = (bf16[256,1024]{1,0:T(8,128)(2,1)S(1)}, bf16[256,1024]{1,0:T(8,128)(2,1)S(1)}, u32[]{:S(2)}, u32[]{:S(2)}) collective-permute-start(bf16[256,1024]{1,0:T(8,128)(2,1)S(1)} %get-tuple-element.49), channel_id=1, source_target_pairs={{0,32},{8,104},{32,64},{40,8},{64,96},{72,40},{96,0},{104,72},{1,3... | collective-permute-start | bytes 1572872 | tf_op jit(solution)/shard_map/ppermute | solution.py:225
  76.1 19.1 %collective-permute-start.19 = (bf16[256,1024]{1,0:T(8,128)(2,1)S(1)}, bf16[256,1024]{1,0:T(8,128)(2,1)S(1)}, u32[]{:S(2)}, u32[]{:S(2)}) collective-permute-start(bf16[256,1024]{1,0:T(8,128)(2,1)S(1)} %get-tuple-element.50), channel_id=1, source_target_pairs={{0,96},{8,40},{32,0},{40,72},{64,32},{72,104},{96,64},{104,8},{1,9... | collective-permute-start | bytes 1572872 | tf_op jit(solution)/shard_map/ppermute | solution.py:225
  83.1 15.7 %collective-permute-start.16 = (bf16[256,1024]{1,0:T(8,128)(2,1)S(1)}, bf16[256,1024]{1,0:T(8,128)(2,1)S(1)}, u32[]{:S(2)}, u32[]{:S(2)}) collective-permute-start(bf16[256,1024]{1,0:T(8,128)(2,1)S(1)} %get-tuple-element.58), channel_id=1, source_target_pairs={{0,1},{8,11},{1,2},{9,8},{2,3},{10,9},{3,0},{11,10},{4,5},{12,15},... | collective-permute-start | bytes 1572872 | tf_op jit(solution)/shard_map/ppermute | solution.py:228
  84.7 14.0 %collective-permute-start.17 = (bf16[256,1024]{1,0:T(8,128)(2,1)S(1)}, bf16[256,1024]{1,0:T(8,128)(2,1)S(1)}, u32[]{:S(2)}, u32[]{:S(2)}) collective-permute-start(bf16[256,1024]{1,0:T(8,128)(2,1)S(1)} %get-tuple-element.59), channel_id=1, source_target_pairs={{0,3},{8,9},{1,0},{9,10},{2,1},{10,11},{3,2},{11,8},{4,7},{12,13},... | collective-permute-start | bytes 1572872 | tf_op jit(solution)/shard_map/ppermute | solution.py:228
  89.9 13.6 %collective-permute-start.23 = (bf16[256,1024]{1,0:T(8,128)(2,1)S(1)}, bf16[256,1024]{1,0:T(8,128)(2,1)S(1)}, u32[]{:S(2)}, u32[]{:S(2)}) collective-permute-start(bf16[256,1024]{1,0:T(8,128)(2,1)S(1)} %add_convert_fusion.3), channel_id=1, source_target_pairs={{0,16},{16,0},{1,17},{17,1},{2,18},{18,2},{3,19},{19,3},{4,20},{20... | collective-permute-start | bytes 1572872 | tf_op jit(solution)/shard_map/ppermute | solution.py:231
  95.4 10.5 %collective-permute-start.22 = (bf16[256,1024]{1,0:T(8,128)(2,1)S(1)}, bf16[256,1024]{1,0:T(8,128)(2,1)S(1)}, u32[]{:S(2)}, u32[]{:S(2)}) collective-permute-start(bf16[256,1024]{1,0:T(8,128)(2,1)S(1)} %add_convert_fusion.2), channel_id=1, source_target_pairs={{0,32},{8,104},{32,64},{40,8},{64,96},{72,40},{96,0},{104,72},{1,3... | collective-permute-start | bytes 1572872 | tf_op jit(solution)/shard_map/ppermute | solution.py:225
  99.0 10.5 %collective-permute-start.21 = (bf16[256,1024]{1,0:T(8,128)(2,1)S(1)}, bf16[256,1024]{1,0:T(8,128)(2,1)S(1)}, u32[]{:S(2)}, u32[]{:S(2)}) collective-permute-start(bf16[256,1024]{1,0:T(8,128)(2,1)S(1)} %add_convert_fusion.1), channel_id=1, source_target_pairs={{0,1},{8,11},{1,2},{9,8},{2,3},{10,9},{3,0},{11,10},{4,5},{12,15},... | collective-permute-start | bytes 1572872 | tf_op jit(solution)/shard_map/ppermute | solution.py:228
  99.1 10.8 %collective-permute-start.9 = (bf16[128,1024]{1,0:T(8,128)(2,1)S(1)}, bf16[128,1024]{1,0:T(8,128)(2,1)S(1)}, u32[]{:S(2)}, u32[]{:S(2)}) collective-permute-start(bf16[128,1024]{1,0:T(8,128)(2,1)S(1)} %get-tuple-element.70), channel_id=1, source_target_pairs={{0,8},{8,0},{1,9},{9,1},{2,10},{10,2},{3,11},{11,3},{4,12},{12,4},... | collective-permute-start | bytes 786440 | tf_op jit(solution)/shard_map/ppermute | solution.py:234
  109.7 1.6 %collective-permute-start.24 = (bf16[128,1024]{1,0:T(8,128)(2,1)S(1)}, bf16[128,1024]{1,0:T(8,128)(2,1)S(1)}, u32[]{:S(2)}, u32[]{:S(2)}) collective-permute-start(bf16[128,1024]{1,0:T(8,128)(2,1)S(1)} %get-tuple-element.68), channel_id=1, source_target_pairs={{0,8},{8,0},{1,9},{9,1},{2,10},{10,2},{3,11},{11,3},{4,12},{12,4},... | collective-permute-start | bytes 786440 | tf_op jit(solution)/shard_map/ppermute | solution.py:234
  (4 other events, 3.7 us)
